TPU v7x, 32 devices: a whole 2x2x4 slice. The times are simulated.
32 devices in a mesh: rep: 2 (over y), prow: 4 (over z), pcol: 4 (over x, core).
Axes of the slice: x: 2, y: 2, z: 4, core: 2. Of those that a mesh axis runs over, the one named last changes fastest.
Arguments:
- homolog_features: bfloat16 [256, 64, 64], P('rep', ('pcol', 'prow')), parts along dimension 0, may hold values from -6 to 6
- subset_homolog_positions: int32 [128], P('rep'), parts along dimension 0, may hold values from 0 to 127, as said below
- first_side_matrix: bfloat16 [64, 32], replicated, may hold values from -0.75 to 0.75
- second_side_matrix: bfloat16 [64, 32], replicated, may hold values from -0.75 to 0.75
- final_mapping_matrix: bfloat16 [1024, 128], replicated, may hold values from -1.5 to 1.5
- final_offset_vector: float32 [128], replicated, may hold values from -6 to 6
- upstream_sensitivity: bfloat16 [128, 64, 128], P(('rep', 'prow'), 'pcol'), parts along dimension 0, may hold values from -0.25 to 0.25
Outputs:
- pair_delta: bfloat16 [128, 64, 128], P(('rep', 'prow'), 'pcol'), parts along dimension 0
- alignment_gradient: bfloat16 [128, 64, 64], P('rep', ('pcol', 'prow')), parts along dimension 0
- left_weight_gradient: float32 [128, 32], P('rep'), parts along dimension 0
- right_weight_gradient: float32 [128, 32], P('rep'), parts along dimension 0
- output_weight_gradient: float32 [2048, 128], P('rep'), parts along dimension 0
There are 2 independent parts, one for each index of `rep`. A program takes and returns all parts, laid end to end along the dimension named above; an argument that names none is the same for every part. Nothing has to cross between parts.
Inputs may be any that keep to these rules, and one draw needn't show every extreme that they name: `subset_homolog_positions`: the indices are distinct; 0 and 127 are always among them.
All inputs are finite; a program needn't handle non-finite values.
Results may differ from a plain program's by a relative error of at most 0.0075.
Values may be sent and summed in bfloat16 or wider, within the bound.
No kernel may reach another device: no remote copies, remote signals or barrier semaphores. Data moves between devices by JAX's collectives and lax.ppermute only.
A program may use at most 64 MiB of HBM per device.

v0:
```python
import jax
import jax.numpy as jnp
from jax import lax
from jax.sharding import PartitionSpec as P


def normalize(values):
    values = values.astype(jnp.float32)
    mean_factor = jnp.mean(values, axis=-1, keepdims=True)
    centered = values - mean_factor
    variance = jnp.mean(centered * centered, axis=-1, keepdims=True)
    inverse_spread = lax.rsqrt(variance + 1e-05)
    return (centered * inverse_spread, inverse_spread)


def local(
    homolog_features,
    subset_homolog_positions,
    first_side_matrix,
    second_side_matrix,
    final_mapping_matrix,
    final_offset_vector,
    upstream_sensitivity,
):
    seq_count = subset_homolog_positions.shape[0]
    row_count = upstream_sensitivity.shape[0]
    col_count = upstream_sensitivity.shape[1]
    pair_width = upstream_sensitivity.shape[2]
    proj_width = first_side_matrix.shape[1]
    picked_homologs = jnp.take(homolog_features, subset_homolog_positions, axis=0)
    normalized_input, inverse_spread = normalize(picked_homologs)
    normed_low = normalized_input.astype(jnp.bfloat16)
    left_proj = jnp.einsum(
        "stc,cp->stp", normed_low, first_side_matrix, preferred_element_type=jnp.float32
    ).astype(jnp.bfloat16)
    right_proj = jnp.einsum(
        "stc,cp->stp", normed_low, second_side_matrix, preferred_element_type=jnp.float32
    ).astype(jnp.bfloat16)
    left_cols, right_cols = (
        lax.all_gather(left_proj, "prow", axis=1, tiled=True),
        lax.all_gather(right_proj, "prow", axis=1, tiled=True),
    )
    row_index = lax.axis_index("prow")
    col_index = lax.axis_index("pcol")
    owner_col = row_index * row_count // col_count
    slot_start = jnp.clip(row_index * row_count - col_index * col_count, 0, col_count - row_count)
    left_all = lax.all_gather(left_cols, "pcol", axis=1, tiled=True)
    left_rows = lax.dynamic_slice_in_dim(left_all, row_index * row_count, row_count, 1)
    row_block = 8
    block_count = row_count // row_block
    left_blocks = left_rows.reshape(seq_count, block_count, row_block, proj_width).transpose(
        1, 0, 2, 3
    )
    cot_blocks = upstream_sensitivity.reshape(block_count, row_block, col_count, pair_width)

    def block_step(totals, inputs):
        grad_out, grad_right = totals
        left_blk, cot_blk = inputs
        outer_sum = jnp.einsum(
            "sip,sjq->ijpq", left_blk, right_cols, preferred_element_type=jnp.float32
        )
        outer_mean = (outer_sum / seq_count).astype(jnp.bfloat16)
        outer_flat = outer_mean.reshape(row_block * col_count, proj_width * proj_width)
        update = (
            jnp.dot(outer_flat, final_mapping_matrix, preferred_element_type=jnp.float32)
            + final_offset_vector
        )
        cot_flat = cot_blk.reshape(row_block * col_count, pair_width)
        grad_out = grad_out + jnp.dot(outer_flat.T, cot_flat, preferred_element_type=jnp.float32)
        grad_outer = jnp.dot(
            cot_flat, final_mapping_matrix.T, preferred_element_type=jnp.float32
        ).astype(jnp.bfloat16)
        grad_outer = grad_outer.reshape(row_block, col_count, proj_width, proj_width)
        grad_left_blk = (
            jnp.einsum("ijpq,sjq->sip", grad_outer, right_cols, preferred_element_type=jnp.float32)
            / seq_count
        )
        grad_right = (
            grad_right
            + jnp.einsum("ijpq,sip->sjq", grad_outer, left_blk, preferred_element_type=jnp.float32)
            / seq_count
        )
        return (
            (grad_out, grad_right),
            (update.astype(jnp.bfloat16).reshape(row_block, col_count, pair_width), grad_left_blk),
        )

    start_totals = (
        jnp.zeros((proj_width * proj_width, pair_width), jnp.float32),
        jnp.zeros((seq_count, col_count, proj_width), jnp.float32),
    )
    (grad_out_part, grad_right_part), (updates, grad_left_blocks) = lax.scan(
        block_step, start_totals, (left_blocks, cot_blocks)
    )
    pair_delta = updates.reshape(row_count, col_count, pair_width)
    grad_left_part = grad_left_blocks.transpose(1, 0, 2, 3).reshape(
        seq_count, row_count, proj_width
    )
    left_summed = lax.psum(grad_left_part, "pcol")
    is_owner = owner_col == col_index
    padded = lax.dynamic_update_slice_in_dim(
        jnp.zeros_like(grad_right_part), left_summed * is_owner.astype(jnp.float32), slot_start, 1
    )
    grad_left_tok, grad_right_tok = (
        lax.psum_scatter(padded, "prow", scatter_dimension=1, tiled=True),
        lax.psum_scatter(grad_right_part, "prow", scatter_dimension=1, tiled=True),
    )
    grad_left = grad_left_tok.astype(jnp.bfloat16)
    grad_right = grad_right_tok.astype(jnp.bfloat16)
    grad_a_part = jnp.einsum(
        "stc,stp->cp", normed_low, grad_left, preferred_element_type=jnp.float32
    )
    grad_b_part = jnp.einsum(
        "stc,stp->cp", normed_low, grad_right, preferred_element_type=jnp.float32
    )
    output_weight_gradient, left_weight_gradient, right_weight_gradient = lax.psum(
        (grad_out_part, grad_a_part, grad_b_part), ("prow", "pcol")
    )
    normalized_gradient = jnp.einsum(
        "stp,cp->stc", grad_left, first_side_matrix, preferred_element_type=jnp.float32
    )
    normalized_gradient = normalized_gradient + jnp.einsum(
        "stp,cp->stc", grad_right, second_side_matrix, preferred_element_type=jnp.float32
    )
    mean_factor = jnp.mean(normalized_gradient, axis=-1, keepdims=True)
    projected_outer = jnp.mean(normalized_gradient * normalized_input, axis=-1, keepdims=True)
    alignment_gradient = (
        inverse_spread * (normalized_gradient - mean_factor - normalized_input * projected_outer)
    ).astype(jnp.bfloat16)
    return (
        pair_delta,
        alignment_gradient,
        left_weight_gradient,
        right_weight_gradient,
        output_weight_gradient,
    )


def solution(mesh):
    return jax.shard_map(
        local,
        mesh=mesh,
        in_specs=(
            P("rep", ("pcol", "prow"), None),
            P("rep"),
            P(),
            P(),
            P(),
            P(),
            P(("rep", "prow"), "pcol", None),
        ),
        out_specs=(
            P(("rep", "prow"), "pcol", None),
            P("rep", ("pcol", "prow"), None),
            P("rep", None),
            P("rep", None),
            P("rep", None),
        ),
        check_vma=False,
    )
```

profile of v0, /device:TPU:0, one launch (start us, length us, event | category | flops | bytes accessed | tf_op | source)
XLA Modules:
  0.0 203.3 jit_solution(8753294090800989414)
XLA Ops:
  8.1 0.7 compare_and_fusion
  9.4 1.0 copy.27
  10.5 0.7 gather_fusion
  11.3 0.8 convolution_convert_fusion.2
  12.3 15.1 %all_gather.11 = bf16[64,16,32]{0,2,1:T(8,128)(2,1)S(1)} all-gather(bf16[64,4,32]{0,2,1:T(8,128)(2,1)S(1)} %convolution_convert_fusion.1), channel_id=1, replica_groups=mesh['rep'=2,'prow'=4,'pcol'=4] {'prow'}, dimensions={1}, use_global_device_ids=true | all-gather | bytes 81920 | tf_op jit(solution)/shard_map/all_gather | solution.py:41
  27.4 13.5 %all_gather.9 = bf16[64,16,32]{0,2,1:T(8,128)(2,1)S(1)} all-gather(bf16[64,4,32]{0,2,1:T(8,128)(2,1)S(1)} %convolution_convert_fusion.2), channel_id=1, replica_groups=mesh['rep'=2,'prow'=4,'pcol'=4] {'prow'}, dimensions={1}, use_global_device_ids=true | all-gather | bytes 81920 | tf_op jit(solution)/shard_map/all_gather | solution.py:40
  40.9 7.2 %all_gather.10 = bf16[64,64,32]{0,2,1:T(8,128)(2,1)S(1)} all-gather(bf16[64,16,32]{0,2,1:T(8,128)(2,1)S(1)} %all_gather.9), channel_id=1, replica_groups=mesh['rep'=2,'prow'=4,'pcol'=4] {'pcol'}, dimensions={1}, use_global_device_ids=true | all-gather | bytes 327680 | tf_op jit(solution)/shard_map/all_gather | solution.py:47
  48.1 8.1 %while.17 = (s32[]{:T(128)}, f32[1024,128]{1,0:T(8,128)S(1)}, f32[64,16,32]{0,2,1:T(8,128)S(1)}, bf16[2,8,16,128]{3,2,1,0:T(8,128)(2,1)S(1)}, f32[2,64,8,32]{1,3...) while((s32[]{:T(128)}, f32[1024,128]{1,0:T(8,128)S(1)}, ...), condition=%wide.region_3.4_spmd.clone, body=%wide.region_2.3_spmd.clone.sunk | while | flops 151797760 | bytes 6914712 | solution.py:92
  48.5 1.1 reshape.86
  50.5 0.8 reshape.87
  52.6 1.1 reshape.86
  54.5 0.8 reshape.87
  56.9 0.7 reduce-scatter.5.cloned.1.call-update
  57.7 32.0 %all-reduce.4.cloned.1.call-done = f32[64,16,32]{0,2,1:T(8,128)} async-done(((f32[64,16,32]{0,2,1:T(8,128)}), f32[64,16,32]{0,2,1:T(8,128)}) %all-reduce.4.cloned.1.call-update) | async-done | bytes 131088 | tf_op jit(solution)/shard_map/psum | solution.py:99
  89.7 1.7 broadcast_multiply_fusion
  91.9 19.8 %reduce-scatter.5.cloned.1.call-done = f32[64,4,32]{0,2,1:T(8,128)} async-done(((f32[64,16,32]{0,2,1:T(8,128)}), f32[64,4,32]{0,2,1:T(8,128)}) %reduce-scatter.5.cloned.1.call-update) | async-done | bytes 32784 | tf_op jit(solution)/shard_map/reduce_scatter | solution.py:106
  111.8 1.0 convolution_bitcast_fusion.2
  112.8 19.3 %reduce-scatter.3.cloned.1.call-done = f32[64,4,32]{0,2,1:T(8,128)} async-done(((f32[64,16,32]{0,2,1:T(8,128)}), f32[64,4,32]{0,2,1:T(8,128)}) %reduce-scatter.3.cloned.1.call-update) | async-done | bytes 32784 | tf_op jit(solution)/shard_map/reduce_scatter | solution.py:105
  132.0 1.0 fusion.28
  133.1 1.1 fusion.38
  134.2 0.7 copy.33
  135.0 1.0 convolution_bitcast_fusion.3
  136.0 58.3 %all-reduce = (f32[64,32]{0,1:T(8,128)}, f32[64,32]{0,1:T(8,128)}) all-reduce(f32[64,32]{0,1:T(8,128)S(1)} %convolution_bitcast_fusion.3, f32[64,32]{0,1:T(8,128)S(1)} %convolution_bitcast_fusion.2), channel_id=1, replica_groups=mesh['rep'=2,'prow'=4,'pcol'=4] {'prow','pcol'}, use_global_device_ids=true, to_apply=%region_9.10 | all-reduce | flops 4096 | bytes 32768 | tf_op jit(solution)/shard_map/psum | solution.py:116
  194.3 1.9 copy.62
  (55 shorter events, 6.6 us)
Async XLA Ops:
  8.0 4.2 %copy-start = (bf16[64,32]{0,1:T(8,128)(2,1)S(1)}, bf16[64,32]{0,1:T(8,128)(2,1)}, u32[]{:S(2)}) copy-start(bf16[64,32]{0,1:T(8,128)(2,1)} %param.12) | copy-start | bytes 12292
  8.0 81.6 %all-reduce.4.cloned.1.call-start = ((), (), s32[]{:S(2)}) async-start(), calls=%async_computation.2 | async-start | bytes 524288 | tf_op jit(solution)/shard_map/psum | solution.py:99
  9.4 38.6 %copy-start.1 = (bf16[1024,128]{1,0:T(8,128)(2,1)S(1)}, bf16[1024,128]{1,0:T(8,128)(2,1)}, u32[]{:S(2)}) copy-start(bf16[1024,128]{1,0:T(8,128)(2,1)} %param.13) | copy-start | bytes 786436
  9.4 38.6 %copy-start.4 = (bf16[16,16,128]{2,1,0:T(8,128)(2,1)S(1)}, bf16[16,16,128]{2,1,0:T(8,128)(2,1)}, u32[]{:S(2)}) copy-start(bf16[16,16,128]{2,1,0:T(8,128)(2,1)} %param.15) | copy-start | bytes 196612
  9.4 38.6 %copy-start.6 = (f32[128]{0:T(128)S(1)}, f32[128]{0:T(128)}, u32[]{:S(2)}) copy-start(f32[128]{0:T(128)} %param.14) | copy-start | bytes 1540
  56.1 0.7 copy-start.5
  56.2 0.8 copy-start.3
  56.2 35.2 %copy-start.2 = (f32[1024,128]{1,0:T(8,128)}, f32[1024,128]{1,0:T(8,128)S(1)}, u32[]{:S(2)}) copy-start(f32[1024,128]{1,0:T(8,128)S(1)} %get-tuple-element.63) | copy-start | bytes 1572868
  56.2 76.9 %copy-start.8 = (bf16[2,8,16,128]{3,2,1,0:T(8,128)(2,1)}, bf16[2,8,16,128]{3,2,1,0:T(8,128)(2,1)S(1)}, u32[]{:S(2)}) copy-start(bf16[2,8,16,128]{3,2,1,0:T(8,128)(2,1)S(1)} %get-tuple-element.60) | copy-start | bytes 196612
  56.2 75.9 %copy-start.7 = (bf16[64,32]{0,1:T(8,128)(2,1)S(1)}, bf16[64,32]{0,1:T(8,128)(2,1)}, u32[]{:S(2)}) copy-start(bf16[64,32]{0,1:T(8,128)(2,1)} %param.11) | copy-start | bytes 12292
  56.9 54.9 %reduce-scatter.5.cloned.1.call-start = ((), (), s32[]{:S(2)}) async-start(), calls=%async_computation.4 | async-start | bytes 327680 | tf_op jit(solution)/shard_map/reduce_scatter | solution.py:106
  57.6 74.4 %reduce-scatter.3.cloned.1.call-start = ((), (), s32[]{:S(2)}) async-start(), calls=%async_computation.3 | async-start | bytes 327680 | tf_op jit(solution)/shard_map/reduce_scatter | solution.py:105
  91.4 102.9 %all-reduce.6.cloned.1.call-start = ((), (), s32[]{:S(2)}) async-start(), calls=%async_computation.5 | async-start | bytes 1048576 | tf_op jit(solution)/shard_map/psum | solution.py:116
Sparse Core Ops, SparseCore 0:
  57.0 32.6 all-reduce.3
  92.0 19.7 reduce-scatter.4
  114.0 17.9 reduce-scatter.2
Sparse Core Ops, SparseCore 1:
  96.2 90.9 all-reduce.5
where the time goes:
time: 204 us; the launch traced here: 203 us
  blocking collectives  94 us (46%)
  waiting for transfers between devices  72.3 us (35%)
  between operations  15.4 us (8%)
  matrix products  9.1 us (4%)
  local copies, waits for them, and re-layouts  8.98 us (4%)
  other arithmetic  3.16 us (2%)
    psum x1, blocking collectives, local(): lax.psum((grad_out_part, grad_a_part, grad_b_part), ('prow', 'pcol'))  58.3 us
    psum x1, waiting for transfers between devices, local(): left_summed = lax.psum(grad_left_part, 'pcol')  32 us
    reduce_scatter x1, waiting for transfers between devices, local(): lax.psum_scatter(grad_right_part, 'prow', scatter_dimension=1, tiled=True)  19.8 us
    reduce_scatter x1, waiting for transfers between devices, local(): lax.psum_scatter(padded, 'prow', scatter_dimension=1, tiled=True)  19.3 us
    all_gather x1, blocking collectives, local(): lax.all_gather(right_proj, 'prow', axis=1, tiled=True)  15.1 us
    all_gather x1, blocking collectives, local(): lax.all_gather(left_proj, 'prow', axis=1, tiled=True)  13.5 us
    all_gather x1, blocking collectives, local(): left_all = lax.all_gather(left_cols, 'pcol', axis=1, tiled=True)  7.16 us
    unnamed x21, local copies, waits for them, and re-layouts  4.33 us
  transfers between devices with their start and end apart: 4, of which 3 were waited for; matrix products, arithmetic and copies ran while one was open for 3% of the time, Pallas kernels for 0%

commit v1 on v0

v1 whole, which is shorter than its diff:
```python
import jax
import jax.numpy as jnp
from jax import lax
from jax.sharding import PartitionSpec as P

PAIRS_AT_ONCE = 1024


def normalize(values):
    values = values.astype(jnp.float32)
    mean_factor = jnp.mean(values, axis=-1, keepdims=True)
    centered = values - mean_factor
    variance = jnp.mean(centered * centered, axis=-1, keepdims=True)
    inverse_spread = lax.rsqrt(variance + 1e-05)
    return (centered * inverse_spread, inverse_spread)


def row_routes(rows_n, cols_n):
    routes = []
    for k in range(cols_n):
        pairs = []
        for l in range(rows_n * cols_n):
            c, r = divmod(l, rows_n)
            pairs.append((r * cols_n + c, (l // cols_n) * cols_n + (l + k) % cols_n))
        routes.append(pairs)
    return routes


def col_routes(rows_n, cols_n):
    return [
        [
            (r * cols_n + c, (r + k) % rows_n * cols_n + c)
            for r in range(rows_n)
            for c in range(cols_n)
        ]
        for k in range(rows_n)
    ]


def back(pairs):
    return [(target, source) for source, target in pairs]


def local(
    homolog_features,
    subset_homolog_positions,
    first_side_matrix,
    second_side_matrix,
    final_mapping_matrix,
    final_offset_vector,
    upstream_sensitivity,
):
    axes = ("prow", "pcol")
    rows_n, cols_n = lax.axis_size("prow"), lax.axis_size("pcol")
    devices = rows_n * cols_n
    row_index, col_index = lax.axis_index("prow"), lax.axis_index("pcol")
    seq_count = subset_homolog_positions.shape[0]
    tokens = homolog_features.shape[1]
    row_count, col_count, pair_width = upstream_sensitivity.shape
    proj = first_side_matrix.shape[1]
    flat = proj * proj

    picked = jnp.take(homolog_features, subset_homolog_positions, axis=0)
    normed, inverse_spread = normalize(picked)
    normed_low = normed.astype(jnp.bfloat16)

    def project(matrix):
        out = jnp.einsum("stc,cp->stp", normed_low, matrix, preferred_element_type=jnp.float32)
        return out.astype(jnp.bfloat16).reshape(seq_count, tokens * proj)

    left_own, right_own = project(first_side_matrix), project(second_side_matrix)
    to_rows, to_cols = row_routes(rows_n, cols_n), col_routes(rows_n, cols_n)
    left_parts = [lax.ppermute(left_own, axes, pairs) for pairs in to_rows]
    right_parts = [right_own] + [lax.ppermute(right_own, axes, pairs) for pairs in to_cols[1:]]
    left = jnp.concatenate(left_parts, axis=1).reshape(seq_count, row_count, proj)
    right = jnp.concatenate(right_parts, axis=1).reshape(seq_count, col_count, proj)

    row_order = (col_index - jnp.arange(cols_n)) % cols_n
    col_order = (row_index - jnp.arange(rows_n)) % rows_n

    def reorder(pairs):
        pairs = pairs.reshape(cols_n, tokens, rows_n, tokens, pair_width)
        return jnp.take(jnp.take(pairs, row_order, axis=0), col_order, axis=2)

    cot = reorder(upstream_sensitivity).reshape(row_count, col_count, pair_width)

    def block_step(left_blk, cot_blk):
        rows = left_blk.shape[1]
        outer = jnp.einsum("sip,sjq->ijpq", left_blk, right, preferred_element_type=jnp.float32)
        outer = (outer / seq_count).astype(jnp.bfloat16).reshape(rows * col_count, flat)
        update = jnp.dot(outer, final_mapping_matrix, preferred_element_type=jnp.float32)
        update = (update + final_offset_vector).astype(jnp.bfloat16)
        cot_flat = cot_blk.reshape(rows * col_count, pair_width)
        grad_out = jnp.dot(outer.T, cot_flat, preferred_element_type=jnp.float32)
        grad_outer = jnp.dot(cot_flat, final_mapping_matrix.T, preferred_element_type=jnp.float32)
        grad_outer = grad_outer.astype(jnp.bfloat16).reshape(rows, col_count, proj, proj)
        grad_left = jnp.einsum(
            "ijpq,sjq->sip", grad_outer, right, preferred_element_type=jnp.float32
        )
        grad_right = jnp.einsum(
            "ijpq,sip->sjq", grad_outer, left_blk, preferred_element_type=jnp.float32
        )
        return update.reshape(rows, col_count, pair_width), grad_out, grad_left, grad_right

    block = max(1, min(row_count, PAIRS_AT_ONCE // col_count))
    blocks = row_count // block
    if blocks == 1:
        update, grad_out, grad_left, grad_right = block_step(left, cot)
    else:
        def step(totals, inputs):
            update, grad_out, grad_left, grad_right = block_step(*inputs)
            return (totals[0] + grad_out, totals[1] + grad_right), (update, grad_left)

        (grad_out, grad_right), (update, grad_left) = lax.scan(
            step,
            (
                jnp.zeros((flat, pair_width), jnp.float32),
                jnp.zeros((seq_count, col_count, proj), jnp.float32),
            ),
            (
                left.reshape(seq_count, blocks, block, proj).transpose(1, 0, 2, 3),
                cot.reshape(blocks, block, col_count, pair_width),
            ),
        )
        grad_left = grad_left.transpose(1, 0, 2, 3)
    pair_delta = reorder(update).reshape(row_count, col_count, pair_width)

    shares = grad_out.astype(jnp.bfloat16).reshape(devices, flat // devices, pair_width)
    shares = lax.all_to_all(shares, axes, 0, 0)
    share = jnp.sum(shares.astype(jnp.float32), axis=0).astype(jnp.bfloat16)

    def send_back(grads, count, routes):
        grads = (grads / seq_count).astype(jnp.bfloat16).reshape(seq_count, count, tokens * proj)
        total = 0.0
        for k, pairs in enumerate(routes):
            part = grads[:, k]
            if pairs[0][0] != pairs[0][1] or any(a != b for a, b in pairs):
                part = lax.ppermute(part, axes, back(pairs))
            total = total + part.astype(jnp.float32)
        return total.astype(jnp.bfloat16).reshape(seq_count, tokens, proj)

    grad_left = send_back(grad_left, cols_n, to_rows)
    grad_right = send_back(grad_right, rows_n, to_cols)

    both = jnp.concatenate([grad_left, grad_right], axis=-1)
    side_part = jnp.einsum("stc,stp->cp", normed_low, both, preferred_element_type=jnp.float32)
    features = side_part.shape[0]
    side_rows = features * 2 * proj // pair_width
    message = jnp.concatenate(
        [share, side_part.astype(jnp.bfloat16).reshape(side_rows, pair_width)], axis=0
    )
    message = jnp.broadcast_to(message[None], (devices,) + message.shape)
    message = lax.all_to_all(message, axes, 0, 0)
    output_weight_gradient = (
        message[:, : flat // devices].reshape(flat, pair_width).astype(jnp.float32)
    )
    side = jnp.sum(message[:, flat // devices :].astype(jnp.float32), axis=0)
    side = side.reshape(features, 2 * proj)
    left_weight_gradient, right_weight_gradient = side[:, :proj], side[:, proj:]

    sides = jnp.concatenate([first_side_matrix, second_side_matrix], axis=1)
    grad_normed = jnp.einsum("stp,cp->stc", both, sides, preferred_element_type=jnp.float32)
    mean_factor = jnp.mean(grad_normed, axis=-1, keepdims=True)
    projected = jnp.mean(grad_normed * normed, axis=-1, keepdims=True)
    alignment_gradient = (
        inverse_spread * (grad_normed - mean_factor - normed * projected)
    ).astype(jnp.bfloat16)
    return (
        pair_delta,
        alignment_gradient,
        left_weight_gradient,
        right_weight_gradient,
        output_weight_gradient,
    )


def solution(mesh):
    return jax.shard_map(
        local,
        mesh=mesh,
        in_specs=(
            P("rep", ("pcol", "prow"), None),
            P("rep"),
            P(),
            P(),
            P(),
            P(),
            P(("rep", "prow"), "pcol", None),
        ),
        out_specs=(
            P(("rep", "prow"), "pcol", None),
            P("rep", ("pcol", "prow"), None),
            P("rep", None),
            P("rep", None),
            P("rep", None),
        ),
        check_vma=False,
    )
```

time: 204 us -> 84.1 us (0.41)
  blocking collectives: 94 us -> 0 us
  waiting for transfers between devices: 72.3 us -> 19.1 us
  starting transfers between devices: 0.16 us -> 35.4 us
  between operations: 15.4 us -> 0.96 us
  local copies, waits for them, and re-layouts: 8.98 us -> 16.2 us
    psum x1 -> x0, blocking collectives: 58.3 us -> none  [local(): lax.psum((grad_out_part, grad_a_part, grad_b_part), ('prow', 'pcol'))]
    reduce_scatter x2 -> x0, waiting for transfers between devices: 39.1 us -> none  [the longest x1 19.8 us: local(): lax.psum_scatter(grad_right_part, 'prow', scatter_dimension=1, tiled=True)]
    all_gather x3 -> x0, blocking collectives: 35.7 us -> none  [the longest x1 15.1 us: local(): lax.all_gather(right_proj, 'prow', axis=1, tiled=True)]
    psum x2 -> x0, waiting for transfers between devices: 32 us -> none  [the longest x1 32 us: local(): left_summed = lax.psum(grad_left_part, 'pcol')]
    ppermute x0 -> x14, starting transfers between devices: none -> 25.8 us  [the longest x7 11.9 us: send_back(): part = lax.ppermute(part, axes, back(pairs))]
    all_to_all x0 -> x2, waiting for transfers between devices: none -> 10.2 us  [the longest x1 10.2 us: local(): message = lax.all_to_all(message, axes, 0, 0)]
    all_to_all x0 -> x2, starting transfers between devices: none -> 9.57 us  [the longest x1 5.13 us: local(): shares = lax.all_to_all(shares, axes, 0, 0)]
    ppermute x0 -> x14, waiting for transfers between devices: none -> 8.85 us  [the longest x7 5.77 us: send_back(): part = lax.ppermute(part, axes, back(pairs))]
  transfers between devices with their start and end apart: 4 -> 16, of which waited for: 3 -> 6; matrix products, arithmetic and copies ran while one was open for 3% -> 11% of each run, Pallas kernels for 0% -> 0%
where the time goes in v1:
time: 84.1 us; the launch traced here: 83.5 us
  starting transfers between devices  35.4 us (42%)
  waiting for transfers between devices  19.1 us (23%)
  local copies, waits for them, and re-layouts  16.2 us (19%)
  matrix products  7.31 us (9%)
  other arithmetic  4.51 us (5%)
  between operations  0.96 us (1%)
    ppermute x7, starting transfers between devices, send_back(): part = lax.ppermute(part, axes, back(pairs))  11.9 us
    all_to_all x1, waiting for transfers between devices, local(): message = lax.all_to_all(message, axes, 0, 0)  10.2 us
    ppermute x4, starting transfers between devices, local(): left_parts = [lax.ppermute(left_own, axes, pairs) for pairs in to_rows]  9.91 us
    ppermute x7, waiting for transfers between devices, send_back(): part = lax.ppermute(part, axes, back(pairs))  5.77 us
    all_to_all x1, starting transfers between devices, local(): shares = lax.all_to_all(shares, axes, 0, 0)  5.13 us
    all_to_all x1, starting transfers between devices, local(): message = lax.all_to_all(message, axes, 0, 0)  4.44 us
    ppermute x3, starting transfers between devices, local(): lax.ppermute(right_own, axes, pairs)  4.01 us
    gather x4, local copies, waits for them, and re-layouts, reorder(): return jnp.take(jnp.take(pairs, row_order, axis=0), col_order, axis=2)  3.31 us
  transfers between devices with their start and end apart: 16, of which 6 were waited for; matrix products, arithmetic and copies ran while one was open for 11% of the time, Pallas kernels for 0%

profile of v1, /device:TPU:0, one launch (start us, length us, event | category | flops | bytes accessed | tf_op | source)
XLA Modules:
  0.0 83.5 jit_solution(9480516905662802374)
XLA Ops:
  2.0 1.0 %copy.33 = bf16[128,4,64]{2,1,0:T(4,128)(2,1)S(1)} copy(bf16[128,4,64]{0,2,1:T(8,128)(2,1)} %param.11) | data formatting | bytes 131072 | tf_op args[0]
  3.9 0.8 %convolution_convert_fusion.2 = bf16[64,4,32]{0,2,1:T(8,128)(2,1)S(1)} fusion(f32[64,4]{0,1:T(4,128)S(1)} %add_rsqrt_fusion, f32[64,4]{0,1:T(4,128)S(1)} %broadcast_multiply_fusion.2, bf16[64,4,64]{0,2,1:T(8,128)(2,1)S(1)} %copy.34, pred[64]{0:T(512)(128)(4,1)S(1)} %compare_and_fusion.2, bf16[64,32]{0,1:T(8,128)(2,1)} %param.13), kind=kOutput, calls=%fused_computation.17 | convolution fusion | flops 1138688 | bytes 55360 | tf_op jit(solution)/shard_map/stc,cp->stp/dot_general | solution.py:68
  5.4 4.4 %collective-permute-start.4 = (bf16[64,128]{0,1:T(8,128)(2,1)S(1)}, bf16[64,128]{0,1:T(8,128)(2,1)S(1)}, u32[]{:S(2)}, u32[]{:S(2)}) collective-permute-start(bf16[64,128]{0,1:T(8,128)(2,1)S(1)} %bitcast.120), channel_id=1, source_target_pairs={{0,1},{4,2},{8,3},{12,0},{1,5},{5,6},{9,7},{13,4},{2,9},{6,10},{10... | collective-permute-start | bytes 49160 | tf_op jit(solution)/shard_map/ppermute | solution.py:73
  9.8 3.5 %collective-permute-start.5 = (bf16[64,128]{0,1:T(8,128)(2,1)S(1)}, bf16[64,128]{0,1:T(8,128)(2,1)S(1)}, u32[]{:S(2)}, u32[]{:S(2)}) collective-permute-start(bf16[64,128]{0,1:T(8,128)(2,1)S(1)} %bitcast.121), channel_id=1, source_target_pairs={{0,2},{4,3},{8,0},{12,1},{1,6},{5,7},{9,4},{13,5},{2,10},{6,11},{1... | collective-permute-start | bytes 49160 | tf_op jit(solution)/shard_map/ppermute | solution.py:73
  13.3 1.3 %collective-permute-start.6 = (bf16[64,128]{0,1:T(8,128)(2,1)S(1)}, bf16[64,128]{0,1:T(8,128)(2,1)S(1)}, u32[]{:S(2)}, u32[]{:S(2)}) collective-permute-start(bf16[64,128]{0,1:T(8,128)(2,1)S(1)} %bitcast.122), channel_id=1, source_target_pairs={{0,3},{4,0},{8,1},{12,2},{1,7},{5,4},{9,5},{13,6},{2,11},{6,8},{10... | collective-permute-start | bytes 49160 | tf_op jit(solution)/shard_map/ppermute | solution.py:73
  17.3 1.4 %gather_fusion.3 = bf16[4,4,4,4,128]{4,3,2,1,0:T(4,128)(2,1)S(1)} fusion(bf16[4,4,4,4,128]{4,3,2,1,0:T(4,128)(2,1)} %bitcast.108, s32[1024]{0:T(1024)S(1)} %pad_clamp_fusion.1), kind=kCustom, calls=%fused_computation.2.clone | custom fusion | bytes 131088 | tf_op jit(solution)/shard_map/jit(_take)/gather | solution.py:83
  18.8 2.5 %collective-permute-start.1 = (bf16[64,128]{0,1:T(8,128)(2,1)S(1)}, bf16[64,128]{0,1:T(8,128)(2,1)S(1)}, u32[]{:S(2)}, u32[]{:S(2)}) collective-permute-start(bf16[64,128]{0,1:T(8,128)(2,1)S(1)} %bitcast.111), channel_id=1, source_target_pairs={{0,8},{1,9},{2,10},{3,11},{4,12},{5,13},{6,14},{7,15},{8,0},{9,1},... | collective-permute-start | bytes 49160 | tf_op jit(solution)/shard_map/ppermute | solution.py:74
  22.1 2.2 %collective-permute-done.1 = bf16[64,128]{0,1:T(8,128)(2,1)S(1)} collective-permute-done((bf16[64,128]{0,1:T(8,128)(2,1)S(1)}, bf16[64,128]{0,1:T(8,128)(2,1)S(1)}, u32[]{:S(2)}, u32[]{:S(2)}) %collective-permute-start.1) | collective-permute-done | bytes 16416 | tf_op jit(solution)/shard_map/ppermute | solution.py:74
  25.2 2.1 %fusion = bf16[16,16,32,32]{2,3,0,1:T(8,128)(2,1)} fusion(bf16[64,16,32,1]{0,2,1,3:T(8,128)(2,1)S(1)} %bitcast.98, bf16[64,4,32]{0,2,1:T(8,128)(2,1)S(1)} %bitcast.117, bf16[64,4,32]{0,2,1:T(8,128)(2,1)S(1)} %bitcast.115, bf16[64,4,32]{0,2,1:T(8,128)(2,1)S(1)} %bitcast.113, bf16[64,4,32]{0,2,1:T(8,128)(2,1)S(1)} %convolution_convert_fusion.3), kind=kOutput, calls=%fused_computation.6 | convolution fusion | flops 34340864 | bytes 655360 | tf_op jit(solution)/shard_map/sip,sjq->ijpq/dot_general | solution.py:89
  27.2 3.0 %copy.37 = bf16[16,16,32,32]{3,2,1,0:T(8,128)(2,1)S(1)} copy(bf16[16,16,32,32]{2,3,0,1:T(8,128)(2,1)} %fusion) | data formatting | bytes 1048576 | tf_op jit(solution)/shard_map/convert_element_type | solution.py:90
  30.3 2.2 %reshape.103 = bf16[256,1024]{1,0:T(8,128)(2,1)S(1)} reshape(bf16[16,16,32,32]{3,2,1,0:T(8,128)(2,1)S(1)} %copy.37) | data formatting | bytes 1048576 | tf_op jit(solution)/shard_map/reshape | solution.py:90
  35.7 1.1 %convolution_convert_fusion.1 = bf16[1024,128]{1,0:T(8,128)(2,1)} fusion(bf16[256,1024]{1,0:T(8,128)(2,1)S(1)} %reshape.103, bf16[256,128]{1,0:T(8,128)(2,1)S(1)} %bitcast.100), kind=kOutput, calls=%fused_computation.8 | convolution fusion | flops 67239936 | bytes 851968 | tf_op jit(solution)/shard_map/dot_general | solution.py:94
  37.0 5.1 %all-to-all-start = ((bf16[16,64,128]{2,1,0:T(8,128)(2,1)}), bf16[16,64,128]{2,1,0:T(8,128)(2,1)S(1)}, u32[]{:S(2)}, u32[]{:S(2)}) async-start(bf16[16,64,128]{2,1,0:T(8,128)(2,1)} %bitcast.37), calls=%async_computation | async-start | bytes 524288 | tf_op jit(solution)/shard_map/all_to_all | solution.py:129
  42.2 1.6 %reshape.106 = bf16[16,16,32,32]{3,2,1,0:T(8,128)(2,1)S(1)} reshape(bf16[256,1024]{1,0:T(8,128)(2,1)S(1)} %convolution_convert_fusion) | data formatting | bytes 1048576 | tf_op jit(solution)/shard_map/reshape | solution.py:96
  44.5 2.0 %collective-permute-start.10 = (bf16[64,128]{0,1:T(8,128)(2,1)S(1)}, bf16[64,128]{0,1:T(8,128)(2,1)S(1)}, u32[]{:S(2)}, u32[]{:S(2)}) collective-permute-start(bf16[64,128]{0,1:T(8,128)(2,1)S(1)} %get-tuple-element.25), channel_id=1, source_target_pairs={{3,0},{0,4},{1,8},{2,12},{7,1},{4,5},{5,9},{6,13},{11,2},{8,6},{9,... | collective-permute-start | bytes 49160 | tf_op jit(solution)/shard_map/ppermute | solution.py:138
  47.1 4.4 %collective-permute-start.8 = (bf16[64,128]{0,1:T(8,128)(2,1)S(1)}, bf16[64,128]{0,1:T(8,128)(2,1)S(1)}, u32[]{:S(2)}, u32[]{:S(2)}) collective-permute-start(bf16[64,128]{0,1:T(8,128)(2,1)S(1)} %get-tuple-element.27), channel_id=1, source_target_pairs={{1,0},{2,4},{3,8},{0,12},{5,1},{6,5},{7,9},{4,13},{9,2},{10,6},{11... | collective-permute-start | bytes 49160 | tf_op jit(solution)/shard_map/ppermute | solution.py:138
  51.5 2.6 %collective-permute-start.9 = (bf16[64,128]{0,1:T(8,128)(2,1)S(1)}, bf16[64,128]{0,1:T(8,128)(2,1)S(1)}, u32[]{:S(2)}, u32[]{:S(2)}) collective-permute-start(bf16[64,128]{0,1:T(8,128)(2,1)S(1)} %get-tuple-element.26), channel_id=1, source_target_pairs={{2,0},{3,4},{0,8},{1,12},{6,1},{7,5},{4,9},{5,13},{10,2},{11,6},{8... | collective-permute-start | bytes 49160 | tf_op jit(solution)/shard_map/ppermute | solution.py:138
  54.9 2.2 %collective-permute-start.12 = (bf16[64,128]{0,1:T(8,128)(2,1)S(1)}, bf16[64,128]{0,1:T(8,128)(2,1)S(1)}, u32[]{:S(2)}, u32[]{:S(2)}) collective-permute-start(bf16[64,128]{0,1:T(8,128)(2,1)S(1)} %get-tuple-element.30), channel_id=1, source_target_pairs={{8,0},{9,1},{10,2},{11,3},{12,4},{13,5},{14,6},{15,7},{0,8},{1,9},... | collective-permute-start | bytes 49160 | tf_op jit(solution)/shard_map/ppermute | solution.py:138
  57.3 1.5 %collective-permute-done.11 = bf16[64,128]{0,1:T(8,128)(2,1)S(1)} collective-permute-done((bf16[64,128]{0,1:T(8,128)(2,1)S(1)}, bf16[64,128]{0,1:T(8,128)(2,1)S(1)}, u32[]{:S(2)}, u32[]{:S(2)}) %collective-permute-start.11) | collective-permute-done | bytes 16416 | tf_op jit(solution)/shard_map/ppermute | solution.py:138
  58.8 1.0 %collective-permute-done.12 = bf16[64,128]{0,1:T(8,128)(2,1)S(1)} collective-permute-done((bf16[64,128]{0,1:T(8,128)(2,1)S(1)}, bf16[64,128]{0,1:T(8,128)(2,1)S(1)}, u32[]{:S(2)}, u32[]{:S(2)}) %collective-permute-start.12) | collective-permute-done | bytes 16416 | tf_op jit(solution)/shard_map/ppermute | solution.py:138
  59.8 3.3 %collective-permute-done.13 = bf16[64,128]{0,1:T(8,128)(2,1)S(1)} collective-permute-done((bf16[64,128]{0,1:T(8,128)(2,1)S(1)}, bf16[64,128]{0,1:T(8,128)(2,1)S(1)}, u32[]{:S(2)}, u32[]{:S(2)}) %collective-permute-start.13) | collective-permute-done | bytes 16416 | tf_op jit(solution)/shard_map/ppermute | solution.py:138
  64.4 4.4 %all-to-all-start.1 = ((bf16[16,96,128]{2,1,0:T(8,128)(2,1)}), bf16[16,96,128]{2,1,0:T(8,128)(2,1)S(1)}, u32[]{:S(2)}, u32[]{:S(2)}) async-start(bf16[16,96,128]{2,1,0:T(8,128)(2,1)} %broadcast_in_dim.44), calls=%async_computation.1 | async-start | bytes 786432 | tf_op jit(solution)/shard_map/all_to_all | solution.py:153
  70.8 10.2 %all-to-all-done.1 = bf16[16,96,128]{2,1,0:T(8,128)(2,1)S(1)} async-done(((bf16[16,96,128]{2,1,0:T(8,128)(2,1)}), bf16[16,96,128]{2,1,0:T(8,128)(2,1)S(1)}, u32[]{:S(2)}, u32[]{:S(2)}) %all-to-all-start.1) | async-done | bytes 393248 | tf_op jit(solution)/shard_map/all_to_all | solution.py:153
  81.1 0.8 %bitcast_convert_fusion = f32[1024,128]{1,0:T(8,128)} fusion(bf16[16,64,128]{2,1,0:T(8,128)(2,1)S(1)} %slice.69), kind=kLoop, calls=%fused_computation.21 | loop fusion | flops 131072 | bytes 786432 | tf_op jit(solution)/shard_map/convert_element_type | solution.py:155
  (78 shorter events, 17.7 us)
Async XLA Ops:
  0.6 31.9 %copy-start = (bf16[1024,128]{1,0:T(8,128)(2,1)S(1)}, bf16[1024,128]{1,0:T(8,128)(2,1)}, u32[]{:S(2)}) copy-start(bf16[1024,128]{1,0:T(8,128)(2,1)} %param.15) | copy-start | bytes 786436
  4.7 14.0 %collective-permute-start.3 = (bf16[64,128]{0,1:T(8,128)(2,1)S(1)}, bf16[64,128]{0,1:T(8,128)(2,1)S(1)}, u32[]{:S(2)}, u32[]{:S(2)}) collective-permute-start(bf16[64,128]{0,1:T(8,128)(2,1)S(1)} %bitcast.119), channel_id=1, source_target_pairs={{0,0},{4,1},{8,2},{12,3},{1,4},{5,5},{9,6},{13,7},{2,8},{6,9},{10,... | collective-permute-start | bytes 49160 | tf_op jit(solution)/shard_map/ppermute | solution.py:73
  5.4 15.9 %collective-permute-start.4 = (bf16[64,128]{0,1:T(8,128)(2,1)S(1)}, bf16[64,128]{0,1:T(8,128)(2,1)S(1)}, u32[]{:S(2)}, u32[]{:S(2)}) collective-permute-start(bf16[64,128]{0,1:T(8,128)(2,1)S(1)} %bitcast.120), channel_id=1, source_target_pairs={{0,1},{4,2},{8,3},{12,0},{1,5},{5,6},{9,7},{13,4},{2,9},{6,10},{10... | collective-permute-start | bytes 49160 | tf_op jit(solution)/shard_map/ppermute | solution.py:73
  9.8 12.2 %collective-permute-start.5 = (bf16[64,128]{0,1:T(8,128)(2,1)S(1)}, bf16[64,128]{0,1:T(8,128)(2,1)S(1)}, u32[]{:S(2)}, u32[]{:S(2)}) collective-permute-start(bf16[64,128]{0,1:T(8,128)(2,1)S(1)} %bitcast.121), channel_id=1, source_target_pairs={{0,2},{4,3},{8,0},{12,1},{1,6},{5,7},{9,4},{13,5},{2,10},{6,11},{1... | collective-permute-start | bytes 49160 | tf_op jit(solution)/shard_map/ppermute | solution.py:73
  13.3 8.8 %collective-permute-start.6 = (bf16[64,128]{0,1:T(8,128)(2,1)S(1)}, bf16[64,128]{0,1:T(8,128)(2,1)S(1)}, u32[]{:S(2)}, u32[]{:S(2)}) collective-permute-start(bf16[64,128]{0,1:T(8,128)(2,1)S(1)} %bitcast.122), channel_id=1, source_target_pairs={{0,3},{4,0},{8,1},{12,2},{1,7},{5,4},{9,5},{13,6},{2,11},{6,8},{10... | collective-permute-start | bytes 49160 | tf_op jit(solution)/shard_map/ppermute | solution.py:73
  15.5 6.6 %collective-permute-start = (bf16[64,128]{0,1:T(8,128)(2,1)S(1)}, bf16[64,128]{0,1:T(8,128)(2,1)S(1)}, u32[]{:S(2)}, u32[]{:S(2)}) collective-permute-start(bf16[64,128]{0,1:T(8,128)(2,1)S(1)} %bitcast.110), channel_id=1, source_target_pairs={{0,4},{1,5},{2,6},{3,7},{4,8},{5,9},{6,10},{7,11},{8,12},{9,13},{1... | collective-permute-start | bytes 49160 | tf_op jit(solution)/shard_map/ppermute | solution.py:74
  18.8 5.6 %collective-permute-start.1 = (bf16[64,128]{0,1:T(8,128)(2,1)S(1)}, bf16[64,128]{0,1:T(8,128)(2,1)S(1)}, u32[]{:S(2)}, u32[]{:S(2)}) collective-permute-start(bf16[64,128]{0,1:T(8,128)(2,1)S(1)} %bitcast.111), channel_id=1, source_target_pairs={{0,8},{1,9},{2,10},{3,11},{4,12},{5,13},{6,14},{7,15},{8,0},{9,1},... | collective-permute-start | bytes 49160 | tf_op jit(solution)/shard_map/ppermute | solution.py:74
  21.3 3.9 %collective-permute-start.2 = (bf16[64,128]{0,1:T(8,128)(2,1)S(1)}, bf16[64,128]{0,1:T(8,128)(2,1)S(1)}, u32[]{:S(2)}, u32[]{:S(2)}) collective-permute-start(bf16[64,128]{0,1:T(8,128)(2,1)S(1)} %bitcast.112), channel_id=1, source_target_pairs={{0,12},{1,13},{2,14},{3,15},{4,0},{5,1},{6,2},{7,3},{8,4},{9,5},{1... | collective-permute-start | bytes 49160 | tf_op jit(solution)/shard_map/ppermute | solution.py:74
  30.3 2.3 %copy-start.3 = (f32[128]{0:T(128)S(1)}, f32[128]{0:T(128)}, u32[]{:S(2)}) copy-start(f32[128]{0:T(128)} %param.16) | copy-start | bytes 1540
  30.3 3.2 %copy-start.4 = (pred[4]{0:T(512)(128)(4,1)S(1)}, pred[4]{0:T(512)(128)(4,1)}, u32[]{:S(2)}) copy-start(pred[4]{0:T(512)(128)(4,1)} %compare_and_fusion.1) | copy-start | bytes 16
  37.0 26.5 %all-to-all-start = ((bf16[16,64,128]{2,1,0:T(8,128)(2,1)}), bf16[16,64,128]{2,1,0:T(8,128)(2,1)S(1)}, u32[]{:S(2)}, u32[]{:S(2)}) async-start(bf16[16,64,128]{2,1,0:T(8,128)(2,1)} %bitcast.37), calls=%async_computation | async-start | bytes 524288 | tf_op jit(solution)/shard_map/all_to_all | solution.py:129
  44.5 10.4 %collective-permute-start.10 = (bf16[64,128]{0,1:T(8,128)(2,1)S(1)}, bf16[64,128]{0,1:T(8,128)(2,1)S(1)}, u32[]{:S(2)}, u32[]{:S(2)}) collective-permute-start(bf16[64,128]{0,1:T(8,128)(2,1)S(1)} %get-tuple-element.25), channel_id=1, source_target_pairs={{3,0},{0,4},{1,8},{2,12},{7,1},{4,5},{5,9},{6,13},{11,2},{8,6},{9,... | collective-permute-start | bytes 49160 | tf_op jit(solution)/shard_map/ppermute | solution.py:138
  46.5 10.7 %collective-permute-start.7 = (bf16[64,128]{0,1:T(8,128)(2,1)S(1)}, bf16[64,128]{0,1:T(8,128)(2,1)S(1)}, u32[]{:S(2)}, u32[]{:S(2)}) collective-permute-start(bf16[64,128]{0,1:T(8,128)(2,1)S(1)} %get-tuple-element.24), channel_id=1, source_target_pairs={{0,0},{1,4},{2,8},{3,12},{4,1},{5,5},{6,9},{7,13},{8,2},{9,6},{10,... | collective-permute-start | bytes 49160 | tf_op jit(solution)/shard_map/ppermute | solution.py:138
  47.1 10.1 %collective-permute-start.8 = (bf16[64,128]{0,1:T(8,128)(2,1)S(1)}, bf16[64,128]{0,1:T(8,128)(2,1)S(1)}, u32[]{:S(2)}, u32[]{:S(2)}) collective-permute-start(bf16[64,128]{0,1:T(8,128)(2,1)S(1)} %get-tuple-element.27), channel_id=1, source_target_pairs={{1,0},{2,4},{3,8},{0,12},{5,1},{6,5},{7,9},{4,13},{9,2},{10,6},{11... | collective-permute-start | bytes 49160 | tf_op jit(solution)/shard_map/ppermute | solution.py:138
  51.5 5.7 %collective-permute-start.9 = (bf16[64,128]{0,1:T(8,128)(2,1)S(1)}, bf16[64,128]{0,1:T(8,128)(2,1)S(1)}, u32[]{:S(2)}, u32[]{:S(2)}) collective-permute-start(bf16[64,128]{0,1:T(8,128)(2,1)S(1)} %get-tuple-element.26), channel_id=1, source_target_pairs={{2,0},{3,4},{0,8},{1,12},{6,1},{7,5},{4,9},{5,13},{10,2},{11,6},{8... | collective-permute-start | bytes 49160 | tf_op jit(solution)/shard_map/ppermute | solution.py:138
  54.1 14.7 %copy-start.1 = (bf16[64,32]{0,1:T(8,128)(2,1)S(1)}, bf16[64,32]{0,1:T(8,128)(2,1)}, u32[]{:S(2)}) copy-start(bf16[64,32]{0,1:T(8,128)(2,1)} %param.13) | copy-start | bytes 12292
  54.1 14.8 %copy-start.2 = (bf16[64,32]{0,1:T(8,128)(2,1)S(1)}, bf16[64,32]{0,1:T(8,128)(2,1)}, u32[]{:S(2)}) copy-start(bf16[64,32]{0,1:T(8,128)(2,1)} %param.14) | copy-start | bytes 12292
  54.9 4.0 %collective-permute-start.11 = (bf16[64,128]{0,1:T(8,128)(2,1)S(1)}, bf16[64,128]{0,1:T(8,128)(2,1)S(1)}, u32[]{:S(2)}, u32[]{:S(2)}) collective-permute-start(bf16[64,128]{0,1:T(8,128)(2,1)S(1)} %get-tuple-element.28), channel_id=1, source_target_pairs={{4,0},{5,1},{6,2},{7,3},{8,4},{9,5},{10,6},{11,7},{12,8},{13,9},{1... | collective-permute-start | bytes 49160 | tf_op jit(solution)/shard_map/ppermute | solution.py:138
  54.9 4.9 %collective-permute-start.12 = (bf16[64,128]{0,1:T(8,128)(2,1)S(1)}, bf16[64,128]{0,1:T(8,128)(2,1)S(1)}, u32[]{:S(2)}, u32[]{:S(2)}) collective-permute-start(bf16[64,128]{0,1:T(8,128)(2,1)S(1)} %get-tuple-element.30), channel_id=1, source_target_pairs={{8,0},{9,1},{10,2},{11,3},{12,4},{13,5},{14,6},{15,7},{0,8},{1,9},... | collective-permute-start | bytes 49160 | tf_op jit(solution)/shard_map/ppermute | solution.py:138
  57.2 5.9 %collective-permute-start.13 = (bf16[64,128]{0,1:T(8,128)(2,1)S(1)}, bf16[64,128]{0,1:T(8,128)(2,1)S(1)}, u32[]{:S(2)}, u32[]{:S(2)}) collective-permute-start(bf16[64,128]{0,1:T(8,128)(2,1)S(1)} %get-tuple-element.29), channel_id=1, source_target_pairs={{12,0},{13,1},{14,2},{15,3},{0,4},{1,5},{2,6},{3,7},{4,8},{5,9},{6... | collective-permute-start | bytes 49160 | tf_op jit(solution)/shard_map/ppermute | solution.py:138
  64.4 16.6 %all-to-all-start.1 = ((bf16[16,96,128]{2,1,0:T(8,128)(2,1)}), bf16[16,96,128]{2,1,0:T(8,128)(2,1)S(1)}, u32[]{:S(2)}, u32[]{:S(2)}) async-start(bf16[16,96,128]{2,1,0:T(8,128)(2,1)} %broadcast_in_dim.44), calls=%async_computation.1 | async-start | bytes 786432 | tf_op jit(solution)/shard_map/all_to_all | solution.py:153

commit v2 on v1

v2 whole, which is shorter than its diff:
```python
import jax
import jax.numpy as jnp
from jax import lax
from jax.sharding import PartitionSpec as P

PAIRS_AT_ONCE = 1024


def normalize(values):
    values = values.astype(jnp.float32)
    mean_factor = jnp.mean(values, axis=-1, keepdims=True)
    centered = values - mean_factor
    variance = jnp.mean(centered * centered, axis=-1, keepdims=True)
    inverse_spread = lax.rsqrt(variance + 1e-05)
    return (centered * inverse_spread, inverse_spread)


def transposed(rows_n, cols_n):
    return [
        (r * cols_n + c, c * rows_n + r) for r in range(rows_n) for c in range(cols_n)
    ]


def spread(values, axes, count):
    return lax.all_to_all(jnp.broadcast_to(values[None], (count,) + values.shape), axes, 0, 0)


def local(
    homolog_features,
    subset_homolog_positions,
    first_side_matrix,
    second_side_matrix,
    final_mapping_matrix,
    final_offset_vector,
    upstream_sensitivity,
):
    axes = ("prow", "pcol")
    rows_n, cols_n = lax.axis_size("prow"), lax.axis_size("pcol")
    devices = rows_n * cols_n
    seq_count = subset_homolog_positions.shape[0]
    tokens, features = homolog_features.shape[1:]
    row_count, col_count, pair_width = upstream_sensitivity.shape
    proj = first_side_matrix.shape[1]
    flat = proj * proj
    to_rows = transposed(rows_n, cols_n)
    to_tokens = [(target, source) for source, target in to_rows]

    picked = jnp.take(homolog_features, subset_homolog_positions, axis=0)
    packed = picked.reshape(seq_count, tokens * features)
    row_own = lax.ppermute(packed, axes, to_rows)
    col_all = spread(packed, "prow", rows_n)
    row_all = spread(row_own, "pcol", cols_n)

    def side_of(chunks, count, matrix):
        chunks = chunks.reshape(count // tokens, seq_count, tokens, features)
        chunks = chunks.transpose(1, 0, 2, 3).reshape(seq_count, count, features)
        normed_low = normalize(chunks)[0].astype(jnp.bfloat16)
        side = jnp.einsum("stc,cp->stp", normed_low, matrix, preferred_element_type=jnp.float32)
        return normed_low, side.astype(jnp.bfloat16)

    row_normed, left = side_of(row_all, row_count, first_side_matrix)
    col_normed, right = side_of(col_all, col_count, second_side_matrix)

    def block_step(left_blk, cot_blk):
        rows = left_blk.shape[1]
        outer = jnp.einsum("sip,sjq->ijpq", left_blk, right, preferred_element_type=jnp.float32)
        outer = (outer / seq_count).astype(jnp.bfloat16).reshape(rows * col_count, flat)
        update = jnp.dot(outer, final_mapping_matrix, preferred_element_type=jnp.float32)
        update = (update + final_offset_vector).astype(jnp.bfloat16)
        cot_flat = cot_blk.reshape(rows * col_count, pair_width)
        grad_out = jnp.dot(outer.T, cot_flat, preferred_element_type=jnp.float32)
        grad_outer = jnp.dot(cot_flat, final_mapping_matrix.T, preferred_element_type=jnp.float32)
        grad_outer = grad_outer.astype(jnp.bfloat16).reshape(rows, col_count, proj, proj)
        grad_left = jnp.einsum(
            "ijpq,sjq->sip", grad_outer, right, preferred_element_type=jnp.float32
        )
        grad_right = jnp.einsum(
            "ijpq,sip->sjq", grad_outer, left_blk, preferred_element_type=jnp.float32
        )
        return update.reshape(rows, col_count, pair_width), grad_out, grad_left, grad_right

    block = max(1, min(row_count, PAIRS_AT_ONCE // col_count))
    blocks = row_count // block
    if blocks == 1:
        update, grad_out, grad_left, grad_right = block_step(left, upstream_sensitivity)
    else:
        def step(totals, inputs):
            update, grad_out, grad_left, grad_right = block_step(*inputs)
            return (totals[0] + grad_out, totals[1] + grad_right), (update, grad_left)

        (grad_out, grad_right), (update, grad_left) = lax.scan(
            step,
            (
                jnp.zeros((flat, pair_width), jnp.float32),
                jnp.zeros((seq_count, col_count, proj), jnp.float32),
            ),
            (
                left.reshape(seq_count, blocks, block, proj).transpose(1, 0, 2, 3),
                upstream_sensitivity.reshape(blocks, block, col_count, pair_width),
            ),
        )
        grad_left = grad_left.transpose(1, 0, 2, 3).reshape(seq_count, row_count, proj)
    pair_delta = update.reshape(row_count, col_count, pair_width)

    grad_left = (grad_left / seq_count).astype(jnp.bfloat16)
    grad_right = (grad_right / seq_count).astype(jnp.bfloat16)

    def weight_part(normed, grads):
        return jnp.einsum("stc,stp->cp", normed, grads, preferred_element_type=jnp.float32)

    side_part = jnp.concatenate(
        [weight_part(row_normed, grad_left), weight_part(col_normed, grad_right)], axis=1
    )
    share_rows = flat // devices
    side_rows = -(-features * 2 * proj // (pair_width * devices))
    side_flat = side_part.reshape(-1, pair_width)
    side_flat = jnp.pad(side_flat, ((0, side_rows * devices - side_flat.shape[0]), (0, 0)))
    shares = jnp.concatenate(
        [
            grad_out.reshape(devices, share_rows, pair_width),
            side_flat.reshape(devices, side_rows, pair_width),
        ],
        axis=1,
    ).astype(jnp.bfloat16)
    shares = lax.all_to_all(shares, axes, 0, 0)

    def chunks_of(grads, count):
        grads = grads.reshape(seq_count, count // tokens, tokens * proj)
        return grads.transpose(1, 0, 2)

    left_back = lax.all_to_all(chunks_of(grad_left, row_count), "pcol", 0, 0)
    right_back = lax.all_to_all(chunks_of(grad_right, col_count), "prow", 0, 0)
    left_back = jnp.sum(left_back.astype(jnp.float32), axis=0).astype(jnp.bfloat16)
    right_back = jnp.sum(right_back.astype(jnp.float32), axis=0).astype(jnp.bfloat16)
    left_back = lax.ppermute(left_back, axes, to_tokens)

    share = jnp.sum(shares.astype(jnp.float32), axis=0).astype(jnp.bfloat16)
    message = spread(share, axes, devices)
    output_weight_gradient = (
        message[:, :share_rows].reshape(flat, pair_width).astype(jnp.float32)
    )
    side = message[:, share_rows:].reshape(-1, pair_width).astype(jnp.float32)
    side = side[: features * 2 * proj // pair_width].reshape(features, 2 * proj)
    left_weight_gradient, right_weight_gradient = side[:, :proj], side[:, proj:]

    normed, inverse_spread = normalize(picked)
    both = jnp.concatenate(
        [
            left_back.reshape(seq_count, tokens, proj),
            right_back.reshape(seq_count, tokens, proj),
        ],
        axis=-1,
    )
    sides = jnp.concatenate([first_side_matrix, second_side_matrix], axis=1)
    grad_normed = jnp.einsum("stp,cp->stc", both, sides, preferred_element_type=jnp.float32)
    mean_factor = jnp.mean(grad_normed, axis=-1, keepdims=True)
    projected = jnp.mean(grad_normed * normed, axis=-1, keepdims=True)
    alignment_gradient = (
        inverse_spread * (grad_normed - mean_factor - normed * projected)
    ).astype(jnp.bfloat16)
    return (
        pair_delta,
        alignment_gradient,
        left_weight_gradient,
        right_weight_gradient,
        output_weight_gradient,
    )


def solution(mesh):
    return jax.shard_map(
        local,
        mesh=mesh,
        in_specs=(
            P("rep", ("pcol", "prow"), None),
            P("rep"),
            P(),
            P(),
            P(),
            P(),
            P(("rep", "prow"), "pcol", None),
        ),
        out_specs=(
            P(("rep", "prow"), "pcol", None),
            P("rep", ("pcol", "prow"), None),
            P("rep", None),
            P("rep", None),
            P("rep", None),
        ),
        check_vma=False,
    )
```

time: 84.1 us -> 91 us (1.082)
  waiting for transfers between devices: 19.1 us -> 24.8 us
  other arithmetic: 4.51 us -> 7.42 us
  starting transfers between devices: 35.4 us -> 32.8 us
    ppermute x14 -> x2, starting transfers between devices: 25.8 us -> 1.33 us  [the longest x1 0.66 us: local(): row_own = lax.ppermute(packed, axes, to_rows)]
    all_to_all x1 -> x5, starting transfers between devices: 4.44 us -> 26.3 us  [the longest x3 19.1 us: spread(): lax.all_to_all(jnp.broadcast_to(values[None], (count,) + values.shape), a...]
    ppermute x14 -> x2, waiting for transfers between devices: 8.85 us -> 0.01 us  [the longest x1 0.01 us: local(): row_own = lax.ppermute(packed, axes, to_rows)]
    all_to_all x1, waiting for transfers between devices: 0.01 us -> 7.32 us  [local(): shares = lax.all_to_all(shares, axes, 0, 0)]
    all_to_all x1 -> x5, waiting for transfers between devices: 10.2 us -> 17.5 us  [the longest x3 14.1 us: spread(): lax.all_to_all(jnp.broadcast_to(values[None], (count,) + values.shape), a...]
    gather x4 -> x0, local copies, waits for them, and re-layouts: 3.31 us -> none  [reorder(): return jnp.take(jnp.take(pairs, row_order, axis=0), col_order, axis=2)]
    reshape x4 -> x5, local copies, waits for them, and re-layouts: 0.37 us -> 1.77 us  [the longest x2 1.46 us: chunks_of(): grads = grads.reshape(seq_count, count // tokens, tokens * proj)]
    reduce_sum x1 -> x3, other arithmetic: 0.04 us -> 1.34 us  [normalize(): variance = jnp.mean(centered * centered, axis=-1, keepdims=True)]
  transfers between devices with their start and end apart: 16 -> 8, of which waited for: 6 -> 5; matrix products, arithmetic and copies ran while one was open for 11% -> 26% of each run, Pallas kernels for 0% -> 0%
where the time goes in v2:
time: 91 us; the launch traced here: 90.1 us
  starting transfers between devices  32.8 us (36%)
  waiting for transfers between devices  24.8 us (27%)
  local copies, waits for them, and re-layouts  16.7 us (18%)
  other arithmetic  7.42 us (8%)
  matrix products  7.26 us (8%)
  between operations  1.08 us (1%)
    all_to_all x3, starting transfers between devices, spread(): lax.all_to_all(jnp.broadcast_to(values[None], (count,) + values.shape), a...  19.1 us
    all_to_all x3, waiting for transfers between devices, spread(): lax.all_to_all(jnp.broadcast_to(values[None], (count,) + values.shape), a...  14.1 us
    all_to_all x1, waiting for transfers between devices, local(): shares = lax.all_to_all(shares, axes, 0, 0)  7.32 us
    all_to_all x1, starting transfers between devices, local(): shares = lax.all_to_all(shares, axes, 0, 0)  5.17 us
    all_to_all x1, starting transfers between devices, local(): right_back = lax.all_to_all(chunks_of(grad_right, col_count), 'prow', 0, 0)  3.89 us
    unnamed x32, local copies, waits for them, and re-layouts  3.78 us
    all_to_all x1, waiting for transfers between devices, local(): left_back = lax.all_to_all(chunks_of(grad_left, row_count), 'pcol', 0, 0)  3.35 us
    all_to_all x1, starting transfers between devices, local(): left_back = lax.all_to_all(chunks_of(grad_left, row_count), 'pcol', 0, 0)  3.28 us
  transfers between devices with their start and end apart: 8, of which 5 were waited for; matrix products, arithmetic and copies ran while one was open for 26% of the time, Pallas kernels for 0%

profile of v2, /device:TPU:0, one launch (start us, length us, event | category | flops | bytes accessed | tf_op | source)
XLA Modules:
  0.0 90.1 jit_solution(3368524992327328340)
XLA Ops:
  2.0 1.0 %copy.93 = bf16[128,4,64]{2,1,0:T(4,128)(2,1)S(1)} copy(bf16[128,4,64]{0,2,1:T(8,128)(2,1)} %param.7) | data formatting | bytes 131072 | tf_op args[0]
  4.7 1.2 %convolution_convert_fusion = bf16[256,1024]{1,0:T(8,128)(2,1)S(1)} fusion(bf16[256,128]{1,0:T(8,128)(2,1)} %bitcast.111, bf16[1024,128]{1,0:T(8,128)(2,1)S(1)} %copy-done), kind=kOutput, calls=%fused_computation.3 | convolution fusion | flops 67371008 | bytes 851968 | tf_op jit(solution)/shard_map/dot_general | solution.py:72
  6.5 10.4 %all-to-all-start.1 = ((bf16[4,64,256]{2,1,0:T(8,128)(2,1)}), bf16[4,64,256]{2,1,0:T(8,128)(2,1)S(1)}, u32[]{:S(2)}, u32[]{:S(2)}) async-start(bf16[4,64,256]{2,1,0:T(8,128)(2,1)} %broadcast_in_dim.46), calls=%async_computation.1 | async-start | bytes 262144 | tf_op jit(solution)/shard_map/all_to_all | solution.py:25
  17.5 1.6 %reshape.167 = bf16[16,16,32,32]{3,2,1,0:T(8,128)(2,1)S(1)} reshape(bf16[256,1024]{1,0:T(8,128)(2,1)S(1)} %convolution_convert_fusion) | data formatting | bytes 1048576 | tf_op jit(solution)/shard_map/reshape | solution.py:73
  19.1 2.5 %all-to-all-done.1 = bf16[4,64,256]{2,1,0:T(8,128)(2,1)S(1)} async-done(((bf16[4,64,256]{2,1,0:T(8,128)(2,1)}), bf16[4,64,256]{2,1,0:T(8,128)(2,1)S(1)}, u32[]{:S(2)}, u32[]{:S(2)}) %all-to-all-start.1) | async-done | bytes 131104 | tf_op jit(solution)/shard_map/all_to_all | solution.py:25
  22.2 5.1 %all-to-all-start = ((bf16[4,64,256]{2,1,0:T(8,128)(2,1)}), bf16[4,64,256]{2,1,0:T(8,128)(2,1)S(1)}, u32[]{:S(2)}, u32[]{:S(2)}) async-start(bf16[4,64,256]{2,1,0:T(8,128)(2,1)} %broadcast_in_dim.25), calls=%async_computation | async-start | bytes 262144 | tf_op jit(solution)/shard_map/all_to_all | solution.py:25
  29.6 0.7 fusion.4
  31.1 2.2 %all-to-all-done = bf16[4,64,256]{2,1,0:T(8,128)(2,1)S(1)} async-done(((bf16[4,64,256]{2,1,0:T(8,128)(2,1)}), bf16[4,64,256]{2,1,0:T(8,128)(2,1)S(1)}, u32[]{:S(2)}, u32[]{:S(2)}) %all-to-all-start) | async-done | bytes 131104 | tf_op jit(solution)/shard_map/all_to_all | solution.py:25
  33.3 3.9 %all-to-all-start.3 = ((bf16[4,64,128]{2,1,0:T(8,128)(2,1)}), bf16[4,64,128]{2,1,0:T(8,128)(2,1)}, u32[]{:S(2)}, u32[]{:S(2)}) async-start(bf16[4,64,128]{2,1,0:T(8,128)(2,1)} %bitcast.25), calls=%async_computation.3 | async-start | bytes 131072 | tf_op jit(solution)/shard_map/all_to_all | solution.py:132
  40.4 2.1 %fusion = bf16[16,16,32,32]{2,3,0,1:T(8,128)(2,1)} fusion(bf16[64,16,32]{0,2,1:T(8,128)(2,1)S(1)} %convolution_convert_fusion.3, bf16[64,16,32]{0,2,1:T(8,128)(2,1)S(1)} %convolution_convert_fusion.2), kind=kOutput, calls=%fused_computation.2 | convolution fusion | flops 34078720 | bytes 655360 | tf_op jit(solution)/shard_map/sip,sjq->ijpq/dot_general | solution.py:66
  42.7 3.1 %copy.102 = bf16[16,16,32,32]{3,2,1,0:T(8,128)(2,1)S(1)} copy(bf16[16,16,32,32]{2,3,0,1:T(8,128)(2,1)} %fusion) | data formatting | bytes 1048576 | tf_op jit(solution)/shard_map/convert_element_type | solution.py:67
  45.8 2.2 %reshape.164 = bf16[256,1024]{1,0:T(8,128)(2,1)S(1)} reshape(bf16[16,16,32,32]{3,2,1,0:T(8,128)(2,1)S(1)} %copy.102) | data formatting | bytes 1048576 | tf_op jit(solution)/shard_map/reshape | solution.py:67
  49.5 3.3 %all-to-all-start.2 = ((bf16[4,64,128]{2,1,0:T(8,128)(2,1)}), bf16[4,64,128]{2,1,0:T(8,128)(2,1)S(1)}, u32[]{:S(2)}, u32[]{:S(2)}) async-start(bf16[4,64,128]{2,1,0:T(8,128)(2,1)} %bitcast.20), calls=%async_computation.2 | async-start | bytes 131072 | tf_op jit(solution)/shard_map/all_to_all | solution.py:131
  52.8 0.7 pad_maximum_fusion
  53.6 3.3 %all-to-all-done.2 = bf16[4,64,128]{2,1,0:T(8,128)(2,1)S(1)} async-done(((bf16[4,64,128]{2,1,0:T(8,128)(2,1)}), bf16[4,64,128]{2,1,0:T(8,128)(2,1)S(1)}, u32[]{:S(2)}, u32[]{:S(2)}) %all-to-all-start.2) | async-done | bytes 65568 | tf_op jit(solution)/shard_map/all_to_all | solution.py:131
  56.9 5.2 %all-to-all-start.4 = ((bf16[16,66,128]{2,1,0:T(8,128)(2,1)}), bf16[16,66,128]{2,1,0:T(8,128)(2,1)S(1)}, u32[]{:S(2)}, u32[]{:S(2)}) async-start(bf16[16,66,128]{2,1,0:T(8,128)(2,1)} %pad_maximum_fusion), calls=%async_computation.4 | async-start | bytes 589824 | tf_op jit(solution)/shard_map/all_to_all | solution.py:125
  63.1 0.9 %fusion.5 = bf16[256,128]{1,0:T(8,128)(2,1)} fusion(bf16[256,1024]{1,0:T(8,128)(2,1)S(1)} %reshape.164, bf16[1024,128]{1,0:T(8,128)(2,1)S(1)} %copy-done, f32[128]{0:T(128)S(1)} %copy-done.10), kind=kOutput, calls=%fused_computation.14 | convolution fusion | flops 67174400 | bytes 852480 | tf_op jit(solution)/shard_map/dot_general | solution.py:68
  64.0 0.9 reduce_sum.115
  65.3 7.3 %all-to-all-done.4 = bf16[16,66,128]{2,1,0:T(8,128)(2,1)S(1)} async-done(((bf16[16,66,128]{2,1,0:T(8,128)(2,1)}), bf16[16,66,128]{2,1,0:T(8,128)(2,1)S(1)}, u32[]{:S(2)}, u32[]{:S(2)}) %all-to-all-start.4) | async-done | bytes 270368 | tf_op jit(solution)/shard_map/all_to_all | solution.py:125
  72.7 0.8 broadcast_in_dim.49
  73.5 3.6 %all-to-all-start.5 = ((bf16[16,66,128]{2,1,0:T(8,128)(2,1)}), bf16[16,66,128]{2,1,0:T(8,128)(2,1)S(1)}, u32[]{:S(2)}, u32[]{:S(2)}) async-start(bf16[16,66,128]{2,1,0:T(8,128)(2,1)} %broadcast_in_dim.49), calls=%async_computation.5 | async-start | bytes 589824 | tf_op jit(solution)/shard_map/all_to_all | solution.py:25
  77.4 0.7 copy.115
  78.2 9.5 %all-to-all-done.5 = bf16[16,66,128]{2,1,0:T(8,128)(2,1)S(1)} async-done(((bf16[16,66,128]{2,1,0:T(8,128)(2,1)}), bf16[16,66,128]{2,1,0:T(8,128)(2,1)S(1)}, u32[]{:S(2)}, u32[]{:S(2)}) %all-to-all-start.5) | async-done | bytes 270368 | tf_op jit(solution)/shard_map/all_to_all | solution.py:25
  89.2 0.8 bitcast_convert_fusion
  (87 shorter events, 16.1 us)
Async XLA Ops:
  0.6 4.0 %copy-start = (bf16[1024,128]{1,0:T(8,128)(2,1)S(1)}, bf16[1024,128]{1,0:T(8,128)(2,1)}, u32[]{:S(2)}) copy-start(bf16[1024,128]{1,0:T(8,128)(2,1)} %param.11) | copy-start | bytes 786436
  1.4 5.2 %copy-start.8 = (pred[64]{0:T(512)(128)(4,1)}, pred[64]{0:T(512)(128)(4,1)S(1)}, u32[]{:S(2)}) copy-start(pred[64]{0:T(512)(128)(4,1)S(1)} %compare_and_fusion) | copy-start | bytes 196
  3.8 2.0 %collective-permute-start = (bf16[64,256]{1,0:T(8,128)(2,1)S(1)}, bf16[64,256]{1,0:T(8,128)(2,1)S(1)}, u32[]{:S(2)}, u32[]{:S(2)}) collective-permute-start(bf16[64,256]{1,0:T(8,128)(2,1)S(1)} %broadcast_select_fusion.1), channel_id=1, source_target_pairs={{0,0},{1,4},{2,8},{3,12},{4,1},{5,5},{6,9},{7,13},{8,2},{9,6},{10,... | collective-permute-start | bytes 98312 | tf_op jit(solution)/shard_map/ppermute | solution.py:50
  4.6 12.3 %copy-start.1 = (bf16[64,4,64]{0,2,1:T(8,128)(2,1)}, bf16[64,4,64]{0,2,1:T(8,128)(2,1)S(1)}, u32[]{:S(2)}) copy-start(bf16[64,4,64]{0,2,1:T(8,128)(2,1)S(1)} %copy.103) | copy-start | bytes 98308
  6.5 15.0 %all-to-all-start.1 = ((bf16[4,64,256]{2,1,0:T(8,128)(2,1)}), bf16[4,64,256]{2,1,0:T(8,128)(2,1)S(1)}, u32[]{:S(2)}, u32[]{:S(2)}) async-start(bf16[4,64,256]{2,1,0:T(8,128)(2,1)} %broadcast_in_dim.46), calls=%async_computation.1 | async-start | bytes 262144 | tf_op jit(solution)/shard_map/all_to_all | solution.py:25
  22.2 11.1 %all-to-all-start = ((bf16[4,64,256]{2,1,0:T(8,128)(2,1)}), bf16[4,64,256]{2,1,0:T(8,128)(2,1)S(1)}, u32[]{:S(2)}, u32[]{:S(2)}) async-start(bf16[4,64,256]{2,1,0:T(8,128)(2,1)} %broadcast_in_dim.25), calls=%async_computation | async-start | bytes 262144 | tf_op jit(solution)/shard_map/all_to_all | solution.py:25
  27.6 1.7 %copy-start.4 = (bf16[64,32]{0,1:T(8,128)(2,1)S(1)}, bf16[64,32]{0,1:T(8,128)(2,1)}, u32[]{:S(2)}) copy-start(bf16[64,32]{0,1:T(8,128)(2,1)} %param.9) | copy-start | bytes 12292
  33.3 16.3 %all-to-all-start.3 = ((bf16[4,64,128]{2,1,0:T(8,128)(2,1)}), bf16[4,64,128]{2,1,0:T(8,128)(2,1)}, u32[]{:S(2)}, u32[]{:S(2)}) async-start(bf16[4,64,128]{2,1,0:T(8,128)(2,1)} %bitcast.25), calls=%async_computation.3 | async-start | bytes 131072 | tf_op jit(solution)/shard_map/all_to_all | solution.py:132
  38.7 0.7 copy-start.6
  45.8 2.5 %copy-start.3 = (bf16[16,16,128]{2,1,0:T(8,128)(2,1)S(1)}, bf16[16,16,128]{2,1,0:T(8,128)(2,1)}, u32[]{:S(2)}) copy-start(bf16[16,16,128]{2,1,0:T(8,128)(2,1)} %param.13) | copy-start | bytes 196612
  48.0 14.1 %copy-start.2 = (bf16[64,4,64]{0,2,1:T(8,128)(2,1)S(1)}, bf16[64,4,64]{0,2,1:T(8,128)(2,1)}, u32[]{:S(2)}) copy-start(bf16[64,4,64]{0,2,1:T(8,128)(2,1)} %copy-done.1) | copy-start | bytes 98308
  48.1 14.1 %copy-start.7 = (f32[64,4]{0,1:T(4,128)S(1)}, f32[64,4]{0,1:T(4,128)}, u32[]{:S(2)}) copy-start(f32[64,4]{0,1:T(4,128)} %broadcast_multiply_fusion.4) | copy-start | bytes 3076
  48.1 14.1 %copy-start.9 = (pred[64]{0:T(512)(128)(4,1)S(1)}, pred[64]{0:T(512)(128)(4,1)}, u32[]{:S(2)}) copy-start(pred[64]{0:T(512)(128)(4,1)} %copy-done.8) | copy-start | bytes 196
  48.1 14.1 %copy-start.5 = (bf16[64,32]{0,1:T(8,128)(2,1)S(1)}, bf16[64,32]{0,1:T(8,128)(2,1)}, u32[]{:S(2)}) copy-start(bf16[64,32]{0,1:T(8,128)(2,1)} %param.9) | copy-start | bytes 12292
  48.1 15.0 %copy-start.10 = (f32[128]{0:T(128)S(1)}, f32[128]{0:T(128)}, u32[]{:S(2)}) copy-start(f32[128]{0:T(128)} %param.12) | copy-start | bytes 1540
  49.5 7.4 %all-to-all-start.2 = ((bf16[4,64,128]{2,1,0:T(8,128)(2,1)}), bf16[4,64,128]{2,1,0:T(8,128)(2,1)S(1)}, u32[]{:S(2)}, u32[]{:S(2)}) async-start(bf16[4,64,128]{2,1,0:T(8,128)(2,1)} %bitcast.20), calls=%async_computation.2 | async-start | bytes 131072 | tf_op jit(solution)/shard_map/all_to_all | solution.py:131
  56.9 15.7 %all-to-all-start.4 = ((bf16[16,66,128]{2,1,0:T(8,128)(2,1)}), bf16[16,66,128]{2,1,0:T(8,128)(2,1)S(1)}, u32[]{:S(2)}, u32[]{:S(2)}) async-start(bf16[16,66,128]{2,1,0:T(8,128)(2,1)} %pad_maximum_fusion), calls=%async_computation.4 | async-start | bytes 589824 | tf_op jit(solution)/shard_map/all_to_all | solution.py:125
  62.4 2.7 %collective-permute-start.1 = (bf16[64,128]{1,0:T(8,128)(2,1)S(1)}, bf16[64,128]{1,0:T(8,128)(2,1)S(1)}, u32[]{:S(2)}, u32[]{:S(2)}) collective-permute-start(bf16[64,128]{1,0:T(8,128)(2,1)S(1)} %reduce_sum.114), channel_id=1, source_target_pairs={{0,0},{4,1},{8,2},{12,3},{1,4},{5,5},{9,6},{13,7},{2,8},{6,9},{10,... | collective-permute-start | bytes 49160 | tf_op jit(solution)/shard_map/ppermute | solution.py:135
  73.5 14.2 %all-to-all-start.5 = ((bf16[16,66,128]{2,1,0:T(8,128)(2,1)}), bf16[16,66,128]{2,1,0:T(8,128)(2,1)S(1)}, u32[]{:S(2)}, u32[]{:S(2)}) async-start(bf16[16,66,128]{2,1,0:T(8,128)(2,1)} %broadcast_in_dim.49), calls=%async_computation.5 | async-start | bytes 589824 | tf_op jit(solution)/shard_map/all_to_all | solution.py:25

commit v3 on v2

--- a/solution.py
+++ b/solution.py
@@ -1,7 +1,16 @@
+import functools
+
 import jax
 import jax.numpy as jnp
 from jax import lax
+from jax.experimental import pallas as pl
+from jax.experimental.pallas import tpu as pltpu
+from jax.sharding import Mesh
 from jax.sharding import PartitionSpec as P
+
+BF16, F32 = jnp.bfloat16, jnp.float32
+LANES = 128
+GATHERED_PAIRS = 4096
 
 PAIRS_AT_ONCE = 1024
 
@@ -25,7 +34,7 @@
     return lax.all_to_all(jnp.broadcast_to(values[None], (count,) + values.shape), axes, 0, 0)
 
 
-def local(
+def local_phased(
     homolog_features,
     subset_homolog_positions,
     first_side_matrix,
@@ -167,25 +176,392 @@
     )
 
 
+def dot(x, y, contract=(1, 0), precision=None):
+    return lax.dot_general(
+        x, y, (((contract[0],), (contract[1],)), ((), ())),
+        precision=precision, preferred_element_type=F32,
+    )
+
+
+def lane_ids(shape):
+    return lax.broadcasted_iota(jnp.int32, shape, len(shape) - 1)
+
+
+def fold_lanes(x, width):
+    shift = LANES // 2
+    while shift >= width:
+        x = x + pltpu.roll(x, shift, x.ndim - 1)
+        shift //= 2
+    return x
+
+
+def group_mean(x, group, precision):
+    lanes = x.shape[1]
+    rows_id = lax.broadcasted_iota(jnp.int32, (lanes, lanes), 0) // group
+    cols_id = lax.broadcasted_iota(jnp.int32, (lanes, lanes), 1) // group
+    block = jnp.where(rows_id == cols_id, 1.0 / group, 0.0).astype(x.dtype)
+    return dot(x, block, precision=precision)
+
+
+def pick_kernel(group, positions_ref, features_ref, normed_ref, inverse_ref, sent_ref):
+    heads = features_ref.shape[0]
+    seqs = normed_ref.shape[0]
+    wanted = positions_ref[...] == lax.broadcasted_iota(jnp.int32, (heads, seqs), 0)
+    chosen = dot(wanted.astype(BF16), features_ref[...], contract=(0, 0))
+    mean_factor = group_mean(chosen.astype(BF16), group, None)
+    centered = chosen - mean_factor
+    variance = group_mean(centered * centered, group, lax.Precision.HIGHEST)
+    inverse = lax.rsqrt(variance + 1e-05)
+    normed = centered * inverse
+    normed_ref[...] = normed
+    inverse_ref[...] = inverse
+    sent_ref[...] = jnp.broadcast_to(normed.astype(BF16)[None], sent_ref.shape)
+
+
+def pair_kernel(
+    place_ref,
+    rows_ref,
+    cot_ref,
+    mapping_ref,
+    left_ref,
+    right_ref,
+    offset_ref,
+    pair_ref,
+    grads_ref,
+    message_ref,
+    expanded,
+    outer,
+    pulled,
+    left_back,
+    right_back,
+    turned,
+    swapped,
+    sums,
+    weights,
+):
+    owners, seqs, packed = rows_ref.shape
+    prow_n, groups, block_rows, block_cols, pair_width = cot_ref.shape
+    tokens = left_ref.shape[1] // LANES
+    proj = LANES // tokens
+    highs = proj // tokens
+    span = highs * block_cols
+    own_row, own_group, core = place_ref[0], place_ref[1], place_ref[2]
+
+    def token_owner(group, row, parity):
+        return (2 * group + parity) * prow_n + row
+
+    rows_all = rows_ref[...].reshape(owners * seqs, packed)
+    expanded[...] = dot(rows_all, left_ref[...]).astype(BF16).reshape(expanded.shape)
+
+    side_rows = []
+    for g in range(groups):
+        chunks = [rows_ref[token_owner(g, r, core)] for r in range(prow_n)]
+        side_rows.append(
+            jnp.concatenate([dot(x, right_ref[...]).astype(BF16) for x in chunks], axis=1)
+        )
+    right = jnp.concatenate(side_rows, axis=0)
+    wide = right.shape[1]
+    source = lax.broadcasted_iota(jnp.int32, (wide, wide), 0)
+    target = lax.broadcasted_iota(jnp.int32, (wide, wide), 1)
+    jj, qh, ql = target % block_cols, target // block_cols % highs, target // span
+    shuffle = (source == jj * proj + qh * tokens + ql).astype(BF16)
+    right = dot(right, shuffle)
+    for g in range(groups):
+        for l in range(tokens):
+            swapped[l * seqs : (l + 1) * seqs, g * span : (g + 1) * span] = right[
+                g * seqs : (g + 1) * seqs, l * span : (l + 1) * span
+            ].astype(BF16)
+    turned[...] = swapped[...].astype(F32).T.astype(BF16)
+
+    sums[...] = jnp.zeros_like(sums)
+    weights[...] = jnp.zeros_like(weights)
+    step_tokens = outer.shape[0] // (groups * block_cols)
+    step_owners = step_tokens // tokens
+    steps_a_block = block_rows // step_tokens
+
+    def step(m, carry):
+        row, part = m // steps_a_block, m % steps_a_block
+        ahead = jnp.concatenate(
+            [expanded[m * step_owners + o] for o in range(step_owners)], axis=1
+        )
+        low = lane_ids(ahead.shape) % LANES // proj
+        block = jnp.concatenate(
+            [jnp.where(low == l, ahead, jnp.zeros_like(ahead)) for l in range(tokens)], axis=0
+        )
+        cot = jnp.concatenate(
+            [
+                cot_ref[row, g, pl.ds(part * step_tokens, step_tokens)].reshape(
+                    step_tokens * block_cols, pair_width
+                )
+                for g in range(groups)
+            ],
+            axis=0,
+        )
+        made = dot(turned[...], block) * (1.0 / seqs)
+        grad = dot(cot, mapping_ref[...], contract=(1, 1))
+        for g in range(groups):
+            for t in range(step_tokens):
+                here = slice((g * step_tokens + t) * block_cols, (g * step_tokens + t + 1) * block_cols)
+                lanes = slice(t * LANES, (t + 1) * LANES)
+                for h in range(highs):
+                    there = slice((g * highs + h) * block_cols, (g * highs + h + 1) * block_cols)
+                    cols = slice(h * LANES, (h + 1) * LANES)
+                    outer[here, cols] = made[there, lanes].astype(BF16)
+                    pulled[there, lanes] = grad[here, cols].astype(BF16)
+        weights[...] += dot(cot, outer[...], contract=(0, 0))
+        back = dot(swapped[...], pulled[...])
+        back = functools.reduce(
+            jnp.add,
+            [
+                jnp.where(low == l, back[l * seqs : (l + 1) * seqs], 0.0)
+                for l in range(tokens)
+            ],
+        )
+        slot = lane_ids((seqs, LANES)) // proj
+        for o in range(step_owners):
+            total = jnp.zeros((seqs, LANES), F32)
+            for t in range(tokens):
+                at = (o * tokens + t) * LANES
+                total = jnp.where(slot == t, fold_lanes(back[:, at : at + LANES], proj), total)
+            left_back[m * step_owners + o] = (total * (1.0 / seqs)).astype(BF16)
+        sums[...] += dot(pulled[...], block, contract=(1, 1))
+
+        @pl.when(row == own_row)
+        def _():
+            half = step_tokens * block_cols
+            mine = outer[pl.ds(pl.multiple_of(own_group * half, half), half)]
+            update = dot(mine, mapping_ref[...]) + offset_ref[...]
+            pair_ref[pl.ds(part * step_tokens, step_tokens)] = update.astype(BF16).reshape(
+                step_tokens, block_cols, pair_width
+            )
+
+        return carry
+
+    lax.fori_loop(0, prow_n * steps_a_block, step, 0)
+
+    back = (sums[...].T * (1.0 / seqs)).astype(BF16)
+    back = jnp.concatenate(
+        [
+            jnp.concatenate(
+                [
+                    back[l * seqs : (l + 1) * seqs, g * span : (g + 1) * span]
+                    for l in range(tokens)
+                ],
+                axis=1,
+            )
+            for g in range(groups)
+        ],
+        axis=0,
+    )
+    back = dot(back, shuffle, contract=(1, 1)).astype(BF16)
+    column_rows = []
+    for g in range(groups):
+        for r in range(prow_n):
+            right_back[g * prow_n + r] = back[
+                g * seqs : (g + 1) * seqs, r * LANES : (r + 1) * LANES
+            ]
+            column_rows.append(rows_ref[token_owner(g, r, core)])
+
+    def side(rows, grads):
+        total = dot(rows, grads, contract=(0, 0))
+        features = packed // tokens
+        slot = lane_ids((features, LANES)) // proj
+        kept = functools.reduce(
+            jnp.add,
+            [
+                jnp.where(slot == t, total[t * features : (t + 1) * features], 0.0)
+                for t in range(tokens)
+            ],
+        )
+        return fold_lanes(kept, proj)
+
+    left_side = side(rows_all, left_back[...].reshape(owners * seqs, LANES))
+    right_side = side(
+        jnp.concatenate(column_rows, axis=0), right_back[...].reshape(-1, LANES)
+    )
+    both = jnp.where(lane_ids(left_side.shape) < proj, left_side, right_side)
+
+    flat = weights.shape[1]
+    outer_f = weights[...].T
+    weight_rows = outer_f.reshape(proj, proj, pair_width).swapaxes(0, 1).reshape(flat, pair_width)
+
+    features = packed // tokens
+    message_ref[:flat] = weight_rows.astype(BF16)
+    message_ref[flat : flat + features] = both.astype(BF16)
+    message_ref[flat + features :] = left_back[token_owner(own_group, own_row, 1 - core)]
+    grads_ref[0] = left_back[token_owner(own_group, own_row, core)]
+    grads_ref[1] = right_back[own_group * prow_n + own_row]
+
+
+def close_kernel(
+    grads_ref,
+    own_ref,
+    message_ref,
+    normed_ref,
+    inverse_ref,
+    left_ref,
+    right_ref,
+    out_ref,
+    left_out_ref,
+    right_out_ref,
+    rows_out_ref,
+):
+    flat = out_ref.shape[0]
+    features, proj = left_out_ref.shape
+    out_ref[...] = own_ref[:flat].astype(F32) + message_ref[:flat].astype(F32)
+    both = own_ref[flat : flat + features].astype(F32)
+    both = both + message_ref[flat : flat + features].astype(F32)
+    left_out_ref[...] = both[:, :proj]
+    right_out_ref[...] = both[:, proj : 2 * proj]
+    left_back = grads_ref[0].astype(F32) + message_ref[flat + features :].astype(F32)
+    grad_normed = dot(left_back.astype(BF16), left_ref[...], contract=(1, 1))
+    grad_normed = grad_normed + dot(grads_ref[1], right_ref[...], contract=(1, 1))
+    normed = normed_ref[...]
+    mean_factor = group_mean(grad_normed, features, lax.Precision.HIGHEST)
+    projected = group_mean(grad_normed * normed, features, lax.Precision.HIGHEST)
+    rows_out_ref[...] = (
+        inverse_ref[...] * (grad_normed - mean_factor - normed * projected)
+    ).astype(BF16)
+
+
+def local_gathered(
+    homolog_features,
+    subset_homolog_positions,
+    first_side_matrix,
+    second_side_matrix,
+    final_mapping_matrix,
+    final_offset_vector,
+    upstream_sensitivity,
+):
+    prow_n, groups = lax.axis_size("prow"), lax.axis_size("px")
+    owners = prow_n * groups * 2
+    heads, tokens, features = homolog_features.shape
+    seqs = subset_homolog_positions.shape[0]
+    block_rows, block_cols, pair_width = upstream_sensitivity.shape
+    proj = first_side_matrix.shape[1]
+    flat = proj * proj
+    packed = tokens * features
+    step_tokens = 2 * tokens
+    shape = jax.ShapeDtypeStruct
+    vmem = pl.BlockSpec(memory_space=pltpu.VMEM)
+    smem = pl.BlockSpec(memory_space=pltpu.SMEM)
+    params = pltpu.CompilerParams(vmem_limit_bytes=48 * 1024 * 1024)
+
+    cot = lax.all_to_all(
+        jnp.broadcast_to(upstream_sensitivity[None], (prow_n * groups,) + upstream_sensitivity.shape),
+        ("prow", "px"), 0, 0,
+    ).reshape((prow_n, groups) + upstream_sensitivity.shape)
+
+    normed, inverse, sent = pl.pallas_call(
+        functools.partial(pick_kernel, features),
+        out_shape=(
+            shape((seqs, packed), F32),
+            shape((seqs, packed), F32),
+            shape((owners, seqs, packed), BF16),
+        ),
+        in_specs=[vmem] * 2,
+        out_specs=(vmem,) * 3,
+        compiler_params=params,
+        name="pick_rows",
+    )(subset_homolog_positions.reshape(1, seqs), homolog_features.reshape(heads, packed))
+    rows = lax.all_to_all(sent, ("px", "pc", "prow"), 0, 0)
+
+    one = jnp.eye(tokens, dtype=BF16)
+    left_one = jnp.kron(one, first_side_matrix)
+    left_wide = jnp.kron(one, jnp.tile(first_side_matrix, (1, tokens)))
+    right_one = jnp.kron(one, second_side_matrix)
+    mapping = final_mapping_matrix.reshape(proj, proj, pair_width)
+    mapping = mapping.swapaxes(0, 1).reshape(flat, pair_width)
+    place = jnp.stack([lax.axis_index("prow"), lax.axis_index("px"), lax.axis_index("pc")])
+
+    pairs = step_tokens * groups * block_cols
+    pair_delta, grads, message = pl.pallas_call(
+        pair_kernel,
+        out_shape=(
+            shape(upstream_sensitivity.shape, BF16),
+            shape((2, seqs, LANES), BF16),
+            shape((flat + features + seqs, LANES), BF16),
+        ),
+        in_specs=[smem] + [vmem] * 6,
+        out_specs=(vmem,) * 3,
+        scratch_shapes=[
+            pltpu.VMEM((owners, seqs, tokens * LANES), BF16),
+            pltpu.VMEM((pairs, flat), BF16),
+            pltpu.VMEM((groups * proj // tokens * block_cols, step_tokens * LANES), BF16),
+            pltpu.VMEM((owners, seqs, LANES), BF16),
+            pltpu.VMEM((groups * prow_n, seqs, LANES), BF16),
+            pltpu.VMEM((groups * proj // tokens * block_cols, tokens * seqs), BF16),
+            pltpu.VMEM((tokens * seqs, groups * proj // tokens * block_cols), BF16),
+            pltpu.VMEM((groups * proj // tokens * block_cols, tokens * seqs), F32),
+            pltpu.VMEM((pair_width, flat), F32),
+        ],
+        compiler_params=params,
+        name="pair_work",
+    )(place, rows, cot, mapping, left_wide, right_one, final_offset_vector.reshape(1, pair_width))
+
+    theirs = lax.ppermute(message, "pc", [(0, 1), (1, 0)])
+    output_weight_gradient, left_weight_gradient, right_weight_gradient, alignment = pl.pallas_call(
+        close_kernel,
+        out_shape=(
+            shape((flat, pair_width), F32),
+            shape((features, proj), F32),
+            shape((features, proj), F32),
+            shape((seqs, packed), BF16),
+        ),
+        in_specs=[vmem] * 7,
+        out_specs=(vmem,) * 4,
+        compiler_params=params,
+        name="close",
+    )(grads, message, theirs, normed, inverse, left_one, right_one)
+    return (
+        pair_delta,
+        alignment.reshape(seqs, tokens, features),
+        left_weight_gradient,
+        right_weight_gradient,
+        output_weight_gradient,
+    )
+
+
+def shapes_allow_gathering(
+    mesh_shape, features, positions, first_side, second_side, mapping, offset, cot
+):
+    rows_n, cols_n = mesh_shape["prow"], mesh_shape["pcol"]
+    parts = mesh_shape["rep"]
+    tokens = features.shape[1] // (rows_n * cols_n)
+    block_rows, block_cols = cot.shape[0] // (parts * rows_n), cot.shape[1] // cols_n
+    proj, width = first_side.shape[1], cot.shape[2]
+    return (
+        cols_n % 2 == 0
+        and cot.shape[1] * cot.shape[1] <= GATHERED_PAIRS
+        and tokens * proj == LANES
+        and proj % tokens == 0
+        and block_rows % (2 * tokens) == 0
+        and block_cols == rows_n * tokens == 16
+        and width % LANES == 0
+        and positions.shape[0] // parts % 16 == 0
+        and features.shape[2] * tokens % LANES == 0
+    )
+
+
 def solution(mesh):
-    return jax.shard_map(
-        local,
-        mesh=mesh,
-        in_specs=(
-            P("rep", ("pcol", "prow"), None),
-            P("rep"),
-            P(),
-            P(),
-            P(),
-            P(),
-            P(("rep", "prow"), "pcol", None),
-        ),
-        out_specs=(
-            P(("rep", "prow"), "pcol", None),
-            P("rep", ("pcol", "prow"), None),
-            P("rep", None),
-            P("rep", None),
-            P("rep", None),
-        ),
-        check_vma=False,
-    )
+    def run(local, over, columns, *args):
+        tokens_split = P("rep", columns + ("prow",), None)
+        pairs_split = P(("rep", "prow"), columns, None)
+        return jax.shard_map(
+            local,
+            mesh=over,
+            in_specs=(tokens_split, P("rep"), P(), P(), P(), P(), pairs_split),
+            out_specs=(pairs_split, tokens_split, P("rep", None), P("rep", None), P("rep", None)),
+            check_vma=False,
+        )(*args)
+
+    def program(*args):
+        if not shapes_allow_gathering(mesh.shape, *args):
+            return run(local_phased, mesh, ("pcol",), *args)
+        reps, rows_n, cols_n = (mesh.shape[name] for name in ("rep", "prow", "pcol"))
+        chips = Mesh(
+            mesh.devices.reshape(reps, rows_n, cols_n // 2, 2), ("rep", "prow", "px", "pc")
+        )
+        return run(local_gathered, chips, ("px", "pc"), *args)
+
+    return program

time: 91 us -> 61.6 us (0.68)
  starting transfers between devices: 32.8 us -> 11.1 us
  Pallas kernels: 0 us -> 14.5 us
  local copies, waits for them, and re-layouts: 16.7 us -> 7.54 us
  matrix products: 7.26 us -> 0 us
  other arithmetic: 7.42 us -> 0.42 us
  waiting for transfers between devices: 24.8 us -> 26.7 us
    all_to_all x6 -> x2, starting transfers between devices: 31.5 us -> 11.1 us  [the longest x1 7.38 us: local_gathered(): lax.all_to_all(jnp.broadcast_to(upstream_sensitivity[None], (prow_n * gro...]
    pallas_call x0 -> x3, Pallas kernels: none -> 14.5 us  [the longest x1 11.8 us: local_gathered(): pl.pallas_call(pair_kernel, out_shape=(shape(upstream_sensitivity.shape,...]
    dot_general x11 -> x0, matrix products: 7.26 us -> none  [the longest x1 2.08 us: block_step(): jnp.einsum('sip,sjq->ijpq', left_blk, right, preferred_element_type=jnp.f...]
    reshape x7 -> x3, local copies, waits for them, and re-layouts: 5.57 us -> 0.94 us  [the longest x1 0.73 us: local_gathered(): alignment.reshape(seqs, tokens, features)]
    convert_element_type x6 -> x1, local copies, waits for them, and re-layouts: 3.77 us -> 0.11 us  [local_gathered(): one = jnp.eye(tokens, dtype=BF16)]
    reduce_sum x9 -> x0, other arithmetic: 2.98 us -> none  [the longest x3 1.34 us: normalize(): variance = jnp.mean(centered * centered, axis=-1, keepdims=True)]
    convert_element_type x5 -> x1, other arithmetic: 1.58 us -> 0.01 us  [local_gathered(): one = jnp.eye(tokens, dtype=BF16)]
    ppermute x2 -> x1, starting transfers between devices: 1.33 us -> 0.01 us  [local_gathered(): theirs = lax.ppermute(message, 'pc', [(0, 1), (1, 0)])]
  transfers between devices with their start and end apart: 8 -> 3, of which waited for: 5 -> 3; matrix products, arithmetic and copies ran while one was open for 26% -> 2% of each run, Pallas kernels for 0% -> 2%
where the time goes in v3:
time: 61.6 us; the launch traced here: 61.1 us
  waiting for transfers between devices  26.7 us (43%)
  Pallas kernels  14.5 us (24%)
  starting transfers between devices  11.1 us (18%)
  local copies, waits for them, and re-layouts  7.54 us (12%)
  between operations  0.76 us (1%)
    all_to_all x1, waiting for transfers between devices, local_gathered(): rows = lax.all_to_all(sent, ('px', 'pc', 'prow'), 0, 0)  13.1 us
    all_to_all x1, waiting for transfers between devices, local_gathered(): lax.all_to_all(jnp.broadcast_to(upstream_sensitivity[None], (prow_n * gro...  12.3 us
    pallas_call x1, Pallas kernels, local_gathered(): pl.pallas_call(pair_kernel, out_shape=(shape(upstream_sensitivity.shape,...  11.8 us
    all_to_all x1, starting transfers between devices, local_gathered(): lax.all_to_all(jnp.broadcast_to(upstream_sensitivity[None], (prow_n * gro...  7.38 us
    unnamed x15, local copies, waits for them, and re-layouts  4.18 us
    all_to_all x1, starting transfers between devices, local_gathered(): rows = lax.all_to_all(sent, ('px', 'pc', 'prow'), 0, 0)  3.74 us
    broadcast_in_dim x1, local copies, waits for them, and re-layouts, local_gathered(): jnp.broadcast_to(upstream_sensitivity[None], (prow_n * groups,) + upstrea...  1.7 us
    pallas_call x1, Pallas kernels, local_gathered(): pl.pallas_call(functools.partial(pick_kernel, features), out_shape=(shape...  1.39 us
  transfers between devices with their start and end apart: 3, of which 3 were waited for; matrix products, arithmetic and copies ran while one was open for 2% of the time, Pallas kernels for 2%

profile of v3, /device:TPU:0, one launch (start us, length us, event | category | flops | bytes accessed | tf_op | source)
XLA Modules:
  0.0 61.1 jit_solution(8359471968343755304)
XLA Ops:
  0.6 1.7 %broadcast_in_dim.16 = bf16[8,16,16,128]{3,2,1,0:T(8,128)(2,1)} broadcast(bf16[16,16,128]{2,1,0:T(8,128)(2,1)} %param.13), dimensions={1,2,3} | broadcast | bytes 589824 | tf_op jit(solution)/shard_map/broadcast_in_dim | solution.py:451
  2.3 7.4 %all-to-all-start.1 = ((bf16[8,16,16,128]{3,2,1,0:T(8,128)(2,1)}), bf16[8,16,16,128]{3,2,1,0:T(8,128)(2,1)S(1)}, u32[]{:S(2)}, u32[]{:S(2)}) async-start(bf16[8,16,16,128]{3,2,1,0:T(8,128)(2,1)} %broadcast_in_dim.16), calls=%async_computation.1 | async-start | bytes 1048576 | tf_op jit(solution)/shard_map/all_to_all | solution.py:450
  9.7 0.1 copy.19.features_ref
  9.8 0.6 %copy-done = s32[64]{0:T(128)S(1)} copy-done((s32[64]{0:T(128)S(1)}, s32[64]{0:T(128)}, u32[]{:S(2)}) %copy-start) | copy-done | bytes 280
  10.5 1.4 %pick_rows.1 = (f32[64,256]{1,0:T(8,128)S(1)}, f32[64,256]{1,0:T(8,128)S(1)}, bf16[16,64,256]{2,1,0:T(8,128)(2,1)}) custom-call(s32[1,64]{1,0:T(1,128)S(1)} %bitcast.24, bf16[128,256]{1,0:T(8,128)(2,1)S(1)} %copy.19.features_ref), custom_call_target="tpu_custom_call" | custom-call | tf_op jit(solution)/shard_map/pick_rows/pallas_call | solution.py:455
  11.9 12.3 %all-to-all-done.1 = bf16[8,16,16,128]{3,2,1,0:T(8,128)(2,1)S(1)} async-done(((bf16[8,16,16,128]{3,2,1,0:T(8,128)(2,1)}), bf16[8,16,16,128]{3,2,1,0:T(8,128)(2,1)S(1)}, u32[]{:S(2)}, u32[]{:S(2)}) %all-to-all-start.1) | async-done | bytes 524320 | tf_op jit(solution)/shard_map/all_to_all | solution.py:450
  24.2 3.7 %all-to-all-start = ((bf16[16,64,256]{2,1,0:T(8,128)(2,1)}), bf16[16,64,256]{2,1,0:T(8,128)(2,1)S(1)}, u32[]{:S(2)}, u32[]{:S(2)}) async-start(bf16[16,64,256]{2,1,0:T(8,128)(2,1)} %get-tuple-element.15), calls=%async_computation | async-start | bytes 1048576 | tf_op jit(solution)/shard_map/all_to_all | solution.py:467
  28.0 0.1 copy.21
  28.1 0.6 copy-done.5
  28.7 0.2 broadcast_multiply_fusion.1
  28.8 0.1 mul.72
  29.0 0.1 copy.23.right_ref
  29.2 0.2 broadcast_multiply_fusion
  29.5 0.9 %copy-done.2 = bf16[1024,128]{1,0:T(8,128)(2,1)S(1)} copy-done((bf16[1024,128]{1,0:T(8,128)(2,1)S(1)}, bf16[1024,128]{1,0:T(8,128)(2,1)}, u32[]{:S(2)}) %copy-start.2) | copy-done | bytes 262168
  30.5 13.1 %all-to-all-done.rows_ref = bf16[16,64,256]{2,1,0:T(8,128)(2,1)S(1)} async-done(((bf16[16,64,256]{2,1,0:T(8,128)(2,1)}), bf16[16,64,256]{2,1,0:T(8,128)(2,1)S(1)}, u32[]{:S(2)}, u32[]{:S(2)}) %all-to-all-start) | async-done | bytes 524320 | tf_op jit(solution)/shard_map/all_to_all | solution.py:467
  43.6 0.7 %copy-done.1 = f32[128]{0:T(128)S(1)} copy-done((f32[128]{0:T(128)S(1)}, f32[128]{0:T(128)}, u32[]{:S(2)}) %copy-start.1) | copy-done | bytes 536
  44.3 11.8 %pair_work.1 = (bf16[16,16,128]{2,1,0:T(8,128)(2,1)}, bf16[2,64,128]{2,1,0:T(8,128)(2,1)S(1)}, bf16[1152,128]{1,0:T(8,128)(2,1)S(1)}) custom-call(s32[3]{0:T(128)S(1)} %pad_add_fusion.place_ref, bf16[16,64,256]{2,1,0:T(8,128)(2,1)S(1)} %all-to-all-done.rows_ref, bf16[4,2,16,16,128]{4,3,2,1,0:T(8,128)(2,1)S(1)} %bitcast.21, bf16[1024,128]{1,0:T(8,128)(2,1)S(1)} %bitcast.23, ...), custom_call_target="tpu_custom_call" | custom-call | tf_op jit(solution)/shard_map/pair_work/pallas_call | solution.py:478
  56.1 0.1 mul.75
  56.3 0.1 copy.24.left_ref
  56.4 1.3 %collective-permute-done.message_ref = bf16[1152,128]{1,0:T(8,128)(2,1)S(1)} collective-permute-done((bf16[1152,128]{1,0:T(8,128)(2,1)S(1)}, bf16[1152,128]{1,0:T(8,128)(2,1)S(1)}, u32[]{:S(2)}, u32[]{:S(2)}) %collective-permute-start) | collective-permute-done | bytes 294944 | tf_op jit(solution)/shard_map/ppermute | solution.py:502
  57.7 1.3 %close.1 = (f32[1024,128]{1,0:T(8,128)}, f32[64,32]{1,0:T(8,128)S(1)}, f32[64,32]{1,0:T(8,128)S(1)}, bf16[64,256]{1,0:T(8,128)(2,1)S(1)}) custom-call(bf16[2,64,128]{2,1,0:T(8,128)(2,1)S(1)} %get-tuple-element.17.grads_ref, bf16[1152,128]{1,0:T(8,128)(2,1)S(1)} %get-tuple-element.18.own_ref, bf16[1152,128]{1,0:T(8,128)(2,1)S(1)} %collective-permute-done.message_ref, ...), custom_call_target="tpu_custom_call" | custom-call | tf_op jit(solution)/shard_map/close/pallas_call | solution.py:503
  59.0 0.7 %reshape.69 = bf16[64,4,64]{2,1,0:T(4,128)(2,1)} reshape(bf16[64,256]{1,0:T(8,128)(2,1)S(1)} %get-tuple-element.21) | data formatting | bytes 65536 | tf_op jit(solution)/shard_map/reshape | solution.py:518
  59.8 0.7 %copy.26 = f32[64,32]{0,1:T(8,128)} copy(f32[64,32]{1,0:T(8,128)S(1)} %get-tuple-element.32) | data formatting | bytes 16384
  60.4 0.7 %copy.27 = f32[64,32]{0,1:T(8,128)} copy(f32[64,32]{1,0:T(8,128)S(1)} %get-tuple-element.33) | data formatting | bytes 16384
  (15 shorter events, 0.4 us)
Async XLA Ops:
  2.3 7.4 %copy-start.3 = (bf16[128,4,64]{0,2,1:T(8,128)(2,1)S(1)}, bf16[128,4,64]{0,2,1:T(8,128)(2,1)}, u32[]{:S(2)}) copy-start(bf16[128,4,64]{0,2,1:T(8,128)(2,1)} %param.7) | copy-start | bytes 196612
  2.3 21.9 %all-to-all-start.1 = ((bf16[8,16,16,128]{3,2,1,0:T(8,128)(2,1)}), bf16[8,16,16,128]{3,2,1,0:T(8,128)(2,1)S(1)}, u32[]{:S(2)}, u32[]{:S(2)}) async-start(bf16[8,16,16,128]{3,2,1,0:T(8,128)(2,1)} %broadcast_in_dim.16), calls=%async_computation.1 | async-start | bytes 1048576 | tf_op jit(solution)/shard_map/all_to_all | solution.py:450
  9.8 0.7 %copy-start = (s32[64]{0:T(128)S(1)}, s32[64]{0:T(128)}, u32[]{:S(2)}) copy-start(s32[64]{0:T(128)} %param.8) | copy-start | bytes 772
  24.2 19.4 %all-to-all-start = ((bf16[16,64,256]{2,1,0:T(8,128)(2,1)}), bf16[16,64,256]{2,1,0:T(8,128)(2,1)S(1)}, u32[]{:S(2)}, u32[]{:S(2)}) async-start(bf16[16,64,256]{2,1,0:T(8,128)(2,1)} %get-tuple-element.15), calls=%async_computation | async-start | bytes 1048576 | tf_op jit(solution)/shard_map/all_to_all | solution.py:467
  28.0 0.7 %copy-start.5 = (bf16[64,32]{0,1:T(8,128)(2,1)S(1)}, bf16[64,32]{0,1:T(8,128)(2,1)}, u32[]{:S(2)}) copy-start(bf16[64,32]{0,1:T(8,128)(2,1)} %param.10) | copy-start | bytes 12292
  28.0 0.7 %copy-start.4 = (bf16[64,32]{0,1:T(8,128)(2,1)S(1)}, bf16[64,32]{0,1:T(8,128)(2,1)}, u32[]{:S(2)}) copy-start(bf16[64,32]{0,1:T(8,128)(2,1)} %param.9) | copy-start | bytes 12292
  29.4 1.0 %copy-start.2 = (bf16[1024,128]{1,0:T(8,128)(2,1)S(1)}, bf16[1024,128]{1,0:T(8,128)(2,1)}, u32[]{:S(2)}) copy-start(bf16[1024,128]{1,0:T(8,128)(2,1)} %param.11) | copy-start | bytes 786436
  43.6 0.7 %copy-start.1 = (f32[128]{0:T(128)S(1)}, f32[128]{0:T(128)}, u32[]{:S(2)}) copy-start(f32[128]{0:T(128)} %param.12) | copy-start | bytes 1540
  56.1 1.6 %collective-permute-start = (bf16[1152,128]{1,0:T(8,128)(2,1)S(1)}, bf16[1152,128]{1,0:T(8,128)(2,1)S(1)}, u32[]{:S(2)}, u32[]{:S(2)}) collective-permute-start(bf16[1152,128]{1,0:T(8,128)(2,1)S(1)} %get-tuple-element.18.own_ref), channel_id=1, source_target_pairs={{0,1},{1,0},{2,3},{3,2},{4,5},{5,4},{6,7},{7,6},{8,9},{9,8},{10,11... | collective-permute-start | bytes 884744 | tf_op jit(solution)/shard_map/ppermute | solution.py:502

commit v4 on v3

--- a/solution.py
+++ b/solution.py
@@ -203,11 +203,11 @@
     return dot(x, block, precision=precision)
 
 
-def pick_kernel(group, positions_ref, features_ref, normed_ref, inverse_ref, sent_ref):
-    heads = features_ref.shape[0]
-    seqs = normed_ref.shape[0]
+def pick_kernel(group, positions_ref, features_ref, cot_ref, normed_ref, inverse_ref, sent_ref):
+    heads = features_ref.shape[1]
+    seqs, packed = normed_ref.shape
     wanted = positions_ref[...] == lax.broadcasted_iota(jnp.int32, (heads, seqs), 0)
-    chosen = dot(wanted.astype(BF16), features_ref[...], contract=(0, 0))
+    chosen = dot(wanted.astype(BF16), features_ref[...], contract=(0, 1))
     mean_factor = group_mean(chosen.astype(BF16), group, None)
     centered = chosen - mean_factor
     variance = group_mean(centered * centered, group, lax.Precision.HIGHEST)
@@ -215,13 +215,19 @@
     normed = centered * inverse
     normed_ref[...] = normed
     inverse_ref[...] = inverse
-    sent_ref[...] = jnp.broadcast_to(normed.astype(BF16)[None], sent_ref.shape)
+    pairs = cot_ref.shape[0]
+    low = normed.astype(BF16)
+    for k in range(sent_ref.shape[0]):
+        sent_ref[k, :pairs] = cot_ref[...]
+        for n in range(packed // LANES):
+            at = pairs + n * seqs
+            sent_ref[k, at : at + seqs] = low[:, n * LANES : (n + 1) * LANES]
 
 
 def pair_kernel(
     place_ref,
-    rows_ref,
-    cot_ref,
+    mine_ref,
+    theirs_ref,
     mapping_ref,
     left_ref,
     right_ref,
@@ -239,8 +245,11 @@
     sums,
     weights,
 ):
-    owners, seqs, packed = rows_ref.shape
-    prow_n, groups, block_rows, block_cols, pair_width = cot_ref.shape
+    prow_n, groups = mine_ref.shape[:2]
+    block_rows, block_cols, pair_width = pair_ref.shape
+    pairs = block_rows * block_cols
+    owners, seqs = left_back.shape[:2]
+    packed = left_ref.shape[0]
     tokens = left_ref.shape[1] // LANES
     proj = LANES // tokens
     highs = proj // tokens
@@ -250,12 +259,29 @@
     def token_owner(group, row, parity):
         return (2 * group + parity) * prow_n + row
 
-    rows_all = rows_ref[...].reshape(owners * seqs, packed)
-    expanded[...] = dot(rows_all, left_ref[...]).astype(BF16).reshape(expanded.shape)
+    def rows_of(ref, g, r, start):
+        return jnp.concatenate(
+            [
+                ref[r, g, start + n * seqs : start + (n + 1) * seqs]
+                for n in range(packed // LANES)
+            ],
+            axis=1,
+        )
+
+    places = [(g, r) for g in range(groups) for r in range(prow_n)]
+    order = [token_owner(g, r, core) for g, r in places]
+    order = order + [token_owner(g, r, 1 - core) for g, r in places]
+    rows_mine = [rows_of(mine_ref, g, r, pairs) for g, r in places]
+    rows_all = jnp.concatenate(
+        rows_mine + [rows_of(theirs_ref, g, r, 0) for g, r in places], axis=0
+    )
+    wide_left = dot(rows_all, left_ref[...]).astype(BF16)
+    for n, owner in enumerate(order):
+        expanded[owner] = wide_left[n * seqs : (n + 1) * seqs]
 
     side_rows = []
     for g in range(groups):
-        chunks = [rows_ref[token_owner(g, r, core)] for r in range(prow_n)]
+        chunks = rows_mine[g * prow_n : (g + 1) * prow_n]
         side_rows.append(
             jnp.concatenate([dot(x, right_ref[...]).astype(BF16) for x in chunks], axis=1)
         )
@@ -278,6 +304,7 @@
     step_tokens = outer.shape[0] // (groups * block_cols)
     step_owners = step_tokens // tokens
     steps_a_block = block_rows // step_tokens
+    share = step_tokens * block_cols
 
     def step(m, carry):
         row, part = m // steps_a_block, m % steps_a_block
@@ -290,9 +317,7 @@
         )
         cot = jnp.concatenate(
             [
-                cot_ref[row, g, pl.ds(part * step_tokens, step_tokens)].reshape(
-                    step_tokens * block_cols, pair_width
-                )
+                mine_ref[row, g, pl.ds(pl.multiple_of(part * share, share), share)]
                 for g in range(groups)
             ],
             axis=0,
@@ -328,8 +353,7 @@
 
         @pl.when(row == own_row)
         def _():
-            half = step_tokens * block_cols
-            mine = outer[pl.ds(pl.multiple_of(own_group * half, half), half)]
+            mine = outer[pl.ds(pl.multiple_of(own_group * share, share), share)]
             update = dot(mine, mapping_ref[...]) + offset_ref[...]
             pair_ref[pl.ds(part * step_tokens, step_tokens)] = update.astype(BF16).reshape(
                 step_tokens, block_cols, pair_width
@@ -354,41 +378,34 @@
         axis=0,
     )
     back = dot(back, shuffle, contract=(1, 1)).astype(BF16)
-    column_rows = []
-    for g in range(groups):
-        for r in range(prow_n):
-            right_back[g * prow_n + r] = back[
-                g * seqs : (g + 1) * seqs, r * LANES : (r + 1) * LANES
-            ]
-            column_rows.append(rows_ref[token_owner(g, r, core)])
-
-    def side(rows, grads):
-        total = dot(rows, grads, contract=(0, 0))
+    for g, r in places:
+        right_back[g * prow_n + r] = back[g * seqs : (g + 1) * seqs, r * LANES : (r + 1) * LANES]
+
+    def side(grads, rows):
+        total = dot(grads, rows, contract=(0, 0))
         features = packed // tokens
-        slot = lane_ids((features, LANES)) // proj
-        kept = functools.reduce(
+        return functools.reduce(
             jnp.add,
             [
-                jnp.where(slot == t, total[t * features : (t + 1) * features], 0.0)
+                total[t * proj : (t + 1) * proj, t * features : (t + 1) * features]
                 for t in range(tokens)
             ],
         )
-        return fold_lanes(kept, proj)
-
-    left_side = side(rows_all, left_back[...].reshape(owners * seqs, LANES))
+
+    left_side = side(jnp.concatenate([left_back[owner] for owner in order], axis=0), rows_all)
     right_side = side(
-        jnp.concatenate(column_rows, axis=0), right_back[...].reshape(-1, LANES)
-    )
-    both = jnp.where(lane_ids(left_side.shape) < proj, left_side, right_side)
+        right_back[...].reshape(-1, LANES), jnp.concatenate(rows_mine, axis=0)
+    )
+    both = jnp.concatenate([left_side, right_side], axis=0).astype(BF16)
+    both = jnp.concatenate([both, jnp.zeros_like(both)], axis=1)
 
     flat = weights.shape[1]
     outer_f = weights[...].T
     weight_rows = outer_f.reshape(proj, proj, pair_width).swapaxes(0, 1).reshape(flat, pair_width)
 
-    features = packed // tokens
     message_ref[:flat] = weight_rows.astype(BF16)
-    message_ref[flat : flat + features] = both.astype(BF16)
-    message_ref[flat + features :] = left_back[token_owner(own_group, own_row, 1 - core)]
+    message_ref[flat : flat + 2 * proj] = both
+    message_ref[flat + 2 * proj :] = left_back[token_owner(own_group, own_row, 1 - core)]
     grads_ref[0] = left_back[token_owner(own_group, own_row, core)]
     grads_ref[1] = right_back[own_group * prow_n + own_row]
 
@@ -407,20 +424,22 @@
     rows_out_ref,
 ):
     flat = out_ref.shape[0]
-    features, proj = left_out_ref.shape
+    proj, features = left_out_ref.shape
     out_ref[...] = own_ref[:flat].astype(F32) + message_ref[:flat].astype(F32)
-    both = own_ref[flat : flat + features].astype(F32)
-    both = both + message_ref[flat : flat + features].astype(F32)
-    left_out_ref[...] = both[:, :proj]
-    right_out_ref[...] = both[:, proj : 2 * proj]
-    left_back = grads_ref[0].astype(F32) + message_ref[flat + features :].astype(F32)
+    sides = slice(flat, flat + 2 * proj)
+    both = own_ref[sides, :features].astype(F32) + message_ref[sides, :features].astype(F32)
+    left_out_ref[...] = both[:proj]
+    right_out_ref[...] = both[proj:]
+    left_back = grads_ref[0].astype(F32) + message_ref[flat + 2 * proj :].astype(F32)
     grad_normed = dot(left_back.astype(BF16), left_ref[...], contract=(1, 1))
     grad_normed = grad_normed + dot(grads_ref[1], right_ref[...], contract=(1, 1))
     normed = normed_ref[...]
     mean_factor = group_mean(grad_normed, features, lax.Precision.HIGHEST)
     projected = group_mean(grad_normed * normed, features, lax.Precision.HIGHEST)
-    rows_out_ref[...] = (
-        inverse_ref[...] * (grad_normed - mean_factor - normed * projected)
+    result = inverse_ref[...] * (grad_normed - mean_factor - normed * projected)
+    rows_out_ref[...] = jnp.stack(
+        [result[:, t * features : (t + 1) * features] for t in range(rows_out_ref.shape[1])],
+        axis=1,
     ).astype(BF16)
 
 
@@ -447,24 +466,27 @@
     smem = pl.BlockSpec(memory_space=pltpu.SMEM)
     params = pltpu.CompilerParams(vmem_limit_bytes=48 * 1024 * 1024)
 
-    cot = lax.all_to_all(
-        jnp.broadcast_to(upstream_sensitivity[None], (prow_n * groups,) + upstream_sensitivity.shape),
-        ("prow", "px"), 0, 0,
-    ).reshape((prow_n, groups) + upstream_sensitivity.shape)
-
+    receivers = prow_n * groups
+    pairs = block_rows * block_cols
+    length = pairs + seqs * packed // LANES
     normed, inverse, sent = pl.pallas_call(
         functools.partial(pick_kernel, features),
         out_shape=(
             shape((seqs, packed), F32),
             shape((seqs, packed), F32),
-            shape((owners, seqs, packed), BF16),
+            shape((receivers, length, LANES), BF16),
         ),
-        in_specs=[vmem] * 2,
+        in_specs=[vmem] * 3,
         out_specs=(vmem,) * 3,
         compiler_params=params,
         name="pick_rows",
-    )(subset_homolog_positions.reshape(1, seqs), homolog_features.reshape(heads, packed))
-    rows = lax.all_to_all(sent, ("px", "pc", "prow"), 0, 0)
+    )(
+        subset_homolog_positions.reshape(1, seqs),
+        homolog_features.transpose(1, 2, 0).reshape(packed, heads),
+        upstream_sensitivity.reshape(pairs, pair_width),
+    )
+    mine = lax.all_to_all(sent, ("prow", "px"), 0, 0).reshape(prow_n, groups, length, LANES)
+    theirs = lax.ppermute(mine[:, :, pairs:], "pc", [(0, 1), (1, 0)])
 
     one = jnp.eye(tokens, dtype=BF16)
     left_one = jnp.kron(one, first_side_matrix)
@@ -474,19 +496,18 @@
     mapping = mapping.swapaxes(0, 1).reshape(flat, pair_width)
     place = jnp.stack([lax.axis_index("prow"), lax.axis_index("px"), lax.axis_index("pc")])
 
-    pairs = step_tokens * groups * block_cols
     pair_delta, grads, message = pl.pallas_call(
         pair_kernel,
         out_shape=(
             shape(upstream_sensitivity.shape, BF16),
             shape((2, seqs, LANES), BF16),
-            shape((flat + features + seqs, LANES), BF16),
+            shape((flat + 2 * proj + seqs, LANES), BF16),
         ),
         in_specs=[smem] + [vmem] * 6,
         out_specs=(vmem,) * 3,
         scratch_shapes=[
             pltpu.VMEM((owners, seqs, tokens * LANES), BF16),
-            pltpu.VMEM((pairs, flat), BF16),
+            pltpu.VMEM((step_tokens * groups * block_cols, flat), BF16),
             pltpu.VMEM((groups * proj // tokens * block_cols, step_tokens * LANES), BF16),
             pltpu.VMEM((owners, seqs, LANES), BF16),
             pltpu.VMEM((groups * prow_n, seqs, LANES), BF16),
@@ -497,16 +518,16 @@
         ],
         compiler_params=params,
         name="pair_work",
-    )(place, rows, cot, mapping, left_wide, right_one, final_offset_vector.reshape(1, pair_width))
+    )(place, mine, theirs, mapping, left_wide, right_one, final_offset_vector.reshape(1, pair_width))
 
     theirs = lax.ppermute(message, "pc", [(0, 1), (1, 0)])
     output_weight_gradient, left_weight_gradient, right_weight_gradient, alignment = pl.pallas_call(
         close_kernel,
         out_shape=(
             shape((flat, pair_width), F32),
-            shape((features, proj), F32),
-            shape((features, proj), F32),
-            shape((seqs, packed), BF16),
+            shape((proj, features), F32),
+            shape((proj, features), F32),
+            shape((seqs, tokens, features), BF16),
         ),
         in_specs=[vmem] * 7,
         out_specs=(vmem,) * 4,
@@ -515,9 +536,9 @@
     )(grads, message, theirs, normed, inverse, left_one, right_one)
     return (
         pair_delta,
-        alignment.reshape(seqs, tokens, features),
-        left_weight_gradient,
-        right_weight_gradient,
+        alignment,
+        left_weight_gradient.T,
+        right_weight_gradient.T,
         output_weight_gradient,
     )
 
@@ -537,7 +558,8 @@
         and proj % tokens == 0
         and block_rows % (2 * tokens) == 0
         and block_cols == rows_n * tokens == 16
-        and width % LANES == 0
+        and width == LANES
+        and features.shape[2] >= 2 * proj
         and positions.shape[0] // parts % 16 == 0
         and features.shape[2] * tokens % LANES == 0
     )

time: 61.6 us -> 49.3 us (0.80)
  waiting for transfers between devices: 26.7 us -> 20.2 us
  starting transfers between devices: 11.1 us -> 7.67 us
  local copies, waits for them, and re-layouts: 7.54 us -> 5.34 us
    all_to_all x2 -> x1, waiting for transfers between devices: 25.4 us -> 18.9 us  [local_gathered(): lax.all_to_all(sent, ('prow', 'px'), 0, 0)]
    all_to_all x2 -> x1, starting transfers between devices: 11.1 us -> 7.25 us  [local_gathered(): lax.all_to_all(sent, ('prow', 'px'), 0, 0)]
    broadcast_in_dim x1 -> x0, local copies, waits for them, and re-layouts: 1.7 us -> none  [local_gathered(): jnp.broadcast_to(upstream_sensitivity[None], (prow_n * groups,) + upstrea...]
    reshape x2 -> x0, local copies, waits for them, and re-layouts: 0.84 us -> none  [the longest x1 0.73 us: local_gathered(): alignment.reshape(seqs, tokens, features)]
  transfers between devices with their start and end apart: 3 -> 3, of which waited for: 3 -> 3; matrix products, arithmetic and copies ran while one was open for 2% -> 3% of each run, Pallas kernels for 2% -> 0%
where the time goes in v4:
time: 49.3 us; the launch traced here: 48.9 us
  waiting for transfers between devices  20.2 us (41%)
  Pallas kernels  14.6 us (30%)
  starting transfers between devices  7.67 us (16%)
  local copies, waits for them, and re-layouts  5.34 us (11%)
  between operations  0.74 us (2%)
    all_to_all x1, waiting for transfers between devices, local_gathered(): lax.all_to_all(sent, ('prow', 'px'), 0, 0)  18.9 us
    pallas_call x1, Pallas kernels, local_gathered(): pl.pallas_call(pair_kernel, out_shape=(shape(upstream_sensitivity.shape,...  11.6 us
    all_to_all x1, starting transfers between devices, local_gathered(): lax.all_to_all(sent, ('prow', 'px'), 0, 0)  7.25 us
    unnamed x15, local copies, waits for them, and re-layouts  4.5 us
    pallas_call x1, Pallas kernels, local_gathered(): pl.pallas_call(close_kernel, out_shape=(shape((flat, pair_width), F32), s...  1.5 us
    pallas_call x1, Pallas kernels, local_gathered(): pl.pallas_call(functools.partial(pick_kernel, features), out_shape=(shape...  1.49 us
    ppermute x1, waiting for transfers between devices, local_gathered(): theirs = lax.ppermute(message, 'pc', [(0, 1), (1, 0)])  1.03 us
  transfers between devices with their start and end apart: 3, of which 3 were waited for; matrix products, arithmetic and copies ran while one was open for 3% of the time, Pallas kernels for 0%

profile of v4, /device:TPU:0, one launch (start us, length us, event | category | flops | bytes accessed | tf_op | source)
XLA Modules:
  0.0 48.9 jit_solution(11647992678539077244)
XLA Ops:
  0.6 0.6 %copy-done.2 = s32[64]{0:T(128)S(1)} copy-done((s32[64]{0:T(128)S(1)}, s32[64]{0:T(128)}, u32[]{:S(2)}) %copy-start.2) | copy-done | bytes 280
  1.3 0.8 %copy-done = bf16[128,4,64]{0,2,1:T(8,128)(2,1)S(1)} copy-done((bf16[128,4,64]{0,2,1:T(8,128)(2,1)S(1)}, bf16[128,4,64]{0,2,1:T(8,128)(2,1)}, u32[]{:S(2)}) %copy-start) | copy-done | bytes 65560
  2.1 0.8 %copy-done.1 = bf16[16,16,128]{2,1,0:T(8,128)(2,1)S(1)} copy-done((bf16[16,16,128]{2,1,0:T(8,128)(2,1)S(1)}, bf16[16,16,128]{2,1,0:T(8,128)(2,1)}, u32[]{:S(2)}) %copy-start.1) | copy-done | bytes 65560
  3.0 1.5 %pick_rows.1 = (f32[64,256]{1,0:T(8,128)S(1)}, f32[64,256]{1,0:T(8,128)S(1)}, bf16[8,384,128]{2,1,0:T(8,128)(2,1)}) custom-call(s32[1,64]{1,0:T(1,128)S(1)} %bitcast.32, bf16[256,128]{1,0:T(8,128)(2,1)S(1)} %bitcast.30, bf16[256,128]{1,0:T(8,128)(2,1)S(1)} %bitcast.31), custom_call_target="tpu_custom_call" | custom-call | tf_op jit(solution)/shard_map/pick_rows/pallas_call | solution.py:472
  4.5 7.3 %all-to-all-start = ((bf16[8,384,128]{2,1,0:T(8,128)(2,1)}), bf16[8,384,128]{2,1,0:T(8,128)(2,1)S(1)}, u32[]{:S(2)}, u32[]{:S(2)}) async-start(bf16[8,384,128]{2,1,0:T(8,128)(2,1)} %get-tuple-element.15), calls=%async_computation | async-start | bytes 1572864 | tf_op jit(solution)/shard_map/all_to_all | solution.py:488
  11.7 0.1 copy.17
  11.8 0.6 %copy-done.6 = bf16[64,32]{0,1:T(8,128)(2,1)S(1)} copy-done((bf16[64,32]{0,1:T(8,128)(2,1)S(1)}, bf16[64,32]{0,1:T(8,128)(2,1)}, u32[]{:S(2)}) %copy-start.6) | copy-done | bytes 4120
  12.4 0.2 broadcast_multiply_fusion.1
  12.6 0.1 mul.72
  12.7 0.1 copy.19.right_ref
  12.9 0.1 copy.18
  13.0 18.9 %all-to-all-done = bf16[8,384,128]{2,1,0:T(8,128)(2,1)S(1)} async-done(((bf16[8,384,128]{2,1,0:T(8,128)(2,1)}), bf16[8,384,128]{2,1,0:T(8,128)(2,1)S(1)}, u32[]{:S(2)}, u32[]{:S(2)}) %all-to-all-start) | async-done | bytes 786464 | tf_op jit(solution)/shard_map/all_to_all | solution.py:488
  32.0 0.2 broadcast_multiply_fusion
  32.2 0.9 %copy-done.4 = bf16[1024,128]{1,0:T(8,128)(2,1)S(1)} copy-done((bf16[1024,128]{1,0:T(8,128)(2,1)S(1)}, bf16[1024,128]{1,0:T(8,128)(2,1)}, u32[]{:S(2)}) %copy-start.4) | copy-done | bytes 262168
  33.1 0.1 copy.16
  33.2 0.1 pad_add_fusion.place_ref
  33.3 0.2 collective-permute-done.theirs_ref
  33.5 0.7 %copy-done.3 = f32[128]{0:T(128)S(1)} copy-done((f32[128]{0:T(128)S(1)}, f32[128]{0:T(128)}, u32[]{:S(2)}) %copy-start.3) | copy-done | bytes 536
  34.2 11.6 %pair_work.1 = (bf16[16,16,128]{2,1,0:T(8,128)(2,1)}, bf16[2,64,128]{2,1,0:T(8,128)(2,1)S(1)}, bf16[1152,128]{1,0:T(8,128)(2,1)S(1)}) custom-call(s32[3]{0:T(128)S(1)} %pad_add_fusion.place_ref, bf16[4,2,384,128]{3,2,1,0:T(8,128)(2,1)S(1)} %bitcast.27, bf16[4,2,128,128]{3,2,1,0:T(8,128)(2,1)S(1)} %collective-permute-done.theirs_ref, ...), custom_call_target="tpu_custom_call" | custom-call | tf_op jit(solution)/shard_map/pair_work/pallas_call | solution.py:499
  45.8 0.3 collective-permute-start.1
  46.1 0.1 mul.75
  46.3 0.1 copy.20.left_ref
  46.4 1.0 %collective-permute-done.1.message_ref = bf16[1152,128]{1,0:T(8,128)(2,1)S(1)} collective-permute-done((bf16[1152,128]{1,0:T(8,128)(2,1)S(1)}, bf16[1152,128]{1,0:T(8,128)(2,1)S(1)}, u32[]{:S(2)}, u32[]{:S(2)}) %collective-permute-start.1) | collective-permute-done | bytes 294944 | tf_op jit(solution)/shard_map/ppermute | solution.py:523
  47.4 1.5 %close.1 = (f32[1024,128]{1,0:T(8,128)}, f32[32,64]{1,0:T(8,128)}, f32[32,64]{1,0:T(8,128)}, bf16[64,4,64]{2,1,0:T(4,128)(2,1)}) custom-call(bf16[2,64,128]{2,1,0:T(8,128)(2,1)S(1)} %get-tuple-element.17.grads_ref, bf16[1152,128]{1,0:T(8,128)(2,1)S(1)} %get-tuple-element.18.own_ref, bf16[1152,128]{1,0:T(8,128)(2,1)S(1)} %collective-permute-done.1.message_ref, ...), custom_call_target="tpu_custom_call" | custom-call | tf_op jit(solution)/shard_map/close/pallas_call | solution.py:524
  (13 shorter events, 0.2 us)
Async XLA Ops:
  0.6 0.7 %copy-start.2 = (s32[64]{0:T(128)S(1)}, s32[64]{0:T(128)}, u32[]{:S(2)}) copy-start(s32[64]{0:T(128)} %param.8) | copy-start | bytes 772
  1.3 0.8 %copy-start = (bf16[128,4,64]{0,2,1:T(8,128)(2,1)S(1)}, bf16[128,4,64]{0,2,1:T(8,128)(2,1)}, u32[]{:S(2)}) copy-start(bf16[128,4,64]{0,2,1:T(8,128)(2,1)} %param.7) | copy-start | bytes 196612
  2.1 0.8 %copy-start.1 = (bf16[16,16,128]{2,1,0:T(8,128)(2,1)S(1)}, bf16[16,16,128]{2,1,0:T(8,128)(2,1)}, u32[]{:S(2)}) copy-start(bf16[16,16,128]{2,1,0:T(8,128)(2,1)} %param.13) | copy-start | bytes 196612
  4.5 27.4 %all-to-all-start = ((bf16[8,384,128]{2,1,0:T(8,128)(2,1)}), bf16[8,384,128]{2,1,0:T(8,128)(2,1)S(1)}, u32[]{:S(2)}, u32[]{:S(2)}) async-start(bf16[8,384,128]{2,1,0:T(8,128)(2,1)} %get-tuple-element.15), calls=%async_computation | async-start | bytes 1572864 | tf_op jit(solution)/shard_map/all_to_all | solution.py:488
  11.7 0.7 %copy-start.6 = (bf16[64,32]{0,1:T(8,128)(2,1)S(1)}, bf16[64,32]{0,1:T(8,128)(2,1)}, u32[]{:S(2)}) copy-start(bf16[64,32]{0,1:T(8,128)(2,1)} %param.10) | copy-start | bytes 12292
  11.7 0.7 %copy-start.5 = (bf16[64,32]{0,1:T(8,128)(2,1)S(1)}, bf16[64,32]{0,1:T(8,128)(2,1)}, u32[]{:S(2)}) copy-start(bf16[64,32]{0,1:T(8,128)(2,1)} %param.9) | copy-start | bytes 12292
  31.9 1.6 %collective-permute-start = (bf16[4,2,128,128]{3,2,1,0:T(8,128)(2,1)S(1)}, bf16[4,2,128,128]{3,2,1,0:T(8,128)(2,1)S(1)}, u32[]{:S(2)}, u32[]{:S(2)}) collective-permute-start(bf16[4,2,128,128]{3,2,1,0:T(8,128)(2,1)S(1)} %slice.4), channel_id=1, source_target_pairs={{0,1},{1,0},{2,3},{3,2},{4,5},{5,4},{6,7},{7,6},{8,9},{9,8},{10,11... | collective-permute-start | bytes 786440 | tf_op jit(solution)/shard_map/ppermute | solution.py:489
  32.2 1.0 %copy-start.4 = (bf16[1024,128]{1,0:T(8,128)(2,1)S(1)}, bf16[1024,128]{1,0:T(8,128)(2,1)}, u32[]{:S(2)}) copy-start(bf16[1024,128]{1,0:T(8,128)(2,1)} %param.11) | copy-start | bytes 786436
  33.5 0.7 %copy-start.3 = (f32[128]{0:T(128)S(1)}, f32[128]{0:T(128)}, u32[]{:S(2)}) copy-start(f32[128]{0:T(128)} %param.12) | copy-start | bytes 1540
  45.8 1.6 %collective-permute-start.1 = (bf16[1152,128]{1,0:T(8,128)(2,1)S(1)}, bf16[1152,128]{1,0:T(8,128)(2,1)S(1)}, u32[]{:S(2)}, u32[]{:S(2)}) collective-permute-start(bf16[1152,128]{1,0:T(8,128)(2,1)S(1)} %get-tuple-element.18.own_ref), channel_id=1, source_target_pairs={{0,1},{1,0},{2,3},{3,2},{4,5},{5,4},{6,7},{7,6},{8,9},{9,8},{10,11... | collective-permute-start | bytes 884744 | tf_op jit(solution)/shard_map/ppermute | solution.py:523

commit v5 on v4

--- a/solution.py
+++ b/solution.py
@@ -187,12 +187,18 @@
     return lax.broadcasted_iota(jnp.int32, shape, len(shape) - 1)
 
 
-def fold_lanes(x, width):
-    shift = LANES // 2
-    while shift >= width:
-        x = x + pltpu.roll(x, shift, x.ndim - 1)
-        shift //= 2
-    return x
+def fold_tokens(parts):
+    quarter = LANES // 4
+    chunk = lane_ids(parts[0].shape) // quarter
+    first, even = chunk < 2, chunk % 2 == 0
+    halves = [
+        jnp.where(first, parts[t], parts[t + 2])
+        + pltpu.roll(jnp.where(first, parts[t + 2], parts[t]), 2 * quarter, 1)
+        for t in range(2)
+    ]
+    other = jnp.where(even, halves[1], halves[0])
+    moved = jnp.where(even, pltpu.roll(other, 3 * quarter, 1), pltpu.roll(other, quarter, 1))
+    return jnp.where(even, halves[0], halves[1]) + moved
 
 
 def group_mean(x, group, precision):
@@ -203,25 +209,93 @@
     return dot(x, block, precision=precision)
 
 
-def pick_kernel(group, positions_ref, features_ref, cot_ref, normed_ref, inverse_ref, sent_ref):
+def pick_kernel(
+    positions_ref,
+    features_ref,
+    cot_ref,
+    left_ref,
+    right_ref,
+    offset_ref,
+    normed_ref,
+    inverse_ref,
+    left_wide_ref,
+    left_one_ref,
+    right_one_ref,
+    offset_out_ref,
+    sent_ref,
+    positions,
+    features,
+    left,
+    right,
+    low,
+    in_sems,
+    cot_sems,
+    low_sems,
+):
+    inputs = [
+        pltpu.make_async_copy(source, target, in_sems.at[n])
+        for n, (source, target) in enumerate(
+            [
+                (positions_ref, positions),
+                (features_ref, features),
+                (left_ref, left),
+                (right_ref, right),
+                (offset_ref, offset_out_ref),
+            ]
+        )
+    ]
+    for copy in inputs:
+        copy.start()
+    receivers = sent_ref.shape[0]
+    pairs = cot_ref.shape[0]
+    cot_copies = [
+        pltpu.make_async_copy(cot_ref, sent_ref.at[k, pl.ds(0, pairs)], cot_sems.at[k])
+        for k in range(receivers)
+    ]
+    for copy in cot_copies:
+        copy.start()
+
     heads = features_ref.shape[1]
     seqs, packed = normed_ref.shape
-    wanted = positions_ref[...] == lax.broadcasted_iota(jnp.int32, (heads, seqs), 0)
-    chosen = dot(wanted.astype(BF16), features_ref[...], contract=(0, 1))
-    mean_factor = group_mean(chosen.astype(BF16), group, None)
+    proj, channels = left_ref.shape
+    tokens = packed // channels
+    for copy in inputs:
+        copy.wait()
+    wanted = positions[...] == lax.broadcasted_iota(jnp.int32, (heads, seqs), 0)
+    chosen = dot(wanted.astype(BF16), features[...], contract=(0, 1))
+    mean_factor = group_mean(chosen.astype(BF16), channels, None)
     centered = chosen - mean_factor
-    variance = group_mean(centered * centered, group, lax.Precision.HIGHEST)
+    variance = group_mean(centered * centered, channels, lax.Precision.HIGHEST)
     inverse = lax.rsqrt(variance + 1e-05)
     normed = centered * inverse
+    pieces = packed // LANES
+    for n in range(pieces):
+        low[n * seqs : (n + 1) * seqs] = normed[:, n * LANES : (n + 1) * LANES].astype(BF16)
+    low_copies = [
+        pltpu.make_async_copy(low, sent_ref.at[k, pl.ds(pairs, pieces * seqs)], low_sems.at[k])
+        for k in range(receivers)
+    ]
+    for copy in low_copies:
+        copy.start()
     normed_ref[...] = normed
     inverse_ref[...] = inverse
-    pairs = cot_ref.shape[0]
-    low = normed.astype(BF16)
-    for k in range(sent_ref.shape[0]):
-        sent_ref[k, :pairs] = cot_ref[...]
-        for n in range(packed // LANES):
-            at = pairs + n * seqs
-            sent_ref[k, at : at + seqs] = low[:, n * LANES : (n + 1) * LANES]
+
+    repeat = lane_ids((proj, LANES)) % proj
+    repeat = (repeat == lax.broadcasted_iota(jnp.int32, (proj, LANES), 0)).astype(BF16)
+    left_row = dot(left[...], repeat, contract=(0, 0))
+    right_row = dot(right[...], repeat, contract=(0, 0))
+    slot = lane_ids(left_row.shape) // proj
+    nothing = jnp.zeros(left_row.shape, BF16)
+    for t in range(tokens):
+        here = slice(t * channels, (t + 1) * channels)
+        left_one_ref[here] = jnp.where(slot == t, left_row, 0.0).astype(BF16)
+        right_one_ref[here] = jnp.where(slot == t, right_row, 0.0).astype(BF16)
+        for other in range(tokens):
+            left_wide_ref[here, other * LANES : (other + 1) * LANES] = (
+                left_row.astype(BF16) if other == t else nothing
+            )
+    for copy in cot_copies + low_copies:
+        copy.wait()
 
 
 def pair_kernel(
@@ -229,6 +303,7 @@
     mine_ref,
     theirs_ref,
     mapping_ref,
+    turned_mapping_ref,
     left_ref,
     right_ref,
     offset_ref,
@@ -294,9 +369,9 @@
     right = dot(right, shuffle)
     for g in range(groups):
         for l in range(tokens):
-            swapped[l * seqs : (l + 1) * seqs, g * span : (g + 1) * span] = right[
-                g * seqs : (g + 1) * seqs, l * span : (l + 1) * span
-            ].astype(BF16)
+            swapped[l * seqs : (l + 1) * seqs, g * span : (g + 1) * span] = (
+                right[g * seqs : (g + 1) * seqs, l * span : (l + 1) * span] * (1.0 / seqs)
+            ).astype(BF16)
     turned[...] = swapped[...].astype(F32).T.astype(BF16)
 
     sums[...] = jnp.zeros_like(sums)
@@ -322,8 +397,8 @@
             ],
             axis=0,
         )
-        made = dot(turned[...], block) * (1.0 / seqs)
-        grad = dot(cot, mapping_ref[...], contract=(1, 1))
+        made = dot(turned[...], block)
+        grad = dot(cot, turned_mapping_ref[...])
         for g in range(groups):
             for t in range(step_tokens):
                 here = slice((g * step_tokens + t) * block_cols, (g * step_tokens + t + 1) * block_cols)
@@ -342,13 +417,12 @@
                 for l in range(tokens)
             ],
         )
-        slot = lane_ids((seqs, LANES)) // proj
         for o in range(step_owners):
-            total = jnp.zeros((seqs, LANES), F32)
-            for t in range(tokens):
-                at = (o * tokens + t) * LANES
-                total = jnp.where(slot == t, fold_lanes(back[:, at : at + LANES], proj), total)
-            left_back[m * step_owners + o] = (total * (1.0 / seqs)).astype(BF16)
+            parts = [
+                back[:, (o * tokens + t) * LANES : (o * tokens + t + 1) * LANES]
+                for t in range(tokens)
+            ]
+            left_back[m * step_owners + o] = fold_tokens(parts).astype(BF16)
         sums[...] += dot(pulled[...], block, contract=(1, 1))
 
         @pl.when(row == own_row)
@@ -460,7 +534,7 @@
     proj = first_side_matrix.shape[1]
     flat = proj * proj
     packed = tokens * features
-    step_tokens = 2 * tokens
+    step_tokens = block_rows
     shape = jax.ShapeDtypeStruct
     vmem = pl.BlockSpec(memory_space=pltpu.VMEM)
     smem = pl.BlockSpec(memory_space=pltpu.SMEM)
@@ -469,29 +543,43 @@
     receivers = prow_n * groups
     pairs = block_rows * block_cols
     length = pairs + seqs * packed // LANES
-    normed, inverse, sent = pl.pallas_call(
-        functools.partial(pick_kernel, features),
+    hbm = pl.BlockSpec(memory_space=pltpu.HBM)
+    normed, inverse, left_wide, left_one, right_one, offset, sent = pl.pallas_call(
+        pick_kernel,
         out_shape=(
             shape((seqs, packed), F32),
             shape((seqs, packed), F32),
+            shape((packed, tokens * LANES), BF16),
+            shape((packed, LANES), BF16),
+            shape((packed, LANES), BF16),
+            shape((1, pair_width), F32),
             shape((receivers, length, LANES), BF16),
         ),
-        in_specs=[vmem] * 3,
-        out_specs=(vmem,) * 3,
+        in_specs=[hbm] * 6,
+        out_specs=(vmem,) * 6 + (hbm,),
+        scratch_shapes=[
+            pltpu.VMEM((1, seqs), jnp.int32),
+            pltpu.VMEM((packed, heads), BF16),
+            pltpu.VMEM((proj, features), BF16),
+            pltpu.VMEM((proj, features), BF16),
+            pltpu.VMEM((seqs * packed // LANES, LANES), BF16),
+            pltpu.SemaphoreType.DMA((5,)),
+            pltpu.SemaphoreType.DMA((receivers,)),
+            pltpu.SemaphoreType.DMA((receivers,)),
+        ],
         compiler_params=params,
         name="pick_rows",
     )(
         subset_homolog_positions.reshape(1, seqs),
         homolog_features.transpose(1, 2, 0).reshape(packed, heads),
         upstream_sensitivity.reshape(pairs, pair_width),
+        first_side_matrix.T,
+        second_side_matrix.T,
+        final_offset_vector.reshape(1, pair_width),
     )
     mine = lax.all_to_all(sent, ("prow", "px"), 0, 0).reshape(prow_n, groups, length, LANES)
     theirs = lax.ppermute(mine[:, :, pairs:], "pc", [(0, 1), (1, 0)])
 
-    one = jnp.eye(tokens, dtype=BF16)
-    left_one = jnp.kron(one, first_side_matrix)
-    left_wide = jnp.kron(one, jnp.tile(first_side_matrix, (1, tokens)))
-    right_one = jnp.kron(one, second_side_matrix)
     mapping = final_mapping_matrix.reshape(proj, proj, pair_width)
     mapping = mapping.swapaxes(0, 1).reshape(flat, pair_width)
     place = jnp.stack([lax.axis_index("prow"), lax.axis_index("px"), lax.axis_index("pc")])
@@ -503,7 +591,7 @@
             shape((2, seqs, LANES), BF16),
             shape((flat + 2 * proj + seqs, LANES), BF16),
         ),
-        in_specs=[smem] + [vmem] * 6,
+        in_specs=[smem] + [vmem] * 7,
         out_specs=(vmem,) * 3,
         scratch_shapes=[
             pltpu.VMEM((owners, seqs, tokens * LANES), BF16),
@@ -518,7 +606,7 @@
         ],
         compiler_params=params,
         name="pair_work",
-    )(place, mine, theirs, mapping, left_wide, right_one, final_offset_vector.reshape(1, pair_width))
+    )(place, mine, theirs, mapping, mapping.T, left_wide, right_one, offset)
 
     theirs = lax.ppermute(message, "pc", [(0, 1), (1, 0)])
     output_weight_gradient, left_weight_gradient, right_weight_gradient, alignment = pl.pallas_call(
@@ -555,8 +643,8 @@
         cols_n % 2 == 0
         and cot.shape[1] * cot.shape[1] <= GATHERED_PAIRS
         and tokens * proj == LANES
-        and proj % tokens == 0
-        and block_rows % (2 * tokens) == 0
+        and tokens == 4
+        and block_rows % tokens == 0
         and block_cols == rows_n * tokens == 16
         and width == LANES
         and features.shape[2] >= 2 * proj

time: 49.3 us -> 48.2 us (0.978)
  blocking collectives: 0 us -> 27.2 us
  waiting for transfers between devices: 20.2 us -> 1.78 us
  starting transfers between devices: 7.67 us -> 0.28 us
  local copies, waits for them, and re-layouts: 5.34 us -> 4.16 us
  Pallas kernels: 14.6 us -> 13.6 us
    all_to_all x0 -> x1, blocking collectives: none -> 27.2 us  [local_gathered(): lax.all_to_all(sent, ('prow', 'px'), 0, 0)]
    all_to_all x1 -> x0, waiting for transfers between devices: 18.9 us -> none  [local_gathered(): lax.all_to_all(sent, ('prow', 'px'), 0, 0)]
    all_to_all x1 -> x0, starting transfers between devices: 7.25 us -> none  [local_gathered(): lax.all_to_all(sent, ('prow', 'px'), 0, 0)]
    pallas_call x1, Pallas kernels: 11.6 us -> 10 us  [local_gathered(): pl.pallas_call(pair_kernel, out_shape=(shape(upstream_sensitivity.shape,...]
    unnamed x15 -> x14, local copies, waits for them, and re-layouts: 4.5 us -> 3.9 us
    pallas_call x1, Pallas kernels: 1.49 us -> 2.06 us  [local_gathered(): pl.pallas_call(pick_kernel, out_shape=(shape((seqs, packed), F32), shape(...]
    mul x4 -> x0, local copies, waits for them, and re-layouts: 0.52 us -> none  [the longest x2 0.26 us: local_gathered(): right_one = jnp.kron(one, second_side_matrix)]
  transfers between devices with their start and end apart: 3 -> 2, of which waited for: 3 -> 2; matrix products, arithmetic and copies ran while one was open for 3% -> 1% of each run, Pallas kernels for 0% -> 0%
where the time goes in v5:
time: 48.2 us; the launch traced here: 47.8 us
  blocking collectives  27.2 us (56%)
  Pallas kernels  13.6 us (28%)
  local copies, waits for them, and re-layouts  4.16 us (9%)
  waiting for transfers between devices  1.78 us (4%)
  between operations  0.71 us (1%)
    all_to_all x1, blocking collectives, local_gathered(): lax.all_to_all(sent, ('prow', 'px'), 0, 0)  27.2 us
    pallas_call x1, Pallas kernels, local_gathered(): pl.pallas_call(pair_kernel, out_shape=(shape(upstream_sensitivity.shape,...  10 us
    unnamed x14, local copies, waits for them, and re-layouts  3.9 us
    pallas_call x1, Pallas kernels, local_gathered(): pl.pallas_call(pick_kernel, out_shape=(shape((seqs, packed), F32), shape(...  2.06 us
    pallas_call x1, Pallas kernels, local_gathered(): pl.pallas_call(close_kernel, out_shape=(shape((flat, pair_width), F32), s...  1.51 us
    ppermute x1, waiting for transfers between devices, local_gathered(): theirs = lax.ppermute(message, 'pc', [(0, 1), (1, 0)])  1.44 us
  transfers between devices with their start and end apart: 2, of which 2 were waited for; matrix products, arithmetic and copies ran while one was open for 1% of the time, Pallas kernels for 0%

profile of v5, /device:TPU:0, one launch (start us, length us, event | category | flops | bytes accessed | tf_op | source)
XLA Modules:
  0.0 47.8 jit_solution(6513472482063678267)
XLA Ops:
  0.6 0.0 copy-start.2
  0.6 0.0 copy-start.4
  0.7 0.0 copy-start.5
  0.7 0.7 %copy-done.2 = bf16[64,32]{0,1:T(8,128)(2,1)S(1)} copy-done((bf16[64,32]{0,1:T(8,128)(2,1)S(1)}, bf16[64,32]{0,1:T(8,128)(2,1)}, u32[]{:S(2)}) %copy-start.2) | copy-done | bytes 4120
  1.3 0.0 copy-done.4
  1.3 0.0 copy-done.5
  1.3 0.0 copy-start
  1.3 0.8 %copy-done = bf16[128,4,64]{0,2,1:T(8,128)(2,1)S(1)} copy-done((bf16[128,4,64]{0,2,1:T(8,128)(2,1)S(1)}, bf16[128,4,64]{0,2,1:T(8,128)(2,1)}, u32[]{:S(2)}) %copy-start) | copy-done | bytes 65560
  2.2 0.0 copy-start.1
  2.2 0.8 %copy-done.1 = bf16[16,16,128]{2,1,0:T(8,128)(2,1)S(1)} copy-done((bf16[16,16,128]{2,1,0:T(8,128)(2,1)S(1)}, bf16[16,16,128]{2,1,0:T(8,128)(2,1)}, u32[]{:S(2)}) %copy-start.1) | copy-done | bytes 65560
  3.0 0.0 copy-start.3
  3.0 0.7 %copy-done.3 = bf16[64,32]{0,1:T(8,128)(2,1)S(1)} copy-done((bf16[64,32]{0,1:T(8,128)(2,1)S(1)}, bf16[64,32]{0,1:T(8,128)(2,1)}, u32[]{:S(2)}) %copy-start.3) | copy-done | bytes 4120
  3.7 2.1 %pick_rows.1 = (f32[64,256]{1,0:T(8,128)S(1)}, f32[64,256]{1,0:T(8,128)S(1)}, bf16[256,512]{1,0:T(8,128)(2,1)S(1)}, bf16[256,128]{1,0:T(8,128)(2,1)S(1)}, bf16[2...) custom-call(s32[1,64]{1,0:T(1,128)S(1)} %bitcast.28, ...), custom_call_target="tpu_custom_call" | custom-call | tf_op jit(solution)/shard_map/pick_rows/pallas_call | solution.py:547
  5.8 27.2 %all_to_all.5 = bf16[8,384,128]{2,1,0:T(8,128)(2,1)S(1)} all-to-all(bf16[8,384,128]{2,1,0:T(8,128)(2,1)S(1)} %get-tuple-element.19), channel_id=1, replica_groups=mesh['rep'=2,'prow'=4,'px'=2,'pc'=2] {'prow','px'}, dimensions={0} | all-to-all | bytes 1572864 | tf_op jit(solution)/shard_map/all_to_all | solution.py:580
  33.0 0.1 collective-permute-start
  33.1 0.8 %copy-done.6 = bf16[1024,128]{1,0:T(8,128)(2,1)S(1)} copy-done((bf16[1024,128]{1,0:T(8,128)(2,1)S(1)}, bf16[1024,128]{1,0:T(8,128)(2,1)}, u32[]{:S(2)}) %copy-start.6) | copy-done | bytes 262168
  33.9 0.1 copy.15
  34.0 0.1 copy.16
  34.2 0.1 pad_add_fusion.place_ref
  34.3 0.3 collective-permute-done.theirs_ref
  34.6 10.0 %pair_work.1 = (bf16[16,16,128]{2,1,0:T(8,128)(2,1)}, bf16[2,64,128]{2,1,0:T(8,128)(2,1)S(1)}, bf16[1152,128]{1,0:T(8,128)(2,1)S(1)}) custom-call(s32[3]{0:T(128)S(1)} %pad_add_fusion.place_ref, bf16[4,2,384,128]{3,2,1,0:T(8,128)(2,1)S(1)} %bitcast.20, bf16[4,2,128,128]{3,2,1,0:T(8,128)(2,1)S(1)} %collective-permute-done.theirs_ref, ...), custom_call_target="tpu_custom_call" | custom-call | tf_op jit(solution)/shard_map/pair_work/pallas_call | solution.py:587
  44.6 0.2 collective-permute-start.1
  44.9 1.4 %collective-permute-done.1.message_ref = bf16[1152,128]{1,0:T(8,128)(2,1)S(1)} collective-permute-done((bf16[1152,128]{1,0:T(8,128)(2,1)S(1)}, bf16[1152,128]{1,0:T(8,128)(2,1)S(1)}, u32[]{:S(2)}, u32[]{:S(2)}) %collective-permute-start.1) | collective-permute-done | bytes 294944 | tf_op jit(solution)/shard_map/ppermute | solution.py:611
  46.3 1.5 %close.1 = (f32[1024,128]{1,0:T(8,128)}, f32[32,64]{1,0:T(8,128)}, f32[32,64]{1,0:T(8,128)}, bf16[64,4,64]{2,1,0:T(4,128)(2,1)}) custom-call(bf16[2,64,128]{2,1,0:T(8,128)(2,1)S(1)} %get-tuple-element.24.grads_ref, bf16[1152,128]{1,0:T(8,128)(2,1)S(1)} %get-tuple-element.25.own_ref, bf16[1152,128]{1,0:T(8,128)(2,1)S(1)} %collective-permute-done.1.message_ref, ...), custom_call_target="tpu_custom_call" | custom-call | tf_op jit(solution)/shard_map/close/pallas_call | solution.py:612
  (2 shorter events, 0.0 us)
Async XLA Ops:
  0.6 0.7 %copy-start.2 = (bf16[64,32]{0,1:T(8,128)(2,1)S(1)}, bf16[64,32]{0,1:T(8,128)(2,1)}, u32[]{:S(2)}) copy-start(bf16[64,32]{0,1:T(8,128)(2,1)} %param.9) | copy-start | bytes 12292
  0.6 0.7 %copy-start.4 = (s32[64]{0:T(128)S(1)}, s32[64]{0:T(128)}, u32[]{:S(2)}) copy-start(s32[64]{0:T(128)} %param.8) | copy-start | bytes 772
  0.7 0.7 %copy-start.5 = (f32[128]{0:T(128)S(1)}, f32[128]{0:T(128)}, u32[]{:S(2)}) copy-start(f32[128]{0:T(128)} %param.12) | copy-start | bytes 1540
  1.3 0.8 %copy-start = (bf16[128,4,64]{0,2,1:T(8,128)(2,1)S(1)}, bf16[128,4,64]{0,2,1:T(8,128)(2,1)}, u32[]{:S(2)}) copy-start(bf16[128,4,64]{0,2,1:T(8,128)(2,1)} %param.7) | copy-start | bytes 196612
  2.2 0.8 %copy-start.1 = (bf16[16,16,128]{2,1,0:T(8,128)(2,1)S(1)}, bf16[16,16,128]{2,1,0:T(8,128)(2,1)}, u32[]{:S(2)}) copy-start(bf16[16,16,128]{2,1,0:T(8,128)(2,1)} %param.13) | copy-start | bytes 196612
  3.0 0.7 %copy-start.3 = (bf16[64,32]{0,1:T(8,128)(2,1)S(1)}, bf16[64,32]{0,1:T(8,128)(2,1)}, u32[]{:S(2)}) copy-start(bf16[64,32]{0,1:T(8,128)(2,1)} %param.10) | copy-start | bytes 12292
  33.0 1.0 %copy-start.6 = (bf16[1024,128]{1,0:T(8,128)(2,1)S(1)}, bf16[1024,128]{1,0:T(8,128)(2,1)}, u32[]{:S(2)}) copy-start(bf16[1024,128]{1,0:T(8,128)(2,1)} %param.11) | copy-start | bytes 786436
  33.0 1.6 %collective-permute-start = (bf16[4,2,128,128]{3,2,1,0:T(8,128)(2,1)S(1)}, bf16[4,2,128,128]{3,2,1,0:T(8,128)(2,1)S(1)}, u32[]{:S(2)}, u32[]{:S(2)}) collective-permute-start(bf16[4,2,128,128]{3,2,1,0:T(8,128)(2,1)S(1)} %slice.4), channel_id=1, source_target_pairs={{0,1},{1,0},{2,3},{3,2},{4,5},{5,4},{6,7},{7,6},{8,9},{9,8},{10,11... | collective-permute-start | bytes 786440 | tf_op jit(solution)/shard_map/ppermute | solution.py:581
  44.6 1.6 %collective-permute-start.1 = (bf16[1152,128]{1,0:T(8,128)(2,1)S(1)}, bf16[1152,128]{1,0:T(8,128)(2,1)S(1)}, u32[]{:S(2)}, u32[]{:S(2)}) collective-permute-start(bf16[1152,128]{1,0:T(8,128)(2,1)S(1)} %get-tuple-element.25.own_ref), channel_id=1, source_target_pairs={{0,1},{1,0},{2,3},{3,2},{4,5},{5,4},{6,7},{7,6},{8,9},{9,8},{10,11... | collective-permute-start | bytes 884744 | tf_op jit(solution)/shard_map/ppermute | solution.py:611

commit v6 on v5

--- a/solution.py
+++ b/solution.py
@@ -212,7 +212,6 @@
 def pick_kernel(
     positions_ref,
     features_ref,
-    cot_ref,
     left_ref,
     right_ref,
     offset_ref,
@@ -222,15 +221,12 @@
     left_one_ref,
     right_one_ref,
     offset_out_ref,
-    sent_ref,
+    low_ref,
     positions,
     features,
     left,
     right,
-    low,
     in_sems,
-    cot_sems,
-    low_sems,
 ):
     inputs = [
         pltpu.make_async_copy(source, target, in_sems.at[n])
@@ -246,15 +242,6 @@
     ]
     for copy in inputs:
         copy.start()
-    receivers = sent_ref.shape[0]
-    pairs = cot_ref.shape[0]
-    cot_copies = [
-        pltpu.make_async_copy(cot_ref, sent_ref.at[k, pl.ds(0, pairs)], cot_sems.at[k])
-        for k in range(receivers)
-    ]
-    for copy in cot_copies:
-        copy.start()
-
     heads = features_ref.shape[1]
     seqs, packed = normed_ref.shape
     proj, channels = left_ref.shape
@@ -270,13 +257,9 @@
     normed = centered * inverse
     pieces = packed // LANES
     for n in range(pieces):
-        low[n * seqs : (n + 1) * seqs] = normed[:, n * LANES : (n + 1) * LANES].astype(BF16)
-    low_copies = [
-        pltpu.make_async_copy(low, sent_ref.at[k, pl.ds(pairs, pieces * seqs)], low_sems.at[k])
-        for k in range(receivers)
-    ]
-    for copy in low_copies:
-        copy.start()
+        low_ref[0, n * seqs : (n + 1) * seqs] = normed[:, n * LANES : (n + 1) * LANES].astype(
+            BF16
+        )
     normed_ref[...] = normed
     inverse_ref[...] = inverse
 
@@ -294,16 +277,52 @@
             left_wide_ref[here, other * LANES : (other + 1) * LANES] = (
                 left_row.astype(BF16) if other == t else nothing
             )
-    for copy in cot_copies + low_copies:
-        copy.wait()
-
-
-def pair_kernel(
+
+
+def place_blocks(place_ref, offsets, refs, out_ref):
+    blocks = [(ref, n) for ref in refs for n in range(ref.shape[0])]
+    for (down, across), (ref, n) in zip(offsets, blocks, strict=True):
+        out_ref[place_ref[0] ^ down, place_ref[1] ^ across] = ref[n]
+
+
+def pull_kernel(offsets, place_ref, mapping_ref, *refs):
+    *cot_refs, cot_ref, pulled_ref = refs
+    prow_n, groups, pairs, pair_width = cot_ref.shape
+    highs = mapping_ref.shape[1] // LANES
+    block_rows = pulled_ref.shape[2] // LANES
+    block_cols = pairs // block_rows
+    place_blocks(place_ref, offsets, cot_refs, cot_ref)
+
+    def step(r, carry):
+        grad = dot(cot_ref[r].reshape(groups * pairs, pair_width), mapping_ref[...])
+        for g in range(groups):
+            for t in range(block_rows):
+                start = (g * block_rows + t) * block_cols
+                lanes = slice(t * LANES, (t + 1) * LANES)
+                for h in range(highs):
+                    there = slice((g * highs + h) * block_cols, (g * highs + h + 1) * block_cols)
+                    pulled_ref[r, there, lanes] = grad[
+                        start : start + block_cols, h * LANES : (h + 1) * LANES
+                    ].astype(BF16)
+        return carry
+
+    lax.fori_loop(0, prow_n, step, 0)
+
+
+def pair_kernel(offsets, pieces, place_ref, theirs_from_ref, *refs):
+    *rest, mine_ref, theirs_ref = refs
+    place_blocks(place_ref, offsets, refs[:pieces], mine_ref)
+    place_blocks(place_ref, offsets, [theirs_from_ref], theirs_ref)
+    pair_work(place_ref, mine_ref, theirs_ref, *rest[pieces:])
+
+
+def pair_work(
     place_ref,
     mine_ref,
     theirs_ref,
+    cot_ref,
+    pulled_ref,
     mapping_ref,
-    turned_mapping_ref,
     left_ref,
     right_ref,
     offset_ref,
@@ -312,7 +331,6 @@
     message_ref,
     expanded,
     outer,
-    pulled,
     left_back,
     right_back,
     turned,
@@ -322,7 +340,6 @@
 ):
     prow_n, groups = mine_ref.shape[:2]
     block_rows, block_cols, pair_width = pair_ref.shape
-    pairs = block_rows * block_cols
     owners, seqs = left_back.shape[:2]
     packed = left_ref.shape[0]
     tokens = left_ref.shape[1] // LANES
@@ -334,21 +351,17 @@
     def token_owner(group, row, parity):
         return (2 * group + parity) * prow_n + row
 
-    def rows_of(ref, g, r, start):
+    def rows_of(ref, g, r):
         return jnp.concatenate(
-            [
-                ref[r, g, start + n * seqs : start + (n + 1) * seqs]
-                for n in range(packed // LANES)
-            ],
-            axis=1,
+            [ref[r, g, n * seqs : (n + 1) * seqs] for n in range(packed // LANES)], axis=1
         )
 
     places = [(g, r) for g in range(groups) for r in range(prow_n)]
     order = [token_owner(g, r, core) for g, r in places]
     order = order + [token_owner(g, r, 1 - core) for g, r in places]
-    rows_mine = [rows_of(mine_ref, g, r, pairs) for g, r in places]
+    rows_mine = [rows_of(mine_ref, g, r) for g, r in places]
     rows_all = jnp.concatenate(
-        rows_mine + [rows_of(theirs_ref, g, r, 0) for g, r in places], axis=0
+        rows_mine + [rows_of(theirs_ref, g, r) for g, r in places], axis=0
     )
     wide_left = dot(rows_all, left_ref[...]).astype(BF16)
     for n, owner in enumerate(order):
@@ -392,13 +405,12 @@
         )
         cot = jnp.concatenate(
             [
-                mine_ref[row, g, pl.ds(pl.multiple_of(part * share, share), share)]
+                cot_ref[row, g, pl.ds(pl.multiple_of(part * share, share), share)]
                 for g in range(groups)
             ],
             axis=0,
         )
         made = dot(turned[...], block)
-        grad = dot(cot, turned_mapping_ref[...])
         for g in range(groups):
             for t in range(step_tokens):
                 here = slice((g * step_tokens + t) * block_cols, (g * step_tokens + t + 1) * block_cols)
@@ -407,9 +419,9 @@
                     there = slice((g * highs + h) * block_cols, (g * highs + h + 1) * block_cols)
                     cols = slice(h * LANES, (h + 1) * LANES)
                     outer[here, cols] = made[there, lanes].astype(BF16)
-                    pulled[there, lanes] = grad[here, cols].astype(BF16)
         weights[...] += dot(cot, outer[...], contract=(0, 0))
-        back = dot(swapped[...], pulled[...])
+        pulled = pulled_ref[row]
+        back = dot(swapped[...], pulled)
         back = functools.reduce(
             jnp.add,
             [
@@ -423,7 +435,7 @@
                 for t in range(tokens)
             ]
             left_back[m * step_owners + o] = fold_tokens(parts).astype(BF16)
-        sums[...] += dot(pulled[...], block, contract=(1, 1))
+        sums[...] += dot(pulled, block, contract=(1, 1))
 
         @pl.when(row == own_row)
         def _():
@@ -538,13 +550,12 @@
     shape = jax.ShapeDtypeStruct
     vmem = pl.BlockSpec(memory_space=pltpu.VMEM)
     smem = pl.BlockSpec(memory_space=pltpu.SMEM)
-    params = pltpu.CompilerParams(vmem_limit_bytes=48 * 1024 * 1024)
-
-    receivers = prow_n * groups
+    params = pltpu.CompilerParams(vmem_limit_bytes=40 * 1024 * 1024)
+
     pairs = block_rows * block_cols
-    length = pairs + seqs * packed // LANES
+    length = seqs * packed // LANES
     hbm = pl.BlockSpec(memory_space=pltpu.HBM)
-    normed, inverse, left_wide, left_one, right_one, offset, sent = pl.pallas_call(
+    normed, inverse, left_wide, left_one, right_one, offset, low = pl.pallas_call(
         pick_kernel,
         out_shape=(
             shape((seqs, packed), F32),
@@ -553,60 +564,91 @@
             shape((packed, LANES), BF16),
             shape((packed, LANES), BF16),
             shape((1, pair_width), F32),
-            shape((receivers, length, LANES), BF16),
+            shape((1, length, LANES), BF16),
         ),
-        in_specs=[hbm] * 6,
-        out_specs=(vmem,) * 6 + (hbm,),
+        in_specs=[hbm] * 5,
+        out_specs=(vmem,) * 7,
         scratch_shapes=[
             pltpu.VMEM((1, seqs), jnp.int32),
             pltpu.VMEM((packed, heads), BF16),
             pltpu.VMEM((proj, features), BF16),
             pltpu.VMEM((proj, features), BF16),
-            pltpu.VMEM((seqs * packed // LANES, LANES), BF16),
             pltpu.SemaphoreType.DMA((5,)),
-            pltpu.SemaphoreType.DMA((receivers,)),
-            pltpu.SemaphoreType.DMA((receivers,)),
         ],
-        compiler_params=params,
+        compiler_params=pltpu.CompilerParams(vmem_limit_bytes=60 * 1024 * 1024),
         name="pick_rows",
     )(
         subset_homolog_positions.reshape(1, seqs),
         homolog_features.transpose(1, 2, 0).reshape(packed, heads),
-        upstream_sensitivity.reshape(pairs, pair_width),
         first_side_matrix.T,
         second_side_matrix.T,
         final_offset_vector.reshape(1, pair_width),
     )
-    mine = lax.all_to_all(sent, ("prow", "px"), 0, 0).reshape(prow_n, groups, length, LANES)
-    theirs = lax.ppermute(mine[:, :, pairs:], "pc", [(0, 1), (1, 0)])
+
+    def gathered(own, order):
+        pieces, offsets = [own], [(0, 0)]
+        for axis, size in order:
+            for bit in range(size.bit_length() - 1):
+                swap = [(n, n ^ (1 << bit)) for n in range(size)]
+                held = pieces[0] if len(pieces) == 1 else jnp.concatenate(pieces, axis=0)
+                pieces.append(lax.ppermute(held, axis, swap))
+                step = (1 << bit, 0) if axis == "prow" else (0, 1 << bit)
+                offsets += [(down + step[0], across + step[1]) for down, across in offsets]
+        return pieces, offsets
+
+    along, across = ("prow", prow_n), ("px", groups)
+    cots, cot_offsets = gathered(
+        upstream_sensitivity.reshape(1, pairs, pair_width), (along, across)
+    )
+    rows, row_offsets = gathered(low, (across, along))
+    theirs = lax.ppermute(jnp.concatenate(rows, axis=0), "pc", [(0, 1), (1, 0)])
 
     mapping = final_mapping_matrix.reshape(proj, proj, pair_width)
     mapping = mapping.swapaxes(0, 1).reshape(flat, pair_width)
     place = jnp.stack([lax.axis_index("prow"), lax.axis_index("px"), lax.axis_index("pc")])
 
+    columns = groups * proj // tokens * block_cols
+    cot, pulled = pl.pallas_call(
+        functools.partial(pull_kernel, cot_offsets),
+        out_shape=(
+            shape((prow_n, groups, pairs, pair_width), BF16),
+            shape((prow_n, columns, block_rows * LANES), BF16),
+        ),
+        in_specs=[smem] + [vmem] * (1 + len(cots)),
+        out_specs=(vmem,) * 2,
+        compiler_params=params,
+        cost_estimate=pl.CostEstimate(
+            flops=2 * prow_n * groups * pairs * pair_width * flat,
+            bytes_accessed=2 * prow_n * groups * pairs * (2 * pair_width + flat),
+            transcendentals=0,
+        ),
+        name="pull_back",
+    )(place, mapping.T, *cots)
+
     pair_delta, grads, message = pl.pallas_call(
-        pair_kernel,
+        functools.partial(pair_kernel, row_offsets, len(rows)),
         out_shape=(
             shape(upstream_sensitivity.shape, BF16),
             shape((2, seqs, LANES), BF16),
             shape((flat + 2 * proj + seqs, LANES), BF16),
         ),
-        in_specs=[smem] + [vmem] * 7,
+        in_specs=[smem] + [vmem] * (7 + len(rows)),
         out_specs=(vmem,) * 3,
         scratch_shapes=[
             pltpu.VMEM((owners, seqs, tokens * LANES), BF16),
             pltpu.VMEM((step_tokens * groups * block_cols, flat), BF16),
-            pltpu.VMEM((groups * proj // tokens * block_cols, step_tokens * LANES), BF16),
             pltpu.VMEM((owners, seqs, LANES), BF16),
             pltpu.VMEM((groups * prow_n, seqs, LANES), BF16),
-            pltpu.VMEM((groups * proj // tokens * block_cols, tokens * seqs), BF16),
-            pltpu.VMEM((tokens * seqs, groups * proj // tokens * block_cols), BF16),
-            pltpu.VMEM((groups * proj // tokens * block_cols, tokens * seqs), F32),
+            pltpu.VMEM((columns, tokens * seqs), BF16),
+            pltpu.VMEM((tokens * seqs, columns), BF16),
+            pltpu.VMEM((columns, tokens * seqs), F32),
             pltpu.VMEM((pair_width, flat), F32),
+            pltpu.VMEM((prow_n, groups, length, LANES), BF16),
+            pltpu.VMEM((prow_n, groups, length, LANES), BF16),
         ],
         compiler_params=params,
         name="pair_work",
-    )(place, mine, theirs, mapping, mapping.T, left_wide, right_one, offset)
+    )(place, theirs, *rows, cot, pulled, mapping, left_wide, right_one, offset)
 
     theirs = lax.ppermute(message, "pc", [(0, 1), (1, 0)])
     output_weight_gradient, left_weight_gradient, right_weight_gradient, alignment = pl.pallas_call(
@@ -646,6 +688,8 @@
         and tokens == 4
         and block_rows % tokens == 0
         and block_cols == rows_n * tokens == 16
+        and rows_n & (rows_n - 1) == 0
+        and cols_n & (cols_n - 1) == 0
         and width == LANES
         and features.shape[2] >= 2 * proj
         and positions.shape[0] // parts % 16 == 0

time: 48.2 us -> 46.9 us (0.973)
  blocking collectives: 27.2 us -> 0 us
  starting transfers between devices: 0.28 us -> 13.6 us
  waiting for transfers between devices: 1.78 us -> 10.2 us
  other arithmetic: 0.08 us -> 4.12 us
  local copies, waits for them, and re-layouts: 4.16 us -> 2.08 us
  Pallas kernels: 13.6 us -> 15.5 us
    all_to_all x1 -> x0, blocking collectives: 27.2 us -> none  [local_gathered(): lax.all_to_all(sent, ('prow', 'px'), 0, 0)]
    ppermute x1 -> x7, starting transfers between devices: 0.07 us -> 13.6 us  [the longest x6 13.5 us: gathered(): pieces.append(lax.ppermute(held, axis, swap))]
    ppermute x1 -> x7, waiting for transfers between devices: 0.34 us -> 8.63 us  [the longest x6 8.63 us: gathered(): pieces.append(lax.ppermute(held, axis, swap))]
    concatenate x0 -> x5, other arithmetic: none -> 4.04 us  [the longest x4 3.26 us: gathered(): held = pieces[0] if len(pieces) == 1 else jnp.concatenate(pieces, axis=0)]
    unnamed x14 -> x16, local copies, waits for them, and re-layouts: 3.9 us -> 0.88 us
    pallas_call x1 -> x2, Pallas kernels: 10 us -> 11.7 us  [the longest x1 9.48 us: local_gathered(): pl.pallas_call(functools.partial(pair_kernel, row_offsets, len(rows)), ou...]
    reshape x1, local copies, waits for them, and re-layouts: 0.14 us -> 1.06 us  [local_gathered(): mapping = final_mapping_matrix.reshape(proj, proj, pair_width)]
  transfers between devices with their start and end apart: 2 -> 8, of which waited for: 2 -> 4; matrix products, arithmetic and copies ran while one was open for 1% -> 11% of each run, Pallas kernels for 0% -> 5%
where the time goes in v6:
time: 46.9 us; the launch traced here: 46.3 us
  Pallas kernels  15.5 us (33%)
  starting transfers between devices  13.6 us (29%)
  waiting for transfers between devices  10.2 us (22%)
  other arithmetic  4.12 us (9%)
  local copies, waits for them, and re-layouts  2.08 us (4%)
  between operations  0.8 us (2%)
    ppermute x6, starting transfers between devices, gathered(): pieces.append(lax.ppermute(held, axis, swap))  13.5 us
    pallas_call x1, Pallas kernels, local_gathered(): pl.pallas_call(functools.partial(pair_kernel, row_offsets, len(rows)), ou...  9.48 us
    ppermute x6, waiting for transfers between devices, gathered(): pieces.append(lax.ppermute(held, axis, swap))  8.63 us
    concatenate x4, other arithmetic, gathered(): held = pieces[0] if len(pieces) == 1 else jnp.concatenate(pieces, axis=0)  3.26 us
    pallas_call x1, Pallas kernels, local_gathered(): pl.pallas_call(functools.partial(pull_kernel, cot_offsets), out_shape=(sh...  2.26 us
    pallas_call x1, Pallas kernels, local_gathered(): pl.pallas_call(pick_kernel, out_shape=(shape((seqs, packed), F32), shape(...  2.26 us
    ppermute x1, waiting for transfers between devices, local_gathered(): theirs = lax.ppermute(message, 'pc', [(0, 1), (1, 0)])  1.57 us
    pallas_call x1, Pallas kernels, local_gathered(): pl.pallas_call(close_kernel, out_shape=(shape((flat, pair_width), F32), s...  1.51 us
  transfers between devices with their start and end apart: 8, of which 4 were waited for; matrix products, arithmetic and copies ran while one was open for 11% of the time, Pallas kernels for 5%

profile of v6, /device:TPU:0, one launch (start us, length us, event | category | flops | bytes accessed | tf_op | source)
XLA Modules:
  0.0 46.3 jit_solution(8031653977714625044)
XLA Ops:
  0.6 2.3 %pick_rows.1 = (f32[64,256]{1,0:T(8,128)}, f32[64,256]{1,0:T(8,128)}, bf16[256,512]{1,0:T(8,128)(2,1)}, bf16[256,128]{1,0:T(8,128)(2,1)}, bf16[256,128]{1,0:T(8,...) custom-call(s32[1,64]{1,0:T(1,128)} %bitcast.29, bf16[256,128]{1,0:T(8,128)(2,1)} %bitcast.26, ...), custom_call_target="tpu_custom_call" | custom-call | tf_op jit(solution)/shard_map/pick_rows/pallas_call | solution.py:558
  2.9 3.0 %collective-permute-start = (bf16[1,128,128]{2,1,0:T(8,128)(2,1)}, bf16[1,128,128]{2,1,0:T(8,128)(2,1)S(1)}, u32[]{:S(2)}, u32[]{:S(2)}) collective-permute-start(bf16[1,128,128]{2,1,0:T(8,128)(2,1)} %get-tuple-element.21.refs_0_), channel_id=1, source_target_pairs={{0,2},{2,0},{1,3},{3,1},{4,6},{6,4},{5,7},{7,5},{8,10},{10,8},{9,1... | collective-permute-start | bytes 98312 | tf_op jit(solution)/shard_map/ppermute | solution.py:594
  5.9 1.6 %collective-permute-start.4 = (bf16[1,256,128]{2,1,0:T(8,128)(2,1)}, bf16[1,256,128]{2,1,0:T(8,128)(2,1)S(1)}, u32[]{:S(2)}, u32[]{:S(2)}) collective-permute-start(bf16[1,256,128]{2,1,0:T(8,128)(2,1)} %bitcast.21), channel_id=1, source_target_pairs={{0,4},{4,0},{8,12},{12,8},{1,5},{5,1},{9,13},{13,9},{2,6},{6,2},{1... | collective-permute-start | bytes 196616 | tf_op jit(solution)/shard_map/ppermute | solution.py:594
  7.5 0.5 %collective-permute-done.refs_1_ = bf16[1,128,128]{2,1,0:T(8,128)(2,1)S(1)} collective-permute-done((bf16[1,128,128]{2,1,0:T(8,128)(2,1)}, bf16[1,128,128]{2,1,0:T(8,128)(2,1)S(1)}, u32[]{:S(2)}, u32[]{:S(2)}) %collective-permute-start) | collective-permute-done | bytes 32800 | tf_op jit(solution)/shard_map/ppermute | solution.py:594
  8.0 0.8 %pad_maximum_fusion.4 = bf16[2,128,128]{2,1,0:T(8,128)(2,1)S(1)} fusion(bf16[1,128,128]{2,1,0:T(8,128)(2,1)S(1)} %collective-permute-done.refs_1_, bf16[1,128,128]{2,1,0:T(8,128)(2,1)} %get-tuple-element.21.refs_0_), kind=kLoop, calls=%fused_computation.4 | loop fusion | flops 32768 | bytes 131072 | tf_op jit(solution)/shard_map/concatenate | solution.py:593
  8.8 2.1 %collective-permute-start.1 = (bf16[2,128,128]{2,1,0:T(8,128)(2,1)S(1)}, bf16[2,128,128]{2,1,0:T(8,128)(2,1)S(1)}, u32[]{:S(2)}, u32[]{:S(2)}) collective-permute-start(bf16[2,128,128]{2,1,0:T(8,128)(2,1)S(1)} %pad_maximum_fusion.4), channel_id=1, source_target_pairs={{0,4},{4,0},{8,12},{12,8},{1,5},{5,1},{9,13},{13,9},{2,6},{6,2},{1... | collective-permute-start | bytes 196616 | tf_op jit(solution)/shard_map/ppermute | solution.py:594
  10.9 0.9 %pad_maximum_fusion.3 = bf16[2,256,128]{2,1,0:T(8,128)(2,1)S(1)} fusion(bf16[1,256,128]{2,1,0:T(8,128)(2,1)S(1)} %collective-permute-done.4.refs_1_, bf16[1,256,128]{2,1,0:T(8,128)(2,1)} %bitcast.22), kind=kLoop, calls=%fused_computation.3 | loop fusion | flops 65536 | bytes 262144 | tf_op jit(solution)/shard_map/concatenate | solution.py:593
  11.8 2.7 %collective-permute-start.5 = (bf16[2,256,128]{2,1,0:T(8,128)(2,1)S(1)}, bf16[2,256,128]{2,1,0:T(8,128)(2,1)S(1)}, u32[]{:S(2)}, u32[]{:S(2)}) collective-permute-start(bf16[2,256,128]{2,1,0:T(8,128)(2,1)S(1)} %pad_maximum_fusion.3), channel_id=1, source_target_pairs={{0,8},{4,12},{8,0},{12,4},{1,9},{5,13},{9,1},{13,5},{2,10},{6,14},... | collective-permute-start | bytes 393224 | tf_op jit(solution)/shard_map/ppermute | solution.py:594
  14.4 0.8 %pad_maximum_fusion.2 = bf16[4,128,128]{2,1,0:T(8,128)(2,1)S(1)} fusion(bf16[2,128,128]{2,1,0:T(8,128)(2,1)S(1)} %collective-permute-done.1.refs_2_, bf16[1,128,128]{2,1,0:T(8,128)(2,1)S(1)} %collective-permute-done.refs_1_, bf16[1,128,128]{2,1,0:T(8,128)(2,1)} %get-tuple-element.21.refs_0_), kind=kLoop, calls=%fused_computation.2 | loop fusion | flops 131072 | bytes 262144 | tf_op jit(solution)/shard_map/concatenate | solution.py:593
  15.2 2.5 %collective-permute-start.2 = (bf16[4,128,128]{2,1,0:T(8,128)(2,1)S(1)}, bf16[4,128,128]{2,1,0:T(8,128)(2,1)S(1)}, u32[]{:S(2)}, u32[]{:S(2)}) collective-permute-start(bf16[4,128,128]{2,1,0:T(8,128)(2,1)S(1)} %pad_maximum_fusion.2), channel_id=1, source_target_pairs={{0,8},{4,12},{8,0},{12,4},{1,9},{5,13},{9,1},{13,5},{2,10},{6,14},... | collective-permute-start | bytes 393224 | tf_op jit(solution)/shard_map/ppermute | solution.py:594
  17.7 5.6 %collective-permute-done.5.refs_2_ = bf16[2,256,128]{2,1,0:T(8,128)(2,1)S(1)} collective-permute-done((bf16[2,256,128]{2,1,0:T(8,128)(2,1)S(1)}, bf16[2,256,128]{2,1,0:T(8,128)(2,1)S(1)}, u32[]{:S(2)}, u32[]{:S(2)}) %collective-permute-start.5) | collective-permute-done | bytes 131104 | tf_op jit(solution)/shard_map/ppermute | solution.py:594
  23.2 0.9 %pad_maximum_fusion.1 = bf16[4,256,128]{2,1,0:T(8,128)(2,1)S(1)} fusion(bf16[2,256,128]{2,1,0:T(8,128)(2,1)S(1)} %collective-permute-done.5.refs_2_, bf16[1,256,128]{2,1,0:T(8,128)(2,1)S(1)} %collective-permute-done.4.refs_1_, bf16[1,256,128]{2,1,0:T(8,128)(2,1)} %bitcast.23), kind=kLoop, calls=%fused_computation.1 | loop fusion | flops 262144 | bytes 524288 | tf_op jit(solution)/shard_map/concatenate | solution.py:593
  24.1 1.7 %collective-permute-start.6 = (bf16[4,256,128]{2,1,0:T(8,128)(2,1)S(1)}, bf16[4,256,128]{2,1,0:T(8,128)(2,1)S(1)}, u32[]{:S(2)}, u32[]{:S(2)}) collective-permute-start(bf16[4,256,128]{2,1,0:T(8,128)(2,1)S(1)} %pad_maximum_fusion.1), channel_id=1, source_target_pairs={{0,2},{2,0},{1,3},{3,1},{4,6},{6,4},{5,7},{7,5},{8,10},{10,8},{9,1... | collective-permute-start | bytes 786440 | tf_op jit(solution)/shard_map/ppermute | solution.py:594
  25.8 0.8 %pad_maximum_fusion = bf16[8,128,128]{2,1,0:T(8,128)(2,1)S(1)} fusion(bf16[4,128,128]{2,1,0:T(8,128)(2,1)S(1)} %collective-permute-done.2.refs_3_, bf16[2,128,128]{2,1,0:T(8,128)(2,1)S(1)} %collective-permute-done.1.refs_2_, bf16[1,128,128]{2,1,0:T(8,128)(2,1)S(1)} %collective-permute-done.refs_1_, bf16[1,128,128]{2,1,0:T(8,128)(2,1)} %get-tuple-element.21.refs_0_), kind=kLoop, calls=%fused_computation | loop fusion | flops 393216 | bytes 524288 | tf_op jit(solution)/shard_map/concatenate | solution.py:604
  26.6 0.1 collective-permute-start.3
  26.7 1.1 %copy.12 = bf16[32,32,128]{2,0,1:T(8,128)(2,1)S(1)} copy(bf16[32,32,128]{2,1,0:T(8,128)(2,1)} %bitcast.25) | data formatting | bytes 524288 | tf_op jit(solution)/shard_map/reshape | solution.py:606
  27.8 0.1 copy.13.mapping_ref
  27.9 0.1 pad_add_fusion.place_ref
  28.0 2.5 %collective-permute-done.6.refs_3_ = bf16[4,256,128]{2,1,0:T(8,128)(2,1)S(1)} collective-permute-done((bf16[4,256,128]{2,1,0:T(8,128)(2,1)S(1)}, bf16[4,256,128]{2,1,0:T(8,128)(2,1)S(1)}, u32[]{:S(2)}, u32[]{:S(2)}) %collective-permute-start.6) | collective-permute-done | bytes 262176 | tf_op jit(solution)/shard_map/ppermute | solution.py:594
  30.5 0.8 %copy-done.3 = bf16[16,16,128]{2,1,0:T(8,128)(2,1)S(1)} copy-done((bf16[16,16,128]{2,1,0:T(8,128)(2,1)S(1)}, bf16[16,16,128]{2,1,0:T(8,128)(2,1)}, u32[]{:S(2)}) %copy-start.3) | copy-done | bytes 65560
  31.4 2.3 %pull_back.1 = (bf16[4,2,256,128]{3,2,1,0:T(8,128)(2,1)S(1)}, bf16[4,256,2048]{2,1,0:T(8,128)(2,1)S(1)}) custom-call(s32[3]{0:T(128)S(1)} %pad_add_fusion.place_ref, bf16[128,1024]{1,0:T(8,128)(2,1)S(1)} %copy.13.mapping_ref, bf16[1,256,128]{2,1,0:T(8,128)(2,1)S(1)} %bitcast.24, bf16[1,256,128]{2,1,0:T(8,128)(2,1)S(1)} %collective-permute-done.4.refs_1_, ...), custom_call_target="tpu_custom_call" | custom-call | flops 536870912 | bytes 5242880 | tf_op jit(solution)/shard_map/pull_back/pallas_call | solution.py:611
  33.7 9.5 %pair_work.1 = (bf16[16,16,128]{2,1,0:T(8,128)(2,1)}, bf16[2,64,128]{2,1,0:T(8,128)(2,1)S(1)}, bf16[1152,128]{1,0:T(8,128)(2,1)S(1)}) custom-call(s32[3]{0:T(128)S(1)} %pad_add_fusion.place_ref, bf16[8,128,128]{2,1,0:T(8,128)(2,1)S(1)} %collective-permute-done.3.theirs_from_ref, bf16[1,128,128]{2,1,0:T(8,128)(2,1)S(1)} %copy-done, ...), custom_call_target="tpu_custom_call" | custom-call | tf_op jit(solution)/shard_map/pair_work/pallas_call | solution.py:628
  43.2 1.6 %collective-permute-done.7.message_ref = bf16[1152,128]{1,0:T(8,128)(2,1)S(1)} collective-permute-done((bf16[1152,128]{1,0:T(8,128)(2,1)S(1)}, bf16[1152,128]{1,0:T(8,128)(2,1)S(1)}, u32[]{:S(2)}, u32[]{:S(2)}) %collective-permute-start.7) | collective-permute-done | bytes 294944 | tf_op jit(solution)/shard_map/ppermute | solution.py:653
  44.8 1.5 %close.1 = (f32[1024,128]{1,0:T(8,128)}, f32[32,64]{1,0:T(8,128)}, f32[32,64]{1,0:T(8,128)}, bf16[64,4,64]{2,1,0:T(4,128)(2,1)}) custom-call(bf16[2,64,128]{2,1,0:T(8,128)(2,1)S(1)} %get-tuple-element.28.grads_ref, bf16[1152,128]{1,0:T(8,128)(2,1)S(1)} %get-tuple-element.29.own_ref, bf16[1152,128]{1,0:T(8,128)(2,1)S(1)} %collective-permute-done.7.message_ref, ...), custom_call_target="tpu_custom_call" | custom-call | tf_op jit(solution)/shard_map/close/pallas_call | solution.py:654
  (20 shorter events, 0.1 us)
Async XLA Ops:
  2.9 30.8 %copy-start = (bf16[1,128,128]{2,1,0:T(8,128)(2,1)S(1)}, bf16[1,128,128]{2,1,0:T(8,128)(2,1)}, u32[]{:S(2)}) copy-start(bf16[1,128,128]{2,1,0:T(8,128)(2,1)} %get-tuple-element.21.refs_0_) | copy-start | bytes 98308
  2.9 30.8 %copy-start.1 = (bf16[256,128]{1,0:T(8,128)(2,1)S(1)}, bf16[256,128]{1,0:T(8,128)(2,1)}, u32[]{:S(2)}) copy-start(bf16[256,128]{1,0:T(8,128)(2,1)} %get-tuple-element.25.refs_8_.right_ref) | copy-start | bytes 196612
  2.9 30.8 %copy-start.2 = (bf16[256,512]{1,0:T(8,128)(2,1)S(1)}, bf16[256,512]{1,0:T(8,128)(2,1)}, u32[]{:S(2)}) copy-start(bf16[256,512]{1,0:T(8,128)(2,1)} %get-tuple-element.24.refs_7_) | copy-start | bytes 786436
  2.9 30.8 %copy-start.7 = (f32[1,128]{1,0:T(1,128)S(1)}, f32[1,128]{1,0:T(1,128)}, u32[]{:S(2)}) copy-start(f32[1,128]{1,0:T(1,128)} %get-tuple-element.26.refs_9_) | copy-start | bytes 1540
  2.9 5.1 %collective-permute-start = (bf16[1,128,128]{2,1,0:T(8,128)(2,1)}, bf16[1,128,128]{2,1,0:T(8,128)(2,1)S(1)}, u32[]{:S(2)}, u32[]{:S(2)}) collective-permute-start(bf16[1,128,128]{2,1,0:T(8,128)(2,1)} %get-tuple-element.21.refs_0_), channel_id=1, source_target_pairs={{0,2},{2,0},{1,3},{3,1},{4,6},{6,4},{5,7},{7,5},{8,10},{10,8},{9,1... | collective-permute-start | bytes 98312 | tf_op jit(solution)/shard_map/ppermute | solution.py:594
  5.9 5.0 %collective-permute-start.4 = (bf16[1,256,128]{2,1,0:T(8,128)(2,1)}, bf16[1,256,128]{2,1,0:T(8,128)(2,1)S(1)}, u32[]{:S(2)}, u32[]{:S(2)}) collective-permute-start(bf16[1,256,128]{2,1,0:T(8,128)(2,1)} %bitcast.21), channel_id=1, source_target_pairs={{0,4},{4,0},{8,12},{12,8},{1,5},{5,1},{9,13},{13,9},{2,6},{6,2},{1... | collective-permute-start | bytes 196616 | tf_op jit(solution)/shard_map/ppermute | solution.py:594
  8.8 5.6 %collective-permute-start.1 = (bf16[2,128,128]{2,1,0:T(8,128)(2,1)S(1)}, bf16[2,128,128]{2,1,0:T(8,128)(2,1)S(1)}, u32[]{:S(2)}, u32[]{:S(2)}) collective-permute-start(bf16[2,128,128]{2,1,0:T(8,128)(2,1)S(1)} %pad_maximum_fusion.4), channel_id=1, source_target_pairs={{0,4},{4,0},{8,12},{12,8},{1,5},{5,1},{9,13},{13,9},{2,6},{6,2},{1... | collective-permute-start | bytes 196616 | tf_op jit(solution)/shard_map/ppermute | solution.py:594
  11.8 11.5 %collective-permute-start.5 = (bf16[2,256,128]{2,1,0:T(8,128)(2,1)S(1)}, bf16[2,256,128]{2,1,0:T(8,128)(2,1)S(1)}, u32[]{:S(2)}, u32[]{:S(2)}) collective-permute-start(bf16[2,256,128]{2,1,0:T(8,128)(2,1)S(1)} %pad_maximum_fusion.3), channel_id=1, source_target_pairs={{0,8},{4,12},{8,0},{12,4},{1,9},{5,13},{9,1},{13,5},{2,10},{6,14},... | collective-permute-start | bytes 393224 | tf_op jit(solution)/shard_map/ppermute | solution.py:594
  15.2 10.6 %collective-permute-start.2 = (bf16[4,128,128]{2,1,0:T(8,128)(2,1)S(1)}, bf16[4,128,128]{2,1,0:T(8,128)(2,1)S(1)}, u32[]{:S(2)}, u32[]{:S(2)}) collective-permute-start(bf16[4,128,128]{2,1,0:T(8,128)(2,1)S(1)} %pad_maximum_fusion.2), channel_id=1, source_target_pairs={{0,8},{4,12},{8,0},{12,4},{1,9},{5,13},{9,1},{13,5},{2,10},{6,14},... | collective-permute-start | bytes 393224 | tf_op jit(solution)/shard_map/ppermute | solution.py:594
  24.1 6.4 %collective-permute-start.6 = (bf16[4,256,128]{2,1,0:T(8,128)(2,1)S(1)}, bf16[4,256,128]{2,1,0:T(8,128)(2,1)S(1)}, u32[]{:S(2)}, u32[]{:S(2)}) collective-permute-start(bf16[4,256,128]{2,1,0:T(8,128)(2,1)S(1)} %pad_maximum_fusion.1), channel_id=1, source_target_pairs={{0,2},{2,0},{1,3},{3,1},{4,6},{6,4},{5,7},{7,5},{8,10},{10,8},{9,1... | collective-permute-start | bytes 786440 | tf_op jit(solution)/shard_map/ppermute | solution.py:594
  26.6 7.1 %collective-permute-start.3 = (bf16[8,128,128]{2,1,0:T(8,128)(2,1)S(1)}, bf16[8,128,128]{2,1,0:T(8,128)(2,1)S(1)}, u32[]{:S(2)}, u32[]{:S(2)}) collective-permute-start(bf16[8,128,128]{2,1,0:T(8,128)(2,1)S(1)} %pad_maximum_fusion), channel_id=1, source_target_pairs={{0,1},{1,0},{2,3},{3,2},{4,5},{5,4},{6,7},{7,6},{8,9},{9,8},{10,11... | collective-permute-start | bytes 786440 | tf_op jit(solution)/shard_map/ppermute | solution.py:604
  27.7 17.1 %copy-start.4 = (f32[64,256]{1,0:T(8,128)S(1)}, f32[64,256]{1,0:T(8,128)}, u32[]{:S(2)}) copy-start(f32[64,256]{1,0:T(8,128)} %get-tuple-element.30.normed_ref) | copy-start | bytes 196612
  27.8 17.1 %copy-start.5 = (f32[64,256]{1,0:T(8,128)S(1)}, f32[64,256]{1,0:T(8,128)}, u32[]{:S(2)}) copy-start(f32[64,256]{1,0:T(8,128)} %get-tuple-element.31.inverse_ref) | copy-start | bytes 196612
  27.8 17.0 %copy-start.6 = (bf16[256,128]{1,0:T(8,128)(2,1)S(1)}, bf16[256,128]{1,0:T(8,128)(2,1)}, u32[]{:S(2)}) copy-start(bf16[256,128]{1,0:T(8,128)(2,1)} %get-tuple-element.32.left_ref) | copy-start | bytes 196612
  30.5 0.8 %copy-start.3 = (bf16[16,16,128]{2,1,0:T(8,128)(2,1)S(1)}, bf16[16,16,128]{2,1,0:T(8,128)(2,1)}, u32[]{:S(2)}) copy-start(bf16[16,16,128]{2,1,0:T(8,128)(2,1)} %param.13) | copy-start | bytes 196612
  43.2 1.6 %collective-permute-start.7 = (bf16[1152,128]{1,0:T(8,128)(2,1)S(1)}, bf16[1152,128]{1,0:T(8,128)(2,1)S(1)}, u32[]{:S(2)}, u32[]{:S(2)}) collective-permute-start(bf16[1152,128]{1,0:T(8,128)(2,1)S(1)} %get-tuple-element.29.own_ref), channel_id=1, source_target_pairs={{0,1},{1,0},{2,3},{3,2},{4,5},{5,4},{6,7},{7,6},{8,9},{9,8},{10,11... | collective-permute-start | bytes 884744 | tf_op jit(solution)/shard_map/ppermute | solution.py:653

commit v7 on v6

--- a/solution.py
+++ b/solution.py
@@ -215,19 +215,21 @@
     left_ref,
     right_ref,
     offset_ref,
+    cot_ref,
     normed_ref,
     inverse_ref,
     left_wide_ref,
     left_one_ref,
     right_one_ref,
     offset_out_ref,
-    low_ref,
+    message_ref,
     positions,
     features,
     left,
     right,
     in_sems,
 ):
+    pairs = cot_ref.shape[0]
     inputs = [
         pltpu.make_async_copy(source, target, in_sems.at[n])
         for n, (source, target) in enumerate(
@@ -237,6 +239,7 @@
                 (left_ref, left),
                 (right_ref, right),
                 (offset_ref, offset_out_ref),
+                (cot_ref, message_ref.at[pl.ds(0, pairs)]),
             ]
         )
     ]
@@ -257,9 +260,9 @@
     normed = centered * inverse
     pieces = packed // LANES
     for n in range(pieces):
-        low_ref[0, n * seqs : (n + 1) * seqs] = normed[:, n * LANES : (n + 1) * LANES].astype(
-            BF16
-        )
+        message_ref[pairs + n * seqs : pairs + (n + 1) * seqs] = normed[
+            :, n * LANES : (n + 1) * LANES
+        ].astype(BF16)
     normed_ref[...] = normed
     inverse_ref[...] = inverse
 
@@ -309,38 +312,29 @@
     lax.fori_loop(0, prow_n, step, 0)
 
 
-def pair_kernel(offsets, pieces, place_ref, theirs_from_ref, *refs):
-    *rest, mine_ref, theirs_ref = refs
-    place_blocks(place_ref, offsets, refs[:pieces], mine_ref)
-    place_blocks(place_ref, offsets, [theirs_from_ref], theirs_ref)
-    pair_work(place_ref, mine_ref, theirs_ref, *rest[pieces:])
-
-
-def pair_work(
+def outer_kernel(
+    offsets,
     place_ref,
-    mine_ref,
-    theirs_ref,
-    cot_ref,
-    pulled_ref,
+    mine_from_ref,
+    theirs_from_ref,
     mapping_ref,
     left_ref,
     right_ref,
     offset_ref,
+    rows_ref,
+    expanded,
+    swapped,
+    outer_ref,
     pair_ref,
-    grads_ref,
-    message_ref,
-    expanded,
-    outer,
-    left_back,
-    right_back,
+    mine_ref,
+    theirs_ref,
     turned,
-    swapped,
-    sums,
-    weights,
 ):
+    place_blocks(place_ref, offsets, [mine_from_ref], mine_ref)
+    place_blocks(place_ref, offsets, [theirs_from_ref], theirs_ref)
     prow_n, groups = mine_ref.shape[:2]
     block_rows, block_cols, pair_width = pair_ref.shape
-    owners, seqs = left_back.shape[:2]
+    owners, seqs = expanded.shape[:2]
     packed = left_ref.shape[0]
     tokens = left_ref.shape[1] // LANES
     proj = LANES // tokens
@@ -348,23 +342,19 @@
     span = highs * block_cols
     own_row, own_group, core = place_ref[0], place_ref[1], place_ref[2]
 
-    def token_owner(group, row, parity):
-        return (2 * group + parity) * prow_n + row
-
     def rows_of(ref, g, r):
         return jnp.concatenate(
             [ref[r, g, n * seqs : (n + 1) * seqs] for n in range(packed // LANES)], axis=1
         )
 
     places = [(g, r) for g in range(groups) for r in range(prow_n)]
-    order = [token_owner(g, r, core) for g, r in places]
-    order = order + [token_owner(g, r, 1 - core) for g, r in places]
     rows_mine = [rows_of(mine_ref, g, r) for g, r in places]
     rows_all = jnp.concatenate(
         rows_mine + [rows_of(theirs_ref, g, r) for g, r in places], axis=0
     )
+    rows_ref[...] = rows_all
     wide_left = dot(rows_all, left_ref[...]).astype(BF16)
-    for n, owner in enumerate(order):
+    for n, owner in enumerate(owner_order(places, prow_n, core)):
         expanded[owner] = wide_left[n * seqs : (n + 1) * seqs]
 
     side_rows = []
@@ -373,13 +363,7 @@
         side_rows.append(
             jnp.concatenate([dot(x, right_ref[...]).astype(BF16) for x in chunks], axis=1)
         )
-    right = jnp.concatenate(side_rows, axis=0)
-    wide = right.shape[1]
-    source = lax.broadcasted_iota(jnp.int32, (wide, wide), 0)
-    target = lax.broadcasted_iota(jnp.int32, (wide, wide), 1)
-    jj, qh, ql = target % block_cols, target // block_cols % highs, target // span
-    shuffle = (source == jj * proj + qh * tokens + ql).astype(BF16)
-    right = dot(right, shuffle)
+    right = dot(jnp.concatenate(side_rows, axis=0), shuffle_matrix(block_cols, proj, tokens))
     for g in range(groups):
         for l in range(tokens):
             swapped[l * seqs : (l + 1) * seqs, g * span : (g + 1) * span] = (
@@ -387,41 +371,85 @@
             ).astype(BF16)
     turned[...] = swapped[...].astype(F32).T.astype(BF16)
 
-    sums[...] = jnp.zeros_like(sums)
-    weights[...] = jnp.zeros_like(weights)
-    step_tokens = outer.shape[0] // (groups * block_cols)
-    step_owners = step_tokens // tokens
-    steps_a_block = block_rows // step_tokens
-    share = step_tokens * block_cols
-
-    def step(m, carry):
-        row, part = m // steps_a_block, m % steps_a_block
-        ahead = jnp.concatenate(
-            [expanded[m * step_owners + o] for o in range(step_owners)], axis=1
-        )
-        low = lane_ids(ahead.shape) % LANES // proj
-        block = jnp.concatenate(
-            [jnp.where(low == l, ahead, jnp.zeros_like(ahead)) for l in range(tokens)], axis=0
-        )
-        cot = jnp.concatenate(
-            [
-                cot_ref[row, g, pl.ds(pl.multiple_of(part * share, share), share)]
-                for g in range(groups)
-            ],
-            axis=0,
-        )
-        made = dot(turned[...], block)
+    def step(row, carry):
+        made = dot(turned[...], left_block(expanded, row, owners // prow_n, tokens))
         for g in range(groups):
-            for t in range(step_tokens):
-                here = slice((g * step_tokens + t) * block_cols, (g * step_tokens + t + 1) * block_cols)
+            for t in range(block_rows):
+                start = (g * block_rows + t) * block_cols
                 lanes = slice(t * LANES, (t + 1) * LANES)
                 for h in range(highs):
                     there = slice((g * highs + h) * block_cols, (g * highs + h + 1) * block_cols)
-                    cols = slice(h * LANES, (h + 1) * LANES)
-                    outer[here, cols] = made[there, lanes].astype(BF16)
-        weights[...] += dot(cot, outer[...], contract=(0, 0))
+                    outer_ref[row, start : start + block_cols, h * LANES : (h + 1) * LANES] = made[
+                        there, lanes
+                    ].astype(BF16)
+        return carry
+
+    lax.fori_loop(0, prow_n, step, 0)
+    share = block_rows * block_cols
+    mine = outer_ref[own_row, pl.ds(pl.multiple_of(own_group * share, share), share)]
+    update = dot(mine, mapping_ref[...]) + offset_ref[...]
+    pair_ref[...] = update.astype(BF16).reshape(pair_ref.shape)
+
+
+def owner_order(places, prow_n, core):
+    mine = [(2 * g + core) * prow_n + r for g, r in places]
+    return mine + [(2 * g + 1 - core) * prow_n + r for g, r in places]
+
+
+def shuffle_matrix(block_cols, proj, tokens):
+    wide, highs = block_cols * proj, proj // tokens
+    source = lax.broadcasted_iota(jnp.int32, (wide, wide), 0)
+    target = lax.broadcasted_iota(jnp.int32, (wide, wide), 1)
+    jj, qh = target % block_cols, target // block_cols % highs
+    ql = target // (highs * block_cols)
+    return (source == jj * proj + qh * tokens + ql).astype(BF16)
+
+
+def left_block(expanded, row, step_owners, tokens):
+    ahead = jnp.concatenate([expanded[row * step_owners + o] for o in range(step_owners)], axis=1)
+    low = lane_ids(ahead.shape) % LANES // (LANES // tokens)
+    return jnp.concatenate(
+        [jnp.where(low == l, ahead, jnp.zeros_like(ahead)) for l in range(tokens)], axis=0
+    )
+
+
+def back_kernel(
+    place_ref,
+    rows_ref,
+    expanded,
+    swapped,
+    outer_ref,
+    cot_ref,
+    pulled_ref,
+    grads_ref,
+    message_ref,
+    left_back,
+    right_back,
+    sums,
+    weights,
+):
+    prow_n, groups, pairs, pair_width = cot_ref.shape
+    owners, seqs = left_back.shape[:2]
+    tokens = swapped.shape[0] // seqs
+    proj = LANES // tokens
+    highs = proj // tokens
+    span = swapped.shape[1] // groups
+    block_cols = span // highs
+    step_owners = owners // prow_n
+    own_row, own_group, core = place_ref[0], place_ref[1], place_ref[2]
+    places = [(g, r) for g in range(groups) for r in range(prow_n)]
+    order = owner_order(places, prow_n, core)
+
+    sums[...] = jnp.zeros_like(sums)
+    weights[...] = jnp.zeros_like(weights)
+
+    def step(row, carry):
+        block = left_block(expanded, row, step_owners, tokens)
+        cot = cot_ref[row].reshape(groups * pairs, pair_width)
+        weights[...] += dot(cot, outer_ref[row], contract=(0, 0))
         pulled = pulled_ref[row]
         back = dot(swapped[...], pulled)
+        low = lane_ids((seqs, back.shape[1])) % LANES // proj
         back = functools.reduce(
             jnp.add,
             [
@@ -434,20 +462,11 @@
                 back[:, (o * tokens + t) * LANES : (o * tokens + t + 1) * LANES]
                 for t in range(tokens)
             ]
-            left_back[m * step_owners + o] = fold_tokens(parts).astype(BF16)
+            left_back[row * step_owners + o] = fold_tokens(parts).astype(BF16)
         sums[...] += dot(pulled, block, contract=(1, 1))
-
-        @pl.when(row == own_row)
-        def _():
-            mine = outer[pl.ds(pl.multiple_of(own_group * share, share), share)]
-            update = dot(mine, mapping_ref[...]) + offset_ref[...]
-            pair_ref[pl.ds(part * step_tokens, step_tokens)] = update.astype(BF16).reshape(
-                step_tokens, block_cols, pair_width
-            )
-
         return carry
 
-    lax.fori_loop(0, prow_n * steps_a_block, step, 0)
+    lax.fori_loop(0, prow_n, step, 0)
 
     back = (sums[...].T * (1.0 / seqs)).astype(BF16)
     back = jnp.concatenate(
@@ -463,13 +482,14 @@
         ],
         axis=0,
     )
+    shuffle = shuffle_matrix(block_cols, proj, tokens)
     back = dot(back, shuffle, contract=(1, 1)).astype(BF16)
     for g, r in places:
         right_back[g * prow_n + r] = back[g * seqs : (g + 1) * seqs, r * LANES : (r + 1) * LANES]
 
     def side(grads, rows):
         total = dot(grads, rows, contract=(0, 0))
-        features = packed // tokens
+        features = rows.shape[1] // tokens
         return functools.reduce(
             jnp.add,
             [
@@ -478,10 +498,11 @@
             ],
         )
 
-    left_side = side(jnp.concatenate([left_back[owner] for owner in order], axis=0), rows_all)
-    right_side = side(
-        right_back[...].reshape(-1, LANES), jnp.concatenate(rows_mine, axis=0)
-    )
+    left_side = side(
+        jnp.concatenate([left_back[owner] for owner in order], axis=0), rows_ref[...]
+    )
+    columns = groups * prow_n * seqs
+    right_side = side(right_back[...].reshape(columns, LANES), rows_ref[:columns])
     both = jnp.concatenate([left_side, right_side], axis=0).astype(BF16)
     both = jnp.concatenate([both, jnp.zeros_like(both)], axis=1)
 
@@ -491,8 +512,8 @@
 
     message_ref[:flat] = weight_rows.astype(BF16)
     message_ref[flat : flat + 2 * proj] = both
-    message_ref[flat + 2 * proj :] = left_back[token_owner(own_group, own_row, 1 - core)]
-    grads_ref[0] = left_back[token_owner(own_group, own_row, core)]
+    message_ref[flat + 2 * proj :] = left_back[(2 * own_group + 1 - core) * prow_n + own_row]
+    grads_ref[0] = left_back[(2 * own_group + core) * prow_n + own_row]
     grads_ref[1] = right_back[own_group * prow_n + own_row]
 
 
@@ -546,16 +567,15 @@
     proj = first_side_matrix.shape[1]
     flat = proj * proj
     packed = tokens * features
-    step_tokens = block_rows
     shape = jax.ShapeDtypeStruct
     vmem = pl.BlockSpec(memory_space=pltpu.VMEM)
     smem = pl.BlockSpec(memory_space=pltpu.SMEM)
-    params = pltpu.CompilerParams(vmem_limit_bytes=40 * 1024 * 1024)
+    params = pltpu.CompilerParams(vmem_limit_bytes=36 * 1024 * 1024)
 
     pairs = block_rows * block_cols
     length = seqs * packed // LANES
     hbm = pl.BlockSpec(memory_space=pltpu.HBM)
-    normed, inverse, left_wide, left_one, right_one, offset, low = pl.pallas_call(
+    normed, inverse, left_wide, left_one, right_one, offset, sent = pl.pallas_call(
         pick_kernel,
         out_shape=(
             shape((seqs, packed), F32),
@@ -564,16 +584,16 @@
             shape((packed, LANES), BF16),
             shape((packed, LANES), BF16),
             shape((1, pair_width), F32),
-            shape((1, length, LANES), BF16),
+            shape((pairs + length, LANES), BF16),
         ),
-        in_specs=[hbm] * 5,
+        in_specs=[hbm] * 6,
         out_specs=(vmem,) * 7,
         scratch_shapes=[
             pltpu.VMEM((1, seqs), jnp.int32),
             pltpu.VMEM((packed, heads), BF16),
             pltpu.VMEM((proj, features), BF16),
             pltpu.VMEM((proj, features), BF16),
-            pltpu.SemaphoreType.DMA((5,)),
+            pltpu.SemaphoreType.DMA((6,)),
         ],
         compiler_params=pltpu.CompilerParams(vmem_limit_bytes=60 * 1024 * 1024),
         name="pick_rows",
@@ -583,25 +603,23 @@
         first_side_matrix.T,
         second_side_matrix.T,
         final_offset_vector.reshape(1, pair_width),
-    )
-
-    def gathered(own, order):
-        pieces, offsets = [own], [(0, 0)]
-        for axis, size in order:
-            for bit in range(size.bit_length() - 1):
-                swap = [(n, n ^ (1 << bit)) for n in range(size)]
-                held = pieces[0] if len(pieces) == 1 else jnp.concatenate(pieces, axis=0)
-                pieces.append(lax.ppermute(held, axis, swap))
-                step = (1 << bit, 0) if axis == "prow" else (0, 1 << bit)
-                offsets += [(down + step[0], across + step[1]) for down, across in offsets]
-        return pieces, offsets
-
-    along, across = ("prow", prow_n), ("px", groups)
-    cots, cot_offsets = gathered(
-        upstream_sensitivity.reshape(1, pairs, pair_width), (along, across)
-    )
-    rows, row_offsets = gathered(low, (across, along))
-    theirs = lax.ppermute(jnp.concatenate(rows, axis=0), "pc", [(0, 1), (1, 0)])
+        upstream_sensitivity.reshape(pairs, pair_width),
+    )
+
+    messages = [sent] + [
+        lax.ppermute(sent, "prow", [(n, n ^ down) for n in range(prow_n)])
+        for down in range(1, prow_n)
+    ]
+    offsets = [(down, 0) for down in range(prow_n)]
+    rows = jnp.stack([one[pairs:] for one in messages])
+    cots = [jnp.stack([one[:pairs] for one in messages])]
+    for bit in range(groups.bit_length() - 1):
+        swap = [(n, n ^ (1 << bit)) for n in range(groups)]
+        rows = jnp.concatenate([rows, lax.ppermute(rows, "px", swap)], axis=0)
+        held = cots[0] if bit == 0 else jnp.concatenate(cots, axis=0)
+        cots.append(lax.ppermute(held, "px", swap))
+        offsets += [(down, across + (1 << bit)) for down, across in offsets]
+    theirs = lax.ppermute(rows, "pc", [(0, 1), (1, 0)])
 
     mapping = final_mapping_matrix.reshape(proj, proj, pair_width)
     mapping = mapping.swapaxes(0, 1).reshape(flat, pair_width)
@@ -609,7 +627,7 @@
 
     columns = groups * proj // tokens * block_cols
     cot, pulled = pl.pallas_call(
-        functools.partial(pull_kernel, cot_offsets),
+        functools.partial(pull_kernel, offsets),
         out_shape=(
             shape((prow_n, groups, pairs, pair_width), BF16),
             shape((prow_n, columns, block_rows * LANES), BF16),
@@ -625,30 +643,47 @@
         name="pull_back",
     )(place, mapping.T, *cots)
 
-    pair_delta, grads, message = pl.pallas_call(
-        functools.partial(pair_kernel, row_offsets, len(rows)),
+    rows_all, expanded, swapped, outer, pair_delta = pl.pallas_call(
+        functools.partial(outer_kernel, offsets),
         out_shape=(
+            shape((owners * seqs, packed), BF16),
+            shape((owners, seqs, tokens * LANES), BF16),
+            shape((tokens * seqs, columns), BF16),
+            shape((prow_n, groups * pairs, flat), BF16),
             shape(upstream_sensitivity.shape, BF16),
+        ),
+        in_specs=[smem] + [vmem] * 6,
+        out_specs=(vmem,) * 5,
+        scratch_shapes=[
+            pltpu.VMEM((prow_n, groups, length, LANES), BF16),
+            pltpu.VMEM((prow_n, groups, length, LANES), BF16),
+            pltpu.VMEM((columns, tokens * seqs), BF16),
+        ],
+        compiler_params=params,
+        cost_estimate=pl.CostEstimate(
+            flops=2 * prow_n * groups * pairs * tokens * seqs * flat,
+            bytes_accessed=2 * prow_n * groups * pairs * flat,
+            transcendentals=0,
+        ),
+        name="outer_products",
+    )(place, rows, theirs, mapping, left_wide, right_one, offset)
+    grads, message = pl.pallas_call(
+        back_kernel,
+        out_shape=(
             shape((2, seqs, LANES), BF16),
             shape((flat + 2 * proj + seqs, LANES), BF16),
         ),
-        in_specs=[smem] + [vmem] * (7 + len(rows)),
-        out_specs=(vmem,) * 3,
+        in_specs=[smem] + [vmem] * 6,
+        out_specs=(vmem,) * 2,
         scratch_shapes=[
-            pltpu.VMEM((owners, seqs, tokens * LANES), BF16),
-            pltpu.VMEM((step_tokens * groups * block_cols, flat), BF16),
             pltpu.VMEM((owners, seqs, LANES), BF16),
             pltpu.VMEM((groups * prow_n, seqs, LANES), BF16),
-            pltpu.VMEM((columns, tokens * seqs), BF16),
-            pltpu.VMEM((tokens * seqs, columns), BF16),
             pltpu.VMEM((columns, tokens * seqs), F32),
             pltpu.VMEM((pair_width, flat), F32),
-            pltpu.VMEM((prow_n, groups, length, LANES), BF16),
-            pltpu.VMEM((prow_n, groups, length, LANES), BF16),
         ],
         compiler_params=params,
-        name="pair_work",
-    )(place, theirs, *rows, cot, pulled, mapping, left_wide, right_one, offset)
+        name="pull_further",
+    )(place, rows_all, expanded, swapped, outer, cot, pulled)
 
     theirs = lax.ppermute(message, "pc", [(0, 1), (1, 0)])
     output_weight_gradient, left_weight_gradient, right_weight_gradient, alignment = pl.pallas_call(

time: 46.9 us -> 41 us (0.87)
  starting transfers between devices: 13.6 us -> 7.98 us
  other arithmetic: 4.12 us -> 0.14 us
  waiting for transfers between devices: 10.2 us -> 12.6 us
  local copies, waits for them, and re-layouts: 2.08 us -> 3.73 us
    ppermute x7 -> x6, starting transfers between devices: 13.6 us -> 7.91 us  [the longest x3 5.68 us: local_gathered(): lax.ppermute(sent, 'prow', [(n, n ^ down) for n in range(prow_n)])]
    concatenate x5 -> x0, other arithmetic: 4.04 us -> none  [the longest x4 3.26 us: gathered(): held = pieces[0] if len(pieces) == 1 else jnp.concatenate(pieces, axis=0)]
    ppermute x7 -> x6, waiting for transfers between devices: 8.63 us -> 11 us  [the longest x3 5.62 us: local_gathered(): lax.ppermute(sent, 'prow', [(n, n ^ down) for n in range(prow_n)])]
    another operation x0 -> x8, local copies, waits for them, and re-layouts: none -> 1.63 us  [the longest x4 0.86 us: local_gathered(): cots = [jnp.stack([one[:pairs] for one in messages])]]
    reshape x1, local copies, waits for them, and re-layouts: 1.06 us -> 0.14 us  [local_gathered(): mapping = mapping.swapaxes(0, 1).reshape(flat, pair_width)]
    transpose x1, local copies, waits for them, and re-layouts: 0.14 us -> 1.06 us  [local_gathered(): mapping = mapping.swapaxes(0, 1).reshape(flat, pair_width)]
    pallas_call x2 -> x3, Pallas kernels: 11.7 us -> 11.5 us  [the longest x1 5.24 us: local_gathered(): pl.pallas_call(back_kernel, out_shape=(shape((2, seqs, LANES), BF16), sha...]
  transfers between devices with their start and end apart: 8 -> 7, of which waited for: 4 -> 5; matrix products, arithmetic and copies ran while one was open for 11% -> 9% of each run, Pallas kernels for 5% -> 6%
where the time goes in v7:
time: 41 us; the launch traced here: 40.6 us
  Pallas kernels  15.4 us (38%)
  waiting for transfers between devices  12.6 us (31%)
  starting transfers between devices  7.98 us (19%)
  local copies, waits for them, and re-layouts  3.73 us (9%)
  between operations  0.79 us (2%)
    ppermute x3, starting transfers between devices, local_gathered(): lax.ppermute(sent, 'prow', [(n, n ^ down) for n in range(prow_n)])  5.68 us
    ppermute x3, waiting for transfers between devices, local_gathered(): lax.ppermute(sent, 'prow', [(n, n ^ down) for n in range(prow_n)])  5.62 us
    pallas_call x1, Pallas kernels, local_gathered(): pl.pallas_call(back_kernel, out_shape=(shape((2, seqs, LANES), BF16), sha...  5.24 us
    pallas_call x1, Pallas kernels, local_gathered(): pl.pallas_call(functools.partial(outer_kernel, offsets), out_shape=(shape...  4.02 us
    ppermute x1, waiting for transfers between devices, local_gathered(): rows = jnp.concatenate([rows, lax.ppermute(rows, 'px', swap)], axis=0)  3.98 us
    pallas_call x1, Pallas kernels, local_gathered(): pl.pallas_call(pick_kernel, out_shape=(shape((seqs, packed), F32), shape(...  2.36 us
    pallas_call x1, Pallas kernels, local_gathered(): pl.pallas_call(functools.partial(pull_kernel, offsets), out_shape=(shape(...  2.26 us
    ppermute x1, waiting for transfers between devices, local_gathered(): theirs = lax.ppermute(message, 'pc', [(0, 1), (1, 0)])  1.57 us
  transfers between devices with their start and end apart: 7, of which 5 were waited for; matrix products, arithmetic and copies ran while one was open for 9% of the time, Pallas kernels for 6%

profile of v7, /device:TPU:0, one launch (start us, length us, event | category | flops | bytes accessed | tf_op | source)
XLA Modules:
  0.0 40.6 jit_solution(8369362862041381121)
XLA Ops:
  0.6 2.4 %pick_rows.1 = (f32[64,256]{1,0:T(8,128)}, f32[64,256]{1,0:T(8,128)}, bf16[256,512]{1,0:T(8,128)(2,1)}, bf16[256,128]{1,0:T(8,128)(2,1)}, bf16[256,128]{1,0:T(8,...) custom-call(s32[1,64]{1,0:T(1,128)} %bitcast.50, bf16[256,128]{1,0:T(8,128)(2,1)} %bitcast.46, ...), custom_call_target="tpu_custom_call" | custom-call | tf_op jit(solution)/shard_map/pick_rows/pallas_call | solution.py:578
  3.0 0.0 copy-start.3
  3.0 0.0 copy-start.4
  3.0 3.1 %collective-permute-start = (bf16[384,128]{1,0:T(8,128)(2,1)}, bf16[384,128]{1,0:T(8,128)(2,1)S(1)}, u32[]{:S(2)}, u32[]{:S(2)}) collective-permute-start(bf16[384,128]{1,0:T(8,128)(2,1)} %get-tuple-element.25), channel_id=1, source_target_pairs={{0,4},{4,0},{8,12},{12,8},{1,5},{5,1},{9,13},{13,9},{2,6},{6,2},{1... | collective-permute-start | bytes 294920 | tf_op jit(solution)/shard_map/ppermute | solution.py:610
  6.1 2.6 %collective-permute-start.1 = (bf16[384,128]{1,0:T(8,128)(2,1)}, bf16[384,128]{1,0:T(8,128)(2,1)S(1)}, u32[]{:S(2)}, u32[]{:S(2)}) collective-permute-start(bf16[384,128]{1,0:T(8,128)(2,1)} %get-tuple-element.25), channel_id=1, source_target_pairs={{0,8},{4,12},{8,0},{12,4},{1,9},{5,13},{9,1},{13,5},{2,10},{6,14},... | collective-permute-start | bytes 294920 | tf_op jit(solution)/shard_map/ppermute | solution.py:610
  8.7 0.8 %constant_dynamic-update-slice_fusion.4 = bf16[8,128,128]{2,1,0:T(8,128)(2,1)S(1)} fusion(bf16[384,128]{1,0:T(8,128)(2,1)} %get-tuple-element.25), kind=kLoop, calls=%fused_computation.14 | loop fusion | bytes 65536
  9.5 0.8 %slice_bitcast_fusion.3 = bf16[1,256,128]{2,1,0:T(8,128)(2,1)S(1)} fusion(bf16[384,128]{1,0:T(8,128)(2,1)} %get-tuple-element.25), kind=kLoop, calls=%fused_computation.5 | loop fusion | bytes 131072 | tf_op jit(solution)/shard_map/stack | solution.py:615
  10.4 0.8 %slice_bitcast_fusion.7 = bf16[1,128,128]{2,1,0:T(8,128)(2,1)S(1)} fusion(bf16[384,128]{1,0:T(8,128)(2,1)} %get-tuple-element.25), kind=kLoop, calls=%fused_computation.9 | loop fusion | bytes 65536 | tf_op jit(solution)/shard_map/stack | solution.py:614
  11.1 4.4 %collective-permute-done.2 = bf16[384,128]{1,0:T(8,128)(2,1)S(1)} collective-permute-done((bf16[384,128]{1,0:T(8,128)(2,1)}, bf16[384,128]{1,0:T(8,128)(2,1)S(1)}, u32[]{:S(2)}, u32[]{:S(2)}) %collective-permute-start.2) | collective-permute-done | bytes 98336 | tf_op jit(solution)/shard_map/ppermute | solution.py:610
  15.5 1.2 %collective-permute-done.1 = bf16[384,128]{1,0:T(8,128)(2,1)S(1)} collective-permute-done((bf16[384,128]{1,0:T(8,128)(2,1)}, bf16[384,128]{1,0:T(8,128)(2,1)S(1)}, u32[]{:S(2)}, u32[]{:S(2)}) %collective-permute-start.1) | collective-permute-done | bytes 98336 | tf_op jit(solution)/shard_map/ppermute | solution.py:610
  16.8 1.6 %collective-permute-start.3 = (bf16[4,128,128]{2,1,0:T(8,128)(2,1)S(1)}, bf16[4,128,128]{2,1,0:T(8,128)(2,1)S(1)}, u32[]{:S(2)}, u32[]{:S(2)}) collective-permute-start(bf16[4,128,128]{2,1,0:T(8,128)(2,1)S(1)} %pad_maximum_fusion.1), channel_id=1, source_target_pairs={{0,2},{2,0},{1,3},{3,1},{4,6},{6,4},{5,7},{7,5},{8,10},{10,8},{9,1... | collective-permute-start | bytes 393224 | tf_op jit(solution)/shard_map/ppermute | solution.py:618
  18.4 0.6 %collective-permute-start.5 = (bf16[4,256,128]{2,1,0:T(8,128)(2,1)S(1)}, bf16[4,256,128]{2,1,0:T(8,128)(2,1)S(1)}, u32[]{:S(2)}, u32[]{:S(2)}) collective-permute-start(bf16[4,256,128]{2,1,0:T(8,128)(2,1)S(1)} %pad_maximum_fusion.refs_0_), channel_id=1, source_target_pairs={{0,2},{2,0},{1,3},{3,1},{4,6},{6,4},{5,7},{7,5},{8,10},{10,8},{9,1... | collective-permute-start | bytes 786440 | tf_op jit(solution)/shard_map/ppermute | solution.py:620
  19.1 4.0 %collective-permute-done.3 = bf16[4,128,128]{2,1,0:T(8,128)(2,1)S(1)} collective-permute-done((bf16[4,128,128]{2,1,0:T(8,128)(2,1)S(1)}, bf16[4,128,128]{2,1,0:T(8,128)(2,1)S(1)}, u32[]{:S(2)}, u32[]{:S(2)}) %collective-permute-start.3) | collective-permute-done | bytes 131104 | tf_op jit(solution)/shard_map/ppermute | solution.py:618
  23.1 0.1 collective-permute-start.4
  23.2 1.1 %copy.15 = bf16[32,32,128]{2,1,0:T(8,128)(2,1)S(1)} copy(bf16[32,32,128]{2,0,1:T(8,128)(2,1)} %bitcast.45) | data formatting | bytes 524288 | tf_op jit(solution)/shard_map/transpose | solution.py:625
  24.2 0.1 copy.16
  24.4 0.1 pad_add_fusion.place_ref
  24.5 1.4 %collective-permute-done.5.refs_1_ = bf16[4,256,128]{2,1,0:T(8,128)(2,1)S(1)} collective-permute-done((bf16[4,256,128]{2,1,0:T(8,128)(2,1)S(1)}, bf16[4,256,128]{2,1,0:T(8,128)(2,1)S(1)}, u32[]{:S(2)}, u32[]{:S(2)}) %collective-permute-start.5) | collective-permute-done | bytes 262176 | tf_op jit(solution)/shard_map/ppermute | solution.py:620
  25.9 2.3 %pull_back.1 = (bf16[4,2,256,128]{3,2,1,0:T(8,128)(2,1)S(1)}, bf16[4,256,2048]{2,1,0:T(8,128)(2,1)S(1)}) custom-call(s32[3]{0:T(128)S(1)} %pad_add_fusion.place_ref, bf16[128,1024]{1,0:T(8,128)(2,1)S(1)} %bitcast.44, bf16[4,256,128]{2,1,0:T(8,128)(2,1)S(1)} %pad_maximum_fusion.refs_0_, bf16[4,256,128]{2,1,0:T(8,128)(2,1)S(1)} %collective-permute-done.5.refs_1_), custom_call_target="tpu_custom_call" | custom-call | flops 536870912 | bytes 5242880 | tf_op jit(solution)/shard_map/pull_back/pallas_call | solution.py:629
  28.2 4.0 %outer_products.1 = (bf16[1024,256]{1,0:T(8,128)(2,1)S(1)}, bf16[16,64,512]{2,1,0:T(8,128)(2,1)S(1)}, bf16[256,256]{1,0:T(8,128)(2,1)S(1)}, bf16[4,512,1024]{2,1,0:T(8,128)(2,1)S(1)}, bf16[16,16,128]{2,1,0:T(8,128)(2,1)}) custom-call(s32[3]{0:T(128)S(1)} %pad_add_fusion.place_ref, bf16[8,128,128]{2,1,0:T(8,128)(2,1)S(1)} %constant_dynamic-update-slice_fusion.mine_from_ref, ...), custom_call_target="tpu_custom_call" | custom-call | flops 1073741824 | bytes 4194304 | tf_op jit(solution)/shard_map/outer_products/pallas_call | solution.py:646
  32.2 5.2 %pull_further.1 = (bf16[2,64,128]{2,1,0:T(8,128)(2,1)S(1)}, bf16[1152,128]{1,0:T(8,128)(2,1)S(1)}) custom-call(s32[3]{0:T(128)S(1)} %pad_add_fusion.place_ref, bf16[1024,256]{1,0:T(8,128)(2,1)S(1)} %get-tuple-element.30.rows_ref, bf16[16,64,512]{2,1,0:T(8,128)(2,1)S(1)} %get-tuple-element.31.expanded, bf16[256,256]{1,0:T(8,128)(2,1)S(1)} %get-tuple-element.32.swapped, ...), custom_call_target="tpu_custom_call" | custom-call | tf_op jit(solution)/shard_map/pull_further/pallas_call | solution.py:670
  37.4 0.1 collective-permute-start.6
  37.5 1.6 %collective-permute-done.6.message_ref = bf16[1152,128]{1,0:T(8,128)(2,1)S(1)} collective-permute-done((bf16[1152,128]{1,0:T(8,128)(2,1)S(1)}, bf16[1152,128]{1,0:T(8,128)(2,1)S(1)}, u32[]{:S(2)}, u32[]{:S(2)}) %collective-permute-start.6) | collective-permute-done | bytes 294944 | tf_op jit(solution)/shard_map/ppermute | solution.py:688
  39.1 1.5 %close.1 = (f32[1024,128]{1,0:T(8,128)}, f32[32,64]{1,0:T(8,128)}, f32[32,64]{1,0:T(8,128)}, bf16[64,4,64]{2,1,0:T(4,128)(2,1)}) custom-call(bf16[2,64,128]{2,1,0:T(8,128)(2,1)S(1)} %get-tuple-element.36.grads_ref, bf16[1152,128]{1,0:T(8,128)(2,1)S(1)} %get-tuple-element.37.own_ref, bf16[1152,128]{1,0:T(8,128)(2,1)S(1)} %collective-permute-done.6.message_ref, ...), custom_call_target="tpu_custom_call" | custom-call | tf_op jit(solution)/shard_map/close/pallas_call | solution.py:689
  (25 shorter events, 0.2 us)
Async XLA Ops:
  3.0 25.1 %copy-start.3 = (bf16[256,128]{1,0:T(8,128)(2,1)S(1)}, bf16[256,128]{1,0:T(8,128)(2,1)}, u32[]{:S(2)}) copy-start(bf16[256,128]{1,0:T(8,128)(2,1)} %get-tuple-element.27.right_ref) | copy-start | bytes 196612
  3.0 25.1 %copy-start.4 = (bf16[256,512]{1,0:T(8,128)(2,1)S(1)}, bf16[256,512]{1,0:T(8,128)(2,1)}, u32[]{:S(2)}) copy-start(bf16[256,512]{1,0:T(8,128)(2,1)} %get-tuple-element.26.left_ref) | copy-start | bytes 786436
  3.0 25.1 %copy-start.5 = (f32[1,128]{1,0:T(1,128)S(1)}, f32[1,128]{1,0:T(1,128)}, u32[]{:S(2)}) copy-start(f32[1,128]{1,0:T(1,128)} %get-tuple-element.28.offset_ref) | copy-start | bytes 1540
  3.0 13.7 %collective-permute-start = (bf16[384,128]{1,0:T(8,128)(2,1)}, bf16[384,128]{1,0:T(8,128)(2,1)S(1)}, u32[]{:S(2)}, u32[]{:S(2)}) collective-permute-start(bf16[384,128]{1,0:T(8,128)(2,1)} %get-tuple-element.25), channel_id=1, source_target_pairs={{0,4},{4,0},{8,12},{12,8},{1,5},{5,1},{9,13},{13,9},{2,6},{6,2},{1... | collective-permute-start | bytes 294920 | tf_op jit(solution)/shard_map/ppermute | solution.py:610
  6.1 10.6 %collective-permute-start.1 = (bf16[384,128]{1,0:T(8,128)(2,1)}, bf16[384,128]{1,0:T(8,128)(2,1)S(1)}, u32[]{:S(2)}, u32[]{:S(2)}) collective-permute-start(bf16[384,128]{1,0:T(8,128)(2,1)} %get-tuple-element.25), channel_id=1, source_target_pairs={{0,8},{4,12},{8,0},{12,4},{1,9},{5,13},{9,1},{13,5},{2,10},{6,14},... | collective-permute-start | bytes 294920 | tf_op jit(solution)/shard_map/ppermute | solution.py:610
  8.7 6.8 %collective-permute-start.2 = (bf16[384,128]{1,0:T(8,128)(2,1)}, bf16[384,128]{1,0:T(8,128)(2,1)S(1)}, u32[]{:S(2)}, u32[]{:S(2)}) collective-permute-start(bf16[384,128]{1,0:T(8,128)(2,1)} %get-tuple-element.25), channel_id=1, source_target_pairs={{0,12},{4,8},{8,4},{12,0},{1,13},{5,9},{9,5},{13,1},{2,14},{6,10},... | collective-permute-start | bytes 294920 | tf_op jit(solution)/shard_map/ppermute | solution.py:610
  16.8 6.2 %collective-permute-start.3 = (bf16[4,128,128]{2,1,0:T(8,128)(2,1)S(1)}, bf16[4,128,128]{2,1,0:T(8,128)(2,1)S(1)}, u32[]{:S(2)}, u32[]{:S(2)}) collective-permute-start(bf16[4,128,128]{2,1,0:T(8,128)(2,1)S(1)} %pad_maximum_fusion.1), channel_id=1, source_target_pairs={{0,2},{2,0},{1,3},{3,1},{4,6},{6,4},{5,7},{7,5},{8,10},{10,8},{9,1... | collective-permute-start | bytes 393224 | tf_op jit(solution)/shard_map/ppermute | solution.py:618
  18.4 7.4 %collective-permute-start.5 = (bf16[4,256,128]{2,1,0:T(8,128)(2,1)S(1)}, bf16[4,256,128]{2,1,0:T(8,128)(2,1)S(1)}, u32[]{:S(2)}, u32[]{:S(2)}) collective-permute-start(bf16[4,256,128]{2,1,0:T(8,128)(2,1)S(1)} %pad_maximum_fusion.refs_0_), channel_id=1, source_target_pairs={{0,2},{2,0},{1,3},{3,1},{4,6},{6,4},{5,7},{7,5},{8,10},{10,8},{9,1... | collective-permute-start | bytes 786440 | tf_op jit(solution)/shard_map/ppermute | solution.py:620
  23.1 5.1 %collective-permute-start.4 = (bf16[8,128,128]{2,1,0:T(8,128)(2,1)S(1)}, bf16[8,128,128]{2,1,0:T(8,128)(2,1)S(1)}, u32[]{:S(2)}, u32[]{:S(2)}) collective-permute-start(bf16[8,128,128]{2,1,0:T(8,128)(2,1)S(1)} %constant_dynamic-update-slice_fusion.mine_from_ref), channel_id=1, source_target_pairs={{0,1},{1,0},{2,3},{3,2},{4,5},{5,4},{6,7},{7,6},{8,9},{9,8},{10,11... | collective-permute-start | bytes 786440 | tf_op jit(solution)/shard_map/ppermute | solution.py:622
  32.2 6.9 %copy-start = (f32[64,256]{1,0:T(8,128)S(1)}, f32[64,256]{1,0:T(8,128)}, u32[]{:S(2)}) copy-start(f32[64,256]{1,0:T(8,128)} %get-tuple-element.38.normed_ref) | copy-start | bytes 196612
  32.2 6.9 %copy-start.1 = (f32[64,256]{1,0:T(8,128)S(1)}, f32[64,256]{1,0:T(8,128)}, u32[]{:S(2)}) copy-start(f32[64,256]{1,0:T(8,128)} %get-tuple-element.39.inverse_ref) | copy-start | bytes 196612
  32.2 6.9 %copy-start.2 = (bf16[256,128]{1,0:T(8,128)(2,1)S(1)}, bf16[256,128]{1,0:T(8,128)(2,1)}, u32[]{:S(2)}) copy-start(bf16[256,128]{1,0:T(8,128)(2,1)} %get-tuple-element.40.left_ref) | copy-start | bytes 196612
  37.4 1.6 %collective-permute-start.6 = (bf16[1152,128]{1,0:T(8,128)(2,1)S(1)}, bf16[1152,128]{1,0:T(8,128)(2,1)S(1)}, u32[]{:S(2)}, u32[]{:S(2)}) collective-permute-start(bf16[1152,128]{1,0:T(8,128)(2,1)S(1)} %get-tuple-element.37.own_ref), channel_id=1, source_target_pairs={{0,1},{1,0},{2,3},{3,2},{4,5},{5,4},{6,7},{7,6},{8,9},{9,8},{10,11... | collective-permute-start | bytes 884744 | tf_op jit(solution)/shard_map/ppermute | solution.py:688

commit v8 on v7

--- a/solution.py
+++ b/solution.py
@@ -212,21 +212,12 @@
 def pick_kernel(
     positions_ref,
     features_ref,
-    left_ref,
-    right_ref,
-    offset_ref,
     cot_ref,
     normed_ref,
     inverse_ref,
-    left_wide_ref,
-    left_one_ref,
-    right_one_ref,
-    offset_out_ref,
     message_ref,
     positions,
     features,
-    left,
-    right,
     in_sems,
 ):
     pairs = cot_ref.shape[0]
@@ -236,9 +227,6 @@
             [
                 (positions_ref, positions),
                 (features_ref, features),
-                (left_ref, left),
-                (right_ref, right),
-                (offset_ref, offset_out_ref),
                 (cot_ref, message_ref.at[pl.ds(0, pairs)]),
             ]
         )
@@ -247,8 +235,7 @@
         copy.start()
     heads = features_ref.shape[1]
     seqs, packed = normed_ref.shape
-    proj, channels = left_ref.shape
-    tokens = packed // channels
+    channels = packed // 4
     for copy in inputs:
         copy.wait()
     wanted = positions[...] == lax.broadcasted_iota(jnp.int32, (heads, seqs), 0)
@@ -258,28 +245,12 @@
     variance = group_mean(centered * centered, channels, lax.Precision.HIGHEST)
     inverse = lax.rsqrt(variance + 1e-05)
     normed = centered * inverse
-    pieces = packed // LANES
-    for n in range(pieces):
+    for n in range(packed // LANES):
         message_ref[pairs + n * seqs : pairs + (n + 1) * seqs] = normed[
             :, n * LANES : (n + 1) * LANES
         ].astype(BF16)
     normed_ref[...] = normed
     inverse_ref[...] = inverse
-
-    repeat = lane_ids((proj, LANES)) % proj
-    repeat = (repeat == lax.broadcasted_iota(jnp.int32, (proj, LANES), 0)).astype(BF16)
-    left_row = dot(left[...], repeat, contract=(0, 0))
-    right_row = dot(right[...], repeat, contract=(0, 0))
-    slot = lane_ids(left_row.shape) // proj
-    nothing = jnp.zeros(left_row.shape, BF16)
-    for t in range(tokens):
-        here = slice(t * channels, (t + 1) * channels)
-        left_one_ref[here] = jnp.where(slot == t, left_row, 0.0).astype(BF16)
-        right_one_ref[here] = jnp.where(slot == t, right_row, 0.0).astype(BF16)
-        for other in range(tokens):
-            left_wide_ref[here, other * LANES : (other + 1) * LANES] = (
-                left_row.astype(BF16) if other == t else nothing
-            )
 
 
 def place_blocks(place_ref, offsets, refs, out_ref):
@@ -312,88 +283,77 @@
     lax.fori_loop(0, prow_n, step, 0)
 
 
-def outer_kernel(
+def rows_of(ref, g, r):
+    half = ref.shape[2] // 2
+    return jnp.concatenate([ref[r, g, :half], ref[r, g, half:]], axis=1)
+
+
+def prepare_kernel(
     offsets,
     place_ref,
     mine_from_ref,
-    theirs_from_ref,
-    mapping_ref,
     left_ref,
     right_ref,
-    offset_ref,
     rows_ref,
-    expanded,
+    ahead_ref,
     swapped,
-    outer_ref,
-    pair_ref,
+    turned,
+    left_wide,
+    left_one_ref,
+    right_one_ref,
     mine_ref,
-    theirs_ref,
-    turned,
 ):
     place_blocks(place_ref, offsets, [mine_from_ref], mine_ref)
-    place_blocks(place_ref, offsets, [theirs_from_ref], theirs_ref)
     prow_n, groups = mine_ref.shape[:2]
-    block_rows, block_cols, pair_width = pair_ref.shape
-    owners, seqs = expanded.shape[:2]
-    packed = left_ref.shape[0]
-    tokens = left_ref.shape[1] // LANES
-    proj = LANES // tokens
+    seqs = ahead_ref.shape[1]
+    proj, channels = left_ref.shape
+    tokens = LANES // proj
     highs = proj // tokens
+    block_cols = prow_n * tokens
     span = highs * block_cols
-    own_row, own_group, core = place_ref[0], place_ref[1], place_ref[2]
-
-    def rows_of(ref, g, r):
-        return jnp.concatenate(
-            [ref[r, g, n * seqs : (n + 1) * seqs] for n in range(packed // LANES)], axis=1
-        )
-
-    places = [(g, r) for g in range(groups) for r in range(prow_n)]
-    rows_mine = [rows_of(mine_ref, g, r) for g, r in places]
-    rows_all = jnp.concatenate(
-        rows_mine + [rows_of(theirs_ref, g, r) for g, r in places], axis=0
-    )
-    rows_ref[...] = rows_all
-    wide_left = dot(rows_all, left_ref[...]).astype(BF16)
-    for n, owner in enumerate(owner_order(places, prow_n, core)):
-        expanded[owner] = wide_left[n * seqs : (n + 1) * seqs]
-
-    side_rows = []
-    for g in range(groups):
-        chunks = rows_mine[g * prow_n : (g + 1) * prow_n]
-        side_rows.append(
-            jnp.concatenate([dot(x, right_ref[...]).astype(BF16) for x in chunks], axis=1)
-        )
-    right = dot(jnp.concatenate(side_rows, axis=0), shuffle_matrix(block_cols, proj, tokens))
+
+    repeat = lane_ids((proj, LANES)) % proj
+    repeat = (repeat == lax.broadcasted_iota(jnp.int32, (proj, LANES), 0)).astype(BF16)
+    left_row = dot(left_ref[...], repeat, contract=(0, 0))
+    right_row = dot(right_ref[...], repeat, contract=(0, 0))
+    slot = lane_ids(left_row.shape) // proj
+    nothing = jnp.zeros(left_row.shape, BF16)
+    for t in range(tokens):
+        here = slice(t * channels, (t + 1) * channels)
+        left_one_ref[here] = jnp.where(slot == t, left_row, 0.0).astype(BF16)
+        right_one_ref[here] = jnp.where(slot == t, right_row, 0.0).astype(BF16)
+        for other in range(tokens):
+            left_wide[here, other * LANES : (other + 1) * LANES] = (
+                left_row.astype(BF16) if other == t else nothing
+            )
+
+    rows = jnp.concatenate(
+        [rows_of(mine_ref, g, r) for g in range(groups) for r in range(prow_n)], axis=0
+    )
+    rows_ref[...] = rows
+    ahead_ref[...] = dot(rows, left_wide[...]).astype(BF16).reshape(ahead_ref.shape)
+
+    right = dot(rows, right_one_ref[...]).astype(BF16)
+    right = jnp.concatenate(
+        [
+            jnp.concatenate(
+                [
+                    right[(g * prow_n + r) * seqs : (g * prow_n + r + 1) * seqs]
+                    for r in range(prow_n)
+                ],
+                axis=1,
+            )
+            for g in range(groups)
+        ],
+        axis=0,
+    )
+    right = dot(right, shuffle_matrix(block_cols, proj, tokens))
     for g in range(groups):
         for l in range(tokens):
             swapped[l * seqs : (l + 1) * seqs, g * span : (g + 1) * span] = (
                 right[g * seqs : (g + 1) * seqs, l * span : (l + 1) * span] * (1.0 / seqs)
             ).astype(BF16)
     turned[...] = swapped[...].astype(F32).T.astype(BF16)
-
-    def step(row, carry):
-        made = dot(turned[...], left_block(expanded, row, owners // prow_n, tokens))
-        for g in range(groups):
-            for t in range(block_rows):
-                start = (g * block_rows + t) * block_cols
-                lanes = slice(t * LANES, (t + 1) * LANES)
-                for h in range(highs):
-                    there = slice((g * highs + h) * block_cols, (g * highs + h + 1) * block_cols)
-                    outer_ref[row, start : start + block_cols, h * LANES : (h + 1) * LANES] = made[
-                        there, lanes
-                    ].astype(BF16)
-        return carry
-
-    lax.fori_loop(0, prow_n, step, 0)
-    share = block_rows * block_cols
-    mine = outer_ref[own_row, pl.ds(pl.multiple_of(own_group * share, share), share)]
-    update = dot(mine, mapping_ref[...]) + offset_ref[...]
-    pair_ref[...] = update.astype(BF16).reshape(pair_ref.shape)
-
-
-def owner_order(places, prow_n, core):
-    mine = [(2 * g + core) * prow_n + r for g, r in places]
-    return mine + [(2 * g + 1 - core) * prow_n + r for g, r in places]
 
 
 def shuffle_matrix(block_cols, proj, tokens):
@@ -405,64 +365,74 @@
     return (source == jj * proj + qh * tokens + ql).astype(BF16)
 
 
-def left_block(expanded, row, step_owners, tokens):
-    ahead = jnp.concatenate([expanded[row * step_owners + o] for o in range(step_owners)], axis=1)
+def left_block(place_ref, prow_n, mine_ref, theirs_ref, row, tokens):
+    columns_n = 2 * (mine_ref.shape[0] // prow_n)
+    parts = []
+    for o in range(columns_n):
+        owner = row * columns_n + o
+        column, at = owner // prow_n, lax.rem(owner, prow_n)
+        at = column // 2 * prow_n + at
+        parts.append(
+            jnp.where(lax.rem(column, 2) == place_ref[2], mine_ref[at], theirs_ref[at])
+        )
+    ahead = jnp.concatenate(parts, axis=1)
     low = lane_ids(ahead.shape) % LANES // (LANES // tokens)
     return jnp.concatenate(
         [jnp.where(low == l, ahead, jnp.zeros_like(ahead)) for l in range(tokens)], axis=0
     )
 
 
-def back_kernel(
+def grads_kernel(
+    offsets,
     place_ref,
+    theirs_from_ref,
     rows_ref,
-    expanded,
+    mine_ahead,
+    left_wide,
     swapped,
-    outer_ref,
-    cot_ref,
     pulled_ref,
     grads_ref,
     message_ref,
+    theirs_ahead,
+    theirs_ref,
     left_back,
     right_back,
     sums,
-    weights,
 ):
-    prow_n, groups, pairs, pair_width = cot_ref.shape
-    owners, seqs = left_back.shape[:2]
+    place_blocks(place_ref, offsets, [theirs_from_ref], theirs_ref)
+    prow_n, groups = theirs_ref.shape[:2]
+    seqs = mine_ahead.shape[1]
     tokens = swapped.shape[0] // seqs
     proj = LANES // tokens
     highs = proj // tokens
     span = swapped.shape[1] // groups
     block_cols = span // highs
-    step_owners = owners // prow_n
+    columns_n = 2 * groups
     own_row, own_group, core = place_ref[0], place_ref[1], place_ref[2]
-    places = [(g, r) for g in range(groups) for r in range(prow_n)]
-    order = owner_order(places, prow_n, core)
-
+    theirs_rows = jnp.concatenate(
+        [rows_of(theirs_ref, g, r) for g in range(groups) for r in range(prow_n)], axis=0
+    )
+    theirs_ahead[...] = dot(theirs_rows, left_wide[...]).astype(BF16).reshape(theirs_ahead.shape)
     sums[...] = jnp.zeros_like(sums)
-    weights[...] = jnp.zeros_like(weights)
 
     def step(row, carry):
-        block = left_block(expanded, row, step_owners, tokens)
-        cot = cot_ref[row].reshape(groups * pairs, pair_width)
-        weights[...] += dot(cot, outer_ref[row], contract=(0, 0))
+        block = left_block(place_ref, prow_n, mine_ahead, theirs_ahead, row, tokens)
         pulled = pulled_ref[row]
         back = dot(swapped[...], pulled)
         low = lane_ids((seqs, back.shape[1])) % LANES // proj
         back = functools.reduce(
             jnp.add,
-            [
-                jnp.where(low == l, back[l * seqs : (l + 1) * seqs], 0.0)
-                for l in range(tokens)
-            ],
+            [jnp.where(low == l, back[l * seqs : (l + 1) * seqs], 0.0) for l in range(tokens)],
         )
-        for o in range(step_owners):
+        for o in range(columns_n):
             parts = [
                 back[:, (o * tokens + t) * LANES : (o * tokens + t + 1) * LANES]
                 for t in range(tokens)
             ]
-            left_back[row * step_owners + o] = fold_tokens(parts).astype(BF16)
+            owner = row * columns_n + o
+            column, at = owner // prow_n, lax.rem(owner, prow_n)
+            other = jnp.where(lax.rem(column, 2) == core, 0, 1)
+            left_back[other, column // 2 * prow_n + at] = fold_tokens(parts).astype(BF16)
         sums[...] += dot(pulled, block, contract=(1, 1))
         return carry
 
@@ -484,7 +454,7 @@
     )
     shuffle = shuffle_matrix(block_cols, proj, tokens)
     back = dot(back, shuffle, contract=(1, 1)).astype(BF16)
-    for g, r in places:
+    for g, r in [(g, r) for g in range(groups) for r in range(prow_n)]:
         right_back[g * prow_n + r] = back[g * seqs : (g + 1) * seqs, r * LANES : (r + 1) * LANES]
 
     def side(grads, rows):
@@ -498,23 +468,70 @@
             ],
         )
 
+    count = groups * prow_n * seqs
     left_side = side(
-        jnp.concatenate([left_back[owner] for owner in order], axis=0), rows_ref[...]
-    )
-    columns = groups * prow_n * seqs
-    right_side = side(right_back[...].reshape(columns, LANES), rows_ref[:columns])
+        left_back[...].reshape(2 * count, LANES),
+        jnp.concatenate([rows_ref[...], theirs_rows], axis=0),
+    )
+    right_side = side(right_back[...].reshape(count, LANES), rows_ref[...])
     both = jnp.concatenate([left_side, right_side], axis=0).astype(BF16)
-    both = jnp.concatenate([both, jnp.zeros_like(both)], axis=1)
+    message_ref[: 2 * proj] = jnp.concatenate([both, jnp.zeros_like(both)], axis=1)
+    own = own_group * prow_n + own_row
+    message_ref[2 * proj :] = left_back[1, own]
+    grads_ref[0] = left_back[0, own]
+    grads_ref[1] = right_back[own]
+
+
+def weights_kernel(
+    place_ref,
+    mine_ahead,
+    theirs_ahead,
+    turned,
+    cot_ref,
+    mapping_ref,
+    offset_ref,
+    pair_ref,
+    message_ref,
+    outer,
+    weights,
+):
+    prow_n, groups, pairs, pair_width = cot_ref.shape
+    block_rows, block_cols, _ = pair_ref.shape
+    seqs = mine_ahead.shape[1]
+    tokens = turned.shape[1] // seqs
+    proj = LANES // tokens
+    highs = proj // tokens
+    own_row, own_group = place_ref[0], place_ref[1]
+    weights[...] = jnp.zeros_like(weights)
+
+    def step(row, carry):
+        block = left_block(place_ref, prow_n, mine_ahead, theirs_ahead, row, tokens)
+        made = dot(turned[...], block)
+        for g in range(groups):
+            for t in range(block_rows):
+                start = (g * block_rows + t) * block_cols
+                lanes = slice(t * LANES, (t + 1) * LANES)
+                for h in range(highs):
+                    there = slice((g * highs + h) * block_cols, (g * highs + h + 1) * block_cols)
+                    outer[start : start + block_cols, h * LANES : (h + 1) * LANES] = made[
+                        there, lanes
+                    ].astype(BF16)
+        cot = cot_ref[row].reshape(groups * pairs, pair_width)
+        weights[...] += dot(cot, outer[...], contract=(0, 0))
+
+        @pl.when(row == own_row)
+        def _():
+            mine = outer[pl.ds(pl.multiple_of(own_group * pairs, pairs), pairs)]
+            update = dot(mine, mapping_ref[...]) + offset_ref[...]
+            pair_ref[...] = update.astype(BF16).reshape(pair_ref.shape)
+
+        return carry
+
+    lax.fori_loop(0, prow_n, step, 0)
 
     flat = weights.shape[1]
-    outer_f = weights[...].T
-    weight_rows = outer_f.reshape(proj, proj, pair_width).swapaxes(0, 1).reshape(flat, pair_width)
-
-    message_ref[:flat] = weight_rows.astype(BF16)
-    message_ref[flat : flat + 2 * proj] = both
-    message_ref[flat + 2 * proj :] = left_back[(2 * own_group + 1 - core) * prow_n + own_row]
-    grads_ref[0] = left_back[(2 * own_group + core) * prow_n + own_row]
-    grads_ref[1] = right_back[own_group * prow_n + own_row]
+    turned_back = weights[...].T.reshape(proj, proj, pair_width)
+    message_ref[...] = turned_back.swapaxes(0, 1).reshape(flat, pair_width).astype(BF16)
 
 
 def close_kernel(
@@ -525,19 +542,16 @@
     inverse_ref,
     left_ref,
     right_ref,
-    out_ref,
     left_out_ref,
     right_out_ref,
     rows_out_ref,
 ):
-    flat = out_ref.shape[0]
     proj, features = left_out_ref.shape
-    out_ref[...] = own_ref[:flat].astype(F32) + message_ref[:flat].astype(F32)
-    sides = slice(flat, flat + 2 * proj)
+    sides = slice(0, 2 * proj)
     both = own_ref[sides, :features].astype(F32) + message_ref[sides, :features].astype(F32)
     left_out_ref[...] = both[:proj]
     right_out_ref[...] = both[proj:]
-    left_back = grads_ref[0].astype(F32) + message_ref[flat + 2 * proj :].astype(F32)
+    left_back = grads_ref[0].astype(F32) + message_ref[2 * proj :].astype(F32)
     grad_normed = dot(left_back.astype(BF16), left_ref[...], contract=(1, 1))
     grad_normed = grad_normed + dot(grads_ref[1], right_ref[...], contract=(1, 1))
     normed = normed_ref[...]
@@ -575,42 +589,33 @@
     pairs = block_rows * block_cols
     length = seqs * packed // LANES
     hbm = pl.BlockSpec(memory_space=pltpu.HBM)
-    normed, inverse, left_wide, left_one, right_one, offset, sent = pl.pallas_call(
+    normed, inverse, sent = pl.pallas_call(
         pick_kernel,
         out_shape=(
             shape((seqs, packed), F32),
             shape((seqs, packed), F32),
-            shape((packed, tokens * LANES), BF16),
-            shape((packed, LANES), BF16),
-            shape((packed, LANES), BF16),
-            shape((1, pair_width), F32),
             shape((pairs + length, LANES), BF16),
         ),
-        in_specs=[hbm] * 6,
-        out_specs=(vmem,) * 7,
+        in_specs=[hbm] * 3,
+        out_specs=(vmem,) * 3,
         scratch_shapes=[
             pltpu.VMEM((1, seqs), jnp.int32),
             pltpu.VMEM((packed, heads), BF16),
-            pltpu.VMEM((proj, features), BF16),
-            pltpu.VMEM((proj, features), BF16),
-            pltpu.SemaphoreType.DMA((6,)),
+            pltpu.SemaphoreType.DMA((3,)),
         ],
         compiler_params=pltpu.CompilerParams(vmem_limit_bytes=60 * 1024 * 1024),
         name="pick_rows",
     )(
         subset_homolog_positions.reshape(1, seqs),
         homolog_features.transpose(1, 2, 0).reshape(packed, heads),
-        first_side_matrix.T,
-        second_side_matrix.T,
-        final_offset_vector.reshape(1, pair_width),
         upstream_sensitivity.reshape(pairs, pair_width),
     )
 
+    downs = list(range(prow_n // 2, prow_n)) + list(range(1, prow_n // 2))
     messages = [sent] + [
-        lax.ppermute(sent, "prow", [(n, n ^ down) for n in range(prow_n)])
-        for down in range(1, prow_n)
+        lax.ppermute(sent, "prow", [(n, n ^ down) for n in range(prow_n)]) for down in downs
     ]
-    offsets = [(down, 0) for down in range(prow_n)]
+    offsets = [(down, 0) for down in [0] + downs]
     rows = jnp.stack([one[pairs:] for one in messages])
     cots = [jnp.stack([one[:pairs] for one in messages])]
     for bit in range(groups.bit_length() - 1):
@@ -643,62 +648,85 @@
         name="pull_back",
     )(place, mapping.T, *cots)
 
-    rows_all, expanded, swapped, outer, pair_delta = pl.pallas_call(
-        functools.partial(outer_kernel, offsets),
+    sided = groups * prow_n
+    rows_mine, mine_ahead, swapped, turned, left_wide, left_one, right_one = pl.pallas_call(
+        functools.partial(prepare_kernel, offsets),
         out_shape=(
-            shape((owners * seqs, packed), BF16),
-            shape((owners, seqs, tokens * LANES), BF16),
+            shape((sided * seqs, packed), BF16),
+            shape((sided, seqs, tokens * LANES), BF16),
             shape((tokens * seqs, columns), BF16),
-            shape((prow_n, groups * pairs, flat), BF16),
-            shape(upstream_sensitivity.shape, BF16),
+            shape((columns, tokens * seqs), BF16),
+            shape((packed, tokens * LANES), BF16),
+            shape((packed, LANES), BF16),
+            shape((packed, LANES), BF16),
+        ),
+        in_specs=[smem] + [vmem] * 3,
+        out_specs=(vmem,) * 7,
+        scratch_shapes=[pltpu.VMEM((prow_n, groups, length, LANES), BF16)],
+        compiler_params=params,
+        cost_estimate=pl.CostEstimate(
+            flops=2 * sided * seqs * packed * tokens * LANES,
+            bytes_accessed=4 * sided * seqs * packed,
+            transcendentals=0,
+        ),
+        name="prepare",
+    )(place, rows, first_side_matrix.T, second_side_matrix.T)
+    grads, side_message, theirs_ahead = pl.pallas_call(
+        functools.partial(grads_kernel, offsets),
+        out_shape=(
+            shape((2, seqs, LANES), BF16),
+            shape((2 * proj + seqs, LANES), BF16),
+            shape((sided, seqs, tokens * LANES), BF16),
         ),
         in_specs=[smem] + [vmem] * 6,
-        out_specs=(vmem,) * 5,
+        out_specs=(vmem,) * 3,
         scratch_shapes=[
             pltpu.VMEM((prow_n, groups, length, LANES), BF16),
-            pltpu.VMEM((prow_n, groups, length, LANES), BF16),
-            pltpu.VMEM((columns, tokens * seqs), BF16),
+            pltpu.VMEM((2, sided, seqs, LANES), BF16),
+            pltpu.VMEM((sided, seqs, LANES), BF16),
+            pltpu.VMEM((columns, tokens * seqs), F32),
+        ],
+        compiler_params=params,
+        name="projection_grads",
+    )(place, theirs, rows_mine, mine_ahead, left_wide, swapped, pulled)
+    side_theirs = lax.ppermute(side_message, "pc", [(0, 1), (1, 0)])
+    pair_delta, message = pl.pallas_call(
+        weights_kernel,
+        out_shape=(
+            shape(upstream_sensitivity.shape, BF16),
+            shape((flat, pair_width), BF16),
+        ),
+        in_specs=[smem] + [vmem] * 6,
+        out_specs=(vmem,) * 2,
+        scratch_shapes=[
+            pltpu.VMEM((groups * pairs, flat), BF16),
+            pltpu.VMEM((pair_width, flat), F32),
         ],
         compiler_params=params,
         cost_estimate=pl.CostEstimate(
-            flops=2 * prow_n * groups * pairs * tokens * seqs * flat,
+            flops=4 * prow_n * groups * pairs * tokens * seqs * flat,
             bytes_accessed=2 * prow_n * groups * pairs * flat,
             transcendentals=0,
         ),
         name="outer_products",
-    )(place, rows, theirs, mapping, left_wide, right_one, offset)
-    grads, message = pl.pallas_call(
-        back_kernel,
-        out_shape=(
-            shape((2, seqs, LANES), BF16),
-            shape((flat + 2 * proj + seqs, LANES), BF16),
-        ),
-        in_specs=[smem] + [vmem] * 6,
-        out_specs=(vmem,) * 2,
-        scratch_shapes=[
-            pltpu.VMEM((owners, seqs, LANES), BF16),
-            pltpu.VMEM((groups * prow_n, seqs, LANES), BF16),
-            pltpu.VMEM((columns, tokens * seqs), F32),
-            pltpu.VMEM((pair_width, flat), F32),
-        ],
-        compiler_params=params,
-        name="pull_further",
-    )(place, rows_all, expanded, swapped, outer, cot, pulled)
-
+    )(
+        place, mine_ahead, theirs_ahead, turned, cot, mapping,
+        final_offset_vector.reshape(1, pair_width),
+    )
     theirs = lax.ppermute(message, "pc", [(0, 1), (1, 0)])
-    output_weight_gradient, left_weight_gradient, right_weight_gradient, alignment = pl.pallas_call(
+    left_weight_gradient, right_weight_gradient, alignment = pl.pallas_call(
         close_kernel,
         out_shape=(
-            shape((flat, pair_width), F32),
             shape((proj, features), F32),
             shape((proj, features), F32),
             shape((seqs, tokens, features), BF16),
         ),
         in_specs=[vmem] * 7,
-        out_specs=(vmem,) * 4,
+        out_specs=(vmem,) * 3,
         compiler_params=params,
-        name="close",
-    )(grads, message, theirs, normed, inverse, left_one, right_one)
+        name="row_gradient",
+    )(grads, side_message, side_theirs, normed, inverse, left_one, right_one)
+    output_weight_gradient = message.astype(F32) + theirs.astype(F32)
     return (
         pair_delta,
         alignment,

time: 41 us -> 44 us (1.073)
  local copies, waits for them, and re-layouts: 3.73 us -> 5.08 us
  other arithmetic: 0.14 us -> 0.98 us
  Pallas kernels: 15.4 us -> 16.2 us
  waiting for transfers between devices: 12.6 us -> 12.1 us
    ppermute x1, waiting for transfers between devices: 1.57 us -> 0.01 us  [local_gathered(): theirs = lax.ppermute(message, 'pc', [(0, 1), (1, 0)])]
    ppermute x1, waiting for transfers between devices: 1.41 us -> 0.01 us  [local_gathered(): cots.append(lax.ppermute(held, 'px', swap))]
    unnamed x16 -> x14, local copies, waits for them, and re-layouts: 0.88 us -> 2.2 us
    ppermute x0 -> x1, waiting for transfers between devices: none -> 1.18 us  [local_gathered(): side_theirs = lax.ppermute(side_message, 'pc', [(0, 1), (1, 0)])]
    ppermute x3, waiting for transfers between devices: 5.62 us -> 6.66 us  [local_gathered(): lax.ppermute(sent, 'prow', [(n, n ^ down) for n in range(prow_n)])]
    pallas_call x3 -> x4, Pallas kernels: 10.8 us -> 11.8 us  [the longest x1 4.76 us: local_gathered(): pl.pallas_call(functools.partial(grads_kernel, offsets), out_shape=(shape...]
    transpose x1, local copies, waits for them, and re-layouts: 1.06 us -> 0.14 us  [local_gathered(): cot, pulled = pl.pallas_call(functools.partial(pull_kernel, offsets), out...]
    reshape x1, local copies, waits for them, and re-layouts: 0.14 us -> 1.06 us  [local_gathered(): mapping = final_mapping_matrix.reshape(proj, proj, pair_width)]
  transfers between devices with their start and end apart: 7 -> 8, of which waited for: 5 -> 4; matrix products, arithmetic and copies ran while one was open for 9% -> 9% of each run, Pallas kernels for 6% -> 11%
where the time goes in v8:
time: 44 us; the launch traced here: 43.5 us
  Pallas kernels  16.2 us (37%)
  waiting for transfers between devices  12.1 us (28%)
  starting transfers between devices  8.42 us (19%)
  local copies, waits for them, and re-layouts  5.08 us (12%)
  other arithmetic  0.98 us (2%)
  between operations  0.77 us (2%)
    ppermute x3, waiting for transfers between devices, local_gathered(): lax.ppermute(sent, 'prow', [(n, n ^ down) for n in range(prow_n)])  6.66 us
    ppermute x3, starting transfers between devices, local_gathered(): lax.ppermute(sent, 'prow', [(n, n ^ down) for n in range(prow_n)])  5.68 us
    pallas_call x1, Pallas kernels, local_gathered(): pl.pallas_call(functools.partial(grads_kernel, offsets), out_shape=(shape...  4.76 us
    pallas_call x1, Pallas kernels, local_gathered(): pl.pallas_call(weights_kernel, out_shape=(shape(upstream_sensitivity.shap...  4.28 us
    ppermute x1, waiting for transfers between devices, local_gathered(): rows = jnp.concatenate([rows, lax.ppermute(rows, 'px', swap)], axis=0)  4.23 us
    pallas_call x1, Pallas kernels, local_gathered(): pl.pallas_call(functools.partial(pull_kernel, offsets), out_shape=(shape(...  2.26 us
    unnamed x14, local copies, waits for them, and re-layouts  2.2 us
    pallas_call x1, Pallas kernels, local_gathered(): pl.pallas_call(pick_kernel, out_shape=(shape((seqs, packed), F32), shape(...  2.15 us
  transfers between devices with their start and end apart: 8, of which 4 were waited for; matrix products, arithmetic and copies ran while one was open for 9% of the time, Pallas kernels for 11%

profile of v8, /device:TPU:0, one launch (start us, length us, event | category | flops | bytes accessed | tf_op | source)
XLA Modules:
  0.0 43.5 jit_solution(8378252820681520225)
XLA Ops:
  0.6 2.1 %pick_rows.1 = (f32[64,256]{1,0:T(8,128)}, f32[64,256]{1,0:T(8,128)}, bf16[384,128]{1,0:T(8,128)(2,1)}) custom-call(s32[1,64]{1,0:T(1,128)} %bitcast.51, bf16[256,128]{1,0:T(8,128)(2,1)} %bitcast.49, bf16[256,128]{1,0:T(8,128)(2,1)} %bitcast.50), custom_call_target="tpu_custom_call" | custom-call | tf_op jit(solution)/shard_map/pick_rows/pallas_call | solution.py:592
  2.8 3.1 %collective-permute-start.2 = (bf16[384,128]{1,0:T(8,128)(2,1)}, bf16[384,128]{1,0:T(8,128)(2,1)S(1)}, u32[]{:S(2)}, u32[]{:S(2)}) collective-permute-start(bf16[384,128]{1,0:T(8,128)(2,1)} %get-tuple-element.25), channel_id=1, source_target_pairs={{0,4},{4,0},{8,12},{12,8},{1,5},{5,1},{9,13},{13,9},{2,6},{6,2},{1... | collective-permute-start | bytes 294920 | tf_op jit(solution)/shard_map/ppermute | solution.py:616
  5.9 2.5 %collective-permute-start.1 = (bf16[384,128]{1,0:T(8,128)(2,1)}, bf16[384,128]{1,0:T(8,128)(2,1)S(1)}, u32[]{:S(2)}, u32[]{:S(2)}) collective-permute-start(bf16[384,128]{1,0:T(8,128)(2,1)} %get-tuple-element.25), channel_id=1, source_target_pairs={{0,12},{4,8},{8,4},{12,0},{1,13},{5,9},{9,5},{13,1},{2,14},{6,10},... | collective-permute-start | bytes 294920 | tf_op jit(solution)/shard_map/ppermute | solution.py:616
  8.4 0.1 collective-permute-start
  8.5 0.8 %slice_bitcast_fusion.7 = bf16[1,128,128]{2,1,0:T(8,128)(2,1)S(1)} fusion(bf16[384,128]{1,0:T(8,128)(2,1)} %get-tuple-element.25), kind=kLoop, calls=%fused_computation.10 | loop fusion | bytes 65536 | tf_op jit(solution)/shard_map/stack | solution.py:619
  9.3 0.8 %slice_bitcast_fusion.3 = bf16[1,256,128]{2,1,0:T(8,128)(2,1)S(1)} fusion(bf16[384,128]{1,0:T(8,128)(2,1)} %get-tuple-element.25), kind=kLoop, calls=%fused_computation.6 | loop fusion | bytes 131072 | tf_op jit(solution)/shard_map/stack | solution.py:620
  10.1 0.8 %constant_dynamic-update-slice_fusion.4 = bf16[8,128,128]{2,1,0:T(8,128)(2,1)S(1)} fusion(bf16[384,128]{1,0:T(8,128)(2,1)} %get-tuple-element.25), kind=kLoop, calls=%fused_computation.15 | loop fusion | bytes 65536
  10.9 3.4 %collective-permute-done.1 = bf16[384,128]{1,0:T(8,128)(2,1)S(1)} collective-permute-done((bf16[384,128]{1,0:T(8,128)(2,1)}, bf16[384,128]{1,0:T(8,128)(2,1)S(1)}, u32[]{:S(2)}, u32[]{:S(2)}) %collective-permute-start.1) | collective-permute-done | bytes 98336 | tf_op jit(solution)/shard_map/ppermute | solution.py:616
  14.3 3.3 %collective-permute-done = bf16[384,128]{1,0:T(8,128)(2,1)S(1)} collective-permute-done((bf16[384,128]{1,0:T(8,128)(2,1)}, bf16[384,128]{1,0:T(8,128)(2,1)S(1)}, u32[]{:S(2)}, u32[]{:S(2)}) %collective-permute-start) | collective-permute-done | bytes 98336 | tf_op jit(solution)/shard_map/ppermute | solution.py:616
  17.6 1.6 %collective-permute-start.3 = (bf16[4,128,128]{2,1,0:T(8,128)(2,1)S(1)}, bf16[4,128,128]{2,1,0:T(8,128)(2,1)S(1)}, u32[]{:S(2)}, u32[]{:S(2)}) collective-permute-start(bf16[4,128,128]{2,1,0:T(8,128)(2,1)S(1)} %pad_maximum_fusion.1), channel_id=1, source_target_pairs={{0,2},{2,0},{1,3},{3,1},{4,6},{6,4},{5,7},{7,5},{8,10},{10,8},{9,1... | collective-permute-start | bytes 393224 | tf_op jit(solution)/shard_map/ppermute | solution.py:623
  19.2 0.6 %collective-permute-start.5 = (bf16[4,256,128]{2,1,0:T(8,128)(2,1)S(1)}, bf16[4,256,128]{2,1,0:T(8,128)(2,1)S(1)}, u32[]{:S(2)}, u32[]{:S(2)}) collective-permute-start(bf16[4,256,128]{2,1,0:T(8,128)(2,1)S(1)} %pad_maximum_fusion.refs_0_), channel_id=1, source_target_pairs={{0,2},{2,0},{1,3},{3,1},{4,6},{6,4},{5,7},{7,5},{8,10},{10,8},{9,1... | collective-permute-start | bytes 786440 | tf_op jit(solution)/shard_map/ppermute | solution.py:625
  19.8 4.2 %collective-permute-done.3 = bf16[4,128,128]{2,1,0:T(8,128)(2,1)S(1)} collective-permute-done((bf16[4,128,128]{2,1,0:T(8,128)(2,1)S(1)}, bf16[4,128,128]{2,1,0:T(8,128)(2,1)S(1)}, u32[]{:S(2)}, u32[]{:S(2)}) %collective-permute-start.3) | collective-permute-done | bytes 131104 | tf_op jit(solution)/shard_map/ppermute | solution.py:623
  24.2 1.1 %copy.12 = bf16[32,32,128]{2,0,1:T(8,128)(2,1)S(1)} copy(bf16[32,32,128]{2,1,0:T(8,128)(2,1)} %bitcast.48) | data formatting | bytes 524288 | tf_op jit(solution)/shard_map/reshape | solution.py:629
  25.2 0.1 copy.13.mapping_ref
  25.5 0.7 %copy-done.2 = bf16[64,32]{0,1:T(8,128)(2,1)S(1)} copy-done((bf16[64,32]{0,1:T(8,128)(2,1)S(1)}, bf16[64,32]{0,1:T(8,128)(2,1)}, u32[]{:S(2)}) %copy-start.2) | copy-done | bytes 4120
  26.2 0.7 %copy-done.3 = bf16[64,32]{0,1:T(8,128)(2,1)S(1)} copy-done((bf16[64,32]{0,1:T(8,128)(2,1)S(1)}, bf16[64,32]{0,1:T(8,128)(2,1)}, u32[]{:S(2)}) %copy-start.3) | copy-done | bytes 4120
  26.9 1.4 %prepare.1 = (bf16[512,256]{1,0:T(8,128)(2,1)S(1)}, bf16[8,64,512]{2,1,0:T(8,128)(2,1)S(1)}, bf16[256,256]{1,0:T(8,128)(2,1)S(1)}, bf16[256,256]{1,0:T(8,128)(2,...) custom-call(s32[3]{0:T(128)S(1)} %pad_add_fusion.place_ref, ...), custom_call_target="tpu_custom_call" | custom-call | flops 134217728 | bytes 524288 | tf_op jit(solution)/shard_map/prepare/pallas_call | solution.py:652
  28.3 2.3 %pull_back.1 = (bf16[4,2,256,128]{3,2,1,0:T(8,128)(2,1)S(1)}, bf16[4,256,2048]{2,1,0:T(8,128)(2,1)S(1)}) custom-call(s32[3]{0:T(128)S(1)} %pad_add_fusion.place_ref, bf16[128,1024]{1,0:T(8,128)(2,1)S(1)} %copy.13.mapping_ref, bf16[4,256,128]{2,1,0:T(8,128)(2,1)S(1)} %pad_maximum_fusion.refs_0_, bf16[4,256,128]{2,1,0:T(8,128)(2,1)S(1)} %collective-permute-done.5.refs_1_), custom_call_target="tpu_custom_call" | custom-call | flops 536870912 | bytes 5242880 | tf_op jit(solution)/shard_map/pull_back/pallas_call | solution.py:634
  30.6 4.8 %projection_grads.1 = (bf16[2,64,128]{2,1,0:T(8,128)(2,1)S(1)}, bf16[128,128]{1,0:T(8,128)(2,1)S(1)}, bf16[8,64,512]{2,1,0:T(8,128)(2,1)S(1)}) custom-call(s32[3]{0:T(128)S(1)} %pad_add_fusion.place_ref, bf16[8,128,128]{2,1,0:T(8,128)(2,1)S(1)} %collective-permute-done.4.theirs_from_ref, bf16[512,256]{1,0:T(8,128)(2,1)S(1)} %get-tuple-element.27.rows_ref, ...), custom_call_target="tpu_custom_call" | custom-call | tf_op jit(solution)/shard_map/projection_grads/pallas_call | solution.py:674
  35.4 4.3 %outer_products.1 = (bf16[16,16,128]{2,1,0:T(8,128)(2,1)}, bf16[1024,128]{1,0:T(8,128)(2,1)S(1)}) custom-call(s32[3]{0:T(128)S(1)} %pad_add_fusion.place_ref, bf16[8,64,512]{2,1,0:T(8,128)(2,1)S(1)} %get-tuple-element.26.mine_ahead, bf16[8,64,512]{2,1,0:T(8,128)(2,1)S(1)} %get-tuple-element.31.theirs_ahead, bf16[256,256]{1,0:T(8,128)(2,1)S(1)} %get-tuple-element.32.turned, ...), custom_call_target="tpu_custom_call" | custom-call | flops 2147483648 | bytes 4194304 | tf_op jit(solution)/shard_map/outer_products/pallas_call | solution.py:693
  39.7 0.5 %collective-permute-start.7 = (bf16[1024,128]{1,0:T(8,128)(2,1)S(1)}, bf16[1024,128]{1,0:T(8,128)(2,1)S(1)}, u32[]{:S(2)}, u32[]{:S(2)}) collective-permute-start(bf16[1024,128]{1,0:T(8,128)(2,1)S(1)} %get-tuple-element.44), channel_id=1, source_target_pairs={{0,1},{1,0},{2,3},{3,2},{4,5},{5,4},{6,7},{7,6},{8,9},{9,8},{10,11... | collective-permute-start | bytes 786440 | tf_op jit(solution)/shard_map/ppermute | solution.py:716
  40.2 1.2 %collective-permute-done.6.message_ref = bf16[128,128]{1,0:T(8,128)(2,1)S(1)} collective-permute-done((bf16[128,128]{1,0:T(8,128)(2,1)S(1)}, bf16[128,128]{1,0:T(8,128)(2,1)S(1)}, u32[]{:S(2)}, u32[]{:S(2)}) %collective-permute-start.6) | collective-permute-done | bytes 32800 | tf_op jit(solution)/shard_map/ppermute | solution.py:692
  41.4 1.3 %row_gradient.1 = (f32[32,64]{1,0:T(8,128)}, f32[32,64]{1,0:T(8,128)}, bf16[64,4,64]{2,1,0:T(4,128)(2,1)}) custom-call(bf16[2,64,128]{2,1,0:T(8,128)(2,1)S(1)} %get-tuple-element.35.grads_ref, bf16[128,128]{1,0:T(8,128)(2,1)S(1)} %get-tuple-element.36.own_ref, bf16[128,128]{1,0:T(8,128)(2,1)S(1)} %collective-permute-done.6.message_ref, ...), custom_call_target="tpu_custom_call" | custom-call | tf_op jit(solution)/shard_map/row_gradient/pallas_call | solution.py:717
  42.6 0.8 %convert_add_fusion = f32[1024,128]{1,0:T(8,128)} fusion(bf16[1024,128]{1,0:T(8,128)(2,1)S(1)} %collective-permute-done.7, bf16[1024,128]{1,0:T(8,128)(2,1)S(1)} %get-tuple-element.44), kind=kLoop, calls=%fused_computation | loop fusion | flops 393216 | bytes 1048576 | tf_op jit(solution)/shard_map/add | solution.py:729
  (27 shorter events, 0.3 us)
Async XLA Ops:
  2.8 8.1 %collective-permute-start.2 = (bf16[384,128]{1,0:T(8,128)(2,1)}, bf16[384,128]{1,0:T(8,128)(2,1)S(1)}, u32[]{:S(2)}, u32[]{:S(2)}) collective-permute-start(bf16[384,128]{1,0:T(8,128)(2,1)} %get-tuple-element.25), channel_id=1, source_target_pairs={{0,4},{4,0},{8,12},{12,8},{1,5},{5,1},{9,13},{13,9},{2,6},{6,2},{1... | collective-permute-start | bytes 294920 | tf_op jit(solution)/shard_map/ppermute | solution.py:616
  5.9 8.4 %collective-permute-start.1 = (bf16[384,128]{1,0:T(8,128)(2,1)}, bf16[384,128]{1,0:T(8,128)(2,1)S(1)}, u32[]{:S(2)}, u32[]{:S(2)}) collective-permute-start(bf16[384,128]{1,0:T(8,128)(2,1)} %get-tuple-element.25), channel_id=1, source_target_pairs={{0,12},{4,8},{8,4},{12,0},{1,13},{5,9},{9,5},{13,1},{2,14},{6,10},... | collective-permute-start | bytes 294920 | tf_op jit(solution)/shard_map/ppermute | solution.py:616
  8.4 9.2 %collective-permute-start = (bf16[384,128]{1,0:T(8,128)(2,1)}, bf16[384,128]{1,0:T(8,128)(2,1)S(1)}, u32[]{:S(2)}, u32[]{:S(2)}) collective-permute-start(bf16[384,128]{1,0:T(8,128)(2,1)} %get-tuple-element.25), channel_id=1, source_target_pairs={{0,8},{4,12},{8,0},{12,4},{1,9},{5,13},{9,1},{13,5},{2,10},{6,14},... | collective-permute-start | bytes 294920 | tf_op jit(solution)/shard_map/ppermute | solution.py:616
  17.6 6.5 %collective-permute-start.3 = (bf16[4,128,128]{2,1,0:T(8,128)(2,1)S(1)}, bf16[4,128,128]{2,1,0:T(8,128)(2,1)S(1)}, u32[]{:S(2)}, u32[]{:S(2)}) collective-permute-start(bf16[4,128,128]{2,1,0:T(8,128)(2,1)S(1)} %pad_maximum_fusion.1), channel_id=1, source_target_pairs={{0,2},{2,0},{1,3},{3,1},{4,6},{6,4},{5,7},{7,5},{8,10},{10,8},{9,1... | collective-permute-start | bytes 393224 | tf_op jit(solution)/shard_map/ppermute | solution.py:623
  19.2 9.1 %collective-permute-start.5 = (bf16[4,256,128]{2,1,0:T(8,128)(2,1)S(1)}, bf16[4,256,128]{2,1,0:T(8,128)(2,1)S(1)}, u32[]{:S(2)}, u32[]{:S(2)}) collective-permute-start(bf16[4,256,128]{2,1,0:T(8,128)(2,1)S(1)} %pad_maximum_fusion.refs_0_), channel_id=1, source_target_pairs={{0,2},{2,0},{1,3},{3,1},{4,6},{6,4},{5,7},{7,5},{8,10},{10,8},{9,1... | collective-permute-start | bytes 786440 | tf_op jit(solution)/shard_map/ppermute | solution.py:625
  24.1 6.5 %collective-permute-start.4 = (bf16[8,128,128]{2,1,0:T(8,128)(2,1)S(1)}, bf16[8,128,128]{2,1,0:T(8,128)(2,1)S(1)}, u32[]{:S(2)}, u32[]{:S(2)}) collective-permute-start(bf16[8,128,128]{2,1,0:T(8,128)(2,1)S(1)} %constant_dynamic-update-slice_fusion.mine_from_ref), channel_id=1, source_target_pairs={{0,1},{1,0},{2,3},{3,2},{4,5},{5,4},{6,7},{7,6},{8,9},{9,8},{10,11... | collective-permute-start | bytes 786440 | tf_op jit(solution)/shard_map/ppermute | solution.py:627
  25.4 10.0 %copy-start.4 = (f32[128]{0:T(128)S(1)}, f32[128]{0:T(128)}, u32[]{:S(2)}) copy-start(f32[128]{0:T(128)} %param.12) | copy-start | bytes 1540
  25.5 0.7 %copy-start.2 = (bf16[64,32]{0,1:T(8,128)(2,1)S(1)}, bf16[64,32]{0,1:T(8,128)(2,1)}, u32[]{:S(2)}) copy-start(bf16[64,32]{0,1:T(8,128)(2,1)} %param.9) | copy-start | bytes 12292
  26.2 0.7 %copy-start.3 = (bf16[64,32]{0,1:T(8,128)(2,1)S(1)}, bf16[64,32]{0,1:T(8,128)(2,1)}, u32[]{:S(2)}) copy-start(bf16[64,32]{0,1:T(8,128)(2,1)} %param.10) | copy-start | bytes 12292
  35.3 6.0 %copy-start = (f32[64,256]{1,0:T(8,128)S(1)}, f32[64,256]{1,0:T(8,128)}, u32[]{:S(2)}) copy-start(f32[64,256]{1,0:T(8,128)} %get-tuple-element.37.normed_ref) | copy-start | bytes 196612
  35.4 6.0 %copy-start.1 = (f32[64,256]{1,0:T(8,128)S(1)}, f32[64,256]{1,0:T(8,128)}, u32[]{:S(2)}) copy-start(f32[64,256]{1,0:T(8,128)} %get-tuple-element.38.inverse_ref) | copy-start | bytes 196612
  39.7 3.0 %collective-permute-start.7 = (bf16[1024,128]{1,0:T(8,128)(2,1)S(1)}, bf16[1024,128]{1,0:T(8,128)(2,1)S(1)}, u32[]{:S(2)}, u32[]{:S(2)}) collective-permute-start(bf16[1024,128]{1,0:T(8,128)(2,1)S(1)} %get-tuple-element.44), channel_id=1, source_target_pairs={{0,1},{1,0},{2,3},{3,2},{4,5},{5,4},{6,7},{7,6},{8,9},{9,8},{10,11... | collective-permute-start | bytes 786440 | tf_op jit(solution)/shard_map/ppermute | solution.py:716
  40.1 1.2 %collective-permute-start.6 = (bf16[128,128]{1,0:T(8,128)(2,1)S(1)}, bf16[128,128]{1,0:T(8,128)(2,1)S(1)}, u32[]{:S(2)}, u32[]{:S(2)}) collective-permute-start(bf16[128,128]{1,0:T(8,128)(2,1)S(1)} %get-tuple-element.36.own_ref), channel_id=1, source_target_pairs={{0,1},{1,0},{2,3},{3,2},{4,5},{5,4},{6,7},{7,6},{8,9},{9,8},{10,11... | collective-permute-start | bytes 98312 | tf_op jit(solution)/shard_map/ppermute | solution.py:692

commit v9 on v7

--- a/solution.py
+++ b/solution.py
@@ -282,19 +282,18 @@
             )
 
 
-def place_blocks(place_ref, offsets, refs, out_ref):
-    blocks = [(ref, n) for ref in refs for n in range(ref.shape[0])]
-    for (down, across), (ref, n) in zip(offsets, blocks, strict=True):
-        out_ref[place_ref[0] ^ down, place_ref[1] ^ across] = ref[n]
+def place_blocks(place_ref, offsets, blocks, out_ref):
+    for (down, across), block in zip(offsets, blocks, strict=True):
+        out_ref[place_ref[0] ^ down, place_ref[1] ^ across] = block
 
 
 def pull_kernel(offsets, place_ref, mapping_ref, *refs):
-    *cot_refs, cot_ref, pulled_ref = refs
+    *message_refs, cot_ref, pulled_ref = refs
     prow_n, groups, pairs, pair_width = cot_ref.shape
     highs = mapping_ref.shape[1] // LANES
     block_rows = pulled_ref.shape[2] // LANES
     block_cols = pairs // block_rows
-    place_blocks(place_ref, offsets, cot_refs, cot_ref)
+    place_blocks(place_ref, offsets, [ref[:pairs] for ref in message_refs], cot_ref)
 
     def step(r, carry):
         grad = dot(cot_ref[r].reshape(groups * pairs, pair_width), mapping_ref[...])
@@ -330,8 +329,8 @@
     theirs_ref,
     turned,
 ):
-    place_blocks(place_ref, offsets, [mine_from_ref], mine_ref)
-    place_blocks(place_ref, offsets, [theirs_from_ref], theirs_ref)
+    for source, target in ((mine_from_ref, mine_ref), (theirs_from_ref, theirs_ref)):
+        place_blocks(place_ref, offsets, [source[n] for n in range(source.shape[0])], target)
     prow_n, groups = mine_ref.shape[:2]
     block_rows, block_cols, pair_width = pair_ref.shape
     owners, seqs = expanded.shape[:2]
@@ -606,19 +605,17 @@
         upstream_sensitivity.reshape(pairs, pair_width),
     )
 
+    def swapped_with(values, axis, size, mask):
+        return lax.ppermute(values, axis, [(n, n ^ mask) for n in range(size)])
+
     messages = [sent] + [
-        lax.ppermute(sent, "prow", [(n, n ^ down) for n in range(prow_n)])
-        for down in range(1, prow_n)
+        swapped_with(sent, "prow", prow_n, down) for down in range(1, prow_n)
     ]
-    offsets = [(down, 0) for down in range(prow_n)]
+    messages += [
+        swapped_with(one, "px", groups, across) for across in range(1, groups) for one in messages
+    ]
+    offsets = [(down, across) for across in range(groups) for down in range(prow_n)]
     rows = jnp.stack([one[pairs:] for one in messages])
-    cots = [jnp.stack([one[:pairs] for one in messages])]
-    for bit in range(groups.bit_length() - 1):
-        swap = [(n, n ^ (1 << bit)) for n in range(groups)]
-        rows = jnp.concatenate([rows, lax.ppermute(rows, "px", swap)], axis=0)
-        held = cots[0] if bit == 0 else jnp.concatenate(cots, axis=0)
-        cots.append(lax.ppermute(held, "px", swap))
-        offsets += [(down, across + (1 << bit)) for down, across in offsets]
     theirs = lax.ppermute(rows, "pc", [(0, 1), (1, 0)])
 
     mapping = final_mapping_matrix.reshape(proj, proj, pair_width)
@@ -632,7 +629,7 @@
             shape((prow_n, groups, pairs, pair_width), BF16),
             shape((prow_n, columns, block_rows * LANES), BF16),
         ),
-        in_specs=[smem] + [vmem] * (1 + len(cots)),
+        in_specs=[smem] + [vmem] * (1 + len(messages)),
         out_specs=(vmem,) * 2,
         compiler_params=params,
         cost_estimate=pl.CostEstimate(
@@ -641,7 +638,7 @@
             transcendentals=0,
         ),
         name="pull_back",
-    )(place, mapping.T, *cots)
+    )(place, mapping.T, *messages)
 
     rows_all, expanded, swapped, outer, pair_delta = pl.pallas_call(
         functools.partial(outer_kernel, offsets),

time: 41 us -> 42.8 us (1.044)
  starting transfers between devices: 7.98 us -> 10.4 us
  waiting for transfers between devices: 12.6 us -> 10.5 us
  local copies, waits for them, and re-layouts: 3.73 us -> 5.36 us
    unnamed x16 -> x23, local copies, waits for them, and re-layouts: 0.88 us -> 4.15 us
    ppermute x5 -> x7, starting transfers between devices: 7.84 us -> 9.8 us  [swapped_with(): return lax.ppermute(values, axis, [(n, n ^ mask) for n in range(size)])]
    ppermute x5 -> x7, waiting for transfers between devices: 11 us -> 9.25 us  [swapped_with(): return lax.ppermute(values, axis, [(n, n ^ mask) for n in range(size)])]
    another operation x4 -> x0, local copies, waits for them, and re-layouts: 0.86 us -> none  [local_gathered(): cots = [jnp.stack([one[:pairs] for one in messages])]]
    another operation x4 -> x1, local copies, waits for them, and re-layouts: 0.77 us -> 0.01 us  [local_gathered(): rows = jnp.stack([one[pairs:] for one in messages])]
    ppermute x1, starting transfers between devices: 0.07 us -> 0.56 us  [local_gathered(): theirs = lax.ppermute(message, 'pc', [(0, 1), (1, 0)])]
  transfers between devices with their start and end apart: 7 -> 9, of which waited for: 5 -> 4; matrix products, arithmetic and copies ran while one was open for 9% -> 5% of each run, Pallas kernels for 6% -> 5%
where the time goes in v9:
time: 42.8 us; the launch traced here: 42.4 us
  Pallas kernels  15.4 us (36%)
  waiting for transfers between devices  10.5 us (25%)
  starting transfers between devices  10.4 us (24%)
  local copies, waits for them, and re-layouts  5.36 us (13%)
  between operations  0.73 us (2%)
    ppermute x7, starting transfers between devices, swapped_with(): return lax.ppermute(values, axis, [(n, n ^ mask) for n in range(size)])  9.8 us
    ppermute x7, waiting for transfers between devices, swapped_with(): return lax.ppermute(values, axis, [(n, n ^ mask) for n in range(size)])  9.25 us
    pallas_call x1, Pallas kernels, local_gathered(): pl.pallas_call(back_kernel, out_shape=(shape((2, seqs, LANES), BF16), sha...  5.24 us
    unnamed x23, local copies, waits for them, and re-layouts  4.15 us
    pallas_call x1, Pallas kernels, local_gathered(): pl.pallas_call(functools.partial(outer_kernel, offsets), out_shape=(shape...  4.02 us
    pallas_call x1, Pallas kernels, local_gathered(): pl.pallas_call(pick_kernel, out_shape=(shape((seqs, packed), F32), shape(...  2.35 us
    pallas_call x1, Pallas kernels, local_gathered(): pl.pallas_call(functools.partial(pull_kernel, offsets), out_shape=(shape(...  2.26 us
    pallas_call x1, Pallas kernels, local_gathered(): pl.pallas_call(close_kernel, out_shape=(shape((flat, pair_width), F32), s...  1.51 us
  transfers between devices with their start and end apart: 9, of which 4 were waited for; matrix products, arithmetic and copies ran while one was open for 5% of the time, Pallas kernels for 5%

profile of v9, /device:TPU:0, one launch (start us, length us, event | category | flops | bytes accessed | tf_op | source)
XLA Modules:
  0.0 42.4 jit_solution(7549774612880933117)
XLA Ops:
  0.6 2.4 %pick_rows.1 = (f32[64,256]{1,0:T(8,128)}, f32[64,256]{1,0:T(8,128)}, bf16[256,512]{1,0:T(8,128)(2,1)}, bf16[256,128]{1,0:T(8,128)(2,1)}, bf16[256,128]{1,0:T(8,...) custom-call(s32[1,64]{1,0:T(1,128)} %bitcast.56, bf16[256,128]{1,0:T(8,128)(2,1)} %bitcast.52, ...), custom_call_target="tpu_custom_call" | custom-call | tf_op jit(solution)/shard_map/pick_rows/pallas_call | solution.py:577
  3.0 3.1 %collective-permute-start = (bf16[384,128]{1,0:T(8,128)(2,1)}, bf16[384,128]{1,0:T(8,128)(2,1)S(1)}, u32[]{:S(2)}, u32[]{:S(2)}) collective-permute-start(bf16[384,128]{1,0:T(8,128)(2,1)} %get-tuple-element.25.refs_0_), channel_id=1, source_target_pairs={{0,4},{4,0},{8,12},{12,8},{1,5},{5,1},{9,13},{13,9},{2,6},{6,2},{1... | collective-permute-start | bytes 294920 | tf_op jit(solution)/shard_map/ppermute | solution.py:609
  6.1 2.6 %collective-permute-start.1 = (bf16[384,128]{1,0:T(8,128)(2,1)}, bf16[384,128]{1,0:T(8,128)(2,1)S(1)}, u32[]{:S(2)}, u32[]{:S(2)}) collective-permute-start(bf16[384,128]{1,0:T(8,128)(2,1)} %get-tuple-element.25.refs_0_), channel_id=1, source_target_pairs={{0,8},{4,12},{8,0},{12,4},{1,9},{5,13},{9,1},{13,5},{2,10},{6,14},... | collective-permute-start | bytes 294920 | tf_op jit(solution)/shard_map/ppermute | solution.py:609
  8.7 1.7 %collective-permute-start.3 = (bf16[384,128]{1,0:T(8,128)(2,1)}, bf16[384,128]{1,0:T(8,128)(2,1)S(1)}, u32[]{:S(2)}, u32[]{:S(2)}) collective-permute-start(bf16[384,128]{1,0:T(8,128)(2,1)} %get-tuple-element.25.refs_0_), channel_id=1, source_target_pairs={{0,2},{2,0},{1,3},{3,1},{4,6},{6,4},{5,7},{7,5},{8,10},{10,8},{9,1... | collective-permute-start | bytes 294920 | tf_op jit(solution)/shard_map/ppermute | solution.py:609
  10.4 0.8 %bitcast_dynamic-update-slice_fusion = bf16[8,128,128]{2,1,0:T(8,128)(2,1)S(1)} fusion(bf16[384,128]{1,0:T(8,128)(2,1)} %get-tuple-element.25.refs_0_), kind=kLoop, calls=%fused_computation.14 | loop fusion | bytes 65536
  11.2 0.3 collective-permute-start.4
  11.5 5.2 %collective-permute-done.1.refs_2_ = bf16[384,128]{1,0:T(8,128)(2,1)S(1)} collective-permute-done((bf16[384,128]{1,0:T(8,128)(2,1)}, bf16[384,128]{1,0:T(8,128)(2,1)S(1)}, u32[]{:S(2)}, u32[]{:S(2)}) %collective-permute-start.1) | collective-permute-done | bytes 98336 | tf_op jit(solution)/shard_map/ppermute | solution.py:609
  16.7 1.5 %collective-permute-start.5 = (bf16[384,128]{1,0:T(8,128)(2,1)S(1)}, bf16[384,128]{1,0:T(8,128)(2,1)S(1)}, u32[]{:S(2)}, u32[]{:S(2)}) collective-permute-start(bf16[384,128]{1,0:T(8,128)(2,1)S(1)} %collective-permute-done.1.refs_2_), channel_id=1, source_target_pairs={{0,2},{2,0},{1,3},{3,1},{4,6},{6,4},{5,7},{7,5},{8,10},{10,8},{9,1... | collective-permute-start | bytes 294920 | tf_op jit(solution)/shard_map/ppermute | solution.py:609
  18.2 0.6 %collective-permute-start.6 = (bf16[384,128]{1,0:T(8,128)(2,1)S(1)}, bf16[384,128]{1,0:T(8,128)(2,1)S(1)}, u32[]{:S(2)}, u32[]{:S(2)}) collective-permute-start(bf16[384,128]{1,0:T(8,128)(2,1)S(1)} %collective-permute-done.2.refs_3_), channel_id=1, source_target_pairs={{0,2},{2,0},{1,3},{3,1},{4,6},{6,4},{5,7},{7,5},{8,10},{10,8},{9,1... | collective-permute-start | bytes 294920 | tf_op jit(solution)/shard_map/ppermute | solution.py:609
  18.9 2.5 %collective-permute-done.5.refs_6_ = bf16[384,128]{1,0:T(8,128)(2,1)S(1)} collective-permute-done((bf16[384,128]{1,0:T(8,128)(2,1)S(1)}, bf16[384,128]{1,0:T(8,128)(2,1)S(1)}, u32[]{:S(2)}, u32[]{:S(2)}) %collective-permute-start.5) | collective-permute-done | bytes 98336 | tf_op jit(solution)/shard_map/ppermute | solution.py:609
  21.4 1.6 %collective-permute-done.6.refs_7_ = bf16[384,128]{1,0:T(8,128)(2,1)S(1)} collective-permute-done((bf16[384,128]{1,0:T(8,128)(2,1)S(1)}, bf16[384,128]{1,0:T(8,128)(2,1)S(1)}, u32[]{:S(2)}, u32[]{:S(2)}) %collective-permute-start.6) | collective-permute-done | bytes 98336 | tf_op jit(solution)/shard_map/ppermute | solution.py:609
  22.9 1.1 %copy.15 = bf16[32,32,128]{2,1,0:T(8,128)(2,1)S(1)} copy(bf16[32,32,128]{2,0,1:T(8,128)(2,1)} %bitcast.51) | data formatting | bytes 524288 | tf_op jit(solution)/shard_map/transpose | solution.py:622
  24.0 0.1 copy.16
  24.1 0.1 pad_add_fusion.place_ref
  24.2 0.9 %copy-done.5 = bf16[384,128]{1,0:T(8,128)(2,1)S(1)} copy-done((bf16[384,128]{1,0:T(8,128)(2,1)S(1)}, bf16[384,128]{1,0:T(8,128)(2,1)}, u32[]{:S(2)}) %copy-start.5) | copy-done | bytes 98328
  25.1 2.3 %pull_back.1 = (bf16[4,2,256,128]{3,2,1,0:T(8,128)(2,1)S(1)}, bf16[4,256,2048]{2,1,0:T(8,128)(2,1)S(1)}) custom-call(s32[3]{0:T(128)S(1)} %pad_add_fusion.place_ref, bf16[128,1024]{1,0:T(8,128)(2,1)S(1)} %bitcast.50, bf16[384,128]{1,0:T(8,128)(2,1)S(1)} %copy-done.5, bf16[384,128]{1,0:T(8,128)(2,1)S(1)} %collective-permute-done.refs_1_, ...), custom_call_target="tpu_custom_call" | custom-call | flops 536870912 | bytes 5242880 | tf_op jit(solution)/shard_map/pull_back/pallas_call | solution.py:626
  27.4 0.8 %copy-done.3 = bf16[256,128]{1,0:T(8,128)(2,1)S(1)} copy-done((bf16[256,128]{1,0:T(8,128)(2,1)S(1)}, bf16[256,128]{1,0:T(8,128)(2,1)}, u32[]{:S(2)}) %copy-start.3) | copy-done | bytes 65560
  28.2 0.9 %copy-done.6 = bf16[256,512]{1,0:T(8,128)(2,1)S(1)} copy-done((bf16[256,512]{1,0:T(8,128)(2,1)S(1)}, bf16[256,512]{1,0:T(8,128)(2,1)}, u32[]{:S(2)}) %copy-start.6) | copy-done | bytes 262168
  29.2 0.6 %copy-done.7 = f32[1,128]{1,0:T(1,128)S(1)} copy-done((f32[1,128]{1,0:T(1,128)S(1)}, f32[1,128]{1,0:T(1,128)}, u32[]{:S(2)}) %copy-start.7) | copy-done | bytes 536
  29.8 4.0 %outer_products.1 = (bf16[1024,256]{1,0:T(8,128)(2,1)S(1)}, bf16[16,64,512]{2,1,0:T(8,128)(2,1)S(1)}, bf16[256,256]{1,0:T(8,128)(2,1)S(1)}, bf16[4,512,1024]{2,1,0:T(8,128)(2,1)S(1)}, bf16[16,16,128]{2,1,0:T(8,128)(2,1)}) custom-call(s32[3]{0:T(128)S(1)} %pad_add_fusion.place_ref, bf16[8,128,128]{2,1,0:T(8,128)(2,1)S(1)} %fusion.mine_from_ref, ...), custom_call_target="tpu_custom_call" | custom-call | flops 1073741824 | bytes 4194304 | tf_op jit(solution)/shard_map/outer_products/pallas_call | solution.py:643
  33.8 5.2 %pull_further.1 = (bf16[2,64,128]{2,1,0:T(8,128)(2,1)S(1)}, bf16[1152,128]{1,0:T(8,128)(2,1)S(1)}) custom-call(s32[3]{0:T(128)S(1)} %pad_add_fusion.place_ref, bf16[1024,256]{1,0:T(8,128)(2,1)S(1)} %get-tuple-element.30.rows_ref, bf16[16,64,512]{2,1,0:T(8,128)(2,1)S(1)} %get-tuple-element.31.expanded, bf16[256,256]{1,0:T(8,128)(2,1)S(1)} %get-tuple-element.32.swapped, ...), custom_call_target="tpu_custom_call" | custom-call | tf_op jit(solution)/shard_map/pull_further/pallas_call | solution.py:667
  39.1 0.6 %collective-permute-start.8 = (bf16[1152,128]{1,0:T(8,128)(2,1)S(1)}, bf16[1152,128]{1,0:T(8,128)(2,1)S(1)}, u32[]{:S(2)}, u32[]{:S(2)}) collective-permute-start(bf16[1152,128]{1,0:T(8,128)(2,1)S(1)} %get-tuple-element.37.own_ref), channel_id=1, source_target_pairs={{0,1},{1,0},{2,3},{3,2},{4,5},{5,4},{6,7},{7,6},{8,9},{9,8},{10,11... | collective-permute-start | bytes 884744 | tf_op jit(solution)/shard_map/ppermute | solution.py:685
  39.6 1.2 %collective-permute-done.8.message_ref = bf16[1152,128]{1,0:T(8,128)(2,1)S(1)} collective-permute-done((bf16[1152,128]{1,0:T(8,128)(2,1)S(1)}, bf16[1152,128]{1,0:T(8,128)(2,1)S(1)}, u32[]{:S(2)}, u32[]{:S(2)}) %collective-permute-start.8) | collective-permute-done | bytes 294944 | tf_op jit(solution)/shard_map/ppermute | solution.py:685
  40.9 1.5 %close.1 = (f32[1024,128]{1,0:T(8,128)}, f32[32,64]{1,0:T(8,128)}, f32[32,64]{1,0:T(8,128)}, bf16[64,4,64]{2,1,0:T(4,128)(2,1)}) custom-call(bf16[2,64,128]{2,1,0:T(8,128)(2,1)S(1)} %get-tuple-element.36.grads_ref, bf16[1152,128]{1,0:T(8,128)(2,1)S(1)} %get-tuple-element.37.own_ref, bf16[1152,128]{1,0:T(8,128)(2,1)S(1)} %collective-permute-done.8.message_ref, ...), custom_call_target="tpu_custom_call" | custom-call | tf_op jit(solution)/shard_map/close/pallas_call | solution.py:686
  (26 shorter events, 0.1 us)
Async XLA Ops:
  3.0 8.2 %collective-permute-start = (bf16[384,128]{1,0:T(8,128)(2,1)}, bf16[384,128]{1,0:T(8,128)(2,1)S(1)}, u32[]{:S(2)}, u32[]{:S(2)}) collective-permute-start(bf16[384,128]{1,0:T(8,128)(2,1)} %get-tuple-element.25.refs_0_), channel_id=1, source_target_pairs={{0,4},{4,0},{8,12},{12,8},{1,5},{5,1},{9,13},{13,9},{2,6},{6,2},{1... | collective-permute-start | bytes 294920 | tf_op jit(solution)/shard_map/ppermute | solution.py:609
  6.1 10.6 %collective-permute-start.1 = (bf16[384,128]{1,0:T(8,128)(2,1)}, bf16[384,128]{1,0:T(8,128)(2,1)S(1)}, u32[]{:S(2)}, u32[]{:S(2)}) collective-permute-start(bf16[384,128]{1,0:T(8,128)(2,1)} %get-tuple-element.25.refs_0_), channel_id=1, source_target_pairs={{0,8},{4,12},{8,0},{12,4},{1,9},{5,13},{9,1},{13,5},{2,10},{6,14},... | collective-permute-start | bytes 294920 | tf_op jit(solution)/shard_map/ppermute | solution.py:609
  8.7 9.6 %collective-permute-start.2 = (bf16[384,128]{1,0:T(8,128)(2,1)}, bf16[384,128]{1,0:T(8,128)(2,1)S(1)}, u32[]{:S(2)}, u32[]{:S(2)}) collective-permute-start(bf16[384,128]{1,0:T(8,128)(2,1)} %get-tuple-element.25.refs_0_), channel_id=1, source_target_pairs={{0,12},{4,8},{8,4},{12,0},{1,13},{5,9},{9,5},{13,1},{2,14},{6,10},... | collective-permute-start | bytes 294920 | tf_op jit(solution)/shard_map/ppermute | solution.py:609
  8.7 10.2 %collective-permute-start.3 = (bf16[384,128]{1,0:T(8,128)(2,1)}, bf16[384,128]{1,0:T(8,128)(2,1)S(1)}, u32[]{:S(2)}, u32[]{:S(2)}) collective-permute-start(bf16[384,128]{1,0:T(8,128)(2,1)} %get-tuple-element.25.refs_0_), channel_id=1, source_target_pairs={{0,2},{2,0},{1,3},{3,1},{4,6},{6,4},{5,7},{7,5},{8,10},{10,8},{9,1... | collective-permute-start | bytes 294920 | tf_op jit(solution)/shard_map/ppermute | solution.py:609
  11.2 7.7 %collective-permute-start.4 = (bf16[384,128]{1,0:T(8,128)(2,1)S(1)}, bf16[384,128]{1,0:T(8,128)(2,1)S(1)}, u32[]{:S(2)}, u32[]{:S(2)}) collective-permute-start(bf16[384,128]{1,0:T(8,128)(2,1)S(1)} %collective-permute-done.refs_1_), channel_id=1, source_target_pairs={{0,2},{2,0},{1,3},{3,1},{4,6},{6,4},{5,7},{7,5},{8,10},{10,8},{9,1... | collective-permute-start | bytes 294920 | tf_op jit(solution)/shard_map/ppermute | solution.py:609
  16.7 4.6 %collective-permute-start.5 = (bf16[384,128]{1,0:T(8,128)(2,1)S(1)}, bf16[384,128]{1,0:T(8,128)(2,1)S(1)}, u32[]{:S(2)}, u32[]{:S(2)}) collective-permute-start(bf16[384,128]{1,0:T(8,128)(2,1)S(1)} %collective-permute-done.1.refs_2_), channel_id=1, source_target_pairs={{0,2},{2,0},{1,3},{3,1},{4,6},{6,4},{5,7},{7,5},{8,10},{10,8},{9,1... | collective-permute-start | bytes 294920 | tf_op jit(solution)/shard_map/ppermute | solution.py:609
  18.2 4.7 %collective-permute-start.6 = (bf16[384,128]{1,0:T(8,128)(2,1)S(1)}, bf16[384,128]{1,0:T(8,128)(2,1)S(1)}, u32[]{:S(2)}, u32[]{:S(2)}) collective-permute-start(bf16[384,128]{1,0:T(8,128)(2,1)S(1)} %collective-permute-done.2.refs_3_), channel_id=1, source_target_pairs={{0,2},{2,0},{1,3},{3,1},{4,6},{6,4},{5,7},{7,5},{8,10},{10,8},{9,1... | collective-permute-start | bytes 294920 | tf_op jit(solution)/shard_map/ppermute | solution.py:609
  22.9 4.5 %collective-permute-start.7 = (bf16[8,128,128]{2,1,0:T(8,128)(2,1)S(1)}, bf16[8,128,128]{2,1,0:T(8,128)(2,1)S(1)}, u32[]{:S(2)}, u32[]{:S(2)}) collective-permute-start(bf16[8,128,128]{2,1,0:T(8,128)(2,1)S(1)} %fusion.mine_from_ref), channel_id=1, source_target_pairs={{0,1},{1,0},{2,3},{3,2},{4,5},{5,4},{6,7},{7,6},{8,9},{9,8},{10,11... | collective-permute-start | bytes 786440 | tf_op jit(solution)/shard_map/ppermute | solution.py:619
  24.2 0.9 %copy-start.5 = (bf16[384,128]{1,0:T(8,128)(2,1)S(1)}, bf16[384,128]{1,0:T(8,128)(2,1)}, u32[]{:S(2)}) copy-start(bf16[384,128]{1,0:T(8,128)(2,1)} %get-tuple-element.25.refs_0_) | copy-start | bytes 294916
  27.4 0.8 %copy-start.3 = (bf16[256,128]{1,0:T(8,128)(2,1)S(1)}, bf16[256,128]{1,0:T(8,128)(2,1)}, u32[]{:S(2)}) copy-start(bf16[256,128]{1,0:T(8,128)(2,1)} %get-tuple-element.27.right_ref) | copy-start | bytes 196612
  28.2 0.9 %copy-start.6 = (bf16[256,512]{1,0:T(8,128)(2,1)S(1)}, bf16[256,512]{1,0:T(8,128)(2,1)}, u32[]{:S(2)}) copy-start(bf16[256,512]{1,0:T(8,128)(2,1)} %get-tuple-element.26.left_ref) | copy-start | bytes 786436
  29.2 0.6 %copy-start.7 = (f32[1,128]{1,0:T(1,128)S(1)}, f32[1,128]{1,0:T(1,128)}, u32[]{:S(2)}) copy-start(f32[1,128]{1,0:T(1,128)} %get-tuple-element.28.offset_ref) | copy-start | bytes 1540
  33.8 7.0 %copy-start = (f32[64,256]{1,0:T(8,128)S(1)}, f32[64,256]{1,0:T(8,128)}, u32[]{:S(2)}) copy-start(f32[64,256]{1,0:T(8,128)} %get-tuple-element.38.normed_ref) | copy-start | bytes 196612
  33.8 7.0 %copy-start.1 = (f32[64,256]{1,0:T(8,128)S(1)}, f32[64,256]{1,0:T(8,128)}, u32[]{:S(2)}) copy-start(f32[64,256]{1,0:T(8,128)} %get-tuple-element.39.inverse_ref) | copy-start | bytes 196612
  33.8 7.0 %copy-start.2 = (bf16[256,128]{1,0:T(8,128)(2,1)S(1)}, bf16[256,128]{1,0:T(8,128)(2,1)}, u32[]{:S(2)}) copy-start(bf16[256,128]{1,0:T(8,128)(2,1)} %get-tuple-element.40.left_ref) | copy-start | bytes 196612
  33.8 7.0 %copy-start.4 = (bf16[256,128]{1,0:T(8,128)(2,1)S(1)}, bf16[256,128]{1,0:T(8,128)(2,1)}, u32[]{:S(2)}) copy-start(bf16[256,128]{1,0:T(8,128)(2,1)} %get-tuple-element.27.right_ref) | copy-start | bytes 196612
  39.1 1.8 %collective-permute-start.8 = (bf16[1152,128]{1,0:T(8,128)(2,1)S(1)}, bf16[1152,128]{1,0:T(8,128)(2,1)S(1)}, u32[]{:S(2)}, u32[]{:S(2)}) collective-permute-start(bf16[1152,128]{1,0:T(8,128)(2,1)S(1)} %get-tuple-element.37.own_ref), channel_id=1, source_target_pairs={{0,1},{1,0},{2,3},{3,2},{4,5},{5,4},{6,7},{7,6},{8,9},{9,8},{10,11... | collective-permute-start | bytes 884744 | tf_op jit(solution)/shard_map/ppermute | solution.py:685

commit v10 on v9

--- a/solution.py
+++ b/solution.py
@@ -212,21 +212,12 @@
 def pick_kernel(
     positions_ref,
     features_ref,
-    left_ref,
-    right_ref,
-    offset_ref,
     cot_ref,
     normed_ref,
     inverse_ref,
-    left_wide_ref,
-    left_one_ref,
-    right_one_ref,
-    offset_out_ref,
     message_ref,
     positions,
     features,
-    left,
-    right,
     in_sems,
 ):
     pairs = cot_ref.shape[0]
@@ -236,9 +227,6 @@
             [
                 (positions_ref, positions),
                 (features_ref, features),
-                (left_ref, left),
-                (right_ref, right),
-                (offset_ref, offset_out_ref),
                 (cot_ref, message_ref.at[pl.ds(0, pairs)]),
             ]
         )
@@ -247,8 +235,7 @@
         copy.start()
     heads = features_ref.shape[1]
     seqs, packed = normed_ref.shape
-    proj, channels = left_ref.shape
-    tokens = packed // channels
+    channels = packed // 4
     for copy in inputs:
         copy.wait()
     wanted = positions[...] == lax.broadcasted_iota(jnp.int32, (heads, seqs), 0)
@@ -258,18 +245,39 @@
     variance = group_mean(centered * centered, channels, lax.Precision.HIGHEST)
     inverse = lax.rsqrt(variance + 1e-05)
     normed = centered * inverse
-    pieces = packed // LANES
-    for n in range(pieces):
+    for n in range(packed // LANES):
         message_ref[pairs + n * seqs : pairs + (n + 1) * seqs] = normed[
             :, n * LANES : (n + 1) * LANES
         ].astype(BF16)
     normed_ref[...] = normed
     inverse_ref[...] = inverse
 
+
+def setup_kernel(
+    first_ref,
+    own_ref,
+    mapping_ref,
+    turned_mapping_ref,
+    left_ref,
+    right_ref,
+    offset_ref,
+    first_out_ref,
+    own_out_ref,
+    left_wide_ref,
+    left_one_ref,
+    right_one_ref,
+    offset_out_ref,
+):
+    del mapping_ref, turned_mapping_ref
+    first_out_ref[...] = first_ref[...]
+    own_out_ref[...] = own_ref[...]
+    offset_out_ref[...] = offset_ref[...]
+    proj, channels = left_ref.shape
+    tokens = left_one_ref.shape[0] // channels
     repeat = lane_ids((proj, LANES)) % proj
     repeat = (repeat == lax.broadcasted_iota(jnp.int32, (proj, LANES), 0)).astype(BF16)
-    left_row = dot(left[...], repeat, contract=(0, 0))
-    right_row = dot(right[...], repeat, contract=(0, 0))
+    left_row = dot(left_ref[...], repeat, contract=(0, 0))
+    right_row = dot(right_ref[...], repeat, contract=(0, 0))
     slot = lane_ids(left_row.shape) // proj
     nothing = jnp.zeros(left_row.shape, BF16)
     for t in range(tokens):
@@ -574,52 +582,69 @@
     pairs = block_rows * block_cols
     length = seqs * packed // LANES
     hbm = pl.BlockSpec(memory_space=pltpu.HBM)
-    normed, inverse, left_wide, left_one, right_one, offset, sent = pl.pallas_call(
+    normed, inverse, sent = pl.pallas_call(
         pick_kernel,
         out_shape=(
             shape((seqs, packed), F32),
             shape((seqs, packed), F32),
-            shape((packed, tokens * LANES), BF16),
-            shape((packed, LANES), BF16),
-            shape((packed, LANES), BF16),
-            shape((1, pair_width), F32),
             shape((pairs + length, LANES), BF16),
         ),
-        in_specs=[hbm] * 6,
-        out_specs=(vmem,) * 7,
+        in_specs=[hbm] * 3,
+        out_specs=(vmem,) * 3,
         scratch_shapes=[
             pltpu.VMEM((1, seqs), jnp.int32),
             pltpu.VMEM((packed, heads), BF16),
-            pltpu.VMEM((proj, features), BF16),
-            pltpu.VMEM((proj, features), BF16),
-            pltpu.SemaphoreType.DMA((6,)),
+            pltpu.SemaphoreType.DMA((3,)),
         ],
         compiler_params=pltpu.CompilerParams(vmem_limit_bytes=60 * 1024 * 1024),
         name="pick_rows",
     )(
         subset_homolog_positions.reshape(1, seqs),
         homolog_features.transpose(1, 2, 0).reshape(packed, heads),
+        upstream_sensitivity.reshape(pairs, pair_width),
+    )
+
+    mapping = final_mapping_matrix.reshape(proj, proj, pair_width)
+    mapping = mapping.swapaxes(0, 1).reshape(flat, pair_width)
+    turned_mapping = mapping.T
+
+    def swapped_with(values, axis, size, mask):
+        return lax.ppermute(values, axis, [(n, n ^ mask) for n in range(size)])
+
+    messages = [sent] + [
+        swapped_with(sent, "prow", prow_n, down) for down in range(1, prow_n)
+    ]
+    messages[1], own, left_wide, left_one, right_one, offset = pl.pallas_call(
+        setup_kernel,
+        out_shape=(
+            shape(sent.shape, BF16),
+            shape(sent.shape, BF16),
+            shape((packed, tokens * LANES), BF16),
+            shape((packed, LANES), BF16),
+            shape((packed, LANES), BF16),
+            shape((1, pair_width), F32),
+        ),
+        in_specs=[vmem] * 7,
+        out_specs=(vmem,) * 6,
+        compiler_params=params,
+        name="setup",
+    )(
+        messages[1],
+        sent,
+        mapping,
+        turned_mapping,
         first_side_matrix.T,
         second_side_matrix.T,
         final_offset_vector.reshape(1, pair_width),
-        upstream_sensitivity.reshape(pairs, pair_width),
-    )
-
-    def swapped_with(values, axis, size, mask):
-        return lax.ppermute(values, axis, [(n, n ^ mask) for n in range(size)])
-
-    messages = [sent] + [
-        swapped_with(sent, "prow", prow_n, down) for down in range(1, prow_n)
-    ]
+    )
     messages += [
         swapped_with(one, "px", groups, across) for across in range(1, groups) for one in messages
     ]
+    messages[0] = own
     offsets = [(down, across) for across in range(groups) for down in range(prow_n)]
     rows = jnp.stack([one[pairs:] for one in messages])
     theirs = lax.ppermute(rows, "pc", [(0, 1), (1, 0)])
 
-    mapping = final_mapping_matrix.reshape(proj, proj, pair_width)
-    mapping = mapping.swapaxes(0, 1).reshape(flat, pair_width)
     place = jnp.stack([lax.axis_index("prow"), lax.axis_index("px"), lax.axis_index("pc")])
 
     columns = groups * proj // tokens * block_cols
@@ -638,7 +663,7 @@
             transcendentals=0,
         ),
         name="pull_back",
-    )(place, mapping.T, *messages)
+    )(place, turned_mapping, *messages)
 
     rows_all, expanded, swapped, outer, pair_delta = pl.pallas_call(
         functools.partial(outer_kernel, offsets),

time: 42.8 us -> 37.9 us (0.89)
  waiting for transfers between devices: 10.5 us -> 6.84 us
  local copies, waits for them, and re-layouts: 5.36 us -> 4.21 us
    ppermute x7, waiting for transfers between devices: 9.25 us -> 5.63 us  [swapped_with(): return lax.ppermute(values, axis, [(n, n ^ mask) for n in range(size)])]
    unnamed x23 -> x19, local copies, waits for them, and re-layouts: 4.15 us -> 3 us
  transfers between devices with their start and end apart: 9 -> 9, of which waited for: 4 -> 5; matrix products, arithmetic and copies ran while one was open for 5% -> 4% of each run, Pallas kernels for 5% -> 7%
where the time goes in v10:
time: 37.9 us; the launch traced here: 37.6 us
  Pallas kernels  15.3 us (40%)
  starting transfers between devices  10.4 us (27%)
  waiting for transfers between devices  6.84 us (18%)
  local copies, waits for them, and re-layouts  4.21 us (11%)
  between operations  0.73 us (2%)
    ppermute x7, starting transfers between devices, swapped_with(): return lax.ppermute(values, axis, [(n, n ^ mask) for n in range(size)])  9.86 us
    ppermute x7, waiting for transfers between devices, swapped_with(): return lax.ppermute(values, axis, [(n, n ^ mask) for n in range(size)])  5.63 us
    pallas_call x1, Pallas kernels, local_gathered(): pl.pallas_call(back_kernel, out_shape=(shape((2, seqs, LANES), BF16), sha...  5.21 us
    pallas_call x1, Pallas kernels, local_gathered(): pl.pallas_call(functools.partial(outer_kernel, offsets), out_shape=(shape...  4.03 us
    unnamed x19, local copies, waits for them, and re-layouts  3 us
    pallas_call x1, Pallas kernels, local_gathered(): pl.pallas_call(functools.partial(pull_kernel, offsets), out_shape=(shape(...  2.26 us
    pallas_call x1, Pallas kernels, local_gathered(): pl.pallas_call(pick_kernel, out_shape=(shape((seqs, packed), F32), shape(...  2.15 us
    pallas_call x1, Pallas kernels, local_gathered(): pl.pallas_call(close_kernel, out_shape=(shape((flat, pair_width), F32), s...  1.51 us
  transfers between devices with their start and end apart: 9, of which 5 were waited for; matrix products, arithmetic and copies ran while one was open for 4% of the time, Pallas kernels for 7%

profile of v10, /device:TPU:0, one launch (start us, length us, event | category | flops | bytes accessed | tf_op | source)
XLA Modules:
  0.0 37.6 jit_solution(2157383763918968696)
XLA Ops:
  0.6 2.1 %pick_rows.1 = (f32[64,256]{1,0:T(8,128)}, f32[64,256]{1,0:T(8,128)}, bf16[384,128]{1,0:T(8,128)(2,1)}) custom-call(s32[1,64]{1,0:T(1,128)} %bitcast.57, bf16[256,128]{1,0:T(8,128)(2,1)} %bitcast.55, bf16[256,128]{1,0:T(8,128)(2,1)} %bitcast.56), custom_call_target="tpu_custom_call" | custom-call | tf_op jit(solution)/shard_map/pick_rows/pallas_call | solution.py:585
  2.8 3.1 %collective-permute-start = (bf16[384,128]{1,0:T(8,128)(2,1)}, bf16[384,128]{1,0:T(8,128)(2,1)S(1)}, u32[]{:S(2)}, u32[]{:S(2)}) collective-permute-start(bf16[384,128]{1,0:T(8,128)(2,1)} %get-tuple-element.27.own_ref), channel_id=1, source_target_pairs={{0,4},{4,0},{8,12},{12,8},{1,5},{5,1},{9,13},{13,9},{2,6},{6,2},{1... | collective-permute-start | bytes 294920 | tf_op jit(solution)/shard_map/ppermute | solution.py:612
  5.9 2.6 %collective-permute-start.1 = (bf16[384,128]{1,0:T(8,128)(2,1)}, bf16[384,128]{1,0:T(8,128)(2,1)S(1)}, u32[]{:S(2)}, u32[]{:S(2)}) collective-permute-start(bf16[384,128]{1,0:T(8,128)(2,1)} %get-tuple-element.27.own_ref), channel_id=1, source_target_pairs={{0,8},{4,12},{8,0},{12,4},{1,9},{5,13},{9,1},{13,5},{2,10},{6,14},... | collective-permute-start | bytes 294920 | tf_op jit(solution)/shard_map/ppermute | solution.py:612
  8.5 1.7 %collective-permute-start.3 = (bf16[384,128]{1,0:T(8,128)(2,1)}, bf16[384,128]{1,0:T(8,128)(2,1)S(1)}, u32[]{:S(2)}, u32[]{:S(2)}) collective-permute-start(bf16[384,128]{1,0:T(8,128)(2,1)} %get-tuple-element.27.own_ref), channel_id=1, source_target_pairs={{0,2},{2,0},{1,3},{3,1},{4,6},{6,4},{5,7},{7,5},{8,10},{10,8},{9,1... | collective-permute-start | bytes 294920 | tf_op jit(solution)/shard_map/ppermute | solution.py:612
  10.2 1.1 %copy.16 = bf16[32,32,128]{2,1,0:T(8,128)(2,1)S(1)} copy(bf16[32,32,128]{2,0,1:T(8,128)(2,1)} %bitcast.54) | data formatting | bytes 524288 | tf_op jit(solution)/shard_map/transpose | solution.py:608
  11.2 0.1 copy.17
  11.4 0.9 %copy-done = bf16[384,128]{1,0:T(8,128)(2,1)S(1)} copy-done((bf16[384,128]{1,0:T(8,128)(2,1)S(1)}, bf16[384,128]{1,0:T(8,128)(2,1)}, u32[]{:S(2)}) %copy-start) | copy-done | bytes 98328
  12.3 0.7 %copy-done.3 = bf16[64,32]{0,1:T(8,128)(2,1)S(1)} copy-done((bf16[64,32]{0,1:T(8,128)(2,1)S(1)}, bf16[64,32]{0,1:T(8,128)(2,1)}, u32[]{:S(2)}) %copy-start.3) | copy-done | bytes 4120
  13.0 0.7 %copy-done.4 = bf16[64,32]{0,1:T(8,128)(2,1)S(1)} copy-done((bf16[64,32]{0,1:T(8,128)(2,1)S(1)}, bf16[64,32]{0,1:T(8,128)(2,1)}, u32[]{:S(2)}) %copy-start.4) | copy-done | bytes 4120
  13.7 0.7 %copy-done.5 = f32[128]{0:T(128)S(1)} copy-done((f32[128]{0:T(128)S(1)}, f32[128]{0:T(128)}, u32[]{:S(2)}) %copy-start.5) | copy-done | bytes 536
  14.3 0.2 setup.1
  14.5 0.4 %collective-permute-start.4 = (bf16[384,128]{1,0:T(8,128)(2,1)S(1)}, bf16[384,128]{1,0:T(8,128)(2,1)S(1)}, u32[]{:S(2)}, u32[]{:S(2)}) collective-permute-start(bf16[384,128]{1,0:T(8,128)(2,1)S(1)} %get-tuple-element.29.refs_1_), channel_id=1, source_target_pairs={{0,2},{2,0},{1,3},{3,1},{4,6},{6,4},{5,7},{7,5},{8,10},{10,8},{9,1... | collective-permute-start | bytes 294920 | tf_op jit(solution)/shard_map/ppermute | solution.py:612
  14.9 1.6 %collective-permute-done.1.refs_2_ = bf16[384,128]{1,0:T(8,128)(2,1)S(1)} collective-permute-done((bf16[384,128]{1,0:T(8,128)(2,1)}, bf16[384,128]{1,0:T(8,128)(2,1)S(1)}, u32[]{:S(2)}, u32[]{:S(2)}) %collective-permute-start.1) | collective-permute-done | bytes 98336 | tf_op jit(solution)/shard_map/ppermute | solution.py:612
  16.5 1.5 %collective-permute-start.5 = (bf16[384,128]{1,0:T(8,128)(2,1)S(1)}, bf16[384,128]{1,0:T(8,128)(2,1)S(1)}, u32[]{:S(2)}, u32[]{:S(2)}) collective-permute-start(bf16[384,128]{1,0:T(8,128)(2,1)S(1)} %collective-permute-done.1.refs_2_), channel_id=1, source_target_pairs={{0,2},{2,0},{1,3},{3,1},{4,6},{6,4},{5,7},{7,5},{8,10},{10,8},{9,1... | collective-permute-start | bytes 294920 | tf_op jit(solution)/shard_map/ppermute | solution.py:612
  18.0 0.6 %collective-permute-start.6 = (bf16[384,128]{1,0:T(8,128)(2,1)S(1)}, bf16[384,128]{1,0:T(8,128)(2,1)S(1)}, u32[]{:S(2)}, u32[]{:S(2)}) collective-permute-start(bf16[384,128]{1,0:T(8,128)(2,1)S(1)} %collective-permute-done.2.refs_3_), channel_id=1, source_target_pairs={{0,2},{2,0},{1,3},{3,1},{4,6},{6,4},{5,7},{7,5},{8,10},{10,8},{9,1... | collective-permute-start | bytes 294920 | tf_op jit(solution)/shard_map/ppermute | solution.py:612
  18.7 1.5 %collective-permute-done.4.refs_5_ = bf16[384,128]{1,0:T(8,128)(2,1)S(1)} collective-permute-done((bf16[384,128]{1,0:T(8,128)(2,1)S(1)}, bf16[384,128]{1,0:T(8,128)(2,1)S(1)}, u32[]{:S(2)}, u32[]{:S(2)}) %collective-permute-start.4) | collective-permute-done | bytes 98336 | tf_op jit(solution)/shard_map/ppermute | solution.py:612
  20.2 1.0 %collective-permute-done.5.refs_6_ = bf16[384,128]{1,0:T(8,128)(2,1)S(1)} collective-permute-done((bf16[384,128]{1,0:T(8,128)(2,1)S(1)}, bf16[384,128]{1,0:T(8,128)(2,1)S(1)}, u32[]{:S(2)}, u32[]{:S(2)}) %collective-permute-start.5) | collective-permute-done | bytes 98336 | tf_op jit(solution)/shard_map/ppermute | solution.py:612
  21.3 1.5 %collective-permute-done.6.refs_7_ = bf16[384,128]{1,0:T(8,128)(2,1)S(1)} collective-permute-done((bf16[384,128]{1,0:T(8,128)(2,1)S(1)}, bf16[384,128]{1,0:T(8,128)(2,1)S(1)}, u32[]{:S(2)}, u32[]{:S(2)}) %collective-permute-start.6) | collective-permute-done | bytes 98336 | tf_op jit(solution)/shard_map/ppermute | solution.py:612
  22.8 2.3 %pull_back.1 = (bf16[4,2,256,128]{3,2,1,0:T(8,128)(2,1)S(1)}, bf16[4,256,2048]{2,1,0:T(8,128)(2,1)S(1)}) custom-call(s32[3]{0:T(128)S(1)} %pad_add_fusion.place_ref, bf16[128,1024]{1,0:T(8,128)(2,1)S(1)} %bitcast.50, bf16[384,128]{1,0:T(8,128)(2,1)S(1)} %get-tuple-element.28.refs_0_, bf16[384,128]{1,0:T(8,128)(2,1)S(1)} %get-tuple-element.29.refs_1_, ...), custom_call_target="tpu_custom_call" | custom-call | flops 536870912 | bytes 5242880 | tf_op jit(solution)/shard_map/pull_back/pallas_call | solution.py:651
  25.1 4.0 %outer_products.1 = (bf16[1024,256]{1,0:T(8,128)(2,1)S(1)}, bf16[16,64,512]{2,1,0:T(8,128)(2,1)S(1)}, bf16[256,256]{1,0:T(8,128)(2,1)S(1)}, bf16[4,512,1024]{2,1,0:T(8,128)(2,1)S(1)}, bf16[16,16,128]{2,1,0:T(8,128)(2,1)}) custom-call(s32[3]{0:T(128)S(1)} %pad_add_fusion.place_ref, bf16[8,128,128]{2,1,0:T(8,128)(2,1)S(1)} %fusion.mine_from_ref, ...), custom_call_target="tpu_custom_call" | custom-call | flops 1073741824 | bytes 4194304 | tf_op jit(solution)/shard_map/outer_products/pallas_call | solution.py:668
  29.1 5.2 %pull_further.1 = (bf16[2,64,128]{2,1,0:T(8,128)(2,1)S(1)}, bf16[1152,128]{1,0:T(8,128)(2,1)S(1)}) custom-call(s32[3]{0:T(128)S(1)} %pad_add_fusion.place_ref, bf16[1024,256]{1,0:T(8,128)(2,1)S(1)} %get-tuple-element.34.rows_ref, bf16[16,64,512]{2,1,0:T(8,128)(2,1)S(1)} %get-tuple-element.35.expanded, bf16[256,256]{1,0:T(8,128)(2,1)S(1)} %get-tuple-element.36.swapped, ...), custom_call_target="tpu_custom_call" | custom-call | tf_op jit(solution)/shard_map/pull_further/pallas_call | solution.py:692
  34.3 0.6 %collective-permute-start.8 = (bf16[1152,128]{1,0:T(8,128)(2,1)S(1)}, bf16[1152,128]{1,0:T(8,128)(2,1)S(1)}, u32[]{:S(2)}, u32[]{:S(2)}) collective-permute-start(bf16[1152,128]{1,0:T(8,128)(2,1)S(1)} %get-tuple-element.41.own_ref), channel_id=1, source_target_pairs={{0,1},{1,0},{2,3},{3,2},{4,5},{5,4},{6,7},{7,6},{8,9},{9,8},{10,11... | collective-permute-start | bytes 884744 | tf_op jit(solution)/shard_map/ppermute | solution.py:710
  34.9 1.2 %collective-permute-done.8.message_ref = bf16[1152,128]{1,0:T(8,128)(2,1)S(1)} collective-permute-done((bf16[1152,128]{1,0:T(8,128)(2,1)S(1)}, bf16[1152,128]{1,0:T(8,128)(2,1)S(1)}, u32[]{:S(2)}, u32[]{:S(2)}) %collective-permute-start.8) | collective-permute-done | bytes 294944 | tf_op jit(solution)/shard_map/ppermute | solution.py:710
  36.1 1.5 %close.1 = (f32[1024,128]{1,0:T(8,128)}, f32[32,64]{1,0:T(8,128)}, f32[32,64]{1,0:T(8,128)}, bf16[64,4,64]{2,1,0:T(4,128)(2,1)}) custom-call(bf16[2,64,128]{2,1,0:T(8,128)(2,1)S(1)} %get-tuple-element.40.grads_ref, bf16[1152,128]{1,0:T(8,128)(2,1)S(1)} %get-tuple-element.41.own_ref, bf16[1152,128]{1,0:T(8,128)(2,1)S(1)} %collective-permute-done.8.message_ref, ...), custom_call_target="tpu_custom_call" | custom-call | tf_op jit(solution)/shard_map/close/pallas_call | solution.py:711
  (23 shorter events, 0.2 us)
Async XLA Ops:
  2.8 8.6 %collective-permute-start = (bf16[384,128]{1,0:T(8,128)(2,1)}, bf16[384,128]{1,0:T(8,128)(2,1)S(1)}, u32[]{:S(2)}, u32[]{:S(2)}) collective-permute-start(bf16[384,128]{1,0:T(8,128)(2,1)} %get-tuple-element.27.own_ref), channel_id=1, source_target_pairs={{0,4},{4,0},{8,12},{12,8},{1,5},{5,1},{9,13},{13,9},{2,6},{6,2},{1... | collective-permute-start | bytes 294920 | tf_op jit(solution)/shard_map/ppermute | solution.py:612
  5.9 10.6 %collective-permute-start.1 = (bf16[384,128]{1,0:T(8,128)(2,1)}, bf16[384,128]{1,0:T(8,128)(2,1)S(1)}, u32[]{:S(2)}, u32[]{:S(2)}) collective-permute-start(bf16[384,128]{1,0:T(8,128)(2,1)} %get-tuple-element.27.own_ref), channel_id=1, source_target_pairs={{0,8},{4,12},{8,0},{12,4},{1,9},{5,13},{9,1},{13,5},{2,10},{6,14},... | collective-permute-start | bytes 294920 | tf_op jit(solution)/shard_map/ppermute | solution.py:612
  8.5 9.6 %collective-permute-start.2 = (bf16[384,128]{1,0:T(8,128)(2,1)}, bf16[384,128]{1,0:T(8,128)(2,1)S(1)}, u32[]{:S(2)}, u32[]{:S(2)}) collective-permute-start(bf16[384,128]{1,0:T(8,128)(2,1)} %get-tuple-element.27.own_ref), channel_id=1, source_target_pairs={{0,12},{4,8},{8,4},{12,0},{1,13},{5,9},{9,5},{13,1},{2,14},{6,10},... | collective-permute-start | bytes 294920 | tf_op jit(solution)/shard_map/ppermute | solution.py:612
  8.5 10.2 %collective-permute-start.3 = (bf16[384,128]{1,0:T(8,128)(2,1)}, bf16[384,128]{1,0:T(8,128)(2,1)S(1)}, u32[]{:S(2)}, u32[]{:S(2)}) collective-permute-start(bf16[384,128]{1,0:T(8,128)(2,1)} %get-tuple-element.27.own_ref), channel_id=1, source_target_pairs={{0,2},{2,0},{1,3},{3,1},{4,6},{6,4},{5,7},{7,5},{8,10},{10,8},{9,1... | collective-permute-start | bytes 294920 | tf_op jit(solution)/shard_map/ppermute | solution.py:612
  11.4 0.9 %copy-start = (bf16[384,128]{1,0:T(8,128)(2,1)S(1)}, bf16[384,128]{1,0:T(8,128)(2,1)}, u32[]{:S(2)}) copy-start(bf16[384,128]{1,0:T(8,128)(2,1)} %get-tuple-element.27.own_ref) | copy-start | bytes 294916
  12.3 0.7 %copy-start.3 = (bf16[64,32]{0,1:T(8,128)(2,1)S(1)}, bf16[64,32]{0,1:T(8,128)(2,1)}, u32[]{:S(2)}) copy-start(bf16[64,32]{0,1:T(8,128)(2,1)} %param.9) | copy-start | bytes 12292
  13.0 0.7 %copy-start.4 = (bf16[64,32]{0,1:T(8,128)(2,1)S(1)}, bf16[64,32]{0,1:T(8,128)(2,1)}, u32[]{:S(2)}) copy-start(bf16[64,32]{0,1:T(8,128)(2,1)} %param.10) | copy-start | bytes 12292
  13.7 0.7 %copy-start.5 = (f32[128]{0:T(128)S(1)}, f32[128]{0:T(128)}, u32[]{:S(2)}) copy-start(f32[128]{0:T(128)} %param.12) | copy-start | bytes 1540
  14.5 5.6 %collective-permute-start.4 = (bf16[384,128]{1,0:T(8,128)(2,1)S(1)}, bf16[384,128]{1,0:T(8,128)(2,1)S(1)}, u32[]{:S(2)}, u32[]{:S(2)}) collective-permute-start(bf16[384,128]{1,0:T(8,128)(2,1)S(1)} %get-tuple-element.29.refs_1_), channel_id=1, source_target_pairs={{0,2},{2,0},{1,3},{3,1},{4,6},{6,4},{5,7},{7,5},{8,10},{10,8},{9,1... | collective-permute-start | bytes 294920 | tf_op jit(solution)/shard_map/ppermute | solution.py:612
  16.5 4.7 %collective-permute-start.5 = (bf16[384,128]{1,0:T(8,128)(2,1)S(1)}, bf16[384,128]{1,0:T(8,128)(2,1)S(1)}, u32[]{:S(2)}, u32[]{:S(2)}) collective-permute-start(bf16[384,128]{1,0:T(8,128)(2,1)S(1)} %collective-permute-done.1.refs_2_), channel_id=1, source_target_pairs={{0,2},{2,0},{1,3},{3,1},{4,6},{6,4},{5,7},{7,5},{8,10},{10,8},{9,1... | collective-permute-start | bytes 294920 | tf_op jit(solution)/shard_map/ppermute | solution.py:612
  18.0 4.7 %collective-permute-start.6 = (bf16[384,128]{1,0:T(8,128)(2,1)S(1)}, bf16[384,128]{1,0:T(8,128)(2,1)S(1)}, u32[]{:S(2)}, u32[]{:S(2)}) collective-permute-start(bf16[384,128]{1,0:T(8,128)(2,1)S(1)} %collective-permute-done.2.refs_3_), channel_id=1, source_target_pairs={{0,2},{2,0},{1,3},{3,1},{4,6},{6,4},{5,7},{7,5},{8,10},{10,8},{9,1... | collective-permute-start | bytes 294920 | tf_op jit(solution)/shard_map/ppermute | solution.py:612
  22.7 2.4 %collective-permute-start.7 = (bf16[8,128,128]{2,1,0:T(8,128)(2,1)S(1)}, bf16[8,128,128]{2,1,0:T(8,128)(2,1)S(1)}, u32[]{:S(2)}, u32[]{:S(2)}) collective-permute-start(bf16[8,128,128]{2,1,0:T(8,128)(2,1)S(1)} %fusion.mine_from_ref), channel_id=1, source_target_pairs={{0,1},{1,0},{2,3},{3,2},{4,5},{5,4},{6,7},{7,6},{8,9},{9,8},{10,11... | collective-permute-start | bytes 786440 | tf_op jit(solution)/shard_map/ppermute | solution.py:646
  29.1 7.0 %copy-start.1 = (f32[64,256]{1,0:T(8,128)S(1)}, f32[64,256]{1,0:T(8,128)}, u32[]{:S(2)}) copy-start(f32[64,256]{1,0:T(8,128)} %get-tuple-element.42.normed_ref) | copy-start | bytes 196612
  29.1 7.0 %copy-start.2 = (f32[64,256]{1,0:T(8,128)S(1)}, f32[64,256]{1,0:T(8,128)}, u32[]{:S(2)}) copy-start(f32[64,256]{1,0:T(8,128)} %get-tuple-element.43.inverse_ref) | copy-start | bytes 196612
  34.3 1.8 %collective-permute-start.8 = (bf16[1152,128]{1,0:T(8,128)(2,1)S(1)}, bf16[1152,128]{1,0:T(8,128)(2,1)S(1)}, u32[]{:S(2)}, u32[]{:S(2)}) collective-permute-start(bf16[1152,128]{1,0:T(8,128)(2,1)S(1)} %get-tuple-element.41.own_ref), channel_id=1, source_target_pairs={{0,1},{1,0},{2,3},{3,2},{4,5},{5,4},{6,7},{7,6},{8,9},{9,8},{10,11... | collective-permute-start | bytes 884744 | tf_op jit(solution)/shard_map/ppermute | solution.py:710

commit v11 on v10

--- a/solution.py
+++ b/solution.py
@@ -295,28 +295,53 @@
         out_ref[place_ref[0] ^ down, place_ref[1] ^ across] = block
 
 
-def pull_kernel(offsets, place_ref, mapping_ref, *refs):
-    *message_refs, cot_ref, pulled_ref = refs
-    prow_n, groups, pairs, pair_width = cot_ref.shape
+def pull_blocks(cot_of, mapping_ref, pulled_ref, rows, at):
+    block_rows = pulled_ref.shape[2] // LANES
     highs = mapping_ref.shape[1] // LANES
-    block_rows = pulled_ref.shape[2] // LANES
-    block_cols = pairs // block_rows
-    place_blocks(place_ref, offsets, [ref[:pairs] for ref in message_refs], cot_ref)
 
     def step(r, carry):
-        grad = dot(cot_ref[r].reshape(groups * pairs, pair_width), mapping_ref[...])
-        for g in range(groups):
+        cot = cot_of(r)
+        block_cols = cot.shape[0] // block_rows
+        for h in range(0, highs, 2):
+            grad = dot(cot, mapping_ref[:, h * LANES : (h + 2) * LANES])
             for t in range(block_rows):
-                start = (g * block_rows + t) * block_cols
-                lanes = slice(t * LANES, (t + 1) * LANES)
-                for h in range(highs):
-                    there = slice((g * highs + h) * block_cols, (g * highs + h + 1) * block_cols)
-                    pulled_ref[r, there, lanes] = grad[
-                        start : start + block_cols, h * LANES : (h + 1) * LANES
+                for k in range(2):
+                    pulled_ref[
+                        r,
+                        pl.ds(pl.multiple_of(at + (h + k) * block_cols, block_cols), block_cols),
+                        t * LANES : (t + 1) * LANES,
+                    ] = grad[
+                        t * block_cols : (t + 1) * block_cols, k * LANES : (k + 1) * LANES
                     ].astype(BF16)
         return carry
 
-    lax.fori_loop(0, prow_n, step, 0)
+    lax.fori_loop(0, rows, step, 0)
+
+
+def pull_own_kernel(downs, place_ref, mapping_ref, *refs):
+    *message_refs, pulled_ref, rows_ref, cot_ref = refs
+    rows, pairs = cot_ref.shape[:2]
+    for n, (down, ref) in enumerate(zip(downs, message_refs, strict=True)):
+        cot_ref[place_ref[0] ^ down] = ref[:pairs]
+        rows_ref[n] = ref[pairs:]
+    pull_blocks(lambda r: cot_ref[r], mapping_ref, pulled_ref, rows, 0)
+
+
+def pull_kernel(offsets, place_ref, mapping_ref, own_ref, *refs):
+    *message_refs, cot_ref, pulled_ref = refs
+    rows, groups, pairs, _ = cot_ref.shape
+    place_blocks(place_ref, offsets, [ref[:pairs] for ref in message_refs], cot_ref)
+    share = own_ref.shape[1]
+    for across in range(1, groups):
+        group = place_ref[1] ^ across
+        pull_blocks(lambda r: cot_ref[r, group], mapping_ref, pulled_ref, rows, group * share)
+
+    def keep(r, carry):
+        at = pl.multiple_of(place_ref[1] * share, share)
+        pulled_ref[r, pl.ds(at, share)] = own_ref[r]
+        return carry
+
+    lax.fori_loop(0, rows, keep, 0)
 
 
 def outer_kernel(
@@ -379,11 +404,13 @@
     turned[...] = swapped[...].astype(F32).T.astype(BF16)
 
     def step(row, carry):
-        made = dot(turned[...], left_block(expanded, row, owners // prow_n, tokens))
-        for g in range(groups):
-            for t in range(block_rows):
+        block = left_block(expanded, row, owners // prow_n, tokens)
+        for t in range(block_rows):
+            if t % 2 == 0:
+                made = dot(turned[...], block[:, t * LANES : (t + 2) * LANES])
+            lanes = slice(t % 2 * LANES, (t % 2 + 1) * LANES)
+            for g in range(groups):
                 start = (g * block_rows + t) * block_cols
-                lanes = slice(t * LANES, (t + 1) * LANES)
                 for h in range(highs):
                     there = slice((g * highs + h) * block_cols, (g * highs + h + 1) * block_cols)
                     outer_ref[row, start : start + block_cols, h * LANES : (h + 1) * LANES] = made[
@@ -453,24 +480,24 @@
     def step(row, carry):
         block = left_block(expanded, row, step_owners, tokens)
         cot = cot_ref[row].reshape(groups * pairs, pair_width)
-        weights[...] += dot(cot, outer_ref[row], contract=(0, 0))
-        pulled = pulled_ref[row]
-        back = dot(swapped[...], pulled)
-        low = lane_ids((seqs, back.shape[1])) % LANES // proj
-        back = functools.reduce(
-            jnp.add,
-            [
-                jnp.where(low == l, back[l * seqs : (l + 1) * seqs], 0.0)
-                for l in range(tokens)
-            ],
-        )
+        turned_cot = cot.astype(F32).T.astype(BF16)
+        for at in range(0, weights.shape[1], 2 * LANES):
+            chunk = slice(at, at + 2 * LANES)
+            weights[:, chunk] += dot(turned_cot, outer_ref[row, :, chunk])
         for o in range(step_owners):
-            parts = [
-                back[:, (o * tokens + t) * LANES : (o * tokens + t + 1) * LANES]
-                for t in range(tokens)
-            ]
+            chunk = slice(o * tokens * LANES, (o + 1) * tokens * LANES)
+            back = dot(swapped[...], pulled_ref[row, :, chunk])
+            low = lane_ids((seqs, back.shape[1])) % LANES // proj
+            back = functools.reduce(
+                jnp.add,
+                [
+                    jnp.where(low == l, back[l * seqs : (l + 1) * seqs], 0.0)
+                    for l in range(tokens)
+                ],
+            )
+            parts = [back[:, t * LANES : (t + 1) * LANES] for t in range(tokens)]
             left_back[row * step_owners + o] = fold_tokens(parts).astype(BF16)
-        sums[...] += dot(pulled, block, contract=(1, 1))
+        sums[...] += dot(pulled_ref[row], block, contract=(1, 1))
         return carry
 
     lax.fori_loop(0, prow_n, step, 0)
@@ -642,28 +669,43 @@
     ]
     messages[0] = own
     offsets = [(down, across) for across in range(groups) for down in range(prow_n)]
-    rows = jnp.stack([one[pairs:] for one in messages])
+    place = jnp.stack([lax.axis_index("prow"), lax.axis_index("px"), lax.axis_index("pc")])
+
+    columns = groups * proj // tokens * block_cols
+    pull_cost = pl.CostEstimate(
+        flops=prow_n * groups * pairs * pair_width * flat,
+        bytes_accessed=prow_n * groups * pairs * (2 * pair_width + flat),
+        transcendentals=0,
+    )
+    pulled_own, rows_own = pl.pallas_call(
+        functools.partial(pull_own_kernel, [down for down, _ in offsets[:prow_n]]),
+        out_shape=(
+            shape((prow_n, columns // groups, block_rows * LANES), BF16),
+            shape((prow_n, length, LANES), BF16),
+        ),
+        in_specs=[smem] + [vmem] * (1 + prow_n),
+        out_specs=(vmem,) * 2,
+        scratch_shapes=[pltpu.VMEM((prow_n, pairs, pair_width), BF16)],
+        compiler_params=params,
+        cost_estimate=pull_cost,
+        name="pull_own",
+    )(place, turned_mapping, *messages[:prow_n])
+    rows = jnp.concatenate(
+        [rows_own] + [one[None, pairs:] for one in messages[prow_n:]], axis=0
+    )
     theirs = lax.ppermute(rows, "pc", [(0, 1), (1, 0)])
-
-    place = jnp.stack([lax.axis_index("prow"), lax.axis_index("px"), lax.axis_index("pc")])
-
-    columns = groups * proj // tokens * block_cols
     cot, pulled = pl.pallas_call(
         functools.partial(pull_kernel, offsets),
         out_shape=(
             shape((prow_n, groups, pairs, pair_width), BF16),
             shape((prow_n, columns, block_rows * LANES), BF16),
         ),
-        in_specs=[smem] + [vmem] * (1 + len(messages)),
+        in_specs=[smem] + [vmem] * (2 + len(messages)),
         out_specs=(vmem,) * 2,
         compiler_params=params,
-        cost_estimate=pl.CostEstimate(
-            flops=2 * prow_n * groups * pairs * pair_width * flat,
-            bytes_accessed=2 * prow_n * groups * pairs * (2 * pair_width + flat),
-            transcendentals=0,
-        ),
+        cost_estimate=pull_cost,
         name="pull_back",
-    )(place, turned_mapping, *messages)
+    )(place, turned_mapping, pulled_own, *messages)
 
     rows_all, expanded, swapped, outer, pair_delta = pl.pallas_call(
         functools.partial(outer_kernel, offsets),

time: 37.9 us -> 41.6 us (1.098)
  waiting for transfers between devices: 6.84 us -> 8.77 us
  Pallas kernels: 15.3 us -> 16.9 us
    ppermute x7, waiting for transfers between devices: 5.63 us -> 7.56 us  [swapped_with(): return lax.ppermute(values, axis, [(n, n ^ mask) for n in range(size)])]
    pallas_call x0 -> x1, Pallas kernels: none -> 1.7 us  [local_gathered(): pl.pallas_call(functools.partial(pull_own_kernel, [down for down, _ in of...]
    unnamed x19 -> x16, local copies, waits for them, and re-layouts: 3 us -> 2.99 us
  transfers between devices with their start and end apart: 9 -> 9, of which waited for: 5 -> 4; matrix products, arithmetic and copies ran while one was open for 4% -> 3% of each run, Pallas kernels for 7% -> 9%
where the time goes in v11:
time: 41.6 us; the launch traced here: 41.3 us
  Pallas kernels  16.9 us (41%)
  starting transfers between devices  10.6 us (25%)
  waiting for transfers between devices  8.77 us (21%)
  local copies, waits for them, and re-layouts  4.19 us (10%)
  between operations  0.73 us (2%)
    ppermute x7, starting transfers between devices, swapped_with(): return lax.ppermute(values, axis, [(n, n ^ mask) for n in range(size)])  10 us
    ppermute x7, waiting for transfers between devices, swapped_with(): return lax.ppermute(values, axis, [(n, n ^ mask) for n in range(size)])  7.56 us
    pallas_call x1, Pallas kernels, local_gathered(): pl.pallas_call(back_kernel, out_shape=(shape((2, seqs, LANES), BF16), sha...  5.34 us
    pallas_call x1, Pallas kernels, local_gathered(): pl.pallas_call(functools.partial(outer_kernel, offsets), out_shape=(shape...  4.05 us
    unnamed x16, local copies, waits for them, and re-layouts  2.99 us
    pallas_call x1, Pallas kernels, local_gathered(): pl.pallas_call(pick_kernel, out_shape=(shape((seqs, packed), F32), shape(...  2.15 us
    pallas_call x1, Pallas kernels, local_gathered(): pl.pallas_call(functools.partial(pull_kernel, offsets), out_shape=(shape(...  1.96 us
    pallas_call x1, Pallas kernels, local_gathered(): pl.pallas_call(functools.partial(pull_own_kernel, [down for down, _ in of...  1.7 us
  transfers between devices with their start and end apart: 9, of which 4 were waited for; matrix products, arithmetic and copies ran while one was open for 3% of the time, Pallas kernels for 9%

profile of v11, /device:TPU:0, one launch (start us, length us, event | category | flops | bytes accessed | tf_op | source)
XLA Modules:
  0.0 41.3 jit_solution(14250087756335967355)
XLA Ops:
  0.6 2.1 %pick_rows.1 = (f32[64,256]{1,0:T(8,128)}, f32[64,256]{1,0:T(8,128)}, bf16[384,128]{1,0:T(8,128)(2,1)}) custom-call(s32[1,64]{1,0:T(1,128)} %bitcast.46, bf16[256,128]{1,0:T(8,128)(2,1)} %bitcast.44, bf16[256,128]{1,0:T(8,128)(2,1)} %bitcast.45), custom_call_target="tpu_custom_call" | custom-call | tf_op jit(solution)/shard_map/pick_rows/pallas_call | solution.py:612
  2.8 3.0 %collective-permute-start.3 = (bf16[384,128]{1,0:T(8,128)(2,1)}, bf16[384,128]{1,0:T(8,128)(2,1)S(1)}, u32[]{:S(2)}, u32[]{:S(2)}) collective-permute-start(bf16[384,128]{1,0:T(8,128)(2,1)} %get-tuple-element.29.own_ref), channel_id=1, source_target_pairs={{0,2},{2,0},{1,3},{3,1},{4,6},{6,4},{5,7},{7,5},{8,10},{10,8},{9,1... | collective-permute-start | bytes 294920 | tf_op jit(solution)/shard_map/ppermute | solution.py:639
  5.8 3.6 %collective-permute-start.2 = (bf16[384,128]{1,0:T(8,128)(2,1)}, bf16[384,128]{1,0:T(8,128)(2,1)S(1)}, u32[]{:S(2)}, u32[]{:S(2)}) collective-permute-start(bf16[384,128]{1,0:T(8,128)(2,1)} %get-tuple-element.29.own_ref), channel_id=1, source_target_pairs={{0,12},{4,8},{8,4},{12,0},{1,13},{5,9},{9,5},{13,1},{2,14},{6,10},... | collective-permute-start | bytes 294920 | tf_op jit(solution)/shard_map/ppermute | solution.py:639
  9.4 0.8 %collective-permute-start = (bf16[384,128]{1,0:T(8,128)(2,1)}, bf16[384,128]{1,0:T(8,128)(2,1)S(1)}, u32[]{:S(2)}, u32[]{:S(2)}) collective-permute-start(bf16[384,128]{1,0:T(8,128)(2,1)} %get-tuple-element.29.own_ref), channel_id=1, source_target_pairs={{0,4},{4,0},{8,12},{12,8},{1,5},{5,1},{9,13},{13,9},{2,6},{6,2},{1... | collective-permute-start | bytes 294920 | tf_op jit(solution)/shard_map/ppermute | solution.py:639
  10.2 1.1 %copy.16 = bf16[32,32,128]{2,1,0:T(8,128)(2,1)S(1)} copy(bf16[32,32,128]{2,0,1:T(8,128)(2,1)} %bitcast.43) | data formatting | bytes 524288 | tf_op jit(solution)/shard_map/transpose | solution.py:635
  11.2 0.1 copy.17
  11.5 4.3 %collective-permute-done.first_ref = bf16[384,128]{1,0:T(8,128)(2,1)S(1)} collective-permute-done((bf16[384,128]{1,0:T(8,128)(2,1)}, bf16[384,128]{1,0:T(8,128)(2,1)S(1)}, u32[]{:S(2)}, u32[]{:S(2)}) %collective-permute-start) | collective-permute-done | bytes 98336 | tf_op jit(solution)/shard_map/ppermute | solution.py:639
  15.7 0.9 %copy-done = bf16[384,128]{1,0:T(8,128)(2,1)S(1)} copy-done((bf16[384,128]{1,0:T(8,128)(2,1)S(1)}, bf16[384,128]{1,0:T(8,128)(2,1)}, u32[]{:S(2)}) %copy-start) | copy-done | bytes 98328
  16.6 0.7 %copy-done.3 = bf16[64,32]{0,1:T(8,128)(2,1)S(1)} copy-done((bf16[64,32]{0,1:T(8,128)(2,1)S(1)}, bf16[64,32]{0,1:T(8,128)(2,1)}, u32[]{:S(2)}) %copy-start.3) | copy-done | bytes 4120
  17.3 0.7 %copy-done.4 = bf16[64,32]{0,1:T(8,128)(2,1)S(1)} copy-done((bf16[64,32]{0,1:T(8,128)(2,1)S(1)}, bf16[64,32]{0,1:T(8,128)(2,1)}, u32[]{:S(2)}) %copy-start.4) | copy-done | bytes 4120
  18.0 0.7 %copy-done.5 = f32[128]{0:T(128)S(1)} copy-done((f32[128]{0:T(128)S(1)}, f32[128]{0:T(128)}, u32[]{:S(2)}) %copy-start.5) | copy-done | bytes 536
  18.7 0.2 setup.1
  18.9 0.6 %collective-permute-start.4 = (bf16[384,128]{1,0:T(8,128)(2,1)S(1)}, bf16[384,128]{1,0:T(8,128)(2,1)S(1)}, u32[]{:S(2)}, u32[]{:S(2)}) collective-permute-start(bf16[384,128]{1,0:T(8,128)(2,1)S(1)} %get-tuple-element.31.refs_1_), channel_id=1, source_target_pairs={{0,2},{2,0},{1,3},{3,1},{4,6},{6,4},{5,7},{7,5},{8,10},{10,8},{9,1... | collective-permute-start | bytes 294920 | tf_op jit(solution)/shard_map/ppermute | solution.py:639
  19.5 1.5 %collective-permute-start.6 = (bf16[384,128]{1,0:T(8,128)(2,1)S(1)}, bf16[384,128]{1,0:T(8,128)(2,1)S(1)}, u32[]{:S(2)}, u32[]{:S(2)}) collective-permute-start(bf16[384,128]{1,0:T(8,128)(2,1)S(1)} %collective-permute-done.2.refs_3_), channel_id=1, source_target_pairs={{0,2},{2,0},{1,3},{3,1},{4,6},{6,4},{5,7},{7,5},{8,10},{10,8},{9,1... | collective-permute-start | bytes 294920 | tf_op jit(solution)/shard_map/ppermute | solution.py:639
  21.0 0.5 %collective-permute-start.5 = (bf16[384,128]{1,0:T(8,128)(2,1)S(1)}, bf16[384,128]{1,0:T(8,128)(2,1)S(1)}, u32[]{:S(2)}, u32[]{:S(2)}) collective-permute-start(bf16[384,128]{1,0:T(8,128)(2,1)S(1)} %collective-permute-done.1.refs_2_), channel_id=1, source_target_pairs={{0,2},{2,0},{1,3},{3,1},{4,6},{6,4},{5,7},{7,5},{8,10},{10,8},{9,1... | collective-permute-start | bytes 294920 | tf_op jit(solution)/shard_map/ppermute | solution.py:639
  21.5 1.7 %pull_own.1 = (bf16[4,128,2048]{2,1,0:T(8,128)(2,1)S(1)}, bf16[4,128,128]{2,1,0:T(8,128)(2,1)S(1)}) custom-call(s32[3]{0:T(128)S(1)} %pad_add_fusion.place_ref, bf16[128,1024]{1,0:T(8,128)(2,1)S(1)} %bitcast.38, bf16[384,128]{1,0:T(8,128)(2,1)S(1)} %get-tuple-element.30.refs_0_, bf16[384,128]{1,0:T(8,128)(2,1)S(1)} %get-tuple-element.31.refs_1_, ...), custom_call_target="tpu_custom_call" | custom-call | flops 268435456 | bytes 2621440 | tf_op jit(solution)/shard_map/pull_own/pallas_call | solution.py:680
  23.3 1.2 %collective-permute-done.4.refs_5_ = bf16[384,128]{1,0:T(8,128)(2,1)S(1)} collective-permute-done((bf16[384,128]{1,0:T(8,128)(2,1)S(1)}, bf16[384,128]{1,0:T(8,128)(2,1)S(1)}, u32[]{:S(2)}, u32[]{:S(2)}) %collective-permute-start.4) | collective-permute-done | bytes 98336 | tf_op jit(solution)/shard_map/ppermute | solution.py:639
  24.5 2.1 %collective-permute-done.5.refs_6_ = bf16[384,128]{1,0:T(8,128)(2,1)S(1)} collective-permute-done((bf16[384,128]{1,0:T(8,128)(2,1)S(1)}, bf16[384,128]{1,0:T(8,128)(2,1)S(1)}, u32[]{:S(2)}, u32[]{:S(2)}) %collective-permute-start.5) | collective-permute-done | bytes 98336 | tf_op jit(solution)/shard_map/ppermute | solution.py:639
  26.7 2.0 %pull_back.1 = (bf16[4,2,256,128]{3,2,1,0:T(8,128)(2,1)S(1)}, bf16[4,256,2048]{2,1,0:T(8,128)(2,1)S(1)}) custom-call(s32[3]{0:T(128)S(1)} %pad_add_fusion.place_ref, bf16[128,1024]{1,0:T(8,128)(2,1)S(1)} %bitcast.39, bf16[4,128,2048]{2,1,0:T(8,128)(2,1)S(1)} %get-tuple-element.41.own_ref, bf16[384,128]{1,0:T(8,128)(2,1)S(1)} %get-tuple-element.30.refs_0_, ...), custom_call_target="tpu_custom_call" | custom-call | flops 268435456 | bytes 2621440 | tf_op jit(solution)/shard_map/pull_back/pallas_call | solution.py:697
  28.6 4.1 %outer_products.1 = (bf16[1024,256]{1,0:T(8,128)(2,1)S(1)}, bf16[16,64,512]{2,1,0:T(8,128)(2,1)S(1)}, bf16[256,256]{1,0:T(8,128)(2,1)S(1)}, bf16[4,512,1024]{2,1,0:T(8,128)(2,1)S(1)}, bf16[16,16,128]{2,1,0:T(8,128)(2,1)}) custom-call(s32[3]{0:T(128)S(1)} %pad_add_fusion.place_ref, bf16[8,128,128]{2,1,0:T(8,128)(2,1)S(1)} %fusion.mine_from_ref, ...), custom_call_target="tpu_custom_call" | custom-call | flops 1073741824 | bytes 4194304 | tf_op jit(solution)/shard_map/outer_products/pallas_call | solution.py:710
  32.7 5.3 %pull_further.1 = (bf16[2,64,128]{2,1,0:T(8,128)(2,1)S(1)}, bf16[1152,128]{1,0:T(8,128)(2,1)S(1)}) custom-call(s32[3]{0:T(128)S(1)} %pad_add_fusion.place_ref, bf16[1024,256]{1,0:T(8,128)(2,1)S(1)} %get-tuple-element.37.rows_ref, bf16[16,64,512]{2,1,0:T(8,128)(2,1)S(1)} %get-tuple-element.38.expanded, bf16[256,256]{1,0:T(8,128)(2,1)S(1)} %get-tuple-element.39.swapped, ...), custom_call_target="tpu_custom_call" | custom-call | tf_op jit(solution)/shard_map/pull_further/pallas_call | solution.py:734
  38.0 0.6 %collective-permute-start.8 = (bf16[1152,128]{1,0:T(8,128)(2,1)S(1)}, bf16[1152,128]{1,0:T(8,128)(2,1)S(1)}, u32[]{:S(2)}, u32[]{:S(2)}) collective-permute-start(bf16[1152,128]{1,0:T(8,128)(2,1)S(1)} %get-tuple-element.45.own_ref), channel_id=1, source_target_pairs={{0,1},{1,0},{2,3},{3,2},{4,5},{5,4},{6,7},{7,6},{8,9},{9,8},{10,11... | collective-permute-start | bytes 884744 | tf_op jit(solution)/shard_map/ppermute | solution.py:752
  38.6 1.2 %collective-permute-done.8.message_ref = bf16[1152,128]{1,0:T(8,128)(2,1)S(1)} collective-permute-done((bf16[1152,128]{1,0:T(8,128)(2,1)S(1)}, bf16[1152,128]{1,0:T(8,128)(2,1)S(1)}, u32[]{:S(2)}, u32[]{:S(2)}) %collective-permute-start.8) | collective-permute-done | bytes 294944 | tf_op jit(solution)/shard_map/ppermute | solution.py:752
  39.8 1.5 %close.1 = (f32[1024,128]{1,0:T(8,128)}, f32[32,64]{1,0:T(8,128)}, f32[32,64]{1,0:T(8,128)}, bf16[64,4,64]{2,1,0:T(4,128)(2,1)}) custom-call(bf16[2,64,128]{2,1,0:T(8,128)(2,1)S(1)} %get-tuple-element.44.grads_ref, bf16[1152,128]{1,0:T(8,128)(2,1)S(1)} %get-tuple-element.45.own_ref, bf16[1152,128]{1,0:T(8,128)(2,1)S(1)} %collective-permute-done.8.message_ref, ...), custom_call_target="tpu_custom_call" | custom-call | tf_op jit(solution)/shard_map/close/pallas_call | solution.py:753
  (21 shorter events, 0.2 us)
Async XLA Ops:
  2.8 20.5 %collective-permute-start.3 = (bf16[384,128]{1,0:T(8,128)(2,1)}, bf16[384,128]{1,0:T(8,128)(2,1)S(1)}, u32[]{:S(2)}, u32[]{:S(2)}) collective-permute-start(bf16[384,128]{1,0:T(8,128)(2,1)} %get-tuple-element.29.own_ref), channel_id=1, source_target_pairs={{0,2},{2,0},{1,3},{3,1},{4,6},{6,4},{5,7},{7,5},{8,10},{10,8},{9,1... | collective-permute-start | bytes 294920 | tf_op jit(solution)/shard_map/ppermute | solution.py:639
  5.8 13.7 %collective-permute-start.2 = (bf16[384,128]{1,0:T(8,128)(2,1)}, bf16[384,128]{1,0:T(8,128)(2,1)S(1)}, u32[]{:S(2)}, u32[]{:S(2)}) collective-permute-start(bf16[384,128]{1,0:T(8,128)(2,1)} %get-tuple-element.29.own_ref), channel_id=1, source_target_pairs={{0,12},{4,8},{8,4},{12,0},{1,13},{5,9},{9,5},{13,1},{2,14},{6,10},... | collective-permute-start | bytes 294920 | tf_op jit(solution)/shard_map/ppermute | solution.py:639
  9.4 11.6 %collective-permute-start.1 = (bf16[384,128]{1,0:T(8,128)(2,1)}, bf16[384,128]{1,0:T(8,128)(2,1)S(1)}, u32[]{:S(2)}, u32[]{:S(2)}) collective-permute-start(bf16[384,128]{1,0:T(8,128)(2,1)} %get-tuple-element.29.own_ref), channel_id=1, source_target_pairs={{0,8},{4,12},{8,0},{12,4},{1,9},{5,13},{9,1},{13,5},{2,10},{6,14},... | collective-permute-start | bytes 294920 | tf_op jit(solution)/shard_map/ppermute | solution.py:639
  9.4 6.3 %collective-permute-start = (bf16[384,128]{1,0:T(8,128)(2,1)}, bf16[384,128]{1,0:T(8,128)(2,1)S(1)}, u32[]{:S(2)}, u32[]{:S(2)}) collective-permute-start(bf16[384,128]{1,0:T(8,128)(2,1)} %get-tuple-element.29.own_ref), channel_id=1, source_target_pairs={{0,4},{4,0},{8,12},{12,8},{1,5},{5,1},{9,13},{13,9},{2,6},{6,2},{1... | collective-permute-start | bytes 294920 | tf_op jit(solution)/shard_map/ppermute | solution.py:639
  15.7 0.9 %copy-start = (bf16[384,128]{1,0:T(8,128)(2,1)S(1)}, bf16[384,128]{1,0:T(8,128)(2,1)}, u32[]{:S(2)}) copy-start(bf16[384,128]{1,0:T(8,128)(2,1)} %get-tuple-element.29.own_ref) | copy-start | bytes 294916
  16.6 0.7 %copy-start.3 = (bf16[64,32]{0,1:T(8,128)(2,1)S(1)}, bf16[64,32]{0,1:T(8,128)(2,1)}, u32[]{:S(2)}) copy-start(bf16[64,32]{0,1:T(8,128)(2,1)} %param.9) | copy-start | bytes 12292
  17.3 0.7 %copy-start.4 = (bf16[64,32]{0,1:T(8,128)(2,1)S(1)}, bf16[64,32]{0,1:T(8,128)(2,1)}, u32[]{:S(2)}) copy-start(bf16[64,32]{0,1:T(8,128)(2,1)} %param.10) | copy-start | bytes 12292
  18.0 0.7 %copy-start.5 = (f32[128]{0:T(128)S(1)}, f32[128]{0:T(128)}, u32[]{:S(2)}) copy-start(f32[128]{0:T(128)} %param.12) | copy-start | bytes 1540
  18.9 5.6 %collective-permute-start.4 = (bf16[384,128]{1,0:T(8,128)(2,1)S(1)}, bf16[384,128]{1,0:T(8,128)(2,1)S(1)}, u32[]{:S(2)}, u32[]{:S(2)}) collective-permute-start(bf16[384,128]{1,0:T(8,128)(2,1)S(1)} %get-tuple-element.31.refs_1_), channel_id=1, source_target_pairs={{0,2},{2,0},{1,3},{3,1},{4,6},{6,4},{5,7},{7,5},{8,10},{10,8},{9,1... | collective-permute-start | bytes 294920 | tf_op jit(solution)/shard_map/ppermute | solution.py:639
  19.5 7.1 %collective-permute-start.6 = (bf16[384,128]{1,0:T(8,128)(2,1)S(1)}, bf16[384,128]{1,0:T(8,128)(2,1)S(1)}, u32[]{:S(2)}, u32[]{:S(2)}) collective-permute-start(bf16[384,128]{1,0:T(8,128)(2,1)S(1)} %collective-permute-done.2.refs_3_), channel_id=1, source_target_pairs={{0,2},{2,0},{1,3},{3,1},{4,6},{6,4},{5,7},{7,5},{8,10},{10,8},{9,1... | collective-permute-start | bytes 294920 | tf_op jit(solution)/shard_map/ppermute | solution.py:639
  21.0 5.6 %collective-permute-start.5 = (bf16[384,128]{1,0:T(8,128)(2,1)S(1)}, bf16[384,128]{1,0:T(8,128)(2,1)S(1)}, u32[]{:S(2)}, u32[]{:S(2)}) collective-permute-start(bf16[384,128]{1,0:T(8,128)(2,1)S(1)} %collective-permute-done.1.refs_2_), channel_id=1, source_target_pairs={{0,2},{2,0},{1,3},{3,1},{4,6},{6,4},{5,7},{7,5},{8,10},{10,8},{9,1... | collective-permute-start | bytes 294920 | tf_op jit(solution)/shard_map/ppermute | solution.py:639
  26.6 2.1 %collective-permute-start.7 = (bf16[8,128,128]{2,1,0:T(8,128)(2,1)S(1)}, bf16[8,128,128]{2,1,0:T(8,128)(2,1)S(1)}, u32[]{:S(2)}, u32[]{:S(2)}) collective-permute-start(bf16[8,128,128]{2,1,0:T(8,128)(2,1)S(1)} %fusion.mine_from_ref), channel_id=1, source_target_pairs={{0,1},{1,0},{2,3},{3,2},{4,5},{5,4},{6,7},{7,6},{8,9},{9,8},{10,11... | collective-permute-start | bytes 786440 | tf_op jit(solution)/shard_map/ppermute | solution.py:696
  32.7 7.1 %copy-start.1 = (f32[64,256]{1,0:T(8,128)S(1)}, f32[64,256]{1,0:T(8,128)}, u32[]{:S(2)}) copy-start(f32[64,256]{1,0:T(8,128)} %get-tuple-element.46.normed_ref) | copy-start | bytes 196612
  32.7 7.1 %copy-start.2 = (f32[64,256]{1,0:T(8,128)S(1)}, f32[64,256]{1,0:T(8,128)}, u32[]{:S(2)}) copy-start(f32[64,256]{1,0:T(8,128)} %get-tuple-element.47.inverse_ref) | copy-start | bytes 196612
  38.0 1.8 %collective-permute-start.8 = (bf16[1152,128]{1,0:T(8,128)(2,1)S(1)}, bf16[1152,128]{1,0:T(8,128)(2,1)S(1)}, u32[]{:S(2)}, u32[]{:S(2)}) collective-permute-start(bf16[1152,128]{1,0:T(8,128)(2,1)S(1)} %get-tuple-element.45.own_ref), channel_id=1, source_target_pairs={{0,1},{1,0},{2,3},{3,2},{4,5},{5,4},{6,7},{7,6},{8,9},{9,8},{10,11... | collective-permute-start | bytes 884744 | tf_op jit(solution)/shard_map/ppermute | solution.py:752

commit v12 on v10

--- a/solution.py
+++ b/solution.py
@@ -316,7 +316,7 @@
                     ].astype(BF16)
         return carry
 
-    lax.fori_loop(0, prow_n, step, 0)
+    lax.fori_loop(0, prow_n, step, 0, unroll=True)
 
 
 def outer_kernel(
@@ -391,7 +391,7 @@
                     ].astype(BF16)
         return carry
 
-    lax.fori_loop(0, prow_n, step, 0)
+    lax.fori_loop(0, prow_n, step, 0, unroll=True)
     share = block_rows * block_cols
     mine = outer_ref[own_row, pl.ds(pl.multiple_of(own_group * share, share), share)]
     update = dot(mine, mapping_ref[...]) + offset_ref[...]
@@ -473,7 +473,7 @@
         sums[...] += dot(pulled, block, contract=(1, 1))
         return carry
 
-    lax.fori_loop(0, prow_n, step, 0)
+    lax.fori_loop(0, prow_n, step, 0, unroll=True)
 
     back = (sums[...].T * (1.0 / seqs)).astype(BF16)
     back = jnp.concatenate(
@@ -536,10 +536,18 @@
     left_out_ref,
     right_out_ref,
     rows_out_ref,
+    total,
+    out_sems,
 ):
     flat = out_ref.shape[0]
     proj, features = left_out_ref.shape
-    out_ref[...] = own_ref[:flat].astype(F32) + message_ref[:flat].astype(F32)
+    copies = []
+    for n in range(out_sems.shape[0]):
+        share = flat // out_sems.shape[0]
+        here = pl.ds(n * share, share)
+        total[here] = own_ref[here].astype(F32) + message_ref[here].astype(F32)
+        copies.append(pltpu.make_async_copy(total.at[here], out_ref.at[here], out_sems.at[n]))
+        copies[-1].start()
     sides = slice(flat, flat + 2 * proj)
     both = own_ref[sides, :features].astype(F32) + message_ref[sides, :features].astype(F32)
     left_out_ref[...] = both[:proj]
@@ -555,6 +563,8 @@
         [result[:, t * features : (t + 1) * features] for t in range(rows_out_ref.shape[1])],
         axis=1,
     ).astype(BF16)
+    for copy in copies:
+        copy.wait()
 
 
 def local_gathered(
@@ -717,7 +727,11 @@
             shape((seqs, tokens, features), BF16),
         ),
         in_specs=[vmem] * 7,
-        out_specs=(vmem,) * 4,
+        out_specs=(hbm,) + (vmem,) * 3,
+        scratch_shapes=[
+            pltpu.VMEM((flat, pair_width), F32),
+            pltpu.SemaphoreType.DMA((2,)),
+        ],
         compiler_params=params,
         name="close",
     )(grads, message, theirs, normed, inverse, left_one, right_one)

time: 37.9 us -> 37.1 us (0.979)
  Pallas kernels: 15.3 us -> 14.5 us
    pallas_call x1, Pallas kernels: 1.51 us -> 2.13 us  [local_gathered(): pl.pallas_call(close_kernel, out_shape=(shape((flat, pair_width), F32), s...]
    pallas_call x1, Pallas kernels: 4.03 us -> 3.47 us  [local_gathered(): pl.pallas_call(functools.partial(outer_kernel, offsets), out_shape=(shape...]
    pallas_call x1, Pallas kernels: 5.21 us -> 4.73 us  [local_gathered(): pl.pallas_call(back_kernel, out_shape=(shape((2, seqs, LANES), BF16), sha...]
    pallas_call x1, Pallas kernels: 2.26 us -> 1.8 us  [local_gathered(): pl.pallas_call(functools.partial(pull_kernel, offsets), out_shape=(shape(...]
  transfers between devices with their start and end apart: 9 -> 9, of which waited for: 5 -> 5; matrix products, arithmetic and copies ran while one was open for 4% -> 4% of each run, Pallas kernels for 7% -> 5%
where the time goes in v12:
time: 37.1 us; the launch traced here: 36.7 us
  Pallas kernels  14.5 us (39%)
  starting transfers between devices  10.4 us (28%)
  waiting for transfers between devices  6.84 us (18%)
  local copies, waits for them, and re-layouts  4.21 us (11%)
  between operations  0.73 us (2%)
    ppermute x7, starting transfers between devices, swapped_with(): return lax.ppermute(values, axis, [(n, n ^ mask) for n in range(size)])  9.86 us
    ppermute x7, waiting for transfers between devices, swapped_with(): return lax.ppermute(values, axis, [(n, n ^ mask) for n in range(size)])  5.63 us
    pallas_call x1, Pallas kernels, local_gathered(): pl.pallas_call(back_kernel, out_shape=(shape((2, seqs, LANES), BF16), sha...  4.73 us
    pallas_call x1, Pallas kernels, local_gathered(): pl.pallas_call(functools.partial(outer_kernel, offsets), out_shape=(shape...  3.47 us
    unnamed x19, local copies, waits for them, and re-layouts  3 us
    pallas_call x1, Pallas kernels, local_gathered(): pl.pallas_call(pick_kernel, out_shape=(shape((seqs, packed), F32), shape(...  2.15 us
    pallas_call x1, Pallas kernels, local_gathered(): pl.pallas_call(close_kernel, out_shape=(shape((flat, pair_width), F32), s...  2.13 us
    pallas_call x1, Pallas kernels, local_gathered(): pl.pallas_call(functools.partial(pull_kernel, offsets), out_shape=(shape(...  1.8 us
  transfers between devices with their start and end apart: 9, of which 5 were waited for; matrix products, arithmetic and copies ran while one was open for 4% of the time, Pallas kernels for 5%

profile of v12, /device:TPU:0, one launch (start us, length us, event | category | flops | bytes accessed | tf_op | source)
XLA Modules:
  0.0 36.7 jit_solution(13694958287310226386)
XLA Ops:
  0.6 2.1 %pick_rows.1 = (f32[64,256]{1,0:T(8,128)}, f32[64,256]{1,0:T(8,128)}, bf16[384,128]{1,0:T(8,128)(2,1)}) custom-call(s32[1,64]{1,0:T(1,128)} %bitcast.57, bf16[256,128]{1,0:T(8,128)(2,1)} %bitcast.55, bf16[256,128]{1,0:T(8,128)(2,1)} %bitcast.56), custom_call_target="tpu_custom_call" | custom-call | tf_op jit(solution)/shard_map/pick_rows/pallas_call | solution.py:595
  2.8 3.1 %collective-permute-start = (bf16[384,128]{1,0:T(8,128)(2,1)}, bf16[384,128]{1,0:T(8,128)(2,1)S(1)}, u32[]{:S(2)}, u32[]{:S(2)}) collective-permute-start(bf16[384,128]{1,0:T(8,128)(2,1)} %get-tuple-element.27.own_ref), channel_id=1, source_target_pairs={{0,4},{4,0},{8,12},{12,8},{1,5},{5,1},{9,13},{13,9},{2,6},{6,2},{1... | collective-permute-start | bytes 294920 | tf_op jit(solution)/shard_map/ppermute | solution.py:622
  5.9 2.6 %collective-permute-start.1 = (bf16[384,128]{1,0:T(8,128)(2,1)}, bf16[384,128]{1,0:T(8,128)(2,1)S(1)}, u32[]{:S(2)}, u32[]{:S(2)}) collective-permute-start(bf16[384,128]{1,0:T(8,128)(2,1)} %get-tuple-element.27.own_ref), channel_id=1, source_target_pairs={{0,8},{4,12},{8,0},{12,4},{1,9},{5,13},{9,1},{13,5},{2,10},{6,14},... | collective-permute-start | bytes 294920 | tf_op jit(solution)/shard_map/ppermute | solution.py:622
  8.5 1.7 %collective-permute-start.3 = (bf16[384,128]{1,0:T(8,128)(2,1)}, bf16[384,128]{1,0:T(8,128)(2,1)S(1)}, u32[]{:S(2)}, u32[]{:S(2)}) collective-permute-start(bf16[384,128]{1,0:T(8,128)(2,1)} %get-tuple-element.27.own_ref), channel_id=1, source_target_pairs={{0,2},{2,0},{1,3},{3,1},{4,6},{6,4},{5,7},{7,5},{8,10},{10,8},{9,1... | collective-permute-start | bytes 294920 | tf_op jit(solution)/shard_map/ppermute | solution.py:622
  10.2 1.1 %copy.16 = bf16[32,32,128]{2,1,0:T(8,128)(2,1)S(1)} copy(bf16[32,32,128]{2,0,1:T(8,128)(2,1)} %bitcast.54) | data formatting | bytes 524288 | tf_op jit(solution)/shard_map/transpose | solution.py:618
  11.2 0.1 copy.17
  11.4 0.9 %copy-done = bf16[384,128]{1,0:T(8,128)(2,1)S(1)} copy-done((bf16[384,128]{1,0:T(8,128)(2,1)S(1)}, bf16[384,128]{1,0:T(8,128)(2,1)}, u32[]{:S(2)}) %copy-start) | copy-done | bytes 98328
  12.3 0.7 %copy-done.3 = bf16[64,32]{0,1:T(8,128)(2,1)S(1)} copy-done((bf16[64,32]{0,1:T(8,128)(2,1)S(1)}, bf16[64,32]{0,1:T(8,128)(2,1)}, u32[]{:S(2)}) %copy-start.3) | copy-done | bytes 4120
  13.0 0.7 %copy-done.4 = bf16[64,32]{0,1:T(8,128)(2,1)S(1)} copy-done((bf16[64,32]{0,1:T(8,128)(2,1)S(1)}, bf16[64,32]{0,1:T(8,128)(2,1)}, u32[]{:S(2)}) %copy-start.4) | copy-done | bytes 4120
  13.7 0.7 %copy-done.5 = f32[128]{0:T(128)S(1)} copy-done((f32[128]{0:T(128)S(1)}, f32[128]{0:T(128)}, u32[]{:S(2)}) %copy-start.5) | copy-done | bytes 536
  14.3 0.2 setup.1
  14.5 0.4 %collective-permute-start.4 = (bf16[384,128]{1,0:T(8,128)(2,1)S(1)}, bf16[384,128]{1,0:T(8,128)(2,1)S(1)}, u32[]{:S(2)}, u32[]{:S(2)}) collective-permute-start(bf16[384,128]{1,0:T(8,128)(2,1)S(1)} %get-tuple-element.29.refs_1_), channel_id=1, source_target_pairs={{0,2},{2,0},{1,3},{3,1},{4,6},{6,4},{5,7},{7,5},{8,10},{10,8},{9,1... | collective-permute-start | bytes 294920 | tf_op jit(solution)/shard_map/ppermute | solution.py:622
  14.9 1.6 %collective-permute-done.1.refs_2_ = bf16[384,128]{1,0:T(8,128)(2,1)S(1)} collective-permute-done((bf16[384,128]{1,0:T(8,128)(2,1)}, bf16[384,128]{1,0:T(8,128)(2,1)S(1)}, u32[]{:S(2)}, u32[]{:S(2)}) %collective-permute-start.1) | collective-permute-done | bytes 98336 | tf_op jit(solution)/shard_map/ppermute | solution.py:622
  16.5 1.5 %collective-permute-start.5 = (bf16[384,128]{1,0:T(8,128)(2,1)S(1)}, bf16[384,128]{1,0:T(8,128)(2,1)S(1)}, u32[]{:S(2)}, u32[]{:S(2)}) collective-permute-start(bf16[384,128]{1,0:T(8,128)(2,1)S(1)} %collective-permute-done.1.refs_2_), channel_id=1, source_target_pairs={{0,2},{2,0},{1,3},{3,1},{4,6},{6,4},{5,7},{7,5},{8,10},{10,8},{9,1... | collective-permute-start | bytes 294920 | tf_op jit(solution)/shard_map/ppermute | solution.py:622
  18.0 0.6 %collective-permute-start.6 = (bf16[384,128]{1,0:T(8,128)(2,1)S(1)}, bf16[384,128]{1,0:T(8,128)(2,1)S(1)}, u32[]{:S(2)}, u32[]{:S(2)}) collective-permute-start(bf16[384,128]{1,0:T(8,128)(2,1)S(1)} %collective-permute-done.2.refs_3_), channel_id=1, source_target_pairs={{0,2},{2,0},{1,3},{3,1},{4,6},{6,4},{5,7},{7,5},{8,10},{10,8},{9,1... | collective-permute-start | bytes 294920 | tf_op jit(solution)/shard_map/ppermute | solution.py:622
  18.7 1.5 %collective-permute-done.4.refs_5_ = bf16[384,128]{1,0:T(8,128)(2,1)S(1)} collective-permute-done((bf16[384,128]{1,0:T(8,128)(2,1)S(1)}, bf16[384,128]{1,0:T(8,128)(2,1)S(1)}, u32[]{:S(2)}, u32[]{:S(2)}) %collective-permute-start.4) | collective-permute-done | bytes 98336 | tf_op jit(solution)/shard_map/ppermute | solution.py:622
  20.2 1.0 %collective-permute-done.5.refs_6_ = bf16[384,128]{1,0:T(8,128)(2,1)S(1)} collective-permute-done((bf16[384,128]{1,0:T(8,128)(2,1)S(1)}, bf16[384,128]{1,0:T(8,128)(2,1)S(1)}, u32[]{:S(2)}, u32[]{:S(2)}) %collective-permute-start.5) | collective-permute-done | bytes 98336 | tf_op jit(solution)/shard_map/ppermute | solution.py:622
  21.3 1.5 %collective-permute-done.6.refs_7_ = bf16[384,128]{1,0:T(8,128)(2,1)S(1)} collective-permute-done((bf16[384,128]{1,0:T(8,128)(2,1)S(1)}, bf16[384,128]{1,0:T(8,128)(2,1)S(1)}, u32[]{:S(2)}, u32[]{:S(2)}) %collective-permute-start.6) | collective-permute-done | bytes 98336 | tf_op jit(solution)/shard_map/ppermute | solution.py:622
  22.8 1.8 %pull_back.1 = (bf16[4,2,256,128]{3,2,1,0:T(8,128)(2,1)S(1)}, bf16[4,256,2048]{2,1,0:T(8,128)(2,1)S(1)}) custom-call(s32[3]{0:T(128)S(1)} %pad_add_fusion.place_ref, bf16[128,1024]{1,0:T(8,128)(2,1)S(1)} %bitcast.50, bf16[384,128]{1,0:T(8,128)(2,1)S(1)} %get-tuple-element.28.refs_0_, bf16[384,128]{1,0:T(8,128)(2,1)S(1)} %get-tuple-element.29.refs_1_, ...), custom_call_target="tpu_custom_call" | custom-call | flops 536870912 | bytes 5242880 | tf_op jit(solution)/shard_map/pull_back/pallas_call | solution.py:661
  24.6 3.5 %outer_products.1 = (bf16[1024,256]{1,0:T(8,128)(2,1)S(1)}, bf16[16,64,512]{2,1,0:T(8,128)(2,1)S(1)}, bf16[256,256]{1,0:T(8,128)(2,1)S(1)}, bf16[4,512,1024]{2,1,0:T(8,128)(2,1)S(1)}, bf16[16,16,128]{2,1,0:T(8,128)(2,1)}) custom-call(s32[3]{0:T(128)S(1)} %pad_add_fusion.place_ref, bf16[8,128,128]{2,1,0:T(8,128)(2,1)S(1)} %fusion.mine_from_ref, ...), custom_call_target="tpu_custom_call" | custom-call | flops 1073741824 | bytes 4194304 | tf_op jit(solution)/shard_map/outer_products/pallas_call | solution.py:678
  28.1 4.7 %pull_further.1 = (bf16[2,64,128]{2,1,0:T(8,128)(2,1)S(1)}, bf16[1152,128]{1,0:T(8,128)(2,1)S(1)}) custom-call(s32[3]{0:T(128)S(1)} %pad_add_fusion.place_ref, bf16[1024,256]{1,0:T(8,128)(2,1)S(1)} %get-tuple-element.34.rows_ref, bf16[16,64,512]{2,1,0:T(8,128)(2,1)S(1)} %get-tuple-element.35.expanded, bf16[256,256]{1,0:T(8,128)(2,1)S(1)} %get-tuple-element.36.swapped, ...), custom_call_target="tpu_custom_call" | custom-call | tf_op jit(solution)/shard_map/pull_further/pallas_call | solution.py:702
  32.8 0.6 %collective-permute-start.8 = (bf16[1152,128]{1,0:T(8,128)(2,1)S(1)}, bf16[1152,128]{1,0:T(8,128)(2,1)S(1)}, u32[]{:S(2)}, u32[]{:S(2)}) collective-permute-start(bf16[1152,128]{1,0:T(8,128)(2,1)S(1)} %get-tuple-element.41.own_ref), channel_id=1, source_target_pairs={{0,1},{1,0},{2,3},{3,2},{4,5},{5,4},{6,7},{7,6},{8,9},{9,8},{10,11... | collective-permute-start | bytes 884744 | tf_op jit(solution)/shard_map/ppermute | solution.py:720
  33.4 1.2 %collective-permute-done.8.message_ref = bf16[1152,128]{1,0:T(8,128)(2,1)S(1)} collective-permute-done((bf16[1152,128]{1,0:T(8,128)(2,1)S(1)}, bf16[1152,128]{1,0:T(8,128)(2,1)S(1)}, u32[]{:S(2)}, u32[]{:S(2)}) %collective-permute-start.8) | collective-permute-done | bytes 294944 | tf_op jit(solution)/shard_map/ppermute | solution.py:720
  34.6 2.1 %close.1 = (f32[1024,128]{1,0:T(8,128)}, f32[32,64]{1,0:T(8,128)}, f32[32,64]{1,0:T(8,128)}, bf16[64,4,64]{2,1,0:T(4,128)(2,1)}) custom-call(bf16[2,64,128]{2,1,0:T(8,128)(2,1)S(1)} %get-tuple-element.40.grads_ref, bf16[1152,128]{1,0:T(8,128)(2,1)S(1)} %get-tuple-element.41.own_ref, bf16[1152,128]{1,0:T(8,128)(2,1)S(1)} %collective-permute-done.8.message_ref, ...), custom_call_target="tpu_custom_call" | custom-call | tf_op jit(solution)/shard_map/close/pallas_call | solution.py:721
  (23 shorter events, 0.2 us)
Async XLA Ops:
  2.8 8.6 %collective-permute-start = (bf16[384,128]{1,0:T(8,128)(2,1)}, bf16[384,128]{1,0:T(8,128)(2,1)S(1)}, u32[]{:S(2)}, u32[]{:S(2)}) collective-permute-start(bf16[384,128]{1,0:T(8,128)(2,1)} %get-tuple-element.27.own_ref), channel_id=1, source_target_pairs={{0,4},{4,0},{8,12},{12,8},{1,5},{5,1},{9,13},{13,9},{2,6},{6,2},{1... | collective-permute-start | bytes 294920 | tf_op jit(solution)/shard_map/ppermute | solution.py:622
  5.9 10.6 %collective-permute-start.1 = (bf16[384,128]{1,0:T(8,128)(2,1)}, bf16[384,128]{1,0:T(8,128)(2,1)S(1)}, u32[]{:S(2)}, u32[]{:S(2)}) collective-permute-start(bf16[384,128]{1,0:T(8,128)(2,1)} %get-tuple-element.27.own_ref), channel_id=1, source_target_pairs={{0,8},{4,12},{8,0},{12,4},{1,9},{5,13},{9,1},{13,5},{2,10},{6,14},... | collective-permute-start | bytes 294920 | tf_op jit(solution)/shard_map/ppermute | solution.py:622
  8.5 9.6 %collective-permute-start.2 = (bf16[384,128]{1,0:T(8,128)(2,1)}, bf16[384,128]{1,0:T(8,128)(2,1)S(1)}, u32[]{:S(2)}, u32[]{:S(2)}) collective-permute-start(bf16[384,128]{1,0:T(8,128)(2,1)} %get-tuple-element.27.own_ref), channel_id=1, source_target_pairs={{0,12},{4,8},{8,4},{12,0},{1,13},{5,9},{9,5},{13,1},{2,14},{6,10},... | collective-permute-start | bytes 294920 | tf_op jit(solution)/shard_map/ppermute | solution.py:622
  8.5 10.2 %collective-permute-start.3 = (bf16[384,128]{1,0:T(8,128)(2,1)}, bf16[384,128]{1,0:T(8,128)(2,1)S(1)}, u32[]{:S(2)}, u32[]{:S(2)}) collective-permute-start(bf16[384,128]{1,0:T(8,128)(2,1)} %get-tuple-element.27.own_ref), channel_id=1, source_target_pairs={{0,2},{2,0},{1,3},{3,1},{4,6},{6,4},{5,7},{7,5},{8,10},{10,8},{9,1... | collective-permute-start | bytes 294920 | tf_op jit(solution)/shard_map/ppermute | solution.py:622
  11.4 0.9 %copy-start = (bf16[384,128]{1,0:T(8,128)(2,1)S(1)}, bf16[384,128]{1,0:T(8,128)(2,1)}, u32[]{:S(2)}) copy-start(bf16[384,128]{1,0:T(8,128)(2,1)} %get-tuple-element.27.own_ref) | copy-start | bytes 294916
  12.3 0.7 %copy-start.3 = (bf16[64,32]{0,1:T(8,128)(2,1)S(1)}, bf16[64,32]{0,1:T(8,128)(2,1)}, u32[]{:S(2)}) copy-start(bf16[64,32]{0,1:T(8,128)(2,1)} %param.9) | copy-start | bytes 12292
  13.0 0.7 %copy-start.4 = (bf16[64,32]{0,1:T(8,128)(2,1)S(1)}, bf16[64,32]{0,1:T(8,128)(2,1)}, u32[]{:S(2)}) copy-start(bf16[64,32]{0,1:T(8,128)(2,1)} %param.10) | copy-start | bytes 12292
  13.7 0.7 %copy-start.5 = (f32[128]{0:T(128)S(1)}, f32[128]{0:T(128)}, u32[]{:S(2)}) copy-start(f32[128]{0:T(128)} %param.12) | copy-start | bytes 1540
  14.5 5.6 %collective-permute-start.4 = (bf16[384,128]{1,0:T(8,128)(2,1)S(1)}, bf16[384,128]{1,0:T(8,128)(2,1)S(1)}, u32[]{:S(2)}, u32[]{:S(2)}) collective-permute-start(bf16[384,128]{1,0:T(8,128)(2,1)S(1)} %get-tuple-element.29.refs_1_), channel_id=1, source_target_pairs={{0,2},{2,0},{1,3},{3,1},{4,6},{6,4},{5,7},{7,5},{8,10},{10,8},{9,1... | collective-permute-start | bytes 294920 | tf_op jit(solution)/shard_map/ppermute | solution.py:622
  16.5 4.7 %collective-permute-start.5 = (bf16[384,128]{1,0:T(8,128)(2,1)S(1)}, bf16[384,128]{1,0:T(8,128)(2,1)S(1)}, u32[]{:S(2)}, u32[]{:S(2)}) collective-permute-start(bf16[384,128]{1,0:T(8,128)(2,1)S(1)} %collective-permute-done.1.refs_2_), channel_id=1, source_target_pairs={{0,2},{2,0},{1,3},{3,1},{4,6},{6,4},{5,7},{7,5},{8,10},{10,8},{9,1... | collective-permute-start | bytes 294920 | tf_op jit(solution)/shard_map/ppermute | solution.py:622
  18.0 4.7 %collective-permute-start.6 = (bf16[384,128]{1,0:T(8,128)(2,1)S(1)}, bf16[384,128]{1,0:T(8,128)(2,1)S(1)}, u32[]{:S(2)}, u32[]{:S(2)}) collective-permute-start(bf16[384,128]{1,0:T(8,128)(2,1)S(1)} %collective-permute-done.2.refs_3_), channel_id=1, source_target_pairs={{0,2},{2,0},{1,3},{3,1},{4,6},{6,4},{5,7},{7,5},{8,10},{10,8},{9,1... | collective-permute-start | bytes 294920 | tf_op jit(solution)/shard_map/ppermute | solution.py:622
  22.7 1.9 %collective-permute-start.7 = (bf16[8,128,128]{2,1,0:T(8,128)(2,1)S(1)}, bf16[8,128,128]{2,1,0:T(8,128)(2,1)S(1)}, u32[]{:S(2)}, u32[]{:S(2)}) collective-permute-start(bf16[8,128,128]{2,1,0:T(8,128)(2,1)S(1)} %fusion.mine_from_ref), channel_id=1, source_target_pairs={{0,1},{1,0},{2,3},{3,2},{4,5},{5,4},{6,7},{7,6},{8,9},{9,8},{10,11... | collective-permute-start | bytes 786440 | tf_op jit(solution)/shard_map/ppermute | solution.py:656
  28.1 6.5 %copy-start.1 = (f32[64,256]{1,0:T(8,128)S(1)}, f32[64,256]{1,0:T(8,128)}, u32[]{:S(2)}) copy-start(f32[64,256]{1,0:T(8,128)} %get-tuple-element.42.normed_ref) | copy-start | bytes 196612
  28.1 6.5 %copy-start.2 = (f32[64,256]{1,0:T(8,128)S(1)}, f32[64,256]{1,0:T(8,128)}, u32[]{:S(2)}) copy-start(f32[64,256]{1,0:T(8,128)} %get-tuple-element.43.inverse_ref) | copy-start | bytes 196612
  32.8 1.8 %collective-permute-start.8 = (bf16[1152,128]{1,0:T(8,128)(2,1)S(1)}, bf16[1152,128]{1,0:T(8,128)(2,1)S(1)}, u32[]{:S(2)}, u32[]{:S(2)}) collective-permute-start(bf16[1152,128]{1,0:T(8,128)(2,1)S(1)} %get-tuple-element.41.own_ref), channel_id=1, source_target_pairs={{0,1},{1,0},{2,3},{3,2},{4,5},{5,4},{6,7},{7,6},{8,9},{9,8},{10,11... | collective-permute-start | bytes 884744 | tf_op jit(solution)/shard_map/ppermute | solution.py:720

commit v13 on v10

--- a/solution.py
+++ b/solution.py
@@ -316,10 +316,32 @@
                     ].astype(BF16)
         return carry
 
-    lax.fori_loop(0, prow_n, step, 0)
-
-
-def outer_kernel(
+    lax.fori_loop(0, prow_n, step, 0, unroll=True)
+
+
+def owner_order(places, prow_n, core):
+    mine = [(2 * g + core) * prow_n + r for g, r in places]
+    return mine + [(2 * g + 1 - core) * prow_n + r for g, r in places]
+
+
+def shuffle_matrix(block_cols, proj, tokens):
+    wide, highs = block_cols * proj, proj // tokens
+    source = lax.broadcasted_iota(jnp.int32, (wide, wide), 0)
+    target = lax.broadcasted_iota(jnp.int32, (wide, wide), 1)
+    jj, qh = target % block_cols, target // block_cols % highs
+    ql = target // (highs * block_cols)
+    return (source == jj * proj + qh * tokens + ql).astype(BF16)
+
+
+def left_block(expanded, row, step_owners, tokens):
+    ahead = jnp.concatenate([expanded[row * step_owners + o] for o in range(step_owners)], axis=1)
+    low = lane_ids(ahead.shape) % LANES // (LANES // tokens)
+    return jnp.concatenate(
+        [jnp.where(low == l, ahead, jnp.zeros_like(ahead)) for l in range(tokens)], axis=0
+    )
+
+
+def pair_kernel(
     offsets,
     place_ref,
     mine_from_ref,
@@ -328,14 +350,22 @@
     left_ref,
     right_ref,
     offset_ref,
+    cot_ref,
+    pulled_ref,
+    pair_ref,
+    grads_ref,
+    message_ref,
     rows_ref,
     expanded,
     swapped,
     outer_ref,
-    pair_ref,
     mine_ref,
     theirs_ref,
     turned,
+    left_back,
+    right_back,
+    sums,
+    weights,
 ):
     for source, target in ((mine_from_ref, mine_ref), (theirs_from_ref, theirs_ref)):
         place_blocks(place_ref, offsets, [source[n] for n in range(source.shape[0])], target)
@@ -378,8 +408,12 @@
             ).astype(BF16)
     turned[...] = swapped[...].astype(F32).T.astype(BF16)
 
-    def step(row, carry):
-        made = dot(turned[...], left_block(expanded, row, owners // prow_n, tokens))
+    order = owner_order(places, prow_n, core)
+    pairs = block_rows * block_cols
+    step_owners = owners // prow_n
+    for row in range(prow_n):
+        block = left_block(expanded, row, step_owners, tokens)
+        made = dot(turned[...], block)
         for g in range(groups):
             for t in range(block_rows):
                 start = (g * block_rows + t) * block_cols
@@ -389,71 +423,9 @@
                     outer_ref[row, start : start + block_cols, h * LANES : (h + 1) * LANES] = made[
                         there, lanes
                     ].astype(BF16)
-        return carry
-
-    lax.fori_loop(0, prow_n, step, 0)
-    share = block_rows * block_cols
-    mine = outer_ref[own_row, pl.ds(pl.multiple_of(own_group * share, share), share)]
-    update = dot(mine, mapping_ref[...]) + offset_ref[...]
-    pair_ref[...] = update.astype(BF16).reshape(pair_ref.shape)
-
-
-def owner_order(places, prow_n, core):
-    mine = [(2 * g + core) * prow_n + r for g, r in places]
-    return mine + [(2 * g + 1 - core) * prow_n + r for g, r in places]
-
-
-def shuffle_matrix(block_cols, proj, tokens):
-    wide, highs = block_cols * proj, proj // tokens
-    source = lax.broadcasted_iota(jnp.int32, (wide, wide), 0)
-    target = lax.broadcasted_iota(jnp.int32, (wide, wide), 1)
-    jj, qh = target % block_cols, target // block_cols % highs
-    ql = target // (highs * block_cols)
-    return (source == jj * proj + qh * tokens + ql).astype(BF16)
-
-
-def left_block(expanded, row, step_owners, tokens):
-    ahead = jnp.concatenate([expanded[row * step_owners + o] for o in range(step_owners)], axis=1)
-    low = lane_ids(ahead.shape) % LANES // (LANES // tokens)
-    return jnp.concatenate(
-        [jnp.where(low == l, ahead, jnp.zeros_like(ahead)) for l in range(tokens)], axis=0
-    )
-
-
-def back_kernel(
-    place_ref,
-    rows_ref,
-    expanded,
-    swapped,
-    outer_ref,
-    cot_ref,
-    pulled_ref,
-    grads_ref,
-    message_ref,
-    left_back,
-    right_back,
-    sums,
-    weights,
-):
-    prow_n, groups, pairs, pair_width = cot_ref.shape
-    owners, seqs = left_back.shape[:2]
-    tokens = swapped.shape[0] // seqs
-    proj = LANES // tokens
-    highs = proj // tokens
-    span = swapped.shape[1] // groups
-    block_cols = span // highs
-    step_owners = owners // prow_n
-    own_row, own_group, core = place_ref[0], place_ref[1], place_ref[2]
-    places = [(g, r) for g in range(groups) for r in range(prow_n)]
-    order = owner_order(places, prow_n, core)
-
-    sums[...] = jnp.zeros_like(sums)
-    weights[...] = jnp.zeros_like(weights)
-
-    def step(row, carry):
-        block = left_block(expanded, row, step_owners, tokens)
         cot = cot_ref[row].reshape(groups * pairs, pair_width)
-        weights[...] += dot(cot, outer_ref[row], contract=(0, 0))
+        weight_part = dot(cot, outer_ref[row], contract=(0, 0))
+        weights[...] = weight_part if row == 0 else weights[...] + weight_part
         pulled = pulled_ref[row]
         back = dot(swapped[...], pulled)
         low = lane_ids((seqs, back.shape[1])) % LANES // proj
@@ -470,10 +442,13 @@
                 for t in range(tokens)
             ]
             left_back[row * step_owners + o] = fold_tokens(parts).astype(BF16)
-        sums[...] += dot(pulled, block, contract=(1, 1))
-        return carry
-
-    lax.fori_loop(0, prow_n, step, 0)
+        sum_part = dot(pulled, block, contract=(1, 1))
+        sums[...] = sum_part if row == 0 else sums[...] + sum_part
+
+    share = block_rows * block_cols
+    mine = outer_ref[own_row, pl.ds(pl.multiple_of(own_group * share, share), share)]
+    update = dot(mine, mapping_ref[...]) + offset_ref[...]
+    pair_ref[...] = update.astype(BF16).reshape(pair_ref.shape)
 
     back = (sums[...].T * (1.0 / seqs)).astype(BF16)
     back = jnp.concatenate(
@@ -665,47 +640,31 @@
         name="pull_back",
     )(place, turned_mapping, *messages)
 
-    rows_all, expanded, swapped, outer, pair_delta = pl.pallas_call(
-        functools.partial(outer_kernel, offsets),
+    pair_delta, grads, message = pl.pallas_call(
+        functools.partial(pair_kernel, offsets),
         out_shape=(
-            shape((owners * seqs, packed), BF16),
-            shape((owners, seqs, tokens * LANES), BF16),
-            shape((tokens * seqs, columns), BF16),
-            shape((prow_n, groups * pairs, flat), BF16),
             shape(upstream_sensitivity.shape, BF16),
+            shape((2, seqs, LANES), BF16),
+            shape((flat + 2 * proj + seqs, LANES), BF16),
         ),
-        in_specs=[smem] + [vmem] * 6,
-        out_specs=(vmem,) * 5,
+        in_specs=[smem] + [vmem] * 8,
+        out_specs=(vmem,) * 3,
         scratch_shapes=[
+            pltpu.VMEM((owners * seqs, packed), BF16),
+            pltpu.VMEM((owners, seqs, tokens * LANES), BF16),
+            pltpu.VMEM((tokens * seqs, columns), BF16),
+            pltpu.VMEM((prow_n, groups * pairs, flat), BF16),
             pltpu.VMEM((prow_n, groups, length, LANES), BF16),
             pltpu.VMEM((prow_n, groups, length, LANES), BF16),
             pltpu.VMEM((columns, tokens * seqs), BF16),
-        ],
-        compiler_params=params,
-        cost_estimate=pl.CostEstimate(
-            flops=2 * prow_n * groups * pairs * tokens * seqs * flat,
-            bytes_accessed=2 * prow_n * groups * pairs * flat,
-            transcendentals=0,
-        ),
-        name="outer_products",
-    )(place, rows, theirs, mapping, left_wide, right_one, offset)
-    grads, message = pl.pallas_call(
-        back_kernel,
-        out_shape=(
-            shape((2, seqs, LANES), BF16),
-            shape((flat + 2 * proj + seqs, LANES), BF16),
-        ),
-        in_specs=[smem] + [vmem] * 6,
-        out_specs=(vmem,) * 2,
-        scratch_shapes=[
             pltpu.VMEM((owners, seqs, LANES), BF16),
             pltpu.VMEM((groups * prow_n, seqs, LANES), BF16),
             pltpu.VMEM((columns, tokens * seqs), F32),
             pltpu.VMEM((pair_width, flat), F32),
         ],
         compiler_params=params,
-        name="pull_further",
-    )(place, rows_all, expanded, swapped, outer, cot, pulled)
+        name="pair_work",
+    )(place, rows, theirs, mapping, left_wide, right_one, offset, cot, pulled)
 
     theirs = lax.ppermute(message, "pc", [(0, 1), (1, 0)])
     output_weight_gradient, left_weight_gradient, right_weight_gradient, alignment = pl.pallas_call(

time: 37.9 us -> 35.3 us (0.931)
  Pallas kernels: 15.3 us -> 12.9 us
    pallas_call x2 -> x1, Pallas kernels: 9.24 us -> 7.22 us  [local_gathered(): pl.pallas_call(functools.partial(pair_kernel, offsets), out_shape=(shape(...]
    reshape x1, local copies, waits for them, and re-layouts: 0.14 us -> 1.05 us  [local_gathered(): mapping = final_mapping_matrix.reshape(proj, proj, pair_width)]
    transpose x1, local copies, waits for them, and re-layouts: 1.05 us -> 0.14 us  [local_gathered(): turned_mapping = mapping.T]
    pallas_call x1, Pallas kernels: 2.26 us -> 1.8 us  [local_gathered(): pl.pallas_call(functools.partial(pull_kernel, offsets), out_shape=(shape(...]
  transfers between devices with their start and end apart: 9 -> 9, of which waited for: 5 -> 5; matrix products, arithmetic and copies ran while one was open for 4% -> 4% of each run, Pallas kernels for 7% -> 6%
where the time goes in v13:
time: 35.3 us; the launch traced here: 35 us
  Pallas kernels  12.9 us (37%)
  starting transfers between devices  10.3 us (29%)
  waiting for transfers between devices  6.83 us (19%)
  local copies, waits for them, and re-layouts  4.21 us (12%)
  between operations  0.72 us (2%)
    ppermute x7, starting transfers between devices, swapped_with(): return lax.ppermute(values, axis, [(n, n ^ mask) for n in range(size)])  9.8 us
    pallas_call x1, Pallas kernels, local_gathered(): pl.pallas_call(functools.partial(pair_kernel, offsets), out_shape=(shape(...  7.22 us
    ppermute x7, waiting for transfers between devices, swapped_with(): return lax.ppermute(values, axis, [(n, n ^ mask) for n in range(size)])  5.62 us
    unnamed x19, local copies, waits for them, and re-layouts  3 us
    pallas_call x1, Pallas kernels, local_gathered(): pl.pallas_call(pick_kernel, out_shape=(shape((seqs, packed), F32), shape(...  2.15 us
    pallas_call x1, Pallas kernels, local_gathered(): pl.pallas_call(functools.partial(pull_kernel, offsets), out_shape=(shape(...  1.8 us
    pallas_call x1, Pallas kernels, local_gathered(): pl.pallas_call(close_kernel, out_shape=(shape((flat, pair_width), F32), s...  1.51 us
    ppermute x1, waiting for transfers between devices, local_gathered(): theirs = lax.ppermute(message, 'pc', [(0, 1), (1, 0)])  1.21 us
  transfers between devices with their start and end apart: 9, of which 5 were waited for; matrix products, arithmetic and copies ran while one was open for 4% of the time, Pallas kernels for 6%

profile of v13, /device:TPU:0, one launch (start us, length us, event | category | flops | bytes accessed | tf_op | source)
XLA Modules:
  0.0 35.0 jit_solution(4398017581540514066)
XLA Ops:
  0.6 2.1 %pick_rows.1 = (f32[64,256]{1,0:T(8,128)}, f32[64,256]{1,0:T(8,128)}, bf16[384,128]{1,0:T(8,128)(2,1)}) custom-call(s32[1,64]{1,0:T(1,128)} %bitcast.56, bf16[256,128]{1,0:T(8,128)(2,1)} %bitcast.54, bf16[256,128]{1,0:T(8,128)(2,1)} %bitcast.55), custom_call_target="tpu_custom_call" | custom-call | tf_op jit(solution)/shard_map/pick_rows/pallas_call | solution.py:560
  2.8 3.1 %collective-permute-start = (bf16[384,128]{1,0:T(8,128)(2,1)}, bf16[384,128]{1,0:T(8,128)(2,1)S(1)}, u32[]{:S(2)}, u32[]{:S(2)}) collective-permute-start(bf16[384,128]{1,0:T(8,128)(2,1)} %get-tuple-element.23.own_ref), channel_id=1, source_target_pairs={{0,4},{4,0},{8,12},{12,8},{1,5},{5,1},{9,13},{13,9},{2,6},{6,2},{1... | collective-permute-start | bytes 294920 | tf_op jit(solution)/shard_map/ppermute | solution.py:587
  5.9 2.6 %collective-permute-start.1 = (bf16[384,128]{1,0:T(8,128)(2,1)}, bf16[384,128]{1,0:T(8,128)(2,1)S(1)}, u32[]{:S(2)}, u32[]{:S(2)}) collective-permute-start(bf16[384,128]{1,0:T(8,128)(2,1)} %get-tuple-element.23.own_ref), channel_id=1, source_target_pairs={{0,8},{4,12},{8,0},{12,4},{1,9},{5,13},{9,1},{13,5},{2,10},{6,14},... | collective-permute-start | bytes 294920 | tf_op jit(solution)/shard_map/ppermute | solution.py:587
  8.5 1.7 %collective-permute-start.3 = (bf16[384,128]{1,0:T(8,128)(2,1)}, bf16[384,128]{1,0:T(8,128)(2,1)S(1)}, u32[]{:S(2)}, u32[]{:S(2)}) collective-permute-start(bf16[384,128]{1,0:T(8,128)(2,1)} %get-tuple-element.23.own_ref), channel_id=1, source_target_pairs={{0,2},{2,0},{1,3},{3,1},{4,6},{6,4},{5,7},{7,5},{8,10},{10,8},{9,1... | collective-permute-start | bytes 294920 | tf_op jit(solution)/shard_map/ppermute | solution.py:587
  10.2 1.1 %copy.12 = bf16[32,32,128]{2,0,1:T(8,128)(2,1)S(1)} copy(bf16[32,32,128]{2,1,0:T(8,128)(2,1)} %bitcast.53) | data formatting | bytes 524288 | tf_op jit(solution)/shard_map/reshape | solution.py:582
  11.2 0.1 copy.13.turned_mapping_ref.mapping_ref
  11.4 0.9 %copy-done = bf16[384,128]{1,0:T(8,128)(2,1)S(1)} copy-done((bf16[384,128]{1,0:T(8,128)(2,1)S(1)}, bf16[384,128]{1,0:T(8,128)(2,1)}, u32[]{:S(2)}) %copy-start) | copy-done | bytes 98328
  12.3 0.7 %copy-done.3 = bf16[64,32]{0,1:T(8,128)(2,1)S(1)} copy-done((bf16[64,32]{0,1:T(8,128)(2,1)S(1)}, bf16[64,32]{0,1:T(8,128)(2,1)}, u32[]{:S(2)}) %copy-start.3) | copy-done | bytes 4120
  13.0 0.7 %copy-done.4 = bf16[64,32]{0,1:T(8,128)(2,1)S(1)} copy-done((bf16[64,32]{0,1:T(8,128)(2,1)S(1)}, bf16[64,32]{0,1:T(8,128)(2,1)}, u32[]{:S(2)}) %copy-start.4) | copy-done | bytes 4120
  13.7 0.7 %copy-done.5 = f32[128]{0:T(128)S(1)} copy-done((f32[128]{0:T(128)S(1)}, f32[128]{0:T(128)}, u32[]{:S(2)}) %copy-start.5) | copy-done | bytes 536
  14.3 0.2 setup.1
  14.5 0.4 %collective-permute-start.4 = (bf16[384,128]{1,0:T(8,128)(2,1)S(1)}, bf16[384,128]{1,0:T(8,128)(2,1)S(1)}, u32[]{:S(2)}, u32[]{:S(2)}) collective-permute-start(bf16[384,128]{1,0:T(8,128)(2,1)S(1)} %get-tuple-element.25.refs_1_), channel_id=1, source_target_pairs={{0,2},{2,0},{1,3},{3,1},{4,6},{6,4},{5,7},{7,5},{8,10},{10,8},{9,1... | collective-permute-start | bytes 294920 | tf_op jit(solution)/shard_map/ppermute | solution.py:587
  14.9 1.6 %collective-permute-done.1.refs_2_ = bf16[384,128]{1,0:T(8,128)(2,1)S(1)} collective-permute-done((bf16[384,128]{1,0:T(8,128)(2,1)}, bf16[384,128]{1,0:T(8,128)(2,1)S(1)}, u32[]{:S(2)}, u32[]{:S(2)}) %collective-permute-start.1) | collective-permute-done | bytes 98336 | tf_op jit(solution)/shard_map/ppermute | solution.py:587
  16.5 1.5 %collective-permute-start.5 = (bf16[384,128]{1,0:T(8,128)(2,1)S(1)}, bf16[384,128]{1,0:T(8,128)(2,1)S(1)}, u32[]{:S(2)}, u32[]{:S(2)}) collective-permute-start(bf16[384,128]{1,0:T(8,128)(2,1)S(1)} %collective-permute-done.1.refs_2_), channel_id=1, source_target_pairs={{0,2},{2,0},{1,3},{3,1},{4,6},{6,4},{5,7},{7,5},{8,10},{10,8},{9,1... | collective-permute-start | bytes 294920 | tf_op jit(solution)/shard_map/ppermute | solution.py:587
  18.0 0.5 %collective-permute-start.6 = (bf16[384,128]{1,0:T(8,128)(2,1)S(1)}, bf16[384,128]{1,0:T(8,128)(2,1)S(1)}, u32[]{:S(2)}, u32[]{:S(2)}) collective-permute-start(bf16[384,128]{1,0:T(8,128)(2,1)S(1)} %collective-permute-done.2.refs_3_), channel_id=1, source_target_pairs={{0,2},{2,0},{1,3},{3,1},{4,6},{6,4},{5,7},{7,5},{8,10},{10,8},{9,1... | collective-permute-start | bytes 294920 | tf_op jit(solution)/shard_map/ppermute | solution.py:587
  18.6 1.6 %collective-permute-done.4.refs_5_ = bf16[384,128]{1,0:T(8,128)(2,1)S(1)} collective-permute-done((bf16[384,128]{1,0:T(8,128)(2,1)S(1)}, bf16[384,128]{1,0:T(8,128)(2,1)S(1)}, u32[]{:S(2)}, u32[]{:S(2)}) %collective-permute-start.4) | collective-permute-done | bytes 98336 | tf_op jit(solution)/shard_map/ppermute | solution.py:587
  20.2 1.0 %collective-permute-done.5.refs_6_ = bf16[384,128]{1,0:T(8,128)(2,1)S(1)} collective-permute-done((bf16[384,128]{1,0:T(8,128)(2,1)S(1)}, bf16[384,128]{1,0:T(8,128)(2,1)S(1)}, u32[]{:S(2)}, u32[]{:S(2)}) %collective-permute-start.5) | collective-permute-done | bytes 98336 | tf_op jit(solution)/shard_map/ppermute | solution.py:587
  21.2 1.4 %collective-permute-done.6.refs_7_ = bf16[384,128]{1,0:T(8,128)(2,1)S(1)} collective-permute-done((bf16[384,128]{1,0:T(8,128)(2,1)S(1)}, bf16[384,128]{1,0:T(8,128)(2,1)S(1)}, u32[]{:S(2)}, u32[]{:S(2)}) %collective-permute-start.6) | collective-permute-done | bytes 98336 | tf_op jit(solution)/shard_map/ppermute | solution.py:587
  22.7 0.1 pad_add_fusion.place_ref
  22.7 1.8 %pull_back.1 = (bf16[4,2,256,128]{3,2,1,0:T(8,128)(2,1)S(1)}, bf16[4,256,2048]{2,1,0:T(8,128)(2,1)S(1)}) custom-call(s32[3]{0:T(128)S(1)} %pad_add_fusion.place_ref, bf16[128,1024]{1,0:T(8,128)(2,1)S(1)} %copy.13.turned_mapping_ref.mapping_ref, bf16[384,128]{1,0:T(8,128)(2,1)S(1)} %get-tuple-element.24.refs_0_, ...), custom_call_target="tpu_custom_call" | custom-call | flops 536870912 | bytes 5242880 | tf_op jit(solution)/shard_map/pull_back/pallas_call | solution.py:626
  24.6 7.2 %pair_work.1 = (bf16[16,16,128]{2,1,0:T(8,128)(2,1)}, bf16[2,64,128]{2,1,0:T(8,128)(2,1)S(1)}, bf16[1152,128]{1,0:T(8,128)(2,1)S(1)}) custom-call(s32[3]{0:T(128)S(1)} %pad_add_fusion.place_ref, bf16[8,128,128]{2,1,0:T(8,128)(2,1)S(1)} %fusion.mine_from_ref, bf16[8,128,128]{2,1,0:T(8,128)(2,1)S(1)} %collective-permute-done.7.theirs_from_ref, ...), custom_call_target="tpu_custom_call" | custom-call | tf_op jit(solution)/shard_map/pair_work/pallas_call | solution.py:643
  31.8 0.5 %collective-permute-start.8 = (bf16[1152,128]{1,0:T(8,128)(2,1)S(1)}, bf16[1152,128]{1,0:T(8,128)(2,1)S(1)}, u32[]{:S(2)}, u32[]{:S(2)}) collective-permute-start(bf16[1152,128]{1,0:T(8,128)(2,1)S(1)} %get-tuple-element.33.own_ref), channel_id=1, source_target_pairs={{0,1},{1,0},{2,3},{3,2},{4,5},{5,4},{6,7},{7,6},{8,9},{9,8},{10,11... | collective-permute-start | bytes 884744 | tf_op jit(solution)/shard_map/ppermute | solution.py:669
  32.3 1.2 %collective-permute-done.8.message_ref = bf16[1152,128]{1,0:T(8,128)(2,1)S(1)} collective-permute-done((bf16[1152,128]{1,0:T(8,128)(2,1)S(1)}, bf16[1152,128]{1,0:T(8,128)(2,1)S(1)}, u32[]{:S(2)}, u32[]{:S(2)}) %collective-permute-start.8) | collective-permute-done | bytes 294944 | tf_op jit(solution)/shard_map/ppermute | solution.py:669
  33.5 1.5 %close.1 = (f32[1024,128]{1,0:T(8,128)}, f32[32,64]{1,0:T(8,128)}, f32[32,64]{1,0:T(8,128)}, bf16[64,4,64]{2,1,0:T(4,128)(2,1)}) custom-call(bf16[2,64,128]{2,1,0:T(8,128)(2,1)S(1)} %get-tuple-element.32.grads_ref, bf16[1152,128]{1,0:T(8,128)(2,1)S(1)} %get-tuple-element.33.own_ref, bf16[1152,128]{1,0:T(8,128)(2,1)S(1)} %collective-permute-done.8.message_ref, ...), custom_call_target="tpu_custom_call" | custom-call | tf_op jit(solution)/shard_map/close/pallas_call | solution.py:670
  (22 shorter events, 0.1 us)
Async XLA Ops:
  2.8 8.6 %collective-permute-start = (bf16[384,128]{1,0:T(8,128)(2,1)}, bf16[384,128]{1,0:T(8,128)(2,1)S(1)}, u32[]{:S(2)}, u32[]{:S(2)}) collective-permute-start(bf16[384,128]{1,0:T(8,128)(2,1)} %get-tuple-element.23.own_ref), channel_id=1, source_target_pairs={{0,4},{4,0},{8,12},{12,8},{1,5},{5,1},{9,13},{13,9},{2,6},{6,2},{1... | collective-permute-start | bytes 294920 | tf_op jit(solution)/shard_map/ppermute | solution.py:587
  5.9 10.6 %collective-permute-start.1 = (bf16[384,128]{1,0:T(8,128)(2,1)}, bf16[384,128]{1,0:T(8,128)(2,1)S(1)}, u32[]{:S(2)}, u32[]{:S(2)}) collective-permute-start(bf16[384,128]{1,0:T(8,128)(2,1)} %get-tuple-element.23.own_ref), channel_id=1, source_target_pairs={{0,8},{4,12},{8,0},{12,4},{1,9},{5,13},{9,1},{13,5},{2,10},{6,14},... | collective-permute-start | bytes 294920 | tf_op jit(solution)/shard_map/ppermute | solution.py:587
  8.5 9.6 %collective-permute-start.2 = (bf16[384,128]{1,0:T(8,128)(2,1)}, bf16[384,128]{1,0:T(8,128)(2,1)S(1)}, u32[]{:S(2)}, u32[]{:S(2)}) collective-permute-start(bf16[384,128]{1,0:T(8,128)(2,1)} %get-tuple-element.23.own_ref), channel_id=1, source_target_pairs={{0,12},{4,8},{8,4},{12,0},{1,13},{5,9},{9,5},{13,1},{2,14},{6,10},... | collective-permute-start | bytes 294920 | tf_op jit(solution)/shard_map/ppermute | solution.py:587
  8.5 10.1 %collective-permute-start.3 = (bf16[384,128]{1,0:T(8,128)(2,1)}, bf16[384,128]{1,0:T(8,128)(2,1)S(1)}, u32[]{:S(2)}, u32[]{:S(2)}) collective-permute-start(bf16[384,128]{1,0:T(8,128)(2,1)} %get-tuple-element.23.own_ref), channel_id=1, source_target_pairs={{0,2},{2,0},{1,3},{3,1},{4,6},{6,4},{5,7},{7,5},{8,10},{10,8},{9,1... | collective-permute-start | bytes 294920 | tf_op jit(solution)/shard_map/ppermute | solution.py:587
  11.4 0.9 %copy-start = (bf16[384,128]{1,0:T(8,128)(2,1)S(1)}, bf16[384,128]{1,0:T(8,128)(2,1)}, u32[]{:S(2)}) copy-start(bf16[384,128]{1,0:T(8,128)(2,1)} %get-tuple-element.23.own_ref) | copy-start | bytes 294916
  12.3 0.7 %copy-start.3 = (bf16[64,32]{0,1:T(8,128)(2,1)S(1)}, bf16[64,32]{0,1:T(8,128)(2,1)}, u32[]{:S(2)}) copy-start(bf16[64,32]{0,1:T(8,128)(2,1)} %param.9) | copy-start | bytes 12292
  13.0 0.7 %copy-start.4 = (bf16[64,32]{0,1:T(8,128)(2,1)S(1)}, bf16[64,32]{0,1:T(8,128)(2,1)}, u32[]{:S(2)}) copy-start(bf16[64,32]{0,1:T(8,128)(2,1)} %param.10) | copy-start | bytes 12292
  13.7 0.7 %copy-start.5 = (f32[128]{0:T(128)S(1)}, f32[128]{0:T(128)}, u32[]{:S(2)}) copy-start(f32[128]{0:T(128)} %param.12) | copy-start | bytes 1540
  14.5 5.6 %collective-permute-start.4 = (bf16[384,128]{1,0:T(8,128)(2,1)S(1)}, bf16[384,128]{1,0:T(8,128)(2,1)S(1)}, u32[]{:S(2)}, u32[]{:S(2)}) collective-permute-start(bf16[384,128]{1,0:T(8,128)(2,1)S(1)} %get-tuple-element.25.refs_1_), channel_id=1, source_target_pairs={{0,2},{2,0},{1,3},{3,1},{4,6},{6,4},{5,7},{7,5},{8,10},{10,8},{9,1... | collective-permute-start | bytes 294920 | tf_op jit(solution)/shard_map/ppermute | solution.py:587
  14.9 18.6 %copy-start.1 = (f32[64,256]{1,0:T(8,128)S(1)}, f32[64,256]{1,0:T(8,128)}, u32[]{:S(2)}) copy-start(f32[64,256]{1,0:T(8,128)} %get-tuple-element.34.normed_ref) | copy-start | bytes 196612
  14.9 18.6 %copy-start.2 = (f32[64,256]{1,0:T(8,128)S(1)}, f32[64,256]{1,0:T(8,128)}, u32[]{:S(2)}) copy-start(f32[64,256]{1,0:T(8,128)} %get-tuple-element.35.inverse_ref) | copy-start | bytes 196612
  16.5 4.7 %collective-permute-start.5 = (bf16[384,128]{1,0:T(8,128)(2,1)S(1)}, bf16[384,128]{1,0:T(8,128)(2,1)S(1)}, u32[]{:S(2)}, u32[]{:S(2)}) collective-permute-start(bf16[384,128]{1,0:T(8,128)(2,1)S(1)} %collective-permute-done.1.refs_2_), channel_id=1, source_target_pairs={{0,2},{2,0},{1,3},{3,1},{4,6},{6,4},{5,7},{7,5},{8,10},{10,8},{9,1... | collective-permute-start | bytes 294920 | tf_op jit(solution)/shard_map/ppermute | solution.py:587
  18.0 4.6 %collective-permute-start.6 = (bf16[384,128]{1,0:T(8,128)(2,1)S(1)}, bf16[384,128]{1,0:T(8,128)(2,1)S(1)}, u32[]{:S(2)}, u32[]{:S(2)}) collective-permute-start(bf16[384,128]{1,0:T(8,128)(2,1)S(1)} %collective-permute-done.2.refs_3_), channel_id=1, source_target_pairs={{0,2},{2,0},{1,3},{3,1},{4,6},{6,4},{5,7},{7,5},{8,10},{10,8},{9,1... | collective-permute-start | bytes 294920 | tf_op jit(solution)/shard_map/ppermute | solution.py:587
  22.6 1.9 %collective-permute-start.7 = (bf16[8,128,128]{2,1,0:T(8,128)(2,1)S(1)}, bf16[8,128,128]{2,1,0:T(8,128)(2,1)S(1)}, u32[]{:S(2)}, u32[]{:S(2)}) collective-permute-start(bf16[8,128,128]{2,1,0:T(8,128)(2,1)S(1)} %fusion.mine_from_ref), channel_id=1, source_target_pairs={{0,1},{1,0},{2,3},{3,2},{4,5},{5,4},{6,7},{7,6},{8,9},{9,8},{10,11... | collective-permute-start | bytes 786440 | tf_op jit(solution)/shard_map/ppermute | solution.py:621
  31.8 1.7 %collective-permute-start.8 = (bf16[1152,128]{1,0:T(8,128)(2,1)S(1)}, bf16[1152,128]{1,0:T(8,128)(2,1)S(1)}, u32[]{:S(2)}, u32[]{:S(2)}) collective-permute-start(bf16[1152,128]{1,0:T(8,128)(2,1)S(1)} %get-tuple-element.33.own_ref), channel_id=1, source_target_pairs={{0,1},{1,0},{2,3},{3,2},{4,5},{5,4},{6,7},{7,6},{8,9},{9,8},{10,11... | collective-permute-start | bytes 884744 | tf_op jit(solution)/shard_map/ppermute | solution.py:669

commit v14 on v13

--- a/solution.py
+++ b/solution.py
@@ -426,6 +426,16 @@
         cot = cot_ref[row].reshape(groups * pairs, pair_width)
         weight_part = dot(cot, outer_ref[row], contract=(0, 0))
         weights[...] = weight_part if row == 0 else weights[...] + weight_part
+        if row == prow_n - 1:
+            share = block_rows * block_cols
+            mine = outer_ref[own_row, pl.ds(pl.multiple_of(own_group * share, share), share)]
+            update = dot(mine, mapping_ref[...]) + offset_ref[...]
+            pair_ref[...] = update.astype(BF16).reshape(pair_ref.shape)
+            flat = weights.shape[1]
+            outer_f = weights[...].T
+            weight_rows = outer_f.reshape(proj, proj, pair_width).swapaxes(0, 1).reshape(flat, pair_width)
+
+            message_ref[:flat] = weight_rows.astype(BF16)
         pulled = pulled_ref[row]
         back = dot(swapped[...], pulled)
         low = lane_ids((seqs, back.shape[1])) % LANES // proj
@@ -444,11 +454,6 @@
             left_back[row * step_owners + o] = fold_tokens(parts).astype(BF16)
         sum_part = dot(pulled, block, contract=(1, 1))
         sums[...] = sum_part if row == 0 else sums[...] + sum_part
-
-    share = block_rows * block_cols
-    mine = outer_ref[own_row, pl.ds(pl.multiple_of(own_group * share, share), share)]
-    update = dot(mine, mapping_ref[...]) + offset_ref[...]
-    pair_ref[...] = update.astype(BF16).reshape(pair_ref.shape)
 
     back = (sums[...].T * (1.0 / seqs)).astype(BF16)
     back = jnp.concatenate(
@@ -488,11 +493,6 @@
     both = jnp.concatenate([left_side, right_side], axis=0).astype(BF16)
     both = jnp.concatenate([both, jnp.zeros_like(both)], axis=1)
 
-    flat = weights.shape[1]
-    outer_f = weights[...].T
-    weight_rows = outer_f.reshape(proj, proj, pair_width).swapaxes(0, 1).reshape(flat, pair_width)
-
-    message_ref[:flat] = weight_rows.astype(BF16)
     message_ref[flat : flat + 2 * proj] = both
     message_ref[flat + 2 * proj :] = left_back[(2 * own_group + 1 - core) * prow_n + own_row]
     grads_ref[0] = left_back[(2 * own_group + core) * prow_n + own_row]
@@ -523,8 +523,9 @@
     grad_normed = dot(left_back.astype(BF16), left_ref[...], contract=(1, 1))
     grad_normed = grad_normed + dot(grads_ref[1], right_ref[...], contract=(1, 1))
     normed = normed_ref[...]
-    mean_factor = group_mean(grad_normed, features, lax.Precision.HIGHEST)
-    projected = group_mean(grad_normed * normed, features, lax.Precision.HIGHEST)
+    means = jnp.concatenate([grad_normed, grad_normed * normed], axis=0)
+    means = group_mean(means, features, lax.Precision.HIGHEST)
+    mean_factor, projected = means[: normed.shape[0]], means[normed.shape[0] :]
     result = inverse_ref[...] * (grad_normed - mean_factor - normed * projected)
     rows_out_ref[...] = jnp.stack(
         [result[:, t * features : (t + 1) * features] for t in range(rows_out_ref.shape[1])],

time: 35.3 us -> 35.2 us (level)
  no operation moved by 1% of the time
where the time goes in v14:
time: 35.2 us; the launch traced here: 34.9 us
  Pallas kernels  12.8 us (36%)
  starting transfers between devices  10.3 us (29%)
  waiting for transfers between devices  6.83 us (19%)
  local copies, waits for them, and re-layouts  4.21 us (12%)
  between operations  0.72 us (2%)
    ppermute x7, starting transfers between devices, swapped_with(): return lax.ppermute(values, axis, [(n, n ^ mask) for n in range(size)])  9.8 us
    pallas_call x1, Pallas kernels, local_gathered(): pl.pallas_call(functools.partial(pair_kernel, offsets), out_shape=(shape(...  7.19 us
    ppermute x7, waiting for transfers between devices, swapped_with(): return lax.ppermute(values, axis, [(n, n ^ mask) for n in range(size)])  5.62 us
    unnamed x19, local copies, waits for them, and re-layouts  3 us
    pallas_call x1, Pallas kernels, local_gathered(): pl.pallas_call(pick_kernel, out_shape=(shape((seqs, packed), F32), shape(...  2.15 us
    pallas_call x1, Pallas kernels, local_gathered(): pl.pallas_call(functools.partial(pull_kernel, offsets), out_shape=(shape(...  1.8 us
    pallas_call x1, Pallas kernels, local_gathered(): pl.pallas_call(close_kernel, out_shape=(shape((flat, pair_width), F32), s...  1.45 us
    ppermute x1, waiting for transfers between devices, local_gathered(): theirs = lax.ppermute(message, 'pc', [(0, 1), (1, 0)])  1.21 us
  transfers between devices with their start and end apart: 9, of which 5 were waited for; matrix products, arithmetic and copies ran while one was open for 4% of the time, Pallas kernels for 6%

profile of v14, /device:TPU:0, one launch (start us, length us, event | category | flops | bytes accessed | tf_op | source)
XLA Modules:
  0.0 34.9 jit_solution(12765971104059434085)
XLA Ops:
  0.6 2.1 %pick_rows.1 = (f32[64,256]{1,0:T(8,128)}, f32[64,256]{1,0:T(8,128)}, bf16[384,128]{1,0:T(8,128)(2,1)}) custom-call(s32[1,64]{1,0:T(1,128)} %bitcast.56, bf16[256,128]{1,0:T(8,128)(2,1)} %bitcast.54, bf16[256,128]{1,0:T(8,128)(2,1)} %bitcast.55), custom_call_target="tpu_custom_call" | custom-call | tf_op jit(solution)/shard_map/pick_rows/pallas_call | solution.py:561
  2.8 3.1 %collective-permute-start = (bf16[384,128]{1,0:T(8,128)(2,1)}, bf16[384,128]{1,0:T(8,128)(2,1)S(1)}, u32[]{:S(2)}, u32[]{:S(2)}) collective-permute-start(bf16[384,128]{1,0:T(8,128)(2,1)} %get-tuple-element.23.own_ref), channel_id=1, source_target_pairs={{0,4},{4,0},{8,12},{12,8},{1,5},{5,1},{9,13},{13,9},{2,6},{6,2},{1... | collective-permute-start | bytes 294920 | tf_op jit(solution)/shard_map/ppermute | solution.py:588
  5.9 2.6 %collective-permute-start.1 = (bf16[384,128]{1,0:T(8,128)(2,1)}, bf16[384,128]{1,0:T(8,128)(2,1)S(1)}, u32[]{:S(2)}, u32[]{:S(2)}) collective-permute-start(bf16[384,128]{1,0:T(8,128)(2,1)} %get-tuple-element.23.own_ref), channel_id=1, source_target_pairs={{0,8},{4,12},{8,0},{12,4},{1,9},{5,13},{9,1},{13,5},{2,10},{6,14},... | collective-permute-start | bytes 294920 | tf_op jit(solution)/shard_map/ppermute | solution.py:588
  8.5 1.7 %collective-permute-start.3 = (bf16[384,128]{1,0:T(8,128)(2,1)}, bf16[384,128]{1,0:T(8,128)(2,1)S(1)}, u32[]{:S(2)}, u32[]{:S(2)}) collective-permute-start(bf16[384,128]{1,0:T(8,128)(2,1)} %get-tuple-element.23.own_ref), channel_id=1, source_target_pairs={{0,2},{2,0},{1,3},{3,1},{4,6},{6,4},{5,7},{7,5},{8,10},{10,8},{9,1... | collective-permute-start | bytes 294920 | tf_op jit(solution)/shard_map/ppermute | solution.py:588
  10.2 1.1 %copy.12 = bf16[32,32,128]{2,0,1:T(8,128)(2,1)S(1)} copy(bf16[32,32,128]{2,1,0:T(8,128)(2,1)} %bitcast.53) | data formatting | bytes 524288 | tf_op jit(solution)/shard_map/reshape | solution.py:583
  11.2 0.1 copy.13.turned_mapping_ref.mapping_ref
  11.4 0.9 %copy-done = bf16[384,128]{1,0:T(8,128)(2,1)S(1)} copy-done((bf16[384,128]{1,0:T(8,128)(2,1)S(1)}, bf16[384,128]{1,0:T(8,128)(2,1)}, u32[]{:S(2)}) %copy-start) | copy-done | bytes 98328
  12.3 0.7 %copy-done.3 = bf16[64,32]{0,1:T(8,128)(2,1)S(1)} copy-done((bf16[64,32]{0,1:T(8,128)(2,1)S(1)}, bf16[64,32]{0,1:T(8,128)(2,1)}, u32[]{:S(2)}) %copy-start.3) | copy-done | bytes 4120
  13.0 0.7 %copy-done.4 = bf16[64,32]{0,1:T(8,128)(2,1)S(1)} copy-done((bf16[64,32]{0,1:T(8,128)(2,1)S(1)}, bf16[64,32]{0,1:T(8,128)(2,1)}, u32[]{:S(2)}) %copy-start.4) | copy-done | bytes 4120
  13.7 0.7 %copy-done.5 = f32[128]{0:T(128)S(1)} copy-done((f32[128]{0:T(128)S(1)}, f32[128]{0:T(128)}, u32[]{:S(2)}) %copy-start.5) | copy-done | bytes 536
  14.3 0.2 setup.1
  14.5 0.4 %collective-permute-start.4 = (bf16[384,128]{1,0:T(8,128)(2,1)S(1)}, bf16[384,128]{1,0:T(8,128)(2,1)S(1)}, u32[]{:S(2)}, u32[]{:S(2)}) collective-permute-start(bf16[384,128]{1,0:T(8,128)(2,1)S(1)} %get-tuple-element.25.refs_1_), channel_id=1, source_target_pairs={{0,2},{2,0},{1,3},{3,1},{4,6},{6,4},{5,7},{7,5},{8,10},{10,8},{9,1... | collective-permute-start | bytes 294920 | tf_op jit(solution)/shard_map/ppermute | solution.py:588
  14.9 1.6 %collective-permute-done.1.refs_2_ = bf16[384,128]{1,0:T(8,128)(2,1)S(1)} collective-permute-done((bf16[384,128]{1,0:T(8,128)(2,1)}, bf16[384,128]{1,0:T(8,128)(2,1)S(1)}, u32[]{:S(2)}, u32[]{:S(2)}) %collective-permute-start.1) | collective-permute-done | bytes 98336 | tf_op jit(solution)/shard_map/ppermute | solution.py:588
  16.5 1.5 %collective-permute-start.5 = (bf16[384,128]{1,0:T(8,128)(2,1)S(1)}, bf16[384,128]{1,0:T(8,128)(2,1)S(1)}, u32[]{:S(2)}, u32[]{:S(2)}) collective-permute-start(bf16[384,128]{1,0:T(8,128)(2,1)S(1)} %collective-permute-done.1.refs_2_), channel_id=1, source_target_pairs={{0,2},{2,0},{1,3},{3,1},{4,6},{6,4},{5,7},{7,5},{8,10},{10,8},{9,1... | collective-permute-start | bytes 294920 | tf_op jit(solution)/shard_map/ppermute | solution.py:588
  18.0 0.5 %collective-permute-start.6 = (bf16[384,128]{1,0:T(8,128)(2,1)S(1)}, bf16[384,128]{1,0:T(8,128)(2,1)S(1)}, u32[]{:S(2)}, u32[]{:S(2)}) collective-permute-start(bf16[384,128]{1,0:T(8,128)(2,1)S(1)} %collective-permute-done.2.refs_3_), channel_id=1, source_target_pairs={{0,2},{2,0},{1,3},{3,1},{4,6},{6,4},{5,7},{7,5},{8,10},{10,8},{9,1... | collective-permute-start | bytes 294920 | tf_op jit(solution)/shard_map/ppermute | solution.py:588
  18.6 1.6 %collective-permute-done.4.refs_5_ = bf16[384,128]{1,0:T(8,128)(2,1)S(1)} collective-permute-done((bf16[384,128]{1,0:T(8,128)(2,1)S(1)}, bf16[384,128]{1,0:T(8,128)(2,1)S(1)}, u32[]{:S(2)}, u32[]{:S(2)}) %collective-permute-start.4) | collective-permute-done | bytes 98336 | tf_op jit(solution)/shard_map/ppermute | solution.py:588
  20.2 1.0 %collective-permute-done.5.refs_6_ = bf16[384,128]{1,0:T(8,128)(2,1)S(1)} collective-permute-done((bf16[384,128]{1,0:T(8,128)(2,1)S(1)}, bf16[384,128]{1,0:T(8,128)(2,1)S(1)}, u32[]{:S(2)}, u32[]{:S(2)}) %collective-permute-start.5) | collective-permute-done | bytes 98336 | tf_op jit(solution)/shard_map/ppermute | solution.py:588
  21.2 1.4 %collective-permute-done.6.refs_7_ = bf16[384,128]{1,0:T(8,128)(2,1)S(1)} collective-permute-done((bf16[384,128]{1,0:T(8,128)(2,1)S(1)}, bf16[384,128]{1,0:T(8,128)(2,1)S(1)}, u32[]{:S(2)}, u32[]{:S(2)}) %collective-permute-start.6) | collective-permute-done | bytes 98336 | tf_op jit(solution)/shard_map/ppermute | solution.py:588
  22.7 0.1 pad_add_fusion.place_ref
  22.7 1.8 %pull_back.1 = (bf16[4,2,256,128]{3,2,1,0:T(8,128)(2,1)S(1)}, bf16[4,256,2048]{2,1,0:T(8,128)(2,1)S(1)}) custom-call(s32[3]{0:T(128)S(1)} %pad_add_fusion.place_ref, bf16[128,1024]{1,0:T(8,128)(2,1)S(1)} %copy.13.turned_mapping_ref.mapping_ref, bf16[384,128]{1,0:T(8,128)(2,1)S(1)} %get-tuple-element.24.refs_0_, ...), custom_call_target="tpu_custom_call" | custom-call | flops 536870912 | bytes 5242880 | tf_op jit(solution)/shard_map/pull_back/pallas_call | solution.py:627
  24.6 7.2 %pair_work.1 = (bf16[16,16,128]{2,1,0:T(8,128)(2,1)}, bf16[2,64,128]{2,1,0:T(8,128)(2,1)S(1)}, bf16[1152,128]{1,0:T(8,128)(2,1)S(1)}) custom-call(s32[3]{0:T(128)S(1)} %pad_add_fusion.place_ref, bf16[8,128,128]{2,1,0:T(8,128)(2,1)S(1)} %fusion.mine_from_ref, bf16[8,128,128]{2,1,0:T(8,128)(2,1)S(1)} %collective-permute-done.7.theirs_from_ref, ...), custom_call_target="tpu_custom_call" | custom-call | tf_op jit(solution)/shard_map/pair_work/pallas_call | solution.py:644
  31.7 0.5 %collective-permute-start.8 = (bf16[1152,128]{1,0:T(8,128)(2,1)S(1)}, bf16[1152,128]{1,0:T(8,128)(2,1)S(1)}, u32[]{:S(2)}, u32[]{:S(2)}) collective-permute-start(bf16[1152,128]{1,0:T(8,128)(2,1)S(1)} %get-tuple-element.33.own_ref), channel_id=1, source_target_pairs={{0,1},{1,0},{2,3},{3,2},{4,5},{5,4},{6,7},{7,6},{8,9},{9,8},{10,11... | collective-permute-start | bytes 884744 | tf_op jit(solution)/shard_map/ppermute | solution.py:670
  32.2 1.2 %collective-permute-done.8.message_ref = bf16[1152,128]{1,0:T(8,128)(2,1)S(1)} collective-permute-done((bf16[1152,128]{1,0:T(8,128)(2,1)S(1)}, bf16[1152,128]{1,0:T(8,128)(2,1)S(1)}, u32[]{:S(2)}, u32[]{:S(2)}) %collective-permute-start.8) | collective-permute-done | bytes 294944 | tf_op jit(solution)/shard_map/ppermute | solution.py:670
  33.5 1.5 %close.1 = (f32[1024,128]{1,0:T(8,128)}, f32[32,64]{1,0:T(8,128)}, f32[32,64]{1,0:T(8,128)}, bf16[64,4,64]{2,1,0:T(4,128)(2,1)}) custom-call(bf16[2,64,128]{2,1,0:T(8,128)(2,1)S(1)} %get-tuple-element.32.grads_ref, bf16[1152,128]{1,0:T(8,128)(2,1)S(1)} %get-tuple-element.33.own_ref, bf16[1152,128]{1,0:T(8,128)(2,1)S(1)} %collective-permute-done.8.message_ref, ...), custom_call_target="tpu_custom_call" | custom-call | tf_op jit(solution)/shard_map/close/pallas_call | solution.py:671
  (22 shorter events, 0.1 us)
Async XLA Ops:
  2.8 8.6 %collective-permute-start = (bf16[384,128]{1,0:T(8,128)(2,1)}, bf16[384,128]{1,0:T(8,128)(2,1)S(1)}, u32[]{:S(2)}, u32[]{:S(2)}) collective-permute-start(bf16[384,128]{1,0:T(8,128)(2,1)} %get-tuple-element.23.own_ref), channel_id=1, source_target_pairs={{0,4},{4,0},{8,12},{12,8},{1,5},{5,1},{9,13},{13,9},{2,6},{6,2},{1... | collective-permute-start | bytes 294920 | tf_op jit(solution)/shard_map/ppermute | solution.py:588
  5.9 10.6 %collective-permute-start.1 = (bf16[384,128]{1,0:T(8,128)(2,1)}, bf16[384,128]{1,0:T(8,128)(2,1)S(1)}, u32[]{:S(2)}, u32[]{:S(2)}) collective-permute-start(bf16[384,128]{1,0:T(8,128)(2,1)} %get-tuple-element.23.own_ref), channel_id=1, source_target_pairs={{0,8},{4,12},{8,0},{12,4},{1,9},{5,13},{9,1},{13,5},{2,10},{6,14},... | collective-permute-start | bytes 294920 | tf_op jit(solution)/shard_map/ppermute | solution.py:588
  8.5 9.6 %collective-permute-start.2 = (bf16[384,128]{1,0:T(8,128)(2,1)}, bf16[384,128]{1,0:T(8,128)(2,1)S(1)}, u32[]{:S(2)}, u32[]{:S(2)}) collective-permute-start(bf16[384,128]{1,0:T(8,128)(2,1)} %get-tuple-element.23.own_ref), channel_id=1, source_target_pairs={{0,12},{4,8},{8,4},{12,0},{1,13},{5,9},{9,5},{13,1},{2,14},{6,10},... | collective-permute-start | bytes 294920 | tf_op jit(solution)/shard_map/ppermute | solution.py:588
  8.5 10.1 %collective-permute-start.3 = (bf16[384,128]{1,0:T(8,128)(2,1)}, bf16[384,128]{1,0:T(8,128)(2,1)S(1)}, u32[]{:S(2)}, u32[]{:S(2)}) collective-permute-start(bf16[384,128]{1,0:T(8,128)(2,1)} %get-tuple-element.23.own_ref), channel_id=1, source_target_pairs={{0,2},{2,0},{1,3},{3,1},{4,6},{6,4},{5,7},{7,5},{8,10},{10,8},{9,1... | collective-permute-start | bytes 294920 | tf_op jit(solution)/shard_map/ppermute | solution.py:588
  11.4 0.9 %copy-start = (bf16[384,128]{1,0:T(8,128)(2,1)S(1)}, bf16[384,128]{1,0:T(8,128)(2,1)}, u32[]{:S(2)}) copy-start(bf16[384,128]{1,0:T(8,128)(2,1)} %get-tuple-element.23.own_ref) | copy-start | bytes 294916
  12.3 0.7 %copy-start.3 = (bf16[64,32]{0,1:T(8,128)(2,1)S(1)}, bf16[64,32]{0,1:T(8,128)(2,1)}, u32[]{:S(2)}) copy-start(bf16[64,32]{0,1:T(8,128)(2,1)} %param.9) | copy-start | bytes 12292
  13.0 0.7 %copy-start.4 = (bf16[64,32]{0,1:T(8,128)(2,1)S(1)}, bf16[64,32]{0,1:T(8,128)(2,1)}, u32[]{:S(2)}) copy-start(bf16[64,32]{0,1:T(8,128)(2,1)} %param.10) | copy-start | bytes 12292
  13.7 0.7 %copy-start.5 = (f32[128]{0:T(128)S(1)}, f32[128]{0:T(128)}, u32[]{:S(2)}) copy-start(f32[128]{0:T(128)} %param.12) | copy-start | bytes 1540
  14.5 5.6 %collective-permute-start.4 = (bf16[384,128]{1,0:T(8,128)(2,1)S(1)}, bf16[384,128]{1,0:T(8,128)(2,1)S(1)}, u32[]{:S(2)}, u32[]{:S(2)}) collective-permute-start(bf16[384,128]{1,0:T(8,128)(2,1)S(1)} %get-tuple-element.25.refs_1_), channel_id=1, source_target_pairs={{0,2},{2,0},{1,3},{3,1},{4,6},{6,4},{5,7},{7,5},{8,10},{10,8},{9,1... | collective-permute-start | bytes 294920 | tf_op jit(solution)/shard_map/ppermute | solution.py:588
  14.9 18.5 %copy-start.1 = (f32[64,256]{1,0:T(8,128)S(1)}, f32[64,256]{1,0:T(8,128)}, u32[]{:S(2)}) copy-start(f32[64,256]{1,0:T(8,128)} %get-tuple-element.34.normed_ref) | copy-start | bytes 196612
  14.9 18.5 %copy-start.2 = (f32[64,256]{1,0:T(8,128)S(1)}, f32[64,256]{1,0:T(8,128)}, u32[]{:S(2)}) copy-start(f32[64,256]{1,0:T(8,128)} %get-tuple-element.35.inverse_ref) | copy-start | bytes 196612
  16.5 4.7 %collective-permute-start.5 = (bf16[384,128]{1,0:T(8,128)(2,1)S(1)}, bf16[384,128]{1,0:T(8,128)(2,1)S(1)}, u32[]{:S(2)}, u32[]{:S(2)}) collective-permute-start(bf16[384,128]{1,0:T(8,128)(2,1)S(1)} %collective-permute-done.1.refs_2_), channel_id=1, source_target_pairs={{0,2},{2,0},{1,3},{3,1},{4,6},{6,4},{5,7},{7,5},{8,10},{10,8},{9,1... | collective-permute-start | bytes 294920 | tf_op jit(solution)/shard_map/ppermute | solution.py:588
  18.0 4.6 %collective-permute-start.6 = (bf16[384,128]{1,0:T(8,128)(2,1)S(1)}, bf16[384,128]{1,0:T(8,128)(2,1)S(1)}, u32[]{:S(2)}, u32[]{:S(2)}) collective-permute-start(bf16[384,128]{1,0:T(8,128)(2,1)S(1)} %collective-permute-done.2.refs_3_), channel_id=1, source_target_pairs={{0,2},{2,0},{1,3},{3,1},{4,6},{6,4},{5,7},{7,5},{8,10},{10,8},{9,1... | collective-permute-start | bytes 294920 | tf_op jit(solution)/shard_map/ppermute | solution.py:588
  22.6 1.9 %collective-permute-start.7 = (bf16[8,128,128]{2,1,0:T(8,128)(2,1)S(1)}, bf16[8,128,128]{2,1,0:T(8,128)(2,1)S(1)}, u32[]{:S(2)}, u32[]{:S(2)}) collective-permute-start(bf16[8,128,128]{2,1,0:T(8,128)(2,1)S(1)} %fusion.mine_from_ref), channel_id=1, source_target_pairs={{0,1},{1,0},{2,3},{3,2},{4,5},{5,4},{6,7},{7,6},{8,9},{9,8},{10,11... | collective-permute-start | bytes 786440 | tf_op jit(solution)/shard_map/ppermute | solution.py:622
  31.7 1.7 %collective-permute-start.8 = (bf16[1152,128]{1,0:T(8,128)(2,1)S(1)}, bf16[1152,128]{1,0:T(8,128)(2,1)S(1)}, u32[]{:S(2)}, u32[]{:S(2)}) collective-permute-start(bf16[1152,128]{1,0:T(8,128)(2,1)S(1)} %get-tuple-element.33.own_ref), channel_id=1, source_target_pairs={{0,1},{1,0},{2,3},{3,2},{4,5},{5,4},{6,7},{7,6},{8,9},{9,8},{10,11... | collective-permute-start | bytes 884744 | tf_op jit(solution)/shard_map/ppermute | solution.py:670

commit v15 on v14

--- a/solution.py
+++ b/solution.py
@@ -201,12 +201,21 @@
     return jnp.where(even, halves[0], halves[1]) + moved
 
 
-def group_mean(x, group, precision):
-    lanes = x.shape[1]
+def group_mean(x, group):
+    rows, lanes = x.shape
     rows_id = lax.broadcasted_iota(jnp.int32, (lanes, lanes), 0) // group
     cols_id = lax.broadcasted_iota(jnp.int32, (lanes, lanes), 1) // group
-    block = jnp.where(rows_id == cols_id, 1.0 / group, 0.0).astype(x.dtype)
-    return dot(x, block, precision=precision)
+    block = (rows_id == cols_id).astype(BF16)
+    pieces = [x.astype(BF16)]
+    if x.dtype == F32:
+        for _ in range(2):
+            x = x - pieces[-1].astype(F32)
+            pieces.append(x.astype(BF16))
+    total = dot(jnp.concatenate(pieces, axis=0), block)
+    total = functools.reduce(
+        jnp.add, [total[n * rows : (n + 1) * rows] for n in reversed(range(len(pieces)))]
+    )
+    return total * (1.0 / group)
 
 
 def pick_kernel(
@@ -240,9 +249,9 @@
         copy.wait()
     wanted = positions[...] == lax.broadcasted_iota(jnp.int32, (heads, seqs), 0)
     chosen = dot(wanted.astype(BF16), features[...], contract=(0, 1))
-    mean_factor = group_mean(chosen.astype(BF16), channels, None)
+    mean_factor = group_mean(chosen.astype(BF16), channels)
     centered = chosen - mean_factor
-    variance = group_mean(centered * centered, channels, lax.Precision.HIGHEST)
+    variance = group_mean(centered * centered, channels)
     inverse = lax.rsqrt(variance + 1e-05)
     normed = centered * inverse
     for n in range(packed // LANES):
@@ -524,7 +533,7 @@
     grad_normed = grad_normed + dot(grads_ref[1], right_ref[...], contract=(1, 1))
     normed = normed_ref[...]
     means = jnp.concatenate([grad_normed, grad_normed * normed], axis=0)
-    means = group_mean(means, features, lax.Precision.HIGHEST)
+    means = group_mean(means, features)
     mean_factor, projected = means[: normed.shape[0]], means[normed.shape[0] :]
     result = inverse_ref[...] * (grad_normed - mean_factor - normed * projected)
     rows_out_ref[...] = jnp.stack(

time: 35.2 us -> 35.1 us (level)
  no operation moved by 1% of the time
where the time goes in v15:
time: 35.1 us; the launch traced here: 34.8 us
  Pallas kernels  12.6 us (36%)
  starting transfers between devices  10.3 us (29%)
  waiting for transfers between devices  6.83 us (19%)
  local copies, waits for them, and re-layouts  4.21 us (12%)
  between operations  0.72 us (2%)
    ppermute x7, starting transfers between devices, swapped_with(): return lax.ppermute(values, axis, [(n, n ^ mask) for n in range(size)])  9.8 us
    pallas_call x1, Pallas kernels, local_gathered(): pl.pallas_call(functools.partial(pair_kernel, offsets), out_shape=(shape(...  7.19 us
    ppermute x7, waiting for transfers between devices, swapped_with(): return lax.ppermute(values, axis, [(n, n ^ mask) for n in range(size)])  5.62 us
    unnamed x19, local copies, waits for them, and re-layouts  3 us
    pallas_call x1, Pallas kernels, local_gathered(): pl.pallas_call(pick_kernel, out_shape=(shape((seqs, packed), F32), shape(...  2.06 us
    pallas_call x1, Pallas kernels, local_gathered(): pl.pallas_call(functools.partial(pull_kernel, offsets), out_shape=(shape(...  1.8 us
    pallas_call x1, Pallas kernels, local_gathered(): pl.pallas_call(close_kernel, out_shape=(shape((flat, pair_width), F32), s...  1.38 us
    ppermute x1, waiting for transfers between devices, local_gathered(): theirs = lax.ppermute(message, 'pc', [(0, 1), (1, 0)])  1.21 us
  transfers between devices with their start and end apart: 9, of which 5 were waited for; matrix products, arithmetic and copies ran while one was open for 4% of the time, Pallas kernels for 6%

profile of v15, /device:TPU:0, one launch (start us, length us, event | category | flops | bytes accessed | tf_op | source)
XLA Modules:
  0.0 34.8 jit_solution(15130293680894771579)
XLA Ops:
  0.6 2.1 %pick_rows.1 = (f32[64,256]{1,0:T(8,128)}, f32[64,256]{1,0:T(8,128)}, bf16[384,128]{1,0:T(8,128)(2,1)}) custom-call(s32[1,64]{1,0:T(1,128)} %bitcast.56, bf16[256,128]{1,0:T(8,128)(2,1)} %bitcast.54, bf16[256,128]{1,0:T(8,128)(2,1)} %bitcast.55), custom_call_target="tpu_custom_call" | custom-call | tf_op jit(solution)/shard_map/pick_rows/pallas_call | solution.py:570
  2.7 3.1 %collective-permute-start = (bf16[384,128]{1,0:T(8,128)(2,1)}, bf16[384,128]{1,0:T(8,128)(2,1)S(1)}, u32[]{:S(2)}, u32[]{:S(2)}) collective-permute-start(bf16[384,128]{1,0:T(8,128)(2,1)} %get-tuple-element.23.own_ref), channel_id=1, source_target_pairs={{0,4},{4,0},{8,12},{12,8},{1,5},{5,1},{9,13},{13,9},{2,6},{6,2},{1... | collective-permute-start | bytes 294920 | tf_op jit(solution)/shard_map/ppermute | solution.py:597
  5.8 2.6 %collective-permute-start.1 = (bf16[384,128]{1,0:T(8,128)(2,1)}, bf16[384,128]{1,0:T(8,128)(2,1)S(1)}, u32[]{:S(2)}, u32[]{:S(2)}) collective-permute-start(bf16[384,128]{1,0:T(8,128)(2,1)} %get-tuple-element.23.own_ref), channel_id=1, source_target_pairs={{0,8},{4,12},{8,0},{12,4},{1,9},{5,13},{9,1},{13,5},{2,10},{6,14},... | collective-permute-start | bytes 294920 | tf_op jit(solution)/shard_map/ppermute | solution.py:597
  8.4 1.7 %collective-permute-start.3 = (bf16[384,128]{1,0:T(8,128)(2,1)}, bf16[384,128]{1,0:T(8,128)(2,1)S(1)}, u32[]{:S(2)}, u32[]{:S(2)}) collective-permute-start(bf16[384,128]{1,0:T(8,128)(2,1)} %get-tuple-element.23.own_ref), channel_id=1, source_target_pairs={{0,2},{2,0},{1,3},{3,1},{4,6},{6,4},{5,7},{7,5},{8,10},{10,8},{9,1... | collective-permute-start | bytes 294920 | tf_op jit(solution)/shard_map/ppermute | solution.py:597
  10.1 1.1 %copy.12 = bf16[32,32,128]{2,0,1:T(8,128)(2,1)S(1)} copy(bf16[32,32,128]{2,1,0:T(8,128)(2,1)} %bitcast.53) | data formatting | bytes 524288 | tf_op jit(solution)/shard_map/reshape | solution.py:592
  11.2 0.1 copy.13.turned_mapping_ref.mapping_ref
  11.3 0.9 %copy-done = bf16[384,128]{1,0:T(8,128)(2,1)S(1)} copy-done((bf16[384,128]{1,0:T(8,128)(2,1)S(1)}, bf16[384,128]{1,0:T(8,128)(2,1)}, u32[]{:S(2)}) %copy-start) | copy-done | bytes 98328
  12.2 0.7 %copy-done.3 = bf16[64,32]{0,1:T(8,128)(2,1)S(1)} copy-done((bf16[64,32]{0,1:T(8,128)(2,1)S(1)}, bf16[64,32]{0,1:T(8,128)(2,1)}, u32[]{:S(2)}) %copy-start.3) | copy-done | bytes 4120
  12.9 0.7 %copy-done.4 = bf16[64,32]{0,1:T(8,128)(2,1)S(1)} copy-done((bf16[64,32]{0,1:T(8,128)(2,1)S(1)}, bf16[64,32]{0,1:T(8,128)(2,1)}, u32[]{:S(2)}) %copy-start.4) | copy-done | bytes 4120
  13.6 0.7 %copy-done.5 = f32[128]{0:T(128)S(1)} copy-done((f32[128]{0:T(128)S(1)}, f32[128]{0:T(128)}, u32[]{:S(2)}) %copy-start.5) | copy-done | bytes 536
  14.3 0.2 setup.1
  14.5 0.4 %collective-permute-start.4 = (bf16[384,128]{1,0:T(8,128)(2,1)S(1)}, bf16[384,128]{1,0:T(8,128)(2,1)S(1)}, u32[]{:S(2)}, u32[]{:S(2)}) collective-permute-start(bf16[384,128]{1,0:T(8,128)(2,1)S(1)} %get-tuple-element.25.refs_1_), channel_id=1, source_target_pairs={{0,2},{2,0},{1,3},{3,1},{4,6},{6,4},{5,7},{7,5},{8,10},{10,8},{9,1... | collective-permute-start | bytes 294920 | tf_op jit(solution)/shard_map/ppermute | solution.py:597
  14.9 1.6 %collective-permute-done.1.refs_2_ = bf16[384,128]{1,0:T(8,128)(2,1)S(1)} collective-permute-done((bf16[384,128]{1,0:T(8,128)(2,1)}, bf16[384,128]{1,0:T(8,128)(2,1)S(1)}, u32[]{:S(2)}, u32[]{:S(2)}) %collective-permute-start.1) | collective-permute-done | bytes 98336 | tf_op jit(solution)/shard_map/ppermute | solution.py:597
  16.4 1.5 %collective-permute-start.5 = (bf16[384,128]{1,0:T(8,128)(2,1)S(1)}, bf16[384,128]{1,0:T(8,128)(2,1)S(1)}, u32[]{:S(2)}, u32[]{:S(2)}) collective-permute-start(bf16[384,128]{1,0:T(8,128)(2,1)S(1)} %collective-permute-done.1.refs_2_), channel_id=1, source_target_pairs={{0,2},{2,0},{1,3},{3,1},{4,6},{6,4},{5,7},{7,5},{8,10},{10,8},{9,1... | collective-permute-start | bytes 294920 | tf_op jit(solution)/shard_map/ppermute | solution.py:597
  17.9 0.5 %collective-permute-start.6 = (bf16[384,128]{1,0:T(8,128)(2,1)S(1)}, bf16[384,128]{1,0:T(8,128)(2,1)S(1)}, u32[]{:S(2)}, u32[]{:S(2)}) collective-permute-start(bf16[384,128]{1,0:T(8,128)(2,1)S(1)} %collective-permute-done.2.refs_3_), channel_id=1, source_target_pairs={{0,2},{2,0},{1,3},{3,1},{4,6},{6,4},{5,7},{7,5},{8,10},{10,8},{9,1... | collective-permute-start | bytes 294920 | tf_op jit(solution)/shard_map/ppermute | solution.py:597
  18.5 1.6 %collective-permute-done.4.refs_5_ = bf16[384,128]{1,0:T(8,128)(2,1)S(1)} collective-permute-done((bf16[384,128]{1,0:T(8,128)(2,1)S(1)}, bf16[384,128]{1,0:T(8,128)(2,1)S(1)}, u32[]{:S(2)}, u32[]{:S(2)}) %collective-permute-start.4) | collective-permute-done | bytes 98336 | tf_op jit(solution)/shard_map/ppermute | solution.py:597
  20.1 1.0 %collective-permute-done.5.refs_6_ = bf16[384,128]{1,0:T(8,128)(2,1)S(1)} collective-permute-done((bf16[384,128]{1,0:T(8,128)(2,1)S(1)}, bf16[384,128]{1,0:T(8,128)(2,1)S(1)}, u32[]{:S(2)}, u32[]{:S(2)}) %collective-permute-start.5) | collective-permute-done | bytes 98336 | tf_op jit(solution)/shard_map/ppermute | solution.py:597
  21.2 1.4 %collective-permute-done.6.refs_7_ = bf16[384,128]{1,0:T(8,128)(2,1)S(1)} collective-permute-done((bf16[384,128]{1,0:T(8,128)(2,1)S(1)}, bf16[384,128]{1,0:T(8,128)(2,1)S(1)}, u32[]{:S(2)}, u32[]{:S(2)}) %collective-permute-start.6) | collective-permute-done | bytes 98336 | tf_op jit(solution)/shard_map/ppermute | solution.py:597
  22.6 0.1 pad_add_fusion.place_ref
  22.7 1.8 %pull_back.1 = (bf16[4,2,256,128]{3,2,1,0:T(8,128)(2,1)S(1)}, bf16[4,256,2048]{2,1,0:T(8,128)(2,1)S(1)}) custom-call(s32[3]{0:T(128)S(1)} %pad_add_fusion.place_ref, bf16[128,1024]{1,0:T(8,128)(2,1)S(1)} %copy.13.turned_mapping_ref.mapping_ref, bf16[384,128]{1,0:T(8,128)(2,1)S(1)} %get-tuple-element.24.refs_0_, ...), custom_call_target="tpu_custom_call" | custom-call | flops 536870912 | bytes 5242880 | tf_op jit(solution)/shard_map/pull_back/pallas_call | solution.py:636
  24.5 7.2 %pair_work.1 = (bf16[16,16,128]{2,1,0:T(8,128)(2,1)}, bf16[2,64,128]{2,1,0:T(8,128)(2,1)S(1)}, bf16[1152,128]{1,0:T(8,128)(2,1)S(1)}) custom-call(s32[3]{0:T(128)S(1)} %pad_add_fusion.place_ref, bf16[8,128,128]{2,1,0:T(8,128)(2,1)S(1)} %fusion.mine_from_ref, bf16[8,128,128]{2,1,0:T(8,128)(2,1)S(1)} %collective-permute-done.7.theirs_from_ref, ...), custom_call_target="tpu_custom_call" | custom-call | tf_op jit(solution)/shard_map/pair_work/pallas_call | solution.py:653
  31.7 0.5 %collective-permute-start.8 = (bf16[1152,128]{1,0:T(8,128)(2,1)S(1)}, bf16[1152,128]{1,0:T(8,128)(2,1)S(1)}, u32[]{:S(2)}, u32[]{:S(2)}) collective-permute-start(bf16[1152,128]{1,0:T(8,128)(2,1)S(1)} %get-tuple-element.33.own_ref), channel_id=1, source_target_pairs={{0,1},{1,0},{2,3},{3,2},{4,5},{5,4},{6,7},{7,6},{8,9},{9,8},{10,11... | collective-permute-start | bytes 884744 | tf_op jit(solution)/shard_map/ppermute | solution.py:679
  32.2 1.2 %collective-permute-done.8.message_ref = bf16[1152,128]{1,0:T(8,128)(2,1)S(1)} collective-permute-done((bf16[1152,128]{1,0:T(8,128)(2,1)S(1)}, bf16[1152,128]{1,0:T(8,128)(2,1)S(1)}, u32[]{:S(2)}, u32[]{:S(2)}) %collective-permute-start.8) | collective-permute-done | bytes 294944 | tf_op jit(solution)/shard_map/ppermute | solution.py:679
  33.4 1.4 %close.1 = (f32[1024,128]{1,0:T(8,128)}, f32[32,64]{1,0:T(8,128)}, f32[32,64]{1,0:T(8,128)}, bf16[64,4,64]{2,1,0:T(4,128)(2,1)}) custom-call(bf16[2,64,128]{2,1,0:T(8,128)(2,1)S(1)} %get-tuple-element.32.grads_ref, bf16[1152,128]{1,0:T(8,128)(2,1)S(1)} %get-tuple-element.33.own_ref, bf16[1152,128]{1,0:T(8,128)(2,1)S(1)} %collective-permute-done.8.message_ref, ...), custom_call_target="tpu_custom_call" | custom-call | tf_op jit(solution)/shard_map/close/pallas_call | solution.py:680
  (22 shorter events, 0.1 us)
Async XLA Ops:
  2.7 8.6 %collective-permute-start = (bf16[384,128]{1,0:T(8,128)(2,1)}, bf16[384,128]{1,0:T(8,128)(2,1)S(1)}, u32[]{:S(2)}, u32[]{:S(2)}) collective-permute-start(bf16[384,128]{1,0:T(8,128)(2,1)} %get-tuple-element.23.own_ref), channel_id=1, source_target_pairs={{0,4},{4,0},{8,12},{12,8},{1,5},{5,1},{9,13},{13,9},{2,6},{6,2},{1... | collective-permute-start | bytes 294920 | tf_op jit(solution)/shard_map/ppermute | solution.py:597
  5.8 10.6 %collective-permute-start.1 = (bf16[384,128]{1,0:T(8,128)(2,1)}, bf16[384,128]{1,0:T(8,128)(2,1)S(1)}, u32[]{:S(2)}, u32[]{:S(2)}) collective-permute-start(bf16[384,128]{1,0:T(8,128)(2,1)} %get-tuple-element.23.own_ref), channel_id=1, source_target_pairs={{0,8},{4,12},{8,0},{12,4},{1,9},{5,13},{9,1},{13,5},{2,10},{6,14},... | collective-permute-start | bytes 294920 | tf_op jit(solution)/shard_map/ppermute | solution.py:597
  8.4 9.6 %collective-permute-start.2 = (bf16[384,128]{1,0:T(8,128)(2,1)}, bf16[384,128]{1,0:T(8,128)(2,1)S(1)}, u32[]{:S(2)}, u32[]{:S(2)}) collective-permute-start(bf16[384,128]{1,0:T(8,128)(2,1)} %get-tuple-element.23.own_ref), channel_id=1, source_target_pairs={{0,12},{4,8},{8,4},{12,0},{1,13},{5,9},{9,5},{13,1},{2,14},{6,10},... | collective-permute-start | bytes 294920 | tf_op jit(solution)/shard_map/ppermute | solution.py:597
  8.4 10.1 %collective-permute-start.3 = (bf16[384,128]{1,0:T(8,128)(2,1)}, bf16[384,128]{1,0:T(8,128)(2,1)S(1)}, u32[]{:S(2)}, u32[]{:S(2)}) collective-permute-start(bf16[384,128]{1,0:T(8,128)(2,1)} %get-tuple-element.23.own_ref), channel_id=1, source_target_pairs={{0,2},{2,0},{1,3},{3,1},{4,6},{6,4},{5,7},{7,5},{8,10},{10,8},{9,1... | collective-permute-start | bytes 294920 | tf_op jit(solution)/shard_map/ppermute | solution.py:597
  11.3 0.9 %copy-start = (bf16[384,128]{1,0:T(8,128)(2,1)S(1)}, bf16[384,128]{1,0:T(8,128)(2,1)}, u32[]{:S(2)}) copy-start(bf16[384,128]{1,0:T(8,128)(2,1)} %get-tuple-element.23.own_ref) | copy-start | bytes 294916
  12.2 0.7 %copy-start.3 = (bf16[64,32]{0,1:T(8,128)(2,1)S(1)}, bf16[64,32]{0,1:T(8,128)(2,1)}, u32[]{:S(2)}) copy-start(bf16[64,32]{0,1:T(8,128)(2,1)} %param.9) | copy-start | bytes 12292
  12.9 0.7 %copy-start.4 = (bf16[64,32]{0,1:T(8,128)(2,1)S(1)}, bf16[64,32]{0,1:T(8,128)(2,1)}, u32[]{:S(2)}) copy-start(bf16[64,32]{0,1:T(8,128)(2,1)} %param.10) | copy-start | bytes 12292
  13.6 0.7 %copy-start.5 = (f32[128]{0:T(128)S(1)}, f32[128]{0:T(128)}, u32[]{:S(2)}) copy-start(f32[128]{0:T(128)} %param.12) | copy-start | bytes 1540
  14.5 5.6 %collective-permute-start.4 = (bf16[384,128]{1,0:T(8,128)(2,1)S(1)}, bf16[384,128]{1,0:T(8,128)(2,1)S(1)}, u32[]{:S(2)}, u32[]{:S(2)}) collective-permute-start(bf16[384,128]{1,0:T(8,128)(2,1)S(1)} %get-tuple-element.25.refs_1_), channel_id=1, source_target_pairs={{0,2},{2,0},{1,3},{3,1},{4,6},{6,4},{5,7},{7,5},{8,10},{10,8},{9,1... | collective-permute-start | bytes 294920 | tf_op jit(solution)/shard_map/ppermute | solution.py:597
  14.8 18.5 %copy-start.1 = (f32[64,256]{1,0:T(8,128)S(1)}, f32[64,256]{1,0:T(8,128)}, u32[]{:S(2)}) copy-start(f32[64,256]{1,0:T(8,128)} %get-tuple-element.34.normed_ref) | copy-start | bytes 196612
  14.8 18.5 %copy-start.2 = (f32[64,256]{1,0:T(8,128)S(1)}, f32[64,256]{1,0:T(8,128)}, u32[]{:S(2)}) copy-start(f32[64,256]{1,0:T(8,128)} %get-tuple-element.35.inverse_ref) | copy-start | bytes 196612
  16.4 4.7 %collective-permute-start.5 = (bf16[384,128]{1,0:T(8,128)(2,1)S(1)}, bf16[384,128]{1,0:T(8,128)(2,1)S(1)}, u32[]{:S(2)}, u32[]{:S(2)}) collective-permute-start(bf16[384,128]{1,0:T(8,128)(2,1)S(1)} %collective-permute-done.1.refs_2_), channel_id=1, source_target_pairs={{0,2},{2,0},{1,3},{3,1},{4,6},{6,4},{5,7},{7,5},{8,10},{10,8},{9,1... | collective-permute-start | bytes 294920 | tf_op jit(solution)/shard_map/ppermute | solution.py:597
  17.9 4.6 %collective-permute-start.6 = (bf16[384,128]{1,0:T(8,128)(2,1)S(1)}, bf16[384,128]{1,0:T(8,128)(2,1)S(1)}, u32[]{:S(2)}, u32[]{:S(2)}) collective-permute-start(bf16[384,128]{1,0:T(8,128)(2,1)S(1)} %collective-permute-done.2.refs_3_), channel_id=1, source_target_pairs={{0,2},{2,0},{1,3},{3,1},{4,6},{6,4},{5,7},{7,5},{8,10},{10,8},{9,1... | collective-permute-start | bytes 294920 | tf_op jit(solution)/shard_map/ppermute | solution.py:597
  22.6 1.9 %collective-permute-start.7 = (bf16[8,128,128]{2,1,0:T(8,128)(2,1)S(1)}, bf16[8,128,128]{2,1,0:T(8,128)(2,1)S(1)}, u32[]{:S(2)}, u32[]{:S(2)}) collective-permute-start(bf16[8,128,128]{2,1,0:T(8,128)(2,1)S(1)} %fusion.mine_from_ref), channel_id=1, source_target_pairs={{0,1},{1,0},{2,3},{3,2},{4,5},{5,4},{6,7},{7,6},{8,9},{9,8},{10,11... | collective-permute-start | bytes 786440 | tf_op jit(solution)/shard_map/ppermute | solution.py:631
  31.7 1.7 %collective-permute-start.8 = (bf16[1152,128]{1,0:T(8,128)(2,1)S(1)}, bf16[1152,128]{1,0:T(8,128)(2,1)S(1)}, u32[]{:S(2)}, u32[]{:S(2)}) collective-permute-start(bf16[1152,128]{1,0:T(8,128)(2,1)S(1)} %get-tuple-element.33.own_ref), channel_id=1, source_target_pairs={{0,1},{1,0},{2,3},{3,2},{4,5},{5,4},{6,7},{7,6},{8,9},{9,8},{10,11... | collective-permute-start | bytes 884744 | tf_op jit(solution)/shard_map/ppermute | solution.py:679

commit v16 on v15

--- a/solution.py
+++ b/solution.py
@@ -304,28 +304,37 @@
         out_ref[place_ref[0] ^ down, place_ref[1] ^ across] = block
 
 
-def pull_kernel(offsets, place_ref, mapping_ref, *refs):
+def pull_blocks(cot, mapping_ref, pulled_ref, r, at):
+    block_rows = pulled_ref.shape[2] // LANES
+    block_cols = cot.shape[0] // block_rows
+    grad = dot(cot, mapping_ref[...])
+    for h in range(mapping_ref.shape[1] // LANES):
+        there = pl.ds(pl.multiple_of(at + h * block_cols, block_cols), block_cols)
+        for t in range(block_rows):
+            pulled_ref[r, there, t * LANES : (t + 1) * LANES] = grad[
+                t * block_cols : (t + 1) * block_cols, h * LANES : (h + 1) * LANES
+            ].astype(BF16)
+
+
+def pull_own_kernel(downs, place_ref, mapping_ref, *refs):
+    *message_refs, pulled_ref, rows_ref = refs
+    pairs = message_refs[0].shape[0] - rows_ref.shape[1]
+    for n, (down, ref) in enumerate(zip(downs, message_refs, strict=True)):
+        rows_ref[n] = ref[pairs:]
+        pull_blocks(ref[:pairs], mapping_ref, pulled_ref, place_ref[0] ^ down, 0)
+
+
+def pull_kernel(offsets, place_ref, mapping_ref, own_ref, *refs):
     *message_refs, cot_ref, pulled_ref = refs
-    prow_n, groups, pairs, pair_width = cot_ref.shape
-    highs = mapping_ref.shape[1] // LANES
-    block_rows = pulled_ref.shape[2] // LANES
-    block_cols = pairs // block_rows
+    rows, groups, pairs, _ = cot_ref.shape
     place_blocks(place_ref, offsets, [ref[:pairs] for ref in message_refs], cot_ref)
-
-    def step(r, carry):
-        grad = dot(cot_ref[r].reshape(groups * pairs, pair_width), mapping_ref[...])
-        for g in range(groups):
-            for t in range(block_rows):
-                start = (g * block_rows + t) * block_cols
-                lanes = slice(t * LANES, (t + 1) * LANES)
-                for h in range(highs):
-                    there = slice((g * highs + h) * block_cols, (g * highs + h + 1) * block_cols)
-                    pulled_ref[r, there, lanes] = grad[
-                        start : start + block_cols, h * LANES : (h + 1) * LANES
-                    ].astype(BF16)
-        return carry
-
-    lax.fori_loop(0, prow_n, step, 0, unroll=True)
+    share = own_ref.shape[1]
+    for r in range(rows):
+        for across in range(1, groups):
+            group = place_ref[1] ^ across
+            pull_blocks(cot_ref[r, group], mapping_ref, pulled_ref, r, group * share)
+        at = pl.multiple_of(place_ref[1] * share, share)
+        pulled_ref[r, pl.ds(at, share)] = own_ref[r]
 
 
 def owner_order(places, prow_n, core):
@@ -627,29 +636,42 @@
     ]
     messages[0] = own
     offsets = [(down, across) for across in range(groups) for down in range(prow_n)]
-    rows = jnp.stack([one[pairs:] for one in messages])
+    place = jnp.stack([lax.axis_index("prow"), lax.axis_index("px"), lax.axis_index("pc")])
+
+    columns = groups * proj // tokens * block_cols
+    pull_cost = pl.CostEstimate(
+        flops=prow_n * groups * pairs * pair_width * flat,
+        bytes_accessed=prow_n * groups * pairs * (2 * pair_width + flat),
+        transcendentals=0,
+    )
+    pulled_own, rows_own = pl.pallas_call(
+        functools.partial(pull_own_kernel, [down for down, _ in offsets[:prow_n]]),
+        out_shape=(
+            shape((prow_n, columns // groups, block_rows * LANES), BF16),
+            shape((prow_n, length, LANES), BF16),
+        ),
+        in_specs=[smem] + [vmem] * (1 + prow_n),
+        out_specs=(vmem,) * 2,
+        compiler_params=params,
+        cost_estimate=pull_cost,
+        name="pull_own",
+    )(place, turned_mapping, *messages[:prow_n])
+    rows = jnp.concatenate(
+        [rows_own] + [one[None, pairs:] for one in messages[prow_n:]], axis=0
+    )
     theirs = lax.ppermute(rows, "pc", [(0, 1), (1, 0)])
-
-    place = jnp.stack([lax.axis_index("prow"), lax.axis_index("px"), lax.axis_index("pc")])
-
-    columns = groups * proj // tokens * block_cols
     cot, pulled = pl.pallas_call(
         functools.partial(pull_kernel, offsets),
         out_shape=(
             shape((prow_n, groups, pairs, pair_width), BF16),
             shape((prow_n, columns, block_rows * LANES), BF16),
         ),
-        in_specs=[smem] + [vmem] * (1 + len(messages)),
+        in_specs=[smem] + [vmem] * (2 + len(messages)),
         out_specs=(vmem,) * 2,
         compiler_params=params,
-        cost_estimate=pl.CostEstimate(
-            flops=2 * prow_n * groups * pairs * pair_width * flat,
-            bytes_accessed=2 * prow_n * groups * pairs * (2 * pair_width + flat),
-            transcendentals=0,
-        ),
+        cost_estimate=pull_cost,
         name="pull_back",
-    )(place, turned_mapping, *messages)
-
+    )(place, turned_mapping, pulled_own, *messages)
     pair_delta, grads, message = pl.pallas_call(
         functools.partial(pair_kernel, offsets),
         out_shape=(

time: 35.1 us -> 34.8 us (level)
  waiting for transfers between devices: 6.83 us -> 5.53 us
  Pallas kernels: 12.6 us -> 13.7 us
    ppermute x7, waiting for transfers between devices: 5.62 us -> 4.32 us  [swapped_with(): return lax.ppermute(values, axis, [(n, n ^ mask) for n in range(size)])]
    pallas_call x0 -> x1, Pallas kernels: none -> 1.23 us  [local_gathered(): pl.pallas_call(functools.partial(pull_own_kernel, [down for down, _ in of...]
    unnamed x19 -> x16, local copies, waits for them, and re-layouts: 3 us -> 2.99 us
  transfers between devices with their start and end apart: 9 -> 9, of which waited for: 5 -> 5; matrix products, arithmetic and copies ran while one was open for 4% -> 4% of each run, Pallas kernels for 6% -> 9%
where the time goes in v16:
time: 34.8 us; the launch traced here: 34.5 us
  Pallas kernels  13.7 us (39%)
  starting transfers between devices  10.3 us (30%)
  waiting for transfers between devices  5.53 us (16%)
  local copies, waits for them, and re-layouts  4.2 us (12%)
  between operations  0.74 us (2%)
    ppermute x7, starting transfers between devices, swapped_with(): return lax.ppermute(values, axis, [(n, n ^ mask) for n in range(size)])  9.8 us
    pallas_call x1, Pallas kernels, local_gathered(): pl.pallas_call(functools.partial(pair_kernel, offsets), out_shape=(shape(...  7.19 us
    ppermute x7, waiting for transfers between devices, swapped_with(): return lax.ppermute(values, axis, [(n, n ^ mask) for n in range(size)])  4.32 us
    unnamed x16, local copies, waits for them, and re-layouts  2.99 us
    pallas_call x1, Pallas kernels, local_gathered(): pl.pallas_call(pick_kernel, out_shape=(shape((seqs, packed), F32), shape(...  2.06 us
    pallas_call x1, Pallas kernels, local_gathered(): pl.pallas_call(functools.partial(pull_kernel, offsets), out_shape=(shape(...  1.63 us
    pallas_call x1, Pallas kernels, local_gathered(): pl.pallas_call(close_kernel, out_shape=(shape((flat, pair_width), F32), s...  1.39 us
    pallas_call x1, Pallas kernels, local_gathered(): pl.pallas_call(functools.partial(pull_own_kernel, [down for down, _ in of...  1.23 us
  transfers between devices with their start and end apart: 9, of which 5 were waited for; matrix products, arithmetic and copies ran while one was open for 4% of the time, Pallas kernels for 9%

profile of v16, /device:TPU:0, one launch (start us, length us, event | category | flops | bytes accessed | tf_op | source)
XLA Modules:
  0.0 34.5 jit_solution(17358002163814523715)
XLA Ops:
  0.6 2.1 %pick_rows.1 = (f32[64,256]{1,0:T(8,128)}, f32[64,256]{1,0:T(8,128)}, bf16[384,128]{1,0:T(8,128)(2,1)}) custom-call(s32[1,64]{1,0:T(1,128)} %bitcast.44, bf16[256,128]{1,0:T(8,128)(2,1)} %bitcast.42, bf16[256,128]{1,0:T(8,128)(2,1)} %bitcast.43), custom_call_target="tpu_custom_call" | custom-call | tf_op jit(solution)/shard_map/pick_rows/pallas_call | solution.py:579
  2.7 3.1 %collective-permute-start = (bf16[384,128]{1,0:T(8,128)(2,1)}, bf16[384,128]{1,0:T(8,128)(2,1)S(1)}, u32[]{:S(2)}, u32[]{:S(2)}) collective-permute-start(bf16[384,128]{1,0:T(8,128)(2,1)} %get-tuple-element.25.own_ref), channel_id=1, source_target_pairs={{0,4},{4,0},{8,12},{12,8},{1,5},{5,1},{9,13},{13,9},{2,6},{6,2},{1... | collective-permute-start | bytes 294920 | tf_op jit(solution)/shard_map/ppermute | solution.py:606
  5.8 2.6 %collective-permute-start.1 = (bf16[384,128]{1,0:T(8,128)(2,1)}, bf16[384,128]{1,0:T(8,128)(2,1)S(1)}, u32[]{:S(2)}, u32[]{:S(2)}) collective-permute-start(bf16[384,128]{1,0:T(8,128)(2,1)} %get-tuple-element.25.own_ref), channel_id=1, source_target_pairs={{0,8},{4,12},{8,0},{12,4},{1,9},{5,13},{9,1},{13,5},{2,10},{6,14},... | collective-permute-start | bytes 294920 | tf_op jit(solution)/shard_map/ppermute | solution.py:606
  8.4 1.7 %collective-permute-start.3 = (bf16[384,128]{1,0:T(8,128)(2,1)}, bf16[384,128]{1,0:T(8,128)(2,1)S(1)}, u32[]{:S(2)}, u32[]{:S(2)}) collective-permute-start(bf16[384,128]{1,0:T(8,128)(2,1)} %get-tuple-element.25.own_ref), channel_id=1, source_target_pairs={{0,2},{2,0},{1,3},{3,1},{4,6},{6,4},{5,7},{7,5},{8,10},{10,8},{9,1... | collective-permute-start | bytes 294920 | tf_op jit(solution)/shard_map/ppermute | solution.py:606
  10.1 1.1 %copy.12 = bf16[32,32,128]{2,0,1:T(8,128)(2,1)S(1)} copy(bf16[32,32,128]{2,1,0:T(8,128)(2,1)} %bitcast.41) | data formatting | bytes 524288 | tf_op jit(solution)/shard_map/reshape | solution.py:601
  11.2 0.1 copy.14.turned_mapping_ref.mapping_ref
  11.4 0.9 %copy-done = bf16[384,128]{1,0:T(8,128)(2,1)S(1)} copy-done((bf16[384,128]{1,0:T(8,128)(2,1)S(1)}, bf16[384,128]{1,0:T(8,128)(2,1)}, u32[]{:S(2)}) %copy-start) | copy-done | bytes 98328
  12.3 0.7 %copy-done.3 = bf16[64,32]{0,1:T(8,128)(2,1)S(1)} copy-done((bf16[64,32]{0,1:T(8,128)(2,1)S(1)}, bf16[64,32]{0,1:T(8,128)(2,1)}, u32[]{:S(2)}) %copy-start.3) | copy-done | bytes 4120
  13.0 0.7 %copy-done.4 = bf16[64,32]{0,1:T(8,128)(2,1)S(1)} copy-done((bf16[64,32]{0,1:T(8,128)(2,1)S(1)}, bf16[64,32]{0,1:T(8,128)(2,1)}, u32[]{:S(2)}) %copy-start.4) | copy-done | bytes 4120
  13.7 0.7 %copy-done.5 = f32[128]{0:T(128)S(1)} copy-done((f32[128]{0:T(128)S(1)}, f32[128]{0:T(128)}, u32[]{:S(2)}) %copy-start.5) | copy-done | bytes 536
  14.3 0.2 setup.1
  14.5 0.4 %collective-permute-start.4 = (bf16[384,128]{1,0:T(8,128)(2,1)S(1)}, bf16[384,128]{1,0:T(8,128)(2,1)S(1)}, u32[]{:S(2)}, u32[]{:S(2)}) collective-permute-start(bf16[384,128]{1,0:T(8,128)(2,1)S(1)} %get-tuple-element.27.refs_1_), channel_id=1, source_target_pairs={{0,2},{2,0},{1,3},{3,1},{4,6},{6,4},{5,7},{7,5},{8,10},{10,8},{9,1... | collective-permute-start | bytes 294920 | tf_op jit(solution)/shard_map/ppermute | solution.py:606
  14.9 1.5 %collective-permute-done.1.refs_2_ = bf16[384,128]{1,0:T(8,128)(2,1)S(1)} collective-permute-done((bf16[384,128]{1,0:T(8,128)(2,1)}, bf16[384,128]{1,0:T(8,128)(2,1)S(1)}, u32[]{:S(2)}, u32[]{:S(2)}) %collective-permute-start.1) | collective-permute-done | bytes 98336 | tf_op jit(solution)/shard_map/ppermute | solution.py:606
  16.4 1.5 %collective-permute-start.5 = (bf16[384,128]{1,0:T(8,128)(2,1)S(1)}, bf16[384,128]{1,0:T(8,128)(2,1)S(1)}, u32[]{:S(2)}, u32[]{:S(2)}) collective-permute-start(bf16[384,128]{1,0:T(8,128)(2,1)S(1)} %collective-permute-done.1.refs_2_), channel_id=1, source_target_pairs={{0,2},{2,0},{1,3},{3,1},{4,6},{6,4},{5,7},{7,5},{8,10},{10,8},{9,1... | collective-permute-start | bytes 294920 | tf_op jit(solution)/shard_map/ppermute | solution.py:606
  17.9 0.5 %collective-permute-start.6 = (bf16[384,128]{1,0:T(8,128)(2,1)S(1)}, bf16[384,128]{1,0:T(8,128)(2,1)S(1)}, u32[]{:S(2)}, u32[]{:S(2)}) collective-permute-start(bf16[384,128]{1,0:T(8,128)(2,1)S(1)} %collective-permute-done.2.refs_3_), channel_id=1, source_target_pairs={{0,2},{2,0},{1,3},{3,1},{4,6},{6,4},{5,7},{7,5},{8,10},{10,8},{9,1... | collective-permute-start | bytes 294920 | tf_op jit(solution)/shard_map/ppermute | solution.py:606
  18.5 1.2 %pull_own.1 = (bf16[4,128,2048]{2,1,0:T(8,128)(2,1)S(1)}, bf16[4,128,128]{2,1,0:T(8,128)(2,1)S(1)}) custom-call(s32[3]{0:T(128)S(1)} %pad_add_fusion.place_ref, bf16[128,1024]{1,0:T(8,128)(2,1)S(1)} %copy.14.turned_mapping_ref.mapping_ref, bf16[384,128]{1,0:T(8,128)(2,1)S(1)} %get-tuple-element.26.refs_0_, bf16[384,128]{1,0:T(8,128)(2,1)S(1)} %get-tuple-element.27.refs_1_, ...), custom_call_target="tpu_custom_call" | custom-call | flops 268435456 | bytes 2621440 | tf_op jit(solution)/shard_map/pull_own/pallas_call | solution.py:647
  19.8 0.4 %collective-permute-done.4.refs_5_ = bf16[384,128]{1,0:T(8,128)(2,1)S(1)} collective-permute-done((bf16[384,128]{1,0:T(8,128)(2,1)S(1)}, bf16[384,128]{1,0:T(8,128)(2,1)S(1)}, u32[]{:S(2)}, u32[]{:S(2)}) %collective-permute-start.4) | collective-permute-done | bytes 98336 | tf_op jit(solution)/shard_map/ppermute | solution.py:606
  20.2 1.0 %collective-permute-done.5.refs_6_ = bf16[384,128]{1,0:T(8,128)(2,1)S(1)} collective-permute-done((bf16[384,128]{1,0:T(8,128)(2,1)S(1)}, bf16[384,128]{1,0:T(8,128)(2,1)S(1)}, u32[]{:S(2)}, u32[]{:S(2)}) %collective-permute-start.5) | collective-permute-done | bytes 98336 | tf_op jit(solution)/shard_map/ppermute | solution.py:606
  21.2 1.3 %collective-permute-done.6.refs_7_ = bf16[384,128]{1,0:T(8,128)(2,1)S(1)} collective-permute-done((bf16[384,128]{1,0:T(8,128)(2,1)S(1)}, bf16[384,128]{1,0:T(8,128)(2,1)S(1)}, u32[]{:S(2)}, u32[]{:S(2)}) %collective-permute-start.6) | collective-permute-done | bytes 98336 | tf_op jit(solution)/shard_map/ppermute | solution.py:606
  22.6 1.6 %pull_back.1 = (bf16[4,2,256,128]{3,2,1,0:T(8,128)(2,1)S(1)}, bf16[4,256,2048]{2,1,0:T(8,128)(2,1)S(1)}) custom-call(s32[3]{0:T(128)S(1)} %pad_add_fusion.place_ref, bf16[128,1024]{1,0:T(8,128)(2,1)S(1)} %copy.14.turned_mapping_ref.mapping_ref, bf16[4,128,2048]{2,1,0:T(8,128)(2,1)S(1)} %get-tuple-element.32.own_ref, ...), custom_call_target="tpu_custom_call" | custom-call | flops 268435456 | bytes 2621440 | tf_op jit(solution)/shard_map/pull_back/pallas_call | solution.py:663
  24.2 7.2 %pair_work.1 = (bf16[16,16,128]{2,1,0:T(8,128)(2,1)}, bf16[2,64,128]{2,1,0:T(8,128)(2,1)S(1)}, bf16[1152,128]{1,0:T(8,128)(2,1)S(1)}) custom-call(s32[3]{0:T(128)S(1)} %pad_add_fusion.place_ref, bf16[8,128,128]{2,1,0:T(8,128)(2,1)S(1)} %fusion.mine_from_ref, bf16[8,128,128]{2,1,0:T(8,128)(2,1)S(1)} %collective-permute-done.7.theirs_from_ref, ...), custom_call_target="tpu_custom_call" | custom-call | tf_op jit(solution)/shard_map/pair_work/pallas_call | solution.py:675
  31.4 0.5 %collective-permute-start.8 = (bf16[1152,128]{1,0:T(8,128)(2,1)S(1)}, bf16[1152,128]{1,0:T(8,128)(2,1)S(1)}, u32[]{:S(2)}, u32[]{:S(2)}) collective-permute-start(bf16[1152,128]{1,0:T(8,128)(2,1)S(1)} %get-tuple-element.37.own_ref), channel_id=1, source_target_pairs={{0,1},{1,0},{2,3},{3,2},{4,5},{5,4},{6,7},{7,6},{8,9},{9,8},{10,11... | collective-permute-start | bytes 884744 | tf_op jit(solution)/shard_map/ppermute | solution.py:701
  31.9 1.2 %collective-permute-done.8.message_ref = bf16[1152,128]{1,0:T(8,128)(2,1)S(1)} collective-permute-done((bf16[1152,128]{1,0:T(8,128)(2,1)S(1)}, bf16[1152,128]{1,0:T(8,128)(2,1)S(1)}, u32[]{:S(2)}, u32[]{:S(2)}) %collective-permute-start.8) | collective-permute-done | bytes 294944 | tf_op jit(solution)/shard_map/ppermute | solution.py:701
  33.1 1.4 %close.1 = (f32[1024,128]{1,0:T(8,128)}, f32[32,64]{1,0:T(8,128)}, f32[32,64]{1,0:T(8,128)}, bf16[64,4,64]{2,1,0:T(4,128)(2,1)}) custom-call(bf16[2,64,128]{2,1,0:T(8,128)(2,1)S(1)} %get-tuple-element.36.grads_ref, bf16[1152,128]{1,0:T(8,128)(2,1)S(1)} %get-tuple-element.37.own_ref, bf16[1152,128]{1,0:T(8,128)(2,1)S(1)} %collective-permute-done.8.message_ref, ...), custom_call_target="tpu_custom_call" | custom-call | tf_op jit(solution)/shard_map/close/pallas_call | solution.py:702
  (20 shorter events, 0.2 us)
Async XLA Ops:
  2.7 8.7 %collective-permute-start = (bf16[384,128]{1,0:T(8,128)(2,1)}, bf16[384,128]{1,0:T(8,128)(2,1)S(1)}, u32[]{:S(2)}, u32[]{:S(2)}) collective-permute-start(bf16[384,128]{1,0:T(8,128)(2,1)} %get-tuple-element.25.own_ref), channel_id=1, source_target_pairs={{0,4},{4,0},{8,12},{12,8},{1,5},{5,1},{9,13},{13,9},{2,6},{6,2},{1... | collective-permute-start | bytes 294920 | tf_op jit(solution)/shard_map/ppermute | solution.py:606
  5.8 10.6 %collective-permute-start.1 = (bf16[384,128]{1,0:T(8,128)(2,1)}, bf16[384,128]{1,0:T(8,128)(2,1)S(1)}, u32[]{:S(2)}, u32[]{:S(2)}) collective-permute-start(bf16[384,128]{1,0:T(8,128)(2,1)} %get-tuple-element.25.own_ref), channel_id=1, source_target_pairs={{0,8},{4,12},{8,0},{12,4},{1,9},{5,13},{9,1},{13,5},{2,10},{6,14},... | collective-permute-start | bytes 294920 | tf_op jit(solution)/shard_map/ppermute | solution.py:606
  8.4 9.6 %collective-permute-start.2 = (bf16[384,128]{1,0:T(8,128)(2,1)}, bf16[384,128]{1,0:T(8,128)(2,1)S(1)}, u32[]{:S(2)}, u32[]{:S(2)}) collective-permute-start(bf16[384,128]{1,0:T(8,128)(2,1)} %get-tuple-element.25.own_ref), channel_id=1, source_target_pairs={{0,12},{4,8},{8,4},{12,0},{1,13},{5,9},{9,5},{13,1},{2,14},{6,10},... | collective-permute-start | bytes 294920 | tf_op jit(solution)/shard_map/ppermute | solution.py:606
  8.4 11.3 %collective-permute-start.3 = (bf16[384,128]{1,0:T(8,128)(2,1)}, bf16[384,128]{1,0:T(8,128)(2,1)S(1)}, u32[]{:S(2)}, u32[]{:S(2)}) collective-permute-start(bf16[384,128]{1,0:T(8,128)(2,1)} %get-tuple-element.25.own_ref), channel_id=1, source_target_pairs={{0,2},{2,0},{1,3},{3,1},{4,6},{6,4},{5,7},{7,5},{8,10},{10,8},{9,1... | collective-permute-start | bytes 294920 | tf_op jit(solution)/shard_map/ppermute | solution.py:606
  11.4 0.9 %copy-start = (bf16[384,128]{1,0:T(8,128)(2,1)S(1)}, bf16[384,128]{1,0:T(8,128)(2,1)}, u32[]{:S(2)}) copy-start(bf16[384,128]{1,0:T(8,128)(2,1)} %get-tuple-element.25.own_ref) | copy-start | bytes 294916
  12.3 0.7 %copy-start.3 = (bf16[64,32]{0,1:T(8,128)(2,1)S(1)}, bf16[64,32]{0,1:T(8,128)(2,1)}, u32[]{:S(2)}) copy-start(bf16[64,32]{0,1:T(8,128)(2,1)} %param.9) | copy-start | bytes 12292
  13.0 0.7 %copy-start.4 = (bf16[64,32]{0,1:T(8,128)(2,1)S(1)}, bf16[64,32]{0,1:T(8,128)(2,1)}, u32[]{:S(2)}) copy-start(bf16[64,32]{0,1:T(8,128)(2,1)} %param.10) | copy-start | bytes 12292
  13.7 0.7 %copy-start.5 = (f32[128]{0:T(128)S(1)}, f32[128]{0:T(128)}, u32[]{:S(2)}) copy-start(f32[128]{0:T(128)} %param.12) | copy-start | bytes 1540
  14.5 5.6 %collective-permute-start.4 = (bf16[384,128]{1,0:T(8,128)(2,1)S(1)}, bf16[384,128]{1,0:T(8,128)(2,1)S(1)}, u32[]{:S(2)}, u32[]{:S(2)}) collective-permute-start(bf16[384,128]{1,0:T(8,128)(2,1)S(1)} %get-tuple-element.27.refs_1_), channel_id=1, source_target_pairs={{0,2},{2,0},{1,3},{3,1},{4,6},{6,4},{5,7},{7,5},{8,10},{10,8},{9,1... | collective-permute-start | bytes 294920 | tf_op jit(solution)/shard_map/ppermute | solution.py:606
  16.4 4.8 %collective-permute-start.5 = (bf16[384,128]{1,0:T(8,128)(2,1)S(1)}, bf16[384,128]{1,0:T(8,128)(2,1)S(1)}, u32[]{:S(2)}, u32[]{:S(2)}) collective-permute-start(bf16[384,128]{1,0:T(8,128)(2,1)S(1)} %collective-permute-done.1.refs_2_), channel_id=1, source_target_pairs={{0,2},{2,0},{1,3},{3,1},{4,6},{6,4},{5,7},{7,5},{8,10},{10,8},{9,1... | collective-permute-start | bytes 294920 | tf_op jit(solution)/shard_map/ppermute | solution.py:606
  17.9 4.6 %collective-permute-start.6 = (bf16[384,128]{1,0:T(8,128)(2,1)S(1)}, bf16[384,128]{1,0:T(8,128)(2,1)S(1)}, u32[]{:S(2)}, u32[]{:S(2)}) collective-permute-start(bf16[384,128]{1,0:T(8,128)(2,1)S(1)} %collective-permute-done.2.refs_3_), channel_id=1, source_target_pairs={{0,2},{2,0},{1,3},{3,1},{4,6},{6,4},{5,7},{7,5},{8,10},{10,8},{9,1... | collective-permute-start | bytes 294920 | tf_op jit(solution)/shard_map/ppermute | solution.py:606
  22.6 1.7 %collective-permute-start.7 = (bf16[8,128,128]{2,1,0:T(8,128)(2,1)S(1)}, bf16[8,128,128]{2,1,0:T(8,128)(2,1)S(1)}, u32[]{:S(2)}, u32[]{:S(2)}) collective-permute-start(bf16[8,128,128]{2,1,0:T(8,128)(2,1)S(1)} %fusion.mine_from_ref), channel_id=1, source_target_pairs={{0,1},{1,0},{2,3},{3,2},{4,5},{5,4},{6,7},{7,6},{8,9},{9,8},{10,11... | collective-permute-start | bytes 786440 | tf_op jit(solution)/shard_map/ppermute | solution.py:662
  22.6 10.6 %copy-start.1 = (f32[64,256]{1,0:T(8,128)S(1)}, f32[64,256]{1,0:T(8,128)}, u32[]{:S(2)}) copy-start(f32[64,256]{1,0:T(8,128)} %get-tuple-element.38.normed_ref) | copy-start | bytes 196612
  22.6 10.5 %copy-start.2 = (f32[64,256]{1,0:T(8,128)S(1)}, f32[64,256]{1,0:T(8,128)}, u32[]{:S(2)}) copy-start(f32[64,256]{1,0:T(8,128)} %get-tuple-element.39.inverse_ref) | copy-start | bytes 196612
  31.4 1.7 %collective-permute-start.8 = (bf16[1152,128]{1,0:T(8,128)(2,1)S(1)}, bf16[1152,128]{1,0:T(8,128)(2,1)S(1)}, u32[]{:S(2)}, u32[]{:S(2)}) collective-permute-start(bf16[1152,128]{1,0:T(8,128)(2,1)S(1)} %get-tuple-element.37.own_ref), channel_id=1, source_target_pairs={{0,1},{1,0},{2,3},{3,2},{4,5},{5,4},{6,7},{7,6},{8,9},{9,8},{10,11... | collective-permute-start | bytes 884744 | tf_op jit(solution)/shard_map/ppermute | solution.py:701

commit v17 on v16

--- a/solution.py
+++ b/solution.py
@@ -187,9 +187,14 @@
     return lax.broadcasted_iota(jnp.int32, shape, len(shape) - 1)
 
 
+def lane_groups(shape, width):
+    row = lax.broadcasted_iota(jnp.int32, (1, shape[1]), 1) % LANES // width
+    return jnp.broadcast_to(row, shape)
+
+
 def fold_tokens(parts):
     quarter = LANES // 4
-    chunk = lane_ids(parts[0].shape) // quarter
+    chunk = lane_groups(parts[0].shape, quarter)
     first, even = chunk < 2, chunk % 2 == 0
     halves = [
         jnp.where(first, parts[t], parts[t + 2])
@@ -276,6 +281,7 @@
     left_one_ref,
     right_one_ref,
     offset_out_ref,
+    shuffle_ref,
 ):
     del mapping_ref, turned_mapping_ref
     first_out_ref[...] = first_ref[...]
@@ -283,6 +289,13 @@
     offset_out_ref[...] = offset_ref[...]
     proj, channels = left_ref.shape
     tokens = left_one_ref.shape[0] // channels
+    wide, highs = shuffle_ref.shape[0], proj // tokens
+    block_cols = wide // proj
+    target = lax.broadcasted_iota(jnp.int32, (1, wide), 1)
+    jj, qh = target % block_cols, target // block_cols % highs
+    source = jj * proj + qh * tokens + target // (highs * block_cols)
+    rows_id = lax.broadcasted_iota(jnp.int32, (wide, wide), 0)
+    shuffle_ref[...] = (rows_id == jnp.broadcast_to(source, (wide, wide))).astype(BF16)
     repeat = lane_ids((proj, LANES)) % proj
     repeat = (repeat == lax.broadcasted_iota(jnp.int32, (proj, LANES), 0)).astype(BF16)
     left_row = dot(left_ref[...], repeat, contract=(0, 0))
@@ -342,18 +355,9 @@
     return mine + [(2 * g + 1 - core) * prow_n + r for g, r in places]
 
 
-def shuffle_matrix(block_cols, proj, tokens):
-    wide, highs = block_cols * proj, proj // tokens
-    source = lax.broadcasted_iota(jnp.int32, (wide, wide), 0)
-    target = lax.broadcasted_iota(jnp.int32, (wide, wide), 1)
-    jj, qh = target % block_cols, target // block_cols % highs
-    ql = target // (highs * block_cols)
-    return (source == jj * proj + qh * tokens + ql).astype(BF16)
-
-
 def left_block(expanded, row, step_owners, tokens):
     ahead = jnp.concatenate([expanded[row * step_owners + o] for o in range(step_owners)], axis=1)
-    low = lane_ids(ahead.shape) % LANES // (LANES // tokens)
+    low = lane_groups(ahead.shape, LANES // tokens)
     return jnp.concatenate(
         [jnp.where(low == l, ahead, jnp.zeros_like(ahead)) for l in range(tokens)], axis=0
     )
@@ -368,6 +372,7 @@
     left_ref,
     right_ref,
     offset_ref,
+    shuffle_ref,
     cot_ref,
     pulled_ref,
     pair_ref,
@@ -418,7 +423,7 @@
         side_rows.append(
             jnp.concatenate([dot(x, right_ref[...]).astype(BF16) for x in chunks], axis=1)
         )
-    right = dot(jnp.concatenate(side_rows, axis=0), shuffle_matrix(block_cols, proj, tokens))
+    right = dot(jnp.concatenate(side_rows, axis=0), shuffle_ref[...])
     for g in range(groups):
         for l in range(tokens):
             swapped[l * seqs : (l + 1) * seqs, g * span : (g + 1) * span] = (
@@ -456,7 +461,7 @@
             message_ref[:flat] = weight_rows.astype(BF16)
         pulled = pulled_ref[row]
         back = dot(swapped[...], pulled)
-        low = lane_ids((seqs, back.shape[1])) % LANES // proj
+        low = lane_groups((seqs, back.shape[1]), proj)
         back = functools.reduce(
             jnp.add,
             [
@@ -487,8 +492,7 @@
         ],
         axis=0,
     )
-    shuffle = shuffle_matrix(block_cols, proj, tokens)
-    back = dot(back, shuffle, contract=(1, 1)).astype(BF16)
+    back = dot(back, shuffle_ref[...], contract=(1, 1)).astype(BF16)
     for g, r in places:
         right_back[g * prow_n + r] = back[g * seqs : (g + 1) * seqs, r * LANES : (r + 1) * LANES]
 
@@ -608,7 +612,7 @@
     messages = [sent] + [
         swapped_with(sent, "prow", prow_n, down) for down in range(1, prow_n)
     ]
-    messages[1], own, left_wide, left_one, right_one, offset = pl.pallas_call(
+    messages[1], own, left_wide, left_one, right_one, offset, shuffle = pl.pallas_call(
         setup_kernel,
         out_shape=(
             shape(sent.shape, BF16),
@@ -617,9 +621,10 @@
             shape((packed, LANES), BF16),
             shape((packed, LANES), BF16),
             shape((1, pair_width), F32),
+            shape((block_cols * proj, block_cols * proj), BF16),
         ),
         in_specs=[vmem] * 7,
-        out_specs=(vmem,) * 6,
+        out_specs=(vmem,) * 7,
         compiler_params=params,
         name="setup",
     )(
@@ -679,7 +684,7 @@
             shape((2, seqs, LANES), BF16),
             shape((flat + 2 * proj + seqs, LANES), BF16),
         ),
-        in_specs=[smem] + [vmem] * 8,
+        in_specs=[smem] + [vmem] * 9,
         out_specs=(vmem,) * 3,
         scratch_shapes=[
             pltpu.VMEM((owners * seqs, packed), BF16),
@@ -696,7 +701,7 @@
         ],
         compiler_params=params,
         name="pair_work",
-    )(place, rows, theirs, mapping, left_wide, right_one, offset, cot, pulled)
+    )(place, rows, theirs, mapping, left_wide, right_one, offset, shuffle, cot, pulled)
 
     theirs = lax.ppermute(message, "pc", [(0, 1), (1, 0)])
     output_weight_gradient, left_weight_gradient, right_weight_gradient, alignment = pl.pallas_call(

time: 34.8 us -> 34.7 us (level)
  no operation moved by 1% of the time
where the time goes in v17:
time: 34.7 us; the launch traced here: 34.4 us
  Pallas kernels  13.7 us (39%)
  starting transfers between devices  10.3 us (30%)
  waiting for transfers between devices  5.34 us (15%)
  local copies, waits for them, and re-layouts  4.2 us (12%)
  between operations  0.74 us (2%)
    ppermute x7, starting transfers between devices, swapped_with(): return lax.ppermute(values, axis, [(n, n ^ mask) for n in range(size)])  9.8 us
    pallas_call x1, Pallas kernels, local_gathered(): pl.pallas_call(functools.partial(pair_kernel, offsets), out_shape=(shape(...  7.03 us
    ppermute x7, waiting for transfers between devices, swapped_with(): return lax.ppermute(values, axis, [(n, n ^ mask) for n in range(size)])  4.12 us
    unnamed x16, local copies, waits for them, and re-layouts  2.99 us
    pallas_call x1, Pallas kernels, local_gathered(): pl.pallas_call(pick_kernel, out_shape=(shape((seqs, packed), F32), shape(...  2.06 us
    pallas_call x1, Pallas kernels, local_gathered(): pl.pallas_call(functools.partial(pull_kernel, offsets), out_shape=(shape(...  1.63 us
    pallas_call x1, Pallas kernels, local_gathered(): pl.pallas_call(close_kernel, out_shape=(shape((flat, pair_width), F32), s...  1.39 us
    pallas_call x1, Pallas kernels, local_gathered(): pl.pallas_call(functools.partial(pull_own_kernel, [down for down, _ in of...  1.23 us
  transfers between devices with their start and end apart: 9, of which 5 were waited for; matrix products, arithmetic and copies ran while one was open for 4% of the time, Pallas kernels for 9%

profile of v17, /device:TPU:0, one launch (start us, length us, event | category | flops | bytes accessed | tf_op | source)
XLA Modules:
  0.0 34.4 jit_solution(5154322446827624268)
XLA Ops:
  0.6 2.1 %pick_rows.1 = (f32[64,256]{1,0:T(8,128)}, f32[64,256]{1,0:T(8,128)}, bf16[384,128]{1,0:T(8,128)(2,1)}) custom-call(s32[1,64]{1,0:T(1,128)} %bitcast.44, bf16[256,128]{1,0:T(8,128)(2,1)} %bitcast.42, bf16[256,128]{1,0:T(8,128)(2,1)} %bitcast.43), custom_call_target="tpu_custom_call" | custom-call | tf_op jit(solution)/shard_map/pick_rows/pallas_call | solution.py:583
  2.7 3.1 %collective-permute-start = (bf16[384,128]{1,0:T(8,128)(2,1)}, bf16[384,128]{1,0:T(8,128)(2,1)S(1)}, u32[]{:S(2)}, u32[]{:S(2)}) collective-permute-start(bf16[384,128]{1,0:T(8,128)(2,1)} %get-tuple-element.26.own_ref), channel_id=1, source_target_pairs={{0,4},{4,0},{8,12},{12,8},{1,5},{5,1},{9,13},{13,9},{2,6},{6,2},{1... | collective-permute-start | bytes 294920 | tf_op jit(solution)/shard_map/ppermute | solution.py:610
  5.8 2.6 %collective-permute-start.1 = (bf16[384,128]{1,0:T(8,128)(2,1)}, bf16[384,128]{1,0:T(8,128)(2,1)S(1)}, u32[]{:S(2)}, u32[]{:S(2)}) collective-permute-start(bf16[384,128]{1,0:T(8,128)(2,1)} %get-tuple-element.26.own_ref), channel_id=1, source_target_pairs={{0,8},{4,12},{8,0},{12,4},{1,9},{5,13},{9,1},{13,5},{2,10},{6,14},... | collective-permute-start | bytes 294920 | tf_op jit(solution)/shard_map/ppermute | solution.py:610
  8.4 1.7 %collective-permute-start.3 = (bf16[384,128]{1,0:T(8,128)(2,1)}, bf16[384,128]{1,0:T(8,128)(2,1)S(1)}, u32[]{:S(2)}, u32[]{:S(2)}) collective-permute-start(bf16[384,128]{1,0:T(8,128)(2,1)} %get-tuple-element.26.own_ref), channel_id=1, source_target_pairs={{0,2},{2,0},{1,3},{3,1},{4,6},{6,4},{5,7},{7,5},{8,10},{10,8},{9,1... | collective-permute-start | bytes 294920 | tf_op jit(solution)/shard_map/ppermute | solution.py:610
  10.1 1.1 %copy.12 = bf16[32,32,128]{2,0,1:T(8,128)(2,1)S(1)} copy(bf16[32,32,128]{2,1,0:T(8,128)(2,1)} %bitcast.41) | data formatting | bytes 524288 | tf_op jit(solution)/shard_map/reshape | solution.py:605
  11.2 0.1 copy.14.turned_mapping_ref.mapping_ref
  11.4 0.9 %copy-done = bf16[384,128]{1,0:T(8,128)(2,1)S(1)} copy-done((bf16[384,128]{1,0:T(8,128)(2,1)S(1)}, bf16[384,128]{1,0:T(8,128)(2,1)}, u32[]{:S(2)}) %copy-start) | copy-done | bytes 98328
  12.3 0.7 %copy-done.3 = bf16[64,32]{0,1:T(8,128)(2,1)S(1)} copy-done((bf16[64,32]{0,1:T(8,128)(2,1)S(1)}, bf16[64,32]{0,1:T(8,128)(2,1)}, u32[]{:S(2)}) %copy-start.3) | copy-done | bytes 4120
  13.0 0.7 %copy-done.4 = bf16[64,32]{0,1:T(8,128)(2,1)S(1)} copy-done((bf16[64,32]{0,1:T(8,128)(2,1)S(1)}, bf16[64,32]{0,1:T(8,128)(2,1)}, u32[]{:S(2)}) %copy-start.4) | copy-done | bytes 4120
  13.7 0.7 %copy-done.5 = f32[128]{0:T(128)S(1)} copy-done((f32[128]{0:T(128)S(1)}, f32[128]{0:T(128)}, u32[]{:S(2)}) %copy-start.5) | copy-done | bytes 536
  14.3 0.4 %setup.1 = (bf16[384,128]{1,0:T(8,128)(2,1)S(1)}, bf16[384,128]{1,0:T(8,128)(2,1)S(1)}, bf16[256,512]{1,0:T(8,128)(2,1)S(1)}, bf16[256,128]{1,0:T(8,128)(2,1)S(1...) custom-call(bf16[384,128]{1,0:T(8,128)(2,1)S(1)} %collective-permute-done.first_ref, ...), custom_call_target="tpu_custom_call" | custom-call | tf_op jit(solution)/shard_map/setup/pallas_call | solution.py:615
  14.7 0.4 %collective-permute-start.4 = (bf16[384,128]{1,0:T(8,128)(2,1)S(1)}, bf16[384,128]{1,0:T(8,128)(2,1)S(1)}, u32[]{:S(2)}, u32[]{:S(2)}) collective-permute-start(bf16[384,128]{1,0:T(8,128)(2,1)S(1)} %get-tuple-element.28.refs_1_), channel_id=1, source_target_pairs={{0,2},{2,0},{1,3},{3,1},{4,6},{6,4},{5,7},{7,5},{8,10},{10,8},{9,1... | collective-permute-start | bytes 294920 | tf_op jit(solution)/shard_map/ppermute | solution.py:610
  15.1 1.3 %collective-permute-done.1.refs_2_ = bf16[384,128]{1,0:T(8,128)(2,1)S(1)} collective-permute-done((bf16[384,128]{1,0:T(8,128)(2,1)}, bf16[384,128]{1,0:T(8,128)(2,1)S(1)}, u32[]{:S(2)}, u32[]{:S(2)}) %collective-permute-start.1) | collective-permute-done | bytes 98336 | tf_op jit(solution)/shard_map/ppermute | solution.py:610
  16.4 1.5 %collective-permute-start.5 = (bf16[384,128]{1,0:T(8,128)(2,1)S(1)}, bf16[384,128]{1,0:T(8,128)(2,1)S(1)}, u32[]{:S(2)}, u32[]{:S(2)}) collective-permute-start(bf16[384,128]{1,0:T(8,128)(2,1)S(1)} %collective-permute-done.1.refs_2_), channel_id=1, source_target_pairs={{0,2},{2,0},{1,3},{3,1},{4,6},{6,4},{5,7},{7,5},{8,10},{10,8},{9,1... | collective-permute-start | bytes 294920 | tf_op jit(solution)/shard_map/ppermute | solution.py:610
  17.9 0.5 %collective-permute-start.6 = (bf16[384,128]{1,0:T(8,128)(2,1)S(1)}, bf16[384,128]{1,0:T(8,128)(2,1)S(1)}, u32[]{:S(2)}, u32[]{:S(2)}) collective-permute-start(bf16[384,128]{1,0:T(8,128)(2,1)S(1)} %collective-permute-done.2.refs_3_), channel_id=1, source_target_pairs={{0,2},{2,0},{1,3},{3,1},{4,6},{6,4},{5,7},{7,5},{8,10},{10,8},{9,1... | collective-permute-start | bytes 294920 | tf_op jit(solution)/shard_map/ppermute | solution.py:610
  18.5 1.2 %pull_own.1 = (bf16[4,128,2048]{2,1,0:T(8,128)(2,1)S(1)}, bf16[4,128,128]{2,1,0:T(8,128)(2,1)S(1)}) custom-call(s32[3]{0:T(128)S(1)} %pad_add_fusion.place_ref, bf16[128,1024]{1,0:T(8,128)(2,1)S(1)} %copy.14.turned_mapping_ref.mapping_ref, bf16[384,128]{1,0:T(8,128)(2,1)S(1)} %get-tuple-element.27.refs_0_, bf16[384,128]{1,0:T(8,128)(2,1)S(1)} %get-tuple-element.28.refs_1_, ...), custom_call_target="tpu_custom_call" | custom-call | flops 268435456 | bytes 2621440 | tf_op jit(solution)/shard_map/pull_own/pallas_call | solution.py:652
  19.8 0.6 %collective-permute-done.4.refs_5_ = bf16[384,128]{1,0:T(8,128)(2,1)S(1)} collective-permute-done((bf16[384,128]{1,0:T(8,128)(2,1)S(1)}, bf16[384,128]{1,0:T(8,128)(2,1)S(1)}, u32[]{:S(2)}, u32[]{:S(2)}) %collective-permute-start.4) | collective-permute-done | bytes 98336 | tf_op jit(solution)/shard_map/ppermute | solution.py:610
  20.4 1.0 %collective-permute-done.5.refs_6_ = bf16[384,128]{1,0:T(8,128)(2,1)S(1)} collective-permute-done((bf16[384,128]{1,0:T(8,128)(2,1)S(1)}, bf16[384,128]{1,0:T(8,128)(2,1)S(1)}, u32[]{:S(2)}, u32[]{:S(2)}) %collective-permute-start.5) | collective-permute-done | bytes 98336 | tf_op jit(solution)/shard_map/ppermute | solution.py:610
  21.4 1.1 %collective-permute-done.6.refs_7_ = bf16[384,128]{1,0:T(8,128)(2,1)S(1)} collective-permute-done((bf16[384,128]{1,0:T(8,128)(2,1)S(1)}, bf16[384,128]{1,0:T(8,128)(2,1)S(1)}, u32[]{:S(2)}, u32[]{:S(2)}) %collective-permute-start.6) | collective-permute-done | bytes 98336 | tf_op jit(solution)/shard_map/ppermute | solution.py:610
  22.6 1.6 %pull_back.1 = (bf16[4,2,256,128]{3,2,1,0:T(8,128)(2,1)S(1)}, bf16[4,256,2048]{2,1,0:T(8,128)(2,1)S(1)}) custom-call(s32[3]{0:T(128)S(1)} %pad_add_fusion.place_ref, bf16[128,1024]{1,0:T(8,128)(2,1)S(1)} %copy.14.turned_mapping_ref.mapping_ref, bf16[4,128,2048]{2,1,0:T(8,128)(2,1)S(1)} %get-tuple-element.34.own_ref, ...), custom_call_target="tpu_custom_call" | custom-call | flops 268435456 | bytes 2621440 | tf_op jit(solution)/shard_map/pull_back/pallas_call | solution.py:668
  24.2 7.0 %pair_work.1 = (bf16[16,16,128]{2,1,0:T(8,128)(2,1)}, bf16[2,64,128]{2,1,0:T(8,128)(2,1)S(1)}, bf16[1152,128]{1,0:T(8,128)(2,1)S(1)}) custom-call(s32[3]{0:T(128)S(1)} %pad_add_fusion.place_ref, bf16[8,128,128]{2,1,0:T(8,128)(2,1)S(1)} %fusion.mine_from_ref, bf16[8,128,128]{2,1,0:T(8,128)(2,1)S(1)} %collective-permute-done.7.theirs_from_ref, ...), custom_call_target="tpu_custom_call" | custom-call | tf_op jit(solution)/shard_map/pair_work/pallas_call | solution.py:680
  31.3 0.5 %collective-permute-start.8 = (bf16[1152,128]{1,0:T(8,128)(2,1)S(1)}, bf16[1152,128]{1,0:T(8,128)(2,1)S(1)}, u32[]{:S(2)}, u32[]{:S(2)}) collective-permute-start(bf16[1152,128]{1,0:T(8,128)(2,1)S(1)} %get-tuple-element.39.own_ref), channel_id=1, source_target_pairs={{0,1},{1,0},{2,3},{3,2},{4,5},{5,4},{6,7},{7,6},{8,9},{9,8},{10,11... | collective-permute-start | bytes 884744 | tf_op jit(solution)/shard_map/ppermute | solution.py:706
  31.8 1.2 %collective-permute-done.8.message_ref = bf16[1152,128]{1,0:T(8,128)(2,1)S(1)} collective-permute-done((bf16[1152,128]{1,0:T(8,128)(2,1)S(1)}, bf16[1152,128]{1,0:T(8,128)(2,1)S(1)}, u32[]{:S(2)}, u32[]{:S(2)}) %collective-permute-start.8) | collective-permute-done | bytes 294944 | tf_op jit(solution)/shard_map/ppermute | solution.py:706
  33.0 1.4 %close.1 = (f32[1024,128]{1,0:T(8,128)}, f32[32,64]{1,0:T(8,128)}, f32[32,64]{1,0:T(8,128)}, bf16[64,4,64]{2,1,0:T(4,128)(2,1)}) custom-call(bf16[2,64,128]{2,1,0:T(8,128)(2,1)S(1)} %get-tuple-element.38.grads_ref, bf16[1152,128]{1,0:T(8,128)(2,1)S(1)} %get-tuple-element.39.own_ref, bf16[1152,128]{1,0:T(8,128)(2,1)S(1)} %collective-permute-done.8.message_ref, ...), custom_call_target="tpu_custom_call" | custom-call | tf_op jit(solution)/shard_map/close/pallas_call | solution.py:707
  (20 shorter events, 0.2 us)
Async XLA Ops:
  2.7 8.7 %collective-permute-start = (bf16[384,128]{1,0:T(8,128)(2,1)}, bf16[384,128]{1,0:T(8,128)(2,1)S(1)}, u32[]{:S(2)}, u32[]{:S(2)}) collective-permute-start(bf16[384,128]{1,0:T(8,128)(2,1)} %get-tuple-element.26.own_ref), channel_id=1, source_target_pairs={{0,4},{4,0},{8,12},{12,8},{1,5},{5,1},{9,13},{13,9},{2,6},{6,2},{1... | collective-permute-start | bytes 294920 | tf_op jit(solution)/shard_map/ppermute | solution.py:610
  5.8 10.6 %collective-permute-start.1 = (bf16[384,128]{1,0:T(8,128)(2,1)}, bf16[384,128]{1,0:T(8,128)(2,1)S(1)}, u32[]{:S(2)}, u32[]{:S(2)}) collective-permute-start(bf16[384,128]{1,0:T(8,128)(2,1)} %get-tuple-element.26.own_ref), channel_id=1, source_target_pairs={{0,8},{4,12},{8,0},{12,4},{1,9},{5,13},{9,1},{13,5},{2,10},{6,14},... | collective-permute-start | bytes 294920 | tf_op jit(solution)/shard_map/ppermute | solution.py:610
  8.4 9.6 %collective-permute-start.2 = (bf16[384,128]{1,0:T(8,128)(2,1)}, bf16[384,128]{1,0:T(8,128)(2,1)S(1)}, u32[]{:S(2)}, u32[]{:S(2)}) collective-permute-start(bf16[384,128]{1,0:T(8,128)(2,1)} %get-tuple-element.26.own_ref), channel_id=1, source_target_pairs={{0,12},{4,8},{8,4},{12,0},{1,13},{5,9},{9,5},{13,1},{2,14},{6,10},... | collective-permute-start | bytes 294920 | tf_op jit(solution)/shard_map/ppermute | solution.py:610
  8.4 11.3 %collective-permute-start.3 = (bf16[384,128]{1,0:T(8,128)(2,1)}, bf16[384,128]{1,0:T(8,128)(2,1)S(1)}, u32[]{:S(2)}, u32[]{:S(2)}) collective-permute-start(bf16[384,128]{1,0:T(8,128)(2,1)} %get-tuple-element.26.own_ref), channel_id=1, source_target_pairs={{0,2},{2,0},{1,3},{3,1},{4,6},{6,4},{5,7},{7,5},{8,10},{10,8},{9,1... | collective-permute-start | bytes 294920 | tf_op jit(solution)/shard_map/ppermute | solution.py:610
  11.4 0.9 %copy-start = (bf16[384,128]{1,0:T(8,128)(2,1)S(1)}, bf16[384,128]{1,0:T(8,128)(2,1)}, u32[]{:S(2)}) copy-start(bf16[384,128]{1,0:T(8,128)(2,1)} %get-tuple-element.26.own_ref) | copy-start | bytes 294916
  12.3 0.7 %copy-start.3 = (bf16[64,32]{0,1:T(8,128)(2,1)S(1)}, bf16[64,32]{0,1:T(8,128)(2,1)}, u32[]{:S(2)}) copy-start(bf16[64,32]{0,1:T(8,128)(2,1)} %param.9) | copy-start | bytes 12292
  13.0 0.7 %copy-start.4 = (bf16[64,32]{0,1:T(8,128)(2,1)S(1)}, bf16[64,32]{0,1:T(8,128)(2,1)}, u32[]{:S(2)}) copy-start(bf16[64,32]{0,1:T(8,128)(2,1)} %param.10) | copy-start | bytes 12292
  13.7 0.7 %copy-start.5 = (f32[128]{0:T(128)S(1)}, f32[128]{0:T(128)}, u32[]{:S(2)}) copy-start(f32[128]{0:T(128)} %param.12) | copy-start | bytes 1540
  14.7 5.6 %collective-permute-start.4 = (bf16[384,128]{1,0:T(8,128)(2,1)S(1)}, bf16[384,128]{1,0:T(8,128)(2,1)S(1)}, u32[]{:S(2)}, u32[]{:S(2)}) collective-permute-start(bf16[384,128]{1,0:T(8,128)(2,1)S(1)} %get-tuple-element.28.refs_1_), channel_id=1, source_target_pairs={{0,2},{2,0},{1,3},{3,1},{4,6},{6,4},{5,7},{7,5},{8,10},{10,8},{9,1... | collective-permute-start | bytes 294920 | tf_op jit(solution)/shard_map/ppermute | solution.py:610
  16.4 5.0 %collective-permute-start.5 = (bf16[384,128]{1,0:T(8,128)(2,1)S(1)}, bf16[384,128]{1,0:T(8,128)(2,1)S(1)}, u32[]{:S(2)}, u32[]{:S(2)}) collective-permute-start(bf16[384,128]{1,0:T(8,128)(2,1)S(1)} %collective-permute-done.1.refs_2_), channel_id=1, source_target_pairs={{0,2},{2,0},{1,3},{3,1},{4,6},{6,4},{5,7},{7,5},{8,10},{10,8},{9,1... | collective-permute-start | bytes 294920 | tf_op jit(solution)/shard_map/ppermute | solution.py:610
  17.9 4.6 %collective-permute-start.6 = (bf16[384,128]{1,0:T(8,128)(2,1)S(1)}, bf16[384,128]{1,0:T(8,128)(2,1)S(1)}, u32[]{:S(2)}, u32[]{:S(2)}) collective-permute-start(bf16[384,128]{1,0:T(8,128)(2,1)S(1)} %collective-permute-done.2.refs_3_), channel_id=1, source_target_pairs={{0,2},{2,0},{1,3},{3,1},{4,6},{6,4},{5,7},{7,5},{8,10},{10,8},{9,1... | collective-permute-start | bytes 294920 | tf_op jit(solution)/shard_map/ppermute | solution.py:610
  22.6 1.7 %collective-permute-start.7 = (bf16[8,128,128]{2,1,0:T(8,128)(2,1)S(1)}, bf16[8,128,128]{2,1,0:T(8,128)(2,1)S(1)}, u32[]{:S(2)}, u32[]{:S(2)}) collective-permute-start(bf16[8,128,128]{2,1,0:T(8,128)(2,1)S(1)} %fusion.mine_from_ref), channel_id=1, source_target_pairs={{0,1},{1,0},{2,3},{3,2},{4,5},{5,4},{6,7},{7,6},{8,9},{9,8},{10,11... | collective-permute-start | bytes 786440 | tf_op jit(solution)/shard_map/ppermute | solution.py:667
  22.6 10.4 %copy-start.1 = (f32[64,256]{1,0:T(8,128)S(1)}, f32[64,256]{1,0:T(8,128)}, u32[]{:S(2)}) copy-start(f32[64,256]{1,0:T(8,128)} %get-tuple-element.40.normed_ref) | copy-start | bytes 196612
  22.6 10.4 %copy-start.2 = (f32[64,256]{1,0:T(8,128)S(1)}, f32[64,256]{1,0:T(8,128)}, u32[]{:S(2)}) copy-start(f32[64,256]{1,0:T(8,128)} %get-tuple-element.41.inverse_ref) | copy-start | bytes 196612
  31.3 1.7 %collective-permute-start.8 = (bf16[1152,128]{1,0:T(8,128)(2,1)S(1)}, bf16[1152,128]{1,0:T(8,128)(2,1)S(1)}, u32[]{:S(2)}, u32[]{:S(2)}) collective-permute-start(bf16[1152,128]{1,0:T(8,128)(2,1)S(1)} %get-tuple-element.39.own_ref), channel_id=1, source_target_pairs={{0,1},{1,0},{2,3},{3,2},{4,5},{5,4},{6,7},{7,6},{8,9},{9,8},{10,11... | collective-permute-start | bytes 884744 | tf_op jit(solution)/shard_map/ppermute | solution.py:706

commit v18 on v17

--- a/solution.py
+++ b/solution.py
@@ -475,10 +475,10 @@
                 for t in range(tokens)
             ]
             left_back[row * step_owners + o] = fold_tokens(parts).astype(BF16)
-        sum_part = dot(pulled, block, contract=(1, 1))
+        sum_part = dot(block, pulled, contract=(1, 1))
         sums[...] = sum_part if row == 0 else sums[...] + sum_part
 
-    back = (sums[...].T * (1.0 / seqs)).astype(BF16)
+    back = (sums[...] * (1.0 / seqs)).astype(BF16)
     back = jnp.concatenate(
         [
             jnp.concatenate(
@@ -696,7 +696,7 @@
             pltpu.VMEM((columns, tokens * seqs), BF16),
             pltpu.VMEM((owners, seqs, LANES), BF16),
             pltpu.VMEM((groups * prow_n, seqs, LANES), BF16),
-            pltpu.VMEM((columns, tokens * seqs), F32),
+            pltpu.VMEM((tokens * seqs, columns), F32),
             pltpu.VMEM((pair_width, flat), F32),
         ],
         compiler_params=params,

time: 34.7 us -> 34.5 us (level)
  no operation moved by 1% of the time
where the time goes in v18:
time: 34.5 us; the launch traced here: 34.2 us
  Pallas kernels  13.5 us (39%)
  starting transfers between devices  10.3 us (30%)
  waiting for transfers between devices  5.34 us (15%)
  local copies, waits for them, and re-layouts  4.2 us (12%)
  between operations  0.74 us (2%)
    ppermute x7, starting transfers between devices, swapped_with(): return lax.ppermute(values, axis, [(n, n ^ mask) for n in range(size)])  9.8 us
    pallas_call x1, Pallas kernels, local_gathered(): pl.pallas_call(functools.partial(pair_kernel, offsets), out_shape=(shape(...  6.82 us
    ppermute x7, waiting for transfers between devices, swapped_with(): return lax.ppermute(values, axis, [(n, n ^ mask) for n in range(size)])  4.12 us
    unnamed x16, local copies, waits for them, and re-layouts  2.99 us
    pallas_call x1, Pallas kernels, local_gathered(): pl.pallas_call(pick_kernel, out_shape=(shape((seqs, packed), F32), shape(...  2.06 us
    pallas_call x1, Pallas kernels, local_gathered(): pl.pallas_call(functools.partial(pull_kernel, offsets), out_shape=(shape(...  1.63 us
    pallas_call x1, Pallas kernels, local_gathered(): pl.pallas_call(close_kernel, out_shape=(shape((flat, pair_width), F32), s...  1.39 us
    pallas_call x1, Pallas kernels, local_gathered(): pl.pallas_call(functools.partial(pull_own_kernel, [down for down, _ in of...  1.23 us
  transfers between devices with their start and end apart: 9, of which 5 were waited for; matrix products, arithmetic and copies ran while one was open for 4% of the time, Pallas kernels for 9%

profile of v18, /device:TPU:0, one launch (start us, length us, event | category | flops | bytes accessed | tf_op | source)
XLA Modules:
  0.0 34.2 jit_solution(6300243219707186704)
XLA Ops:
  0.6 2.1 %pick_rows.1 = (f32[64,256]{1,0:T(8,128)}, f32[64,256]{1,0:T(8,128)}, bf16[384,128]{1,0:T(8,128)(2,1)}) custom-call(s32[1,64]{1,0:T(1,128)} %bitcast.44, bf16[256,128]{1,0:T(8,128)(2,1)} %bitcast.42, bf16[256,128]{1,0:T(8,128)(2,1)} %bitcast.43), custom_call_target="tpu_custom_call" | custom-call | tf_op jit(solution)/shard_map/pick_rows/pallas_call | solution.py:583
  2.7 3.1 %collective-permute-start = (bf16[384,128]{1,0:T(8,128)(2,1)}, bf16[384,128]{1,0:T(8,128)(2,1)S(1)}, u32[]{:S(2)}, u32[]{:S(2)}) collective-permute-start(bf16[384,128]{1,0:T(8,128)(2,1)} %get-tuple-element.26.own_ref), channel_id=1, source_target_pairs={{0,4},{4,0},{8,12},{12,8},{1,5},{5,1},{9,13},{13,9},{2,6},{6,2},{1... | collective-permute-start | bytes 294920 | tf_op jit(solution)/shard_map/ppermute | solution.py:610
  5.8 2.6 %collective-permute-start.1 = (bf16[384,128]{1,0:T(8,128)(2,1)}, bf16[384,128]{1,0:T(8,128)(2,1)S(1)}, u32[]{:S(2)}, u32[]{:S(2)}) collective-permute-start(bf16[384,128]{1,0:T(8,128)(2,1)} %get-tuple-element.26.own_ref), channel_id=1, source_target_pairs={{0,8},{4,12},{8,0},{12,4},{1,9},{5,13},{9,1},{13,5},{2,10},{6,14},... | collective-permute-start | bytes 294920 | tf_op jit(solution)/shard_map/ppermute | solution.py:610
  8.4 1.7 %collective-permute-start.3 = (bf16[384,128]{1,0:T(8,128)(2,1)}, bf16[384,128]{1,0:T(8,128)(2,1)S(1)}, u32[]{:S(2)}, u32[]{:S(2)}) collective-permute-start(bf16[384,128]{1,0:T(8,128)(2,1)} %get-tuple-element.26.own_ref), channel_id=1, source_target_pairs={{0,2},{2,0},{1,3},{3,1},{4,6},{6,4},{5,7},{7,5},{8,10},{10,8},{9,1... | collective-permute-start | bytes 294920 | tf_op jit(solution)/shard_map/ppermute | solution.py:610
  10.1 1.1 %copy.12 = bf16[32,32,128]{2,0,1:T(8,128)(2,1)S(1)} copy(bf16[32,32,128]{2,1,0:T(8,128)(2,1)} %bitcast.41) | data formatting | bytes 524288 | tf_op jit(solution)/shard_map/reshape | solution.py:605
  11.2 0.1 copy.14.turned_mapping_ref.mapping_ref
  11.4 0.9 %copy-done = bf16[384,128]{1,0:T(8,128)(2,1)S(1)} copy-done((bf16[384,128]{1,0:T(8,128)(2,1)S(1)}, bf16[384,128]{1,0:T(8,128)(2,1)}, u32[]{:S(2)}) %copy-start) | copy-done | bytes 98328
  12.3 0.7 %copy-done.3 = bf16[64,32]{0,1:T(8,128)(2,1)S(1)} copy-done((bf16[64,32]{0,1:T(8,128)(2,1)S(1)}, bf16[64,32]{0,1:T(8,128)(2,1)}, u32[]{:S(2)}) %copy-start.3) | copy-done | bytes 4120
  13.0 0.7 %copy-done.4 = bf16[64,32]{0,1:T(8,128)(2,1)S(1)} copy-done((bf16[64,32]{0,1:T(8,128)(2,1)S(1)}, bf16[64,32]{0,1:T(8,128)(2,1)}, u32[]{:S(2)}) %copy-start.4) | copy-done | bytes 4120
  13.7 0.7 %copy-done.5 = f32[128]{0:T(128)S(1)} copy-done((f32[128]{0:T(128)S(1)}, f32[128]{0:T(128)}, u32[]{:S(2)}) %copy-start.5) | copy-done | bytes 536
  14.3 0.4 %setup.1 = (bf16[384,128]{1,0:T(8,128)(2,1)S(1)}, bf16[384,128]{1,0:T(8,128)(2,1)S(1)}, bf16[256,512]{1,0:T(8,128)(2,1)S(1)}, bf16[256,128]{1,0:T(8,128)(2,1)S(1...) custom-call(bf16[384,128]{1,0:T(8,128)(2,1)S(1)} %collective-permute-done.first_ref, ...), custom_call_target="tpu_custom_call" | custom-call | tf_op jit(solution)/shard_map/setup/pallas_call | solution.py:615
  14.7 0.4 %collective-permute-start.4 = (bf16[384,128]{1,0:T(8,128)(2,1)S(1)}, bf16[384,128]{1,0:T(8,128)(2,1)S(1)}, u32[]{:S(2)}, u32[]{:S(2)}) collective-permute-start(bf16[384,128]{1,0:T(8,128)(2,1)S(1)} %get-tuple-element.28.refs_1_), channel_id=1, source_target_pairs={{0,2},{2,0},{1,3},{3,1},{4,6},{6,4},{5,7},{7,5},{8,10},{10,8},{9,1... | collective-permute-start | bytes 294920 | tf_op jit(solution)/shard_map/ppermute | solution.py:610
  15.1 1.3 %collective-permute-done.1.refs_2_ = bf16[384,128]{1,0:T(8,128)(2,1)S(1)} collective-permute-done((bf16[384,128]{1,0:T(8,128)(2,1)}, bf16[384,128]{1,0:T(8,128)(2,1)S(1)}, u32[]{:S(2)}, u32[]{:S(2)}) %collective-permute-start.1) | collective-permute-done | bytes 98336 | tf_op jit(solution)/shard_map/ppermute | solution.py:610
  16.4 1.5 %collective-permute-start.5 = (bf16[384,128]{1,0:T(8,128)(2,1)S(1)}, bf16[384,128]{1,0:T(8,128)(2,1)S(1)}, u32[]{:S(2)}, u32[]{:S(2)}) collective-permute-start(bf16[384,128]{1,0:T(8,128)(2,1)S(1)} %collective-permute-done.1.refs_2_), channel_id=1, source_target_pairs={{0,2},{2,0},{1,3},{3,1},{4,6},{6,4},{5,7},{7,5},{8,10},{10,8},{9,1... | collective-permute-start | bytes 294920 | tf_op jit(solution)/shard_map/ppermute | solution.py:610
  17.9 0.5 %collective-permute-start.6 = (bf16[384,128]{1,0:T(8,128)(2,1)S(1)}, bf16[384,128]{1,0:T(8,128)(2,1)S(1)}, u32[]{:S(2)}, u32[]{:S(2)}) collective-permute-start(bf16[384,128]{1,0:T(8,128)(2,1)S(1)} %collective-permute-done.2.refs_3_), channel_id=1, source_target_pairs={{0,2},{2,0},{1,3},{3,1},{4,6},{6,4},{5,7},{7,5},{8,10},{10,8},{9,1... | collective-permute-start | bytes 294920 | tf_op jit(solution)/shard_map/ppermute | solution.py:610
  18.5 1.2 %pull_own.1 = (bf16[4,128,2048]{2,1,0:T(8,128)(2,1)S(1)}, bf16[4,128,128]{2,1,0:T(8,128)(2,1)S(1)}) custom-call(s32[3]{0:T(128)S(1)} %pad_add_fusion.place_ref, bf16[128,1024]{1,0:T(8,128)(2,1)S(1)} %copy.14.turned_mapping_ref.mapping_ref, bf16[384,128]{1,0:T(8,128)(2,1)S(1)} %get-tuple-element.27.refs_0_, bf16[384,128]{1,0:T(8,128)(2,1)S(1)} %get-tuple-element.28.refs_1_, ...), custom_call_target="tpu_custom_call" | custom-call | flops 268435456 | bytes 2621440 | tf_op jit(solution)/shard_map/pull_own/pallas_call | solution.py:652
  19.8 0.6 %collective-permute-done.4.refs_5_ = bf16[384,128]{1,0:T(8,128)(2,1)S(1)} collective-permute-done((bf16[384,128]{1,0:T(8,128)(2,1)S(1)}, bf16[384,128]{1,0:T(8,128)(2,1)S(1)}, u32[]{:S(2)}, u32[]{:S(2)}) %collective-permute-start.4) | collective-permute-done | bytes 98336 | tf_op jit(solution)/shard_map/ppermute | solution.py:610
  20.4 1.0 %collective-permute-done.5.refs_6_ = bf16[384,128]{1,0:T(8,128)(2,1)S(1)} collective-permute-done((bf16[384,128]{1,0:T(8,128)(2,1)S(1)}, bf16[384,128]{1,0:T(8,128)(2,1)S(1)}, u32[]{:S(2)}, u32[]{:S(2)}) %collective-permute-start.5) | collective-permute-done | bytes 98336 | tf_op jit(solution)/shard_map/ppermute | solution.py:610
  21.4 1.1 %collective-permute-done.6.refs_7_ = bf16[384,128]{1,0:T(8,128)(2,1)S(1)} collective-permute-done((bf16[384,128]{1,0:T(8,128)(2,1)S(1)}, bf16[384,128]{1,0:T(8,128)(2,1)S(1)}, u32[]{:S(2)}, u32[]{:S(2)}) %collective-permute-start.6) | collective-permute-done | bytes 98336 | tf_op jit(solution)/shard_map/ppermute | solution.py:610
  22.6 1.6 %pull_back.1 = (bf16[4,2,256,128]{3,2,1,0:T(8,128)(2,1)S(1)}, bf16[4,256,2048]{2,1,0:T(8,128)(2,1)S(1)}) custom-call(s32[3]{0:T(128)S(1)} %pad_add_fusion.place_ref, bf16[128,1024]{1,0:T(8,128)(2,1)S(1)} %copy.14.turned_mapping_ref.mapping_ref, bf16[4,128,2048]{2,1,0:T(8,128)(2,1)S(1)} %get-tuple-element.34.own_ref, ...), custom_call_target="tpu_custom_call" | custom-call | flops 268435456 | bytes 2621440 | tf_op jit(solution)/shard_map/pull_back/pallas_call | solution.py:668
  24.2 6.8 %pair_work.1 = (bf16[16,16,128]{2,1,0:T(8,128)(2,1)}, bf16[2,64,128]{2,1,0:T(8,128)(2,1)S(1)}, bf16[1152,128]{1,0:T(8,128)(2,1)S(1)}) custom-call(s32[3]{0:T(128)S(1)} %pad_add_fusion.place_ref, bf16[8,128,128]{2,1,0:T(8,128)(2,1)S(1)} %fusion.mine_from_ref, bf16[8,128,128]{2,1,0:T(8,128)(2,1)S(1)} %collective-permute-done.7.theirs_from_ref, ...), custom_call_target="tpu_custom_call" | custom-call | tf_op jit(solution)/shard_map/pair_work/pallas_call | solution.py:680
  31.1 0.5 %collective-permute-start.8 = (bf16[1152,128]{1,0:T(8,128)(2,1)S(1)}, bf16[1152,128]{1,0:T(8,128)(2,1)S(1)}, u32[]{:S(2)}, u32[]{:S(2)}) collective-permute-start(bf16[1152,128]{1,0:T(8,128)(2,1)S(1)} %get-tuple-element.39.own_ref), channel_id=1, source_target_pairs={{0,1},{1,0},{2,3},{3,2},{4,5},{5,4},{6,7},{7,6},{8,9},{9,8},{10,11... | collective-permute-start | bytes 884744 | tf_op jit(solution)/shard_map/ppermute | solution.py:706
  31.6 1.2 %collective-permute-done.8.message_ref = bf16[1152,128]{1,0:T(8,128)(2,1)S(1)} collective-permute-done((bf16[1152,128]{1,0:T(8,128)(2,1)S(1)}, bf16[1152,128]{1,0:T(8,128)(2,1)S(1)}, u32[]{:S(2)}, u32[]{:S(2)}) %collective-permute-start.8) | collective-permute-done | bytes 294944 | tf_op jit(solution)/shard_map/ppermute | solution.py:706
  32.8 1.4 %close.1 = (f32[1024,128]{1,0:T(8,128)}, f32[32,64]{1,0:T(8,128)}, f32[32,64]{1,0:T(8,128)}, bf16[64,4,64]{2,1,0:T(4,128)(2,1)}) custom-call(bf16[2,64,128]{2,1,0:T(8,128)(2,1)S(1)} %get-tuple-element.38.grads_ref, bf16[1152,128]{1,0:T(8,128)(2,1)S(1)} %get-tuple-element.39.own_ref, bf16[1152,128]{1,0:T(8,128)(2,1)S(1)} %collective-permute-done.8.message_ref, ...), custom_call_target="tpu_custom_call" | custom-call | tf_op jit(solution)/shard_map/close/pallas_call | solution.py:707
  (20 shorter events, 0.2 us)
Async XLA Ops:
  2.7 8.7 %collective-permute-start = (bf16[384,128]{1,0:T(8,128)(2,1)}, bf16[384,128]{1,0:T(8,128)(2,1)S(1)}, u32[]{:S(2)}, u32[]{:S(2)}) collective-permute-start(bf16[384,128]{1,0:T(8,128)(2,1)} %get-tuple-element.26.own_ref), channel_id=1, source_target_pairs={{0,4},{4,0},{8,12},{12,8},{1,5},{5,1},{9,13},{13,9},{2,6},{6,2},{1... | collective-permute-start | bytes 294920 | tf_op jit(solution)/shard_map/ppermute | solution.py:610
  5.8 10.6 %collective-permute-start.1 = (bf16[384,128]{1,0:T(8,128)(2,1)}, bf16[384,128]{1,0:T(8,128)(2,1)S(1)}, u32[]{:S(2)}, u32[]{:S(2)}) collective-permute-start(bf16[384,128]{1,0:T(8,128)(2,1)} %get-tuple-element.26.own_ref), channel_id=1, source_target_pairs={{0,8},{4,12},{8,0},{12,4},{1,9},{5,13},{9,1},{13,5},{2,10},{6,14},... | collective-permute-start | bytes 294920 | tf_op jit(solution)/shard_map/ppermute | solution.py:610
  8.4 9.6 %collective-permute-start.2 = (bf16[384,128]{1,0:T(8,128)(2,1)}, bf16[384,128]{1,0:T(8,128)(2,1)S(1)}, u32[]{:S(2)}, u32[]{:S(2)}) collective-permute-start(bf16[384,128]{1,0:T(8,128)(2,1)} %get-tuple-element.26.own_ref), channel_id=1, source_target_pairs={{0,12},{4,8},{8,4},{12,0},{1,13},{5,9},{9,5},{13,1},{2,14},{6,10},... | collective-permute-start | bytes 294920 | tf_op jit(solution)/shard_map/ppermute | solution.py:610
  8.4 11.3 %collective-permute-start.3 = (bf16[384,128]{1,0:T(8,128)(2,1)}, bf16[384,128]{1,0:T(8,128)(2,1)S(1)}, u32[]{:S(2)}, u32[]{:S(2)}) collective-permute-start(bf16[384,128]{1,0:T(8,128)(2,1)} %get-tuple-element.26.own_ref), channel_id=1, source_target_pairs={{0,2},{2,0},{1,3},{3,1},{4,6},{6,4},{5,7},{7,5},{8,10},{10,8},{9,1... | collective-permute-start | bytes 294920 | tf_op jit(solution)/shard_map/ppermute | solution.py:610
  11.4 0.9 %copy-start = (bf16[384,128]{1,0:T(8,128)(2,1)S(1)}, bf16[384,128]{1,0:T(8,128)(2,1)}, u32[]{:S(2)}) copy-start(bf16[384,128]{1,0:T(8,128)(2,1)} %get-tuple-element.26.own_ref) | copy-start | bytes 294916
  12.3 0.7 %copy-start.3 = (bf16[64,32]{0,1:T(8,128)(2,1)S(1)}, bf16[64,32]{0,1:T(8,128)(2,1)}, u32[]{:S(2)}) copy-start(bf16[64,32]{0,1:T(8,128)(2,1)} %param.9) | copy-start | bytes 12292
  13.0 0.7 %copy-start.4 = (bf16[64,32]{0,1:T(8,128)(2,1)S(1)}, bf16[64,32]{0,1:T(8,128)(2,1)}, u32[]{:S(2)}) copy-start(bf16[64,32]{0,1:T(8,128)(2,1)} %param.10) | copy-start | bytes 12292
  13.7 0.7 %copy-start.5 = (f32[128]{0:T(128)S(1)}, f32[128]{0:T(128)}, u32[]{:S(2)}) copy-start(f32[128]{0:T(128)} %param.12) | copy-start | bytes 1540
  14.7 5.6 %collective-permute-start.4 = (bf16[384,128]{1,0:T(8,128)(2,1)S(1)}, bf16[384,128]{1,0:T(8,128)(2,1)S(1)}, u32[]{:S(2)}, u32[]{:S(2)}) collective-permute-start(bf16[384,128]{1,0:T(8,128)(2,1)S(1)} %get-tuple-element.28.refs_1_), channel_id=1, source_target_pairs={{0,2},{2,0},{1,3},{3,1},{4,6},{6,4},{5,7},{7,5},{8,10},{10,8},{9,1... | collective-permute-start | bytes 294920 | tf_op jit(solution)/shard_map/ppermute | solution.py:610
  16.4 5.0 %collective-permute-start.5 = (bf16[384,128]{1,0:T(8,128)(2,1)S(1)}, bf16[384,128]{1,0:T(8,128)(2,1)S(1)}, u32[]{:S(2)}, u32[]{:S(2)}) collective-permute-start(bf16[384,128]{1,0:T(8,128)(2,1)S(1)} %collective-permute-done.1.refs_2_), channel_id=1, source_target_pairs={{0,2},{2,0},{1,3},{3,1},{4,6},{6,4},{5,7},{7,5},{8,10},{10,8},{9,1... | collective-permute-start | bytes 294920 | tf_op jit(solution)/shard_map/ppermute | solution.py:610
  17.9 4.6 %collective-permute-start.6 = (bf16[384,128]{1,0:T(8,128)(2,1)S(1)}, bf16[384,128]{1,0:T(8,128)(2,1)S(1)}, u32[]{:S(2)}, u32[]{:S(2)}) collective-permute-start(bf16[384,128]{1,0:T(8,128)(2,1)S(1)} %collective-permute-done.2.refs_3_), channel_id=1, source_target_pairs={{0,2},{2,0},{1,3},{3,1},{4,6},{6,4},{5,7},{7,5},{8,10},{10,8},{9,1... | collective-permute-start | bytes 294920 | tf_op jit(solution)/shard_map/ppermute | solution.py:610
  22.6 1.7 %collective-permute-start.7 = (bf16[8,128,128]{2,1,0:T(8,128)(2,1)S(1)}, bf16[8,128,128]{2,1,0:T(8,128)(2,1)S(1)}, u32[]{:S(2)}, u32[]{:S(2)}) collective-permute-start(bf16[8,128,128]{2,1,0:T(8,128)(2,1)S(1)} %fusion.mine_from_ref), channel_id=1, source_target_pairs={{0,1},{1,0},{2,3},{3,2},{4,5},{5,4},{6,7},{7,6},{8,9},{9,8},{10,11... | collective-permute-start | bytes 786440 | tf_op jit(solution)/shard_map/ppermute | solution.py:667
  22.6 10.2 %copy-start.1 = (f32[64,256]{1,0:T(8,128)S(1)}, f32[64,256]{1,0:T(8,128)}, u32[]{:S(2)}) copy-start(f32[64,256]{1,0:T(8,128)} %get-tuple-element.40.normed_ref) | copy-start | bytes 196612
  22.6 10.2 %copy-start.2 = (f32[64,256]{1,0:T(8,128)S(1)}, f32[64,256]{1,0:T(8,128)}, u32[]{:S(2)}) copy-start(f32[64,256]{1,0:T(8,128)} %get-tuple-element.41.inverse_ref) | copy-start | bytes 196612
  31.1 1.7 %collective-permute-start.8 = (bf16[1152,128]{1,0:T(8,128)(2,1)S(1)}, bf16[1152,128]{1,0:T(8,128)(2,1)S(1)}, u32[]{:S(2)}, u32[]{:S(2)}) collective-permute-start(bf16[1152,128]{1,0:T(8,128)(2,1)S(1)} %get-tuple-element.39.own_ref), channel_id=1, source_target_pairs={{0,1},{1,0},{2,3},{3,2},{4,5},{5,4},{6,7},{7,6},{8,9},{9,8},{10,11... | collective-permute-start | bytes 884744 | tf_op jit(solution)/shard_map/ppermute | solution.py:706
